TPU v7x, 32 devices: a whole 2x2x4 slice. The times are simulated.
32 devices in a mesh: dp: 8 (over y, x, core), mp: 4 (over z).
Axes of the slice: x: 2, y: 2, z: 4, core: 2. Of those that a mesh axis runs over, the one named last changes fastest.
Arguments:
- hidden_in: bfloat16 [8192, 2048], P(('dp', 'mp')), may hold values from -6 to 6
- cotangent: bfloat16 [8192, 2048], P(('dp', 'mp')), may hold values from -6 to 6
- doc_lengths: int32 [8, 4], P('dp'), may hold values from 1 to 640, 1024 in all within a row
- owner: int32 [8], replicated, may hold values from 0 to 7, each once
- projection_master_weight: float32 [2048, 4096], P('dp', 'mp'), may hold values from -0.125 to 0.125
- gateup_weight: float32 [2048, 12288], P('dp', 'mp'), may hold values from -0.125 to 0.125
- out_weight: float32 [2048, 2048], P(('mp', 'dp')), may hold values from -0.75 to 0.75
- down_weight: float32 [6144, 2048], P(('mp', 'dp')), may hold values from -0.078125 to 0.078125
- projection_first_moment: float32 [2048, 4096], P('dp', 'mp'), may hold values from -9.1552734e-05 to 9.1552734e-05
- gateup_first: float32 [2048, 12288], P('dp', 'mp'), may hold values from -9.1552734e-05 to 9.1552734e-05
- out_first: float32 [2048, 2048], P(('mp', 'dp')), may hold values from -3.0517578e-05 to 3.0517578e-05
- down_first: float32 [6144, 2048], P(('mp', 'dp')), may hold values from -9.1552734e-05 to 9.1552734e-05
- projection_second_moment: float32 [2048, 4096], P('dp', 'mp'), may hold values from 1.0529243e-09 to 4.1719646e-09
- gateup_second: float32 [2048, 12288], P('dp', 'mp'), may hold values from 1.0529243e-09 to 4.1719646e-09
- out_second: float32 [2048, 2048], P(('mp', 'dp')), may hold values from 1.5893198e-10 to 6.357279e-10
- down_second: float32 [6144, 2048], P(('mp', 'dp')), may hold values from 1.0529243e-09 to 4.1719646e-09
- gains: float32 [4352], replicated, may hold values from 0.3 to 1.5
- gain_first: float32 [4352], replicated, may hold values from -0.00024414062 to 0.00024414062
- gain_second: float32 [4352], replicated, may hold values from 9.337254e-09 to 3.7746343e-08
Outputs:
- output: bfloat16 [8192, 2048], P(('dp', 'mp'))
- input_grad: float32 [8192, 2048], P(('dp', 'mp'))
- qkv_new: float32 [2048, 4096], P('dp', 'mp')
- gateup_new: float32 [2048, 12288], P('dp', 'mp')
- out_new: float32 [2048, 2048], P(('mp', 'dp'))
- down_new: float32 [6144, 2048], P(('mp', 'dp'))
- qkv_first_new: float32 [2048, 4096], P('dp', 'mp')
- gateup_first_new: float32 [2048, 12288], P('dp', 'mp')
- out_first_new: float32 [2048, 2048], P(('mp', 'dp'))
- down_first_new: float32 [6144, 2048], P(('mp', 'dp'))
- qkv_second_new: float32 [2048, 4096], P('dp', 'mp')
- gateup_second_new: float32 [2048, 12288], P('dp', 'mp')
- out_second_new: float32 [2048, 2048], P(('mp', 'dp'))
- down_second_new: float32 [6144, 2048], P(('mp', 'dp'))
- gains_new: float32 [4352], replicated
- gain_first_new: float32 [4352], replicated
- gain_second_new: float32 [4352], replicated
- grad_norm: float32 [], replicated
Inputs may be any that keep to these rules, and one draw needn't show every extreme that they name: `doc_lengths`: each row sums to 1024; its longest document has exactly 640 tokens. `owner`: a permutation: each stored block number once.
All inputs are finite; a program needn't handle non-finite values.
Results may differ from a plain program's by a relative error of at most 0.02.
Values may be sent and summed in bfloat16 or wider, within the bound.
A program may use at most 256 MiB of HBM per device.

v0:
```python
import jax
import jax.numpy as jnp
from jax import lax
from jax.sharding import PartitionSpec as P

MODEL_WIDTH = 2048
QUERY_HEADS = 16
KEY_VALUE_HEADS = 8
HEAD_SIZE = 128
FF = 6144
STEP = 10


EPS_NORM = 1e-06
THETA = 1000000.0
LEARN = 0.03
GAIN_LEARN = 0.5
FIRST_DECAY = 0.9
SECOND_DECAY = 0.95
ADAM_EPS = 1e-08
WEIGHT_DECAY = 0.1
CLIP_LIMIT = 1.0
MASKED = -1e30


def rms_norm(value_rows, gain):
    return (
        value_rows
        * lax.rsqrt(jnp.mean(value_rows * value_rows, axis=-1, keepdims=True) + EPS_NORM)
        * gain
    )


def norm_back(value_rows, gain, grad):
    score_scale = lax.rsqrt(jnp.mean(value_rows * value_rows, axis=-1, keepdims=True) + EPS_NORM)
    normed_input = value_rows * score_scale
    d_normal = grad * gain
    d_values = score_scale * (
        d_normal - normed_input * jnp.mean(d_normal * normed_input, axis=-1, keepdims=True)
    )
    d_gain = jnp.sum((grad * normed_input).reshape(-1, value_rows.shape[-1]), axis=0)
    return (d_values, d_gain)


def turned(value_rows):
    half = value_rows.shape[-1] // 2
    return jnp.concatenate([-value_rows[..., half:], value_rows[..., :half]], axis=-1)


def rotate(value_rows, cosine, sine):
    return value_rows * cosine + turned(value_rows) * sine


def rotate_back(grad, cosine, sine):
    return grad * cosine - turned(grad * sine)


def rope_tables(lengths, count):
    ends = jnp.cumsum(lengths)
    starts = ends - lengths
    places = jnp.arange(count, dtype=jnp.int32)
    doc_of = jnp.sum((places[:, None] >= ends[None, :]).astype(jnp.int32), axis=1)
    chosen = doc_of[:, None] == jnp.arange(lengths.shape[0], dtype=jnp.int32)[None, :]
    begin = jnp.sum(jnp.where(chosen, starts[None, :], 0), axis=1)
    offset = (places - begin).astype(jnp.float32)
    half = HEAD_SIZE // 2
    freq = THETA ** (-(2.0 * jnp.arange(half, dtype=jnp.float32)) / HEAD_SIZE)
    angle = offset[:, None] * freq[None, :]
    angle = jnp.concatenate([angle, angle], axis=-1)
    return (doc_of, jnp.cos(angle), jnp.sin(angle))


def arrange(gathered, order, blocks_count):
    blocks = gathered.reshape(blocks_count, gathered.shape[0] // blocks_count, gathered.shape[1])
    return jnp.take(blocks, order, axis=0).reshape(gathered.shape)


def fetch_weights(
    projection_master_weight, gateup_weight, out_weight, down_weight, owner, blocks_count
):
    gathered = (
        lax.all_gather(projection_master_weight.astype(jnp.bfloat16), "dp", axis=0, tiled=True),
        lax.all_gather(gateup_weight.astype(jnp.bfloat16), "dp", axis=0, tiled=True),
        lax.all_gather(out_weight.astype(jnp.bfloat16), "dp", axis=0, tiled=True),
        lax.all_gather(down_weight.astype(jnp.bfloat16), "dp", axis=0, tiled=True),
    )
    return tuple((arrange(piece, owner, blocks_count) for piece in gathered))


def fetch_again(
    projection_master_weight, gateup_weight, out_weight, down_weight, owner, blocks_count
):
    gathered = (
        lax.all_gather(projection_master_weight.astype(jnp.bfloat16), "dp", axis=0, tiled=True),
        lax.all_gather(gateup_weight.astype(jnp.bfloat16), "dp", axis=0, tiled=True),
        lax.all_gather(out_weight.astype(jnp.bfloat16), "dp", axis=0, tiled=True),
        lax.all_gather(down_weight.astype(jnp.bfloat16), "dp", axis=0, tiled=True),
    )
    return tuple((arrange(piece, owner, blocks_count) for piece in gathered))


def collect(rows):
    return lax.all_gather(rows, "mp", axis=0, tiled=True)


def collect_back(rows):
    return lax.all_gather(rows, "mp", axis=0, tiled=True)


def spread(operand, weight, rows):

    def term(start, count):
        return jnp.dot(operand, weight, preferred_element_type=jnp.float32)

    return lax.psum_scatter(
        term(jnp.int32(0), rows * lax.axis_size("mp")), "mp", scatter_dimension=0, tiled=True
    )


def spread_back(operand, weight, rows):

    def term(start, count):
        return jnp.einsum("tc,dc->td", operand, weight, preferred_element_type=jnp.float32)

    return lax.psum_scatter(
        term(jnp.int32(0), rows * lax.axis_size("mp")), "mp", scatter_dimension=0, tiled=True
    )


def adam(weight, first, second, grad, factor, rate, decay):
    clipped = grad * factor
    first_new = FIRST_DECAY * first + (1.0 - FIRST_DECAY) * clipped
    second_new = SECOND_DECAY * second + (1.0 - SECOND_DECAY) * clipped * clipped
    first_hat = first_new / (1.0 - FIRST_DECAY**STEP)
    second_hat = second_new / (1.0 - SECOND_DECAY**STEP)
    weight_new = weight * (1.0 - rate * decay) - rate * first_hat / (
        jnp.sqrt(second_hat) + ADAM_EPS
    )
    return (weight_new, first_new, second_new)


def shards(
    hidden_in,
    cotangent,
    doc_lengths,
    owner,
    projection_master_weight,
    gateup_weight,
    out_weight,
    down_weight,
    projection_first_moment,
    gateup_first,
    out_first,
    down_first,
    projection_second_moment,
    gateup_second,
    out_second,
    down_second,
    gains,
    gain_first,
    gain_second,
):
    total_width = lax.axis_size("mp")
    blocks_count = lax.axis_size("dp")
    heads = QUERY_HEADS // total_width
    key_value_heads = KEY_VALUE_HEADS // total_width
    query_group = heads // key_value_heads
    query_width = heads * HEAD_SIZE
    key_width = key_value_heads * HEAD_SIZE
    units = FF // total_width
    rows_here = hidden_in.shape[0]
    inverse = jnp.argsort(owner)
    out_rate = float(QUERY_HEADS * HEAD_SIZE // 32) ** (-0.5)
    w_qkv, w_gateup, w_out, w_down = fetch_weights(
        projection_master_weight, gateup_weight, out_weight, down_weight, owner, blocks_count
    )
    ln_in = gains[:MODEL_WIDTH]
    ln_mid = gains[MODEL_WIDTH : 2 * MODEL_WIDTH]
    q_gain = gains[2 * MODEL_WIDTH : 2 * MODEL_WIDTH + HEAD_SIZE]
    k_gain = gains[2 * MODEL_WIDTH + HEAD_SIZE :]
    x_rows = hidden_in.astype(jnp.float32)
    full_in = collect(rms_norm(x_rows, ln_in).astype(jnp.bfloat16))
    projected = jnp.dot(full_in, w_qkv, preferred_element_type=jnp.float32)
    count = projected.shape[0]
    doc_of, cosine, sine = rope_tables(doc_lengths[0], count)
    cosine = cosine[:, None, :]
    sine = sine[:, None, :]
    query_raw = projected[:, :query_width].reshape(count, heads, HEAD_SIZE)
    unrotated_key = projected[:, query_width : query_width + key_width].reshape(
        count, key_value_heads, HEAD_SIZE
    )
    projected_value = projected[:, query_width + key_width :].reshape(
        count, key_value_heads, HEAD_SIZE
    )
    query_rows = rotate(rms_norm(query_raw, q_gain), cosine, sine).astype(jnp.bfloat16)
    key_rows = rotate(rms_norm(unrotated_key, k_gain), cosine, sine).astype(jnp.bfloat16)
    value_rows = projected_value.astype(jnp.bfloat16)
    block = min(512, count)
    nblocks = count // block
    score_scale = HEAD_SIZE ** (-0.5)
    places = jnp.arange(count, dtype=jnp.int32)

    def scores_of(start):
        query_block = lax.dynamic_slice_in_dim(query_rows, start, block, 0).reshape(
            block, key_value_heads, query_group, HEAD_SIZE
        )
        raw = (
            jnp.einsum("tlwd,uld->lwtu", query_block, key_rows, preferred_element_type=jnp.float32)
            * score_scale
        )
        row_doc = lax.dynamic_slice_in_dim(doc_of, start, block, 0)
        row_place = start + jnp.arange(block, dtype=jnp.int32)
        allowed = (row_doc[:, None] == doc_of[None, :]) & (places[None, :] <= row_place[:, None])
        return (jnp.where(allowed[None, None], raw, MASKED), query_block)

    def forward_block(index):
        score_matrix, query_block = scores_of(index * block)
        top = jnp.max(score_matrix, axis=-1, keepdims=True)
        total = jnp.log(jnp.sum(jnp.exp(score_matrix - top), axis=-1, keepdims=True)) + top
        probabilities = jnp.exp(score_matrix - total).astype(jnp.bfloat16)
        attention_result = jnp.einsum(
            "cpyx,xca->ycpa", probabilities, value_rows, preferred_element_type=jnp.float32
        )
        return (attention_result.reshape(block, query_width), total)

    outs, totals = lax.map(forward_block, jnp.arange(nblocks, dtype=jnp.int32))
    attn_heads = outs.reshape(count, query_width).astype(jnp.bfloat16)
    attn_rows = spread(attn_heads, w_out, rows_here)
    mixed = x_rows + attn_rows
    full_mid = collect(rms_norm(mixed, ln_mid).astype(jnp.bfloat16))
    gateup = jnp.dot(full_mid, w_gateup, preferred_element_type=jnp.float32)
    gate = gateup[:, :units]
    upper = gateup[:, units:]
    sigma = jax.nn.sigmoid(gate)
    act = (gate * sigma * upper).astype(jnp.bfloat16)
    mlp_rows = spread(act, w_down, rows_here)
    result_rows = mixed + mlp_rows
    w_qkv, w_gateup, w_out, w_down = fetch_again(
        projection_master_weight, gateup_weight, out_weight, down_weight, owner, blocks_count
    )
    grad_out = cotangent.astype(jnp.float32)
    d_branch = collect_back(grad_out.astype(jnp.bfloat16))
    g_down = jnp.einsum("tf,td->fd", act, d_branch, preferred_element_type=jnp.float32)
    d_act = jnp.einsum("td,fd->tf", d_branch, w_down, preferred_element_type=jnp.float32)
    d_upper = d_act * gate * sigma
    d_gate = d_act * upper * sigma * (1.0 + gate * (1.0 - sigma))
    d_gateup = jnp.concatenate([d_gate, d_upper], axis=1).astype(jnp.bfloat16)
    g_gateup = jnp.einsum("td,tf->df", full_mid, d_gateup, preferred_element_type=jnp.float32)
    d_mid_rows = spread_back(d_gateup, w_gateup, rows_here)
    d_mixed, g_ln_mid = norm_back(mixed, ln_mid, d_mid_rows)
    d_mixed = d_mixed + grad_out
    d_attn = collect_back(d_mixed.astype(jnp.bfloat16))
    g_out = jnp.einsum("th,td->hd", attn_heads, d_attn, preferred_element_type=jnp.float32)
    d_heads = jnp.einsum("td,hd->th", d_attn, w_out, preferred_element_type=jnp.float32).astype(
        jnp.bfloat16
    )
    d_heads = d_heads.reshape(count, key_value_heads, query_group, HEAD_SIZE)

    def backward_block(carry, index):
        d_key_sum, d_value_sum = carry
        start = index * block
        score_matrix, query_block = scores_of(start)
        probabilities = jnp.exp(score_matrix - totals[index])
        block_gradient = lax.dynamic_slice_in_dim(d_heads, start, block, 0)
        probability_gradient = jnp.einsum(
            "tlwd,uld->lwtu", block_gradient, value_rows, preferred_element_type=jnp.float32
        )
        d_value_sum = d_value_sum + jnp.einsum(
            "zxrb,rzxd->bzd",
            probabilities.astype(jnp.bfloat16),
            block_gradient,
            preferred_element_type=jnp.float32,
        )
        score_gradient = (
            probabilities
            * (
                probability_gradient
                - jnp.sum(probabilities * probability_gradient, axis=-1, keepdims=True)
            )
        ).astype(jnp.bfloat16)
        d_query = (
            jnp.einsum(
                "cpyx,xca->ycpa", score_gradient, key_rows, preferred_element_type=jnp.float32
            )
            * score_scale
        )
        d_key_sum = (
            d_key_sum
            + jnp.einsum(
                "zxrb,rzxd->bzd", score_gradient, query_block, preferred_element_type=jnp.float32
            )
            * score_scale
        )
        return ((d_key_sum, d_value_sum), d_query.reshape(block, heads, HEAD_SIZE))

    empty = jnp.zeros((count, key_value_heads, HEAD_SIZE), jnp.float32)
    (d_keys, d_values), d_queries = lax.scan(
        backward_block, (empty, empty), jnp.arange(nblocks, dtype=jnp.int32)
    )
    d_queries = d_queries.reshape(count, heads, HEAD_SIZE)
    d_query_raw, g_q = norm_back(query_raw, q_gain, rotate_back(d_queries, cosine, sine))
    d_key_raw, g_k = norm_back(unrotated_key, k_gain, rotate_back(d_keys, cosine, sine))
    d_projected = jnp.concatenate(
        [
            d_query_raw.reshape(count, query_width),
            d_key_raw.reshape(count, key_width),
            d_values.reshape(count, key_width),
        ],
        axis=1,
    ).astype(jnp.bfloat16)
    g_qkv = jnp.einsum("td,tc->dc", full_in, d_projected, preferred_element_type=jnp.float32)
    d_in_rows = spread_back(d_projected, w_qkv, rows_here)
    d_input, g_ln_in = norm_back(x_rows, ln_in, d_in_rows)
    input_grad = d_input + d_mixed
    gain_terms = jnp.concatenate([g_ln_in, g_ln_mid, g_q, g_k])
    red_qkv, red_gateup, red_out, red_down = (
        lax.psum_scatter(
            arrange(g_qkv, inverse, blocks_count).astype(jnp.bfloat16),
            "dp",
            scatter_dimension=0,
            tiled=True,
        ).astype(jnp.float32),
        lax.psum_scatter(
            arrange(g_gateup, inverse, blocks_count).astype(jnp.bfloat16),
            "dp",
            scatter_dimension=0,
            tiled=True,
        ).astype(jnp.float32),
        lax.psum_scatter(
            arrange(g_out, inverse, blocks_count).astype(jnp.bfloat16),
            "dp",
            scatter_dimension=0,
            tiled=True,
        ).astype(jnp.float32),
        lax.psum_scatter(
            arrange(g_down, inverse, blocks_count).astype(jnp.bfloat16),
            "dp",
            scatter_dimension=0,
            tiled=True,
        ).astype(jnp.float32),
    )
    squares = jnp.sum(red_qkv * red_qkv) + jnp.sum(red_gateup * red_gateup)
    squares = squares + jnp.sum(red_out * red_out) + jnp.sum(red_down * red_down)
    total_squares, gain_grad = lax.psum((squares, gain_terms), ("dp", "mp"))
    grad_norm = jnp.sqrt(total_squares + jnp.sum(gain_grad * gain_grad))
    factor = jnp.minimum(1.0, CLIP_LIMIT / (grad_norm + 1e-06))
    qkv_new, qkv_first_new, qkv_second_new = adam(
        projection_master_weight,
        projection_first_moment,
        projection_second_moment,
        red_qkv,
        factor,
        LEARN,
        WEIGHT_DECAY,
    )
    gateup_new, gateup_first_new, gateup_second_new = adam(
        gateup_weight, gateup_first, gateup_second, red_gateup, factor, LEARN, WEIGHT_DECAY
    )
    out_new, out_first_new, out_second_new = adam(
        out_weight, out_first, out_second, red_out, factor, out_rate, WEIGHT_DECAY
    )
    down_new, down_first_new, down_second_new = adam(
        down_weight, down_first, down_second, red_down, factor, LEARN, WEIGHT_DECAY
    )
    gains_new, gain_first_new, gain_second_new = adam(
        gains, gain_first, gain_second, gain_grad, factor, GAIN_LEARN, 0.0
    )
    return (
        result_rows.astype(jnp.bfloat16),
        input_grad,
        qkv_new,
        gateup_new,
        out_new,
        down_new,
        qkv_first_new,
        gateup_first_new,
        out_first_new,
        down_first_new,
        qkv_second_new,
        gateup_second_new,
        out_second_new,
        down_second_new,
        gains_new,
        gain_first_new,
        gain_second_new,
        grad_norm,
    )


def solution(mesh):
    placed = (
        P(("dp", "mp"), None),
        P(("dp", "mp"), None),
        P("dp", None),
        P(),
        P("dp", "mp"),
        P("dp", "mp"),
        P(("mp", "dp"), None),
        P(("mp", "dp"), None),
        P("dp", "mp"),
        P("dp", "mp"),
        P(("mp", "dp"), None),
        P(("mp", "dp"), None),
        P("dp", "mp"),
        P("dp", "mp"),
        P(("mp", "dp"), None),
        P(("mp", "dp"), None),
        P(),
        P(),
        P(),
    )
    return jax.shard_map(
        shards,
        mesh=mesh,
        in_specs=placed,
        out_specs=(
            P(("dp", "mp"), None),
            P(("dp", "mp"), None),
            P("dp", "mp"),
            P("dp", "mp"),
            P(("mp", "dp"), None),
            P(("mp", "dp"), None),
            P("dp", "mp"),
            P("dp", "mp"),
            P(("mp", "dp"), None),
            P(("mp", "dp"), None),
            P("dp", "mp"),
            P("dp", "mp"),
            P(("mp", "dp"), None),
            P(("mp", "dp"), None),
            P(),
            P(),
            P(),
            P(),
        ),
        check_vma=False,
    )
```

profile of v0, /device:TPU:0, one launch (start us, length us, event | category | flops | bytes accessed | tf_op | source)
XLA Modules:
  0.0 1492.8 jit_solution(1398384597444708085)
XLA Ops:
  16.5 24.6 %all-gather.13.cloned.1.call-done = bf16[512,2048]{1,0:T(8,128)(2,1)} async-done(((bf16[64,2048]{1,0:T(8,128)(2,1)}), bf16[512,2048]{1,0:T(8,128)(2,1)}) %all-gather.13.cloned.1.call-update) | async-done | bytes 2097168 | tf_op jit(solution)/shard_map/all_gather | solution.py:84
  47.9 32.4 %all-gather.11.cloned.1.call-done = bf16[2048,1024]{1,0:T(8,128)(2,1)} async-done(((bf16[256,1024]{1,0:T(8,128)(2,1)}), bf16[2048,1024]{1,0:T(8,128)(2,1)}) %all-gather.11.cloned.1.call-update) | async-done | bytes 4194320 | tf_op jit(solution)/shard_map/all_gather | solution.py:82
  80.3 5.0 gather_fusion.4
  85.3 4.6 broadcast_select_fusion.2
  90.0 73.3 %all-gather.9.cloned.1.call-done = bf16[1024,2048]{1,0:T(8,128)(2,1)} async-done(((bf16[256,2048]{1,0:T(8,128)(2,1)}), bf16[1024,2048]{1,0:T(8,128)(2,1)}) %all-gather.9.cloned.1.call-update) | async-done | bytes 4194320 | tf_op jit(solution)/shard_map/all_gather | solution.py:103
  163.3 7.6 fusion.116
  183.1 23.5 %while.28 = (s32[]{:T(128)}, bf16[2,512,512]{2,1,0:T(8,128)(2,1)}, f32[2,2,2,512,1]{3,2,1,4,0:T(2,128)S(1)}, s32[2]{0:T(128)S(1)}, s32[1024]{0:T(1024)S(1)}, /*i...) while((s32[]{:T(128)}, bf16[2,512,512]{2,1,0:T(8,128)(2,1)}, ...), condition=%wide.region_9.11_spmd.clone, body=%wide.region_6.10_spmd.clone.sunk | while | flops 1098381824 | bytes 34683108 | solution.py:226
  206.6 8.1 fusion.117
  220.4 137.4 %reduce-scatter.9.cloned.1.call-done = f32[256,2048]{1,0:T(8,128)} async-done(((f32[1024,2048]{1,0:T(8,128)}), f32[256,2048]{1,0:T(8,128)}) %reduce-scatter.9.cloned.1.call-update) | async-done | bytes 2097168 | tf_op jit(solution)/shard_map/reduce_scatter | solution.py:115
  362.1 44.4 %all-gather.19.cloned.1.call-done = bf16[1536,2048]{1,0:T(8,128)(2,1)} async-done(((bf16[192,2048]{1,0:T(8,128)(2,1)}), bf16[1536,2048]{1,0:T(8,128)(2,1)}) %all-gather.19.cloned.1.call-update) | async-done | bytes 6291472 | tf_op jit(solution)/shard_map/all_gather | solution.py:85
  406.4 6.4 gather_fusion.7
  412.8 6.6 broadcast_select_fusion.1
  419.4 61.6 %all-gather.17.cloned.1.call-done = bf16[2048,3072]{1,0:T(8,128)(2,1)} async-done(((bf16[256,3072]{1,0:T(8,128)(2,1)}), bf16[2048,3072]{1,0:T(8,128)(2,1)}) %all-gather.17.cloned.1.call-update) | async-done | bytes 12582928 | tf_op jit(solution)/shard_map/all_gather | solution.py:83
  480.9 11.5 gather_fusion.6
  492.4 11.1 broadcast_select_fusion
  503.5 60.3 %all-gather.15.cloned.1.call-done = bf16[1024,2048]{1,0:T(8,128)(2,1)} async-done(((bf16[256,2048]{1,0:T(8,128)(2,1)}), bf16[1024,2048]{1,0:T(8,128)(2,1)}) %all-gather.15.cloned.1.call-update) | async-done | bytes 4194320 | tf_op jit(solution)/shard_map/all_gather | solution.py:103
  563.8 19.2 %fusion.118 = f32[1024,3072]{1,0:T(8,128)} fusion(bf16[1024,2048]{1,0:T(8,128)(2,1)} %all-gather.15.cloned.1.call-done, bf16[2048,3072]{1,0:T(8,128)(2,1)} %bitcast.301), kind=kOutput, calls=%fused_computation.226 | convolution fusion | flops 12884901888 | bytes 29360128 | tf_op jit(solution)/shard_map/dot_general | solution.py:231
  583.0 61.7 %all-gather.21.cloned.1.call-done = bf16[1024,2048]{1,0:T(8,128)(2,1)} async-done(((bf16[256,2048]{1,0:T(8,128)(2,1)}), bf16[1024,2048]{1,0:T(8,128)(2,1)}) %all-gather.21.cloned.1.call-update) | async-done | bytes 4194320 | tf_op jit(solution)/shard_map/all_gather | solution.py:107
  644.7 17.0 %fusion.51 = (bf16[1024,1536]{1,0:T(8,128)(2,1)}, bf16[1024,1536]{1,0:T(8,128)(2,1)}, bf16[1024,1536]{1,0:T(8,128)(2,1)}) fusion(f32[1024,3072]{1,0:T(8,128)} %fusion.118, bf16[1536,2048]{1,0:T(8,128)(2,1)} %bitcast.306, bf16[1024,2048]{1,0:T(8,128)(2,1)} %all-gather.21.cloned.1.call-done), kind=kOutput, calls=%fused_computation.78 | convolution fusion | flops 6467616768 | bytes 32505856 | tf_op jit(solution)/shard_map/td,fd->tf/dot_general | solution.py:244
  661.8 17.3 %fusion.58 = f32[1024,2048]{1,0:T(8,128)} fusion(bf16[2048,3072]{1,0:T(8,128)(2,1)S(1)} %bitcast.302, bf16[1024,1536]{1,0:T(8,128)(2,1)} %get-tuple-element.346, bf16[1024,1536]{1,0:T(8,128)(2,1)} %get-tuple-element.345), kind=kOutput, calls=%fused_computation.91 | convolution fusion | flops 12897484800 | bytes 27262976 | tf_op jit(solution)/shard_map/tc,dc->td/dot_general | solution.py:123
  679.1 143.1 %reduce-scatter.13.cloned.1.call-done = f32[256,2048]{1,0:T(8,128)} async-done(((f32[1024,2048]{1,0:T(8,128)}), f32[256,2048]{1,0:T(8,128)}) %reduce-scatter.13.cloned.1.call-update) | async-done | bytes 2097168 | tf_op jit(solution)/shard_map/reduce_scatter | solution.py:125
  828.1 11.3 fusion.120
  839.4 6.4 gather_fusion.3
  845.8 6.5 fusion.47
  852.5 20.0 %fusion.57 = bf16[2048,3072]{1,0:T(8,128)(2,1)} fusion(bf16[1024,2048]{1,0:T(8,128)(2,1)} %all-gather.15.cloned.1.call-done, bf16[1024,1536]{1,0:T(8,128)(2,1)} %get-tuple-element.346, bf16[1024,1536]{1,0:T(8,128)(2,1)} %get-tuple-element.345), kind=kOutput, calls=%fused_computation.90 | convolution fusion | flops 12897484800 | bytes 23068672 | tf_op jit(solution)/shard_map/td,tf->df/dot_general | solution.py:248
  872.5 11.1 gather_fusion.1
  883.6 11.9 fusion.46
  896.6 7.9 maximum_cosine_fusion
  904.8 4.1 reshape.509
  910.2 6.3 convolution_convert_fusion
  916.5 37.6 %while.29 = (s32[]{:T(128)}, f32[1024,2,128]{0,2,1:T(8,128)S(1)}, f32[1024,2,128]{0,2,1:T(8,128)}, f32[2,512,4,128]{3,1,2,0:T(8,128)}, s32[2]{0:T(128)S(1)}, /*i...) while((s32[]{:T(128)}, f32[1024,2,128]{0,2,1:T(8,128)S(1)}, ...), condition=%wide.region_17.22_spmd.clone, body=%wide.region_15.21_spmd.clone.sunk | while | flops 2718956032 | bytes 106502576 | solution.py:297
  925.3 3.9 fusion.181
  961.1 5.9 fusion.55
  981.1 6.5 multiply_reduce_fusion
  992.0 4.0 pad_maximum_fusion.3
  1007.2 7.6 fusion.90
  1014.8 4.9 gather_fusion
  1019.8 4.3 fusion.48
  1025.3 9.1 fusion.91
  1036.4 11.1 fusion.119
  1050.2 18.2 %reduce-scatter.19.cloned.1.call-done = bf16[256,3072]{1,0:T(8,128)(2,1)} async-done(((bf16[2048,3072]{1,0:T(8,128)(2,1)}), bf16[256,3072]{1,0:T(8,128)(2,1)}) %reduce-scatter.19.cloned.1.call-update) | async-done | bytes 1572880 | tf_op jit(solution)/shard_map/reduce_scatter | solution.py:323
  1071.2 42.0 %reduce-scatter.21.cloned.1.call-done = bf16[64,2048]{1,0:T(8,128)(2,1)} async-done(((bf16[512,2048]{1,0:T(8,128)(2,1)}), bf16[64,2048]{1,0:T(8,128)(2,1)}) %reduce-scatter.21.cloned.1.call-update) | async-done | bytes 262160 | tf_op jit(solution)/shard_map/reduce_scatter | solution.py:329
  1114.9 52.9 %reduce-scatter.17.cloned.1.call-done = bf16[256,1024]{1,0:T(8,128)(2,1)} async-done(((bf16[2048,1024]{1,0:T(8,128)(2,1)}), bf16[256,1024]{1,0:T(8,128)(2,1)}) %reduce-scatter.17.cloned.1.call-update) | async-done | bytes 524304 | tf_op jit(solution)/shard_map/reduce_scatter | solution.py:317
  1172.3 142.3 %reduce-scatter.15.cloned.1.call-done = f32[256,2048]{1,0:T(8,128)} async-done(((f32[1024,2048]{1,0:T(8,128)}), f32[256,2048]{1,0:T(8,128)}) %reduce-scatter.15.cloned.1.call-update) | async-done | bytes 2097168 | tf_op jit(solution)/shard_map/reduce_scatter | solution.py:125
  1316.9 46.7 %all-reduce = (f32[]{:T(128)}, f32[4352]{0:T(1024)S(1)}) all-reduce(f32[]{:T(128)S(6)} %add.257, f32[4352]{0:T(1024)S(1)} %pad_maximum_fusion.8), channel_id=1, replica_groups=mesh['dp'=8,'mp'=4] {'dp','mp'}, use_global_device_ids=true, to_apply=%region_31.36 | all-reduce | flops 4353 | bytes 34824 | tf_op jit(solution)/shard_map/psum | solution.py:344
  1366.3 96.8 %reduce-scatter.11.cloned.1.call-done = f32[256,2048]{1,0:T(8,128)} async-done(((f32[1024,2048]{1,0:T(8,128)}), f32[256,2048]{1,0:T(8,128)}) %reduce-scatter.11.cloned.1.call-update) | async-done | bytes 2097168 | tf_op jit(solution)/shard_map/reduce_scatter | solution.py:115
  1463.3 6.1 fusion.71
  1479.4 5.2 divide_subtract_fusion
  (385 shorter events, 158.1 us)
Async XLA Ops:
  7.2 33.9 %all-gather.13.cloned.1.call-start = ((), (), s32[]{:S(2)}) async-start(), calls=%async_computation.10 | async-start | bytes 2359296 | tf_op jit(solution)/shard_map/all_gather | solution.py:84
  9.1 71.2 %all-gather.11.cloned.1.call-start = ((), (), s32[]{:S(2)}) async-start(), calls=%async_computation.9 | async-start | bytes 4718592 | tf_op jit(solution)/shard_map/all_gather | solution.py:82
  11.3 152.0 %all-gather.9.cloned.1.call-start = ((), (), s32[]{:S(2)}) async-start(), calls=%async_computation.8 | async-start | bytes 5242880 | tf_op jit(solution)/shard_map/all_gather | solution.py:103
  11.7 813.4 %copy-start.63 = (f32[2048]{0:T(1024)}, f32[2048]{0:T(1024)S(1)}, u32[]{:S(2)}) copy-start(f32[2048]{0:T(1024)S(1)} %get-tuple-element.360) | copy-start | bytes 24580
  13.0 344.8 %reduce-scatter.9.cloned.1.call-start = ((), (), s32[]{:S(2)}) async-start(), calls=%async_computation.11 | async-start | bytes 10485760 | tf_op jit(solution)/shard_map/reduce_scatter | solution.py:115
  13.3 31.4 %copy-start.88 = (f32[64]{0:T(128)}, f32[64]{0:T(128)S(1)}, u32[]{:S(2)}) copy-start(f32[64]{0:T(128)S(1)} %multiply_power_fusion) | copy-start | bytes 772
  13.5 31.2 %copy-start.71 = (s32[1024]{0:T(1024)}, s32[1024]{0:T(1024)S(1)}, u32[]{:S(2)}) copy-start(s32[1024]{0:T(1024)S(1)} %select_reduce_fusion) | copy-start | bytes 12292
  15.9 28.8 %copy-start.29 = (f32[1024,128]{1,0:T(8,128)}, f32[1024,128]{1,0:T(8,128)S(1)}, u32[]{:S(2)}) copy-start(f32[1024,128]{1,0:T(8,128)S(1)} %get-tuple-element.358) | copy-start | bytes 1572868
  16.0 164.9 %copy-start.16 = (f32[1024,128]{1,0:T(8,128)}, f32[1024,128]{1,0:T(8,128)S(1)}, u32[]{:S(2)}) copy-start(f32[1024,128]{1,0:T(8,128)S(1)} %get-tuple-element.359) | copy-start | bytes 1572868
  16.2 158.2 %copy-start.19 = (f32[1024,128]{0,1:T(8,128)}, f32[1024,128]{0,1:T(8,128)S(1)}, u32[]{:S(2)}) copy-start(f32[1024,128]{0,1:T(8,128)S(1)} %copy.95) | copy-start | bytes 1572868
  16.4 158.0 %copy-start.31 = (f32[1024,128]{0,1:T(8,128)}, f32[1024,128]{0,1:T(8,128)S(1)}, u32[]{:S(2)}) copy-start(f32[1024,128]{0,1:T(8,128)S(1)} %copy.96) | copy-start | bytes 1572868
  16.5 157.9 %copy-start.84 = (f32[128]{0:T(128)}, f32[128]{0:T(128)S(1)}, u32[]{:S(2)}) copy-start(f32[128]{0:T(128)S(1)} %get-tuple-element.362) | copy-start | bytes 1540
  16.5 164.4 %copy-start.82 = (f32[128]{0:T(128)}, f32[128]{0:T(128)S(1)}, u32[]{:S(2)}) copy-start(f32[128]{0:T(128)S(1)} %get-tuple-element.363) | copy-start | bytes 1540
  206.6 8.1 copy-start.45
  206.6 8.1 copy-start.67
  214.7 191.7 %all-gather.19.cloned.1.call-start = ((), (), s32[]{:S(2)}) async-start(), calls=%async_computation.14 | async-start | bytes 7077888 | tf_op jit(solution)/shard_map/all_gather | solution.py:85
  217.1 263.8 %all-gather.17.cloned.1.call-start = ((), (), s32[]{:S(2)}) async-start(), calls=%async_computation.13 | async-start | bytes 14155776 | tf_op jit(solution)/shard_map/all_gather | solution.py:83
  220.4 343.4 %all-gather.15.cloned.1.call-start = ((), (), s32[]{:S(2)}) async-start(), calls=%async_computation.12 | async-start | bytes 5242880 | tf_op jit(solution)/shard_map/all_gather | solution.py:103
  359.8 465.3 %copy-start.2 = (f32[256,2048]{1,0:T(8,128)}, f32[256,2048]{1,0:T(8,128)S(1)}, u32[]{:S(2)}) copy-start(f32[256,2048]{1,0:T(8,128)S(1)} %get-tuple-element.340) | copy-start | bytes 6291460
  359.8 465.3 %copy-start.74 = (f32[256]{0:T(256)}, f32[256]{0:T(256)S(1)}, u32[]{:S(2)}) copy-start(f32[256]{0:T(256)S(1)} %add_rsqrt_fusion.2) | copy-start | bytes 3076
  361.3 283.5 %all-gather.21.cloned.1.call-start = ((), (), s32[]{:S(2)}) async-start(), calls=%async_computation.16 | async-start | bytes 5242880 | tf_op jit(solution)/shard_map/all_gather | solution.py:107
  362.0 460.2 %reduce-scatter.13.cloned.1.call-start = ((), (), s32[]{:S(2)}) async-start(), calls=%async_computation.17 | async-start | bytes 10485760 | tf_op jit(solution)/shard_map/reduce_scatter | solution.py:125
  644.7 17.0 %copy-start.13 = (bf16[8,256,3072]{2,1,0:T(8,128)(2,1)S(1)}, bf16[8,256,3072]{2,1,0:T(8,128)(2,1)}, u32[]{:S(2)}) copy-start(bf16[8,256,3072]{2,1,0:T(8,128)(2,1)} %broadcast_select_fusion) | copy-start | bytes 37748740
  679.1 146.1 %copy-start.15 = (bf16[256,2048]{1,0:T(8,128)(2,1)S(1)}, bf16[256,2048]{1,0:T(8,128)(2,1)}, u32[]{:S(2)}) copy-start(bf16[256,2048]{1,0:T(8,128)(2,1)} %param.32) | copy-start | bytes 3145732
  679.1 231.1 %all-gather.23.cloned.1.call-start = ((), (), s32[]{:S(2)}) async-start(), calls=%async_computation.18 | async-start | bytes 5242880 | tf_op jit(solution)/shard_map/all_gather | solution.py:107
  826.8 220.8 %reduce-scatter.23.cloned.1.call-start = ((), (), s32[]{:S(2)}) async-start(), calls=%async_computation.23 | async-start | bytes 7077888 | tf_op jit(solution)/shard_map/reduce_scatter | solution.py:335
  852.3 216.0 %reduce-scatter.19.cloned.1.call-start = ((), (), s32[]{:S(2)}) async-start(), calls=%async_computation.21 | async-start | bytes 14155776 | tf_op jit(solution)/shard_map/reduce_scatter | solution.py:323
  852.5 31.2 %copy-start.78 = (pred[2048]{0:T(1024)(128)(4,1)}, pred[2048]{0:T(1024)(128)(4,1)S(1)}, u32[]{:S(2)}) copy-start(pred[2048]{0:T(1024)(128)(4,1)S(1)} %broadcast_in_dim.196) | copy-start | bytes 6148
  895.6 8.9 copy-start.83
  895.6 8.9 copy-start.60
  895.6 8.9 copy-start.38
  895.6 217.6 %reduce-scatter.21.cloned.1.call-start = ((), (), s32[]{:S(2)}) async-start(), calls=%async_computation.22 | async-start | bytes 2359296 | tf_op jit(solution)/shard_map/reduce_scatter | solution.py:329
  957.3 15.6 %copy-start.11 = (f32[2,512,4,128]{1,0,3,2:T(2,128)}, f32[2,512,4,128]{1,0,3,2:T(2,128)S(1)}, u32[]{:S(2)}) copy-start(f32[2,512,4,128]{1,0,3,2:T(2,128)S(1)} %copy.104) | copy-start | bytes 6291460
  991.9 175.9 %reduce-scatter.17.cloned.1.call-start = ((), (), s32[]{:S(2)}) async-start(), calls=%async_computation.20 | async-start | bytes 4718592 | tf_op jit(solution)/shard_map/reduce_scatter | solution.py:317
  1024.1 290.5 %reduce-scatter.15.cloned.1.call-start = ((), (), s32[]{:S(2)}) async-start(), calls=%async_computation.19 | async-start | bytes 10485760 | tf_op jit(solution)/shard_map/reduce_scatter | solution.py:125
  1034.5 428.7 %reduce-scatter.11.cloned.1.call-start = ((), (), s32[]{:S(2)}) async-start(), calls=%async_computation.15 | async-start | bytes 10485760 | tf_op jit(solution)/shard_map/reduce_scatter | solution.py:115
  1047.5 267.2 %copy-start.66 = (f32[2048]{0:T(1024)S(1)}, f32[2048]{0:T(1024)}, u32[]{:S(2)}) copy-start(f32[2048]{0:T(1024)} %copy-done.65) | copy-start | bytes 24580
  1047.5 267.2 %copy-start.81 = (f32[256]{0:T(256)S(1)}, f32[256]{0:T(256)}, u32[]{:S(2)}) copy-start(f32[256]{0:T(256)} %copy-done.80) | copy-start | bytes 3076
  1047.5 267.1 %copy-start.9 = (bf16[256,2048]{1,0:T(8,128)(2,1)S(1)}, bf16[256,2048]{1,0:T(8,128)(2,1)}, u32[]{:S(2)}) copy-start(bf16[256,2048]{1,0:T(8,128)(2,1)} %param.31) | copy-start | bytes 3145732
  1047.5 269.4 %copy-start.73 = (f32[2048]{0:T(1024)S(1)}, f32[2048]{0:T(1024)}, u32[]{:S(2)}) copy-start(f32[2048]{0:T(1024)} %get-tuple-element.275) | copy-start | bytes 24580
  1047.5 318.1 %copy-start.70 = (f32[4352]{0:T(1024)S(1)}, f32[4352]{0:T(1024)}, u32[]{:S(2)}) copy-start(f32[4352]{0:T(1024)} %param.47) | copy-start | bytes 52228
  1047.5 318.1 %copy-start.76 = (f32[4352]{0:T(1024)S(1)}, f32[4352]{0:T(1024)}, u32[]{:S(2)}) copy-start(f32[4352]{0:T(1024)} %param.48) | copy-start | bytes 52228
  1047.6 318.1 %copy-start.77 = (f32[4352]{0:T(1024)S(1)}, f32[4352]{0:T(1024)}, u32[]{:S(2)}) copy-start(f32[4352]{0:T(1024)} %param.49) | copy-start | bytes 52228
  1047.6 415.6 %copy-start.3 = (f32[256,2048]{1,0:T(8,128)S(1)}, f32[256,2048]{1,0:T(8,128)}, u32[]{:S(2)}) copy-start(f32[256,2048]{1,0:T(8,128)} %copy-done.2) | copy-start | bytes 6291460
  1047.6 415.6 %copy-start.64 = (f32[2048]{0:T(1024)S(1)}, f32[2048]{0:T(1024)}, u32[]{:S(2)}) copy-start(f32[2048]{0:T(1024)} %copy-done.63) | copy-start | bytes 24580
  1047.6 415.6 %copy-start.75 = (f32[256]{0:T(256)S(1)}, f32[256]{0:T(256)}, u32[]{:S(2)}) copy-start(f32[256]{0:T(256)} %copy-done.74) | copy-start | bytes 3076
  1047.6 415.6 %copy-start.87 = (f32[256]{0:T(256)S(1)}, f32[256]{0:T(256)}, u32[]{:S(2)}) copy-start(f32[256]{0:T(256)} %copy-done.86) | copy-start | bytes 3076
  1366.3 103.0 %copy-start.49 = (bf16[64,2048]{1,0:T(8,128)(2,1)S(1)}, bf16[64,2048]{1,0:T(8,128)(2,1)}, u32[]{:S(2)}) copy-start(bf16[64,2048]{1,0:T(8,128)(2,1)} %reduce-scatter.21.cloned.1.call-done) | copy-start | bytes 786436
  (70 other events, 253.5 us)
Sparse Core Ops, SparseCore 0:
  10.5 30.5 all-gather.12
  43.6 36.7 all-gather.10
  82.5 80.7 all-gather.8
  214.8 142.9 reduce-scatter.8
  360.1 46.2 all-gather.18
  408.7 72.1 all-gather.16
  483.0 80.7 all-gather.14
  565.4 79.2 all-gather.20
  679.2 142.9 reduce-scatter.12
  827.0 81.4 all-gather.22
  911.9 60.2 reduce-scatter.22
  976.0 92.3 reduce-scatter.18
  1072.0 41.1 reduce-scatter.20
  1116.5 51.3 reduce-scatter.16
  1170.1 144.4 reduce-scatter.14
  1317.0 146.1 reduce-scatter.10
where the time goes:
time: 1500 us; the launch traced here: 1490 us
  waiting for transfers between devices  992 us (66%)
  matrix products  171 us (11%)
  other arithmetic  147 us (10%)
  local copies, waits for them, and re-layouts  108 us (7%)
  blocking collectives  46.7 us (3%)
  between operations  20.7 us (1%)
    reduce_scatter x2, waiting for transfers between devices, spread_back(): lax.psum_scatter(term(jnp.int32(0), rows * lax.axis_size('mp')), 'mp', sc...  285 us
    reduce_scatter x2, waiting for transfers between devices, spread(): lax.psum_scatter(term(jnp.int32(0), rows * lax.axis_size('mp')), 'mp', sc...  234 us
    all_gather x2, waiting for transfers between devices, collect(): return lax.all_gather(rows, 'mp', axis=0, tiled=True)  134 us
    all_gather x2, waiting for transfers between devices, collect_back(): return lax.all_gather(rows, 'mp', axis=0, tiled=True)  61.8 us
    all_gather x1, waiting for transfers between devices, fetch_weights(): lax.all_gather(gateup_weight.astype(jnp.bfloat16), 'dp', axis=0, tiled=True)  61.6 us
    reduce_scatter x1, waiting for transfers between devices, shards(): lax.psum_scatter(arrange(g_qkv, inverse, blocks_count).astype(jnp.bfloat1...  52.9 us
    gather x8, local copies, waits for them, and re-layouts, arrange(): return jnp.take(blocks, order, axis=0).reshape(gathered.shape)  52.5 us
    psum x1, blocking collectives, shards(): total_squares, gain_grad = lax.psum((squares, gain_terms), ('dp', 'mp'))  46.7 us
  transfers between devices with their start and end apart: 16, of which 14 were waited for; matrix products, arithmetic and copies ran while one was open for 20% of the time, Pallas kernels for 0%

commit v1 on v0

--- a/solution.py
+++ b/solution.py
@@ -113,8 +113,11 @@
         return jnp.dot(operand, weight, preferred_element_type=jnp.float32)
 
     return lax.psum_scatter(
-        term(jnp.int32(0), rows * lax.axis_size("mp")), "mp", scatter_dimension=0, tiled=True
-    )
+        term(jnp.int32(0), rows * lax.axis_size("mp")).astype(jnp.bfloat16),
+        "mp",
+        scatter_dimension=0,
+        tiled=True,
+    ).astype(jnp.float32)
 
 
 def spread_back(operand, weight, rows):
@@ -123,8 +126,11 @@
         return jnp.einsum("tc,dc->td", operand, weight, preferred_element_type=jnp.float32)
 
     return lax.psum_scatter(
-        term(jnp.int32(0), rows * lax.axis_size("mp")), "mp", scatter_dimension=0, tiled=True
-    )
+        term(jnp.int32(0), rows * lax.axis_size("mp")).astype(jnp.bfloat16),
+        "mp",
+        scatter_dimension=0,
+        tiled=True,
+    ).astype(jnp.float32)
 
 
 def adam(weight, first, second, grad, factor, rate, decay):
@@ -139,7 +145,7 @@
     return (weight_new, first_new, second_new)
 
 
-def shards(
+def shards_general(
     hidden_in,
     cotangent,
     doc_lengths,
@@ -387,6 +393,354 @@
     )
 
 
+def steps(move):
+    pairs = []
+    for index in range(32):
+        y, x, c, zh, zl = (index >> 4) & 1, (index >> 3) & 1, (index >> 2) & 1, (index >> 1) & 1, index & 1
+        source = move(y, x, c, zh, zl)
+        if source is not None:
+            sy, sx, sc, sh, sl = source
+            pairs.append(((sy << 4) | (sx << 3) | (sc << 2) | (sh << 1) | sl, index))
+    return pairs
+
+
+OVER_X = steps(lambda y, x, c, h, l: (y, 1 - x, c, h, l))
+OVER_Y = steps(lambda y, x, c, h, l: (1 - y, x, c, h, l))
+OVER_C = steps(lambda y, x, c, h, l: (y, x, 1 - c, h, l))
+OVER_L = steps(lambda y, x, c, h, l: (y, x, c, h, 1 - l))
+TO_GROUP = (
+    steps(lambda y, x, c, h, l: (y, x, h, c, l)),
+    steps(lambda y, x, c, h, l: (y, x, 1 - h, c, l)),
+)
+FROM_GROUP = tuple([(b, a) for a, b in pairs] for pairs in TO_GROUP)
+UPWARD = steps(lambda y, x, c, h, l: (y, x, c, 0, l) if h == 1 else None)
+DOWNWARD = steps(lambda y, x, c, h, l: (y, x, c, 1, l) if h == 0 else None)
+
+
+def move(value, pairs):
+    return lax.ppermute(value, ("dp", "mp"), pairs)
+
+
+def after(value, *others):
+    return lax.optimization_barrier((value, *others))[0]
+
+
+def gather_weight(shard):
+    a = move(shard, TO_GROUP[0])
+    b = move(shard, TO_GROUP[1])
+    ax, ay = move(a, OVER_X), move(a, OVER_Y)
+    by, bx = move(b, OVER_Y), move(b, OVER_X)
+    axy, bxy = move(ax, OVER_Y), move(by, OVER_X)
+    return [a, b, ax, bx, ay, by, axy, bxy]
+
+
+def reduce_weight(grads):
+    def plus(left, right):
+        return (left.astype(jnp.float32) + right.astype(jnp.float32)).astype(jnp.bfloat16)
+
+    a = move(jnp.stack([grads[4], grads[6]]), OVER_Y)
+    b = move(jnp.stack([grads[3], grads[7]]), OVER_X)
+    a_far = plus(grads[2], a[1])
+    b_far = plus(grads[5], b[1])
+    a_far = move(a_far, OVER_X)
+    b_far = move(b_far, OVER_Y)
+    a_own = plus(plus(grads[0], a[0]), a_far)
+    b_own = plus(plus(grads[1], b[0]), b_far)
+    return move(a_own, FROM_GROUP[0]).astype(jnp.float32) + move(b_own, FROM_GROUP[1]).astype(
+        jnp.float32
+    )
+
+
+def gather_rows(rows):
+    pair = jnp.concatenate([rows, move(rows, OVER_L)], axis=0)
+    return jnp.concatenate([pair, move(pair, OVER_C)], axis=0)
+
+
+def sum_rows(partial):
+    half = partial.shape[0] // 2
+    quarter = half // 2
+    near = move(partial[half:].astype(jnp.bfloat16), OVER_C).astype(jnp.float32)
+    summed = partial[:half] + near
+    return summed[:quarter] + move(summed[quarter:].astype(jnp.bfloat16), OVER_L).astype(
+        jnp.float32
+    )
+
+
+def shards_paired(
+    hidden_in,
+    cotangent,
+    doc_lengths,
+    owner,
+    projection_master_weight,
+    gateup_weight,
+    out_weight,
+    down_weight,
+    projection_first_moment,
+    gateup_first,
+    out_first,
+    down_first,
+    projection_second_moment,
+    gateup_second,
+    out_second,
+    down_second,
+    gains,
+    gain_first,
+    gain_second,
+):
+    dp, mp = lax.axis_index("dp"), lax.axis_index("mp")
+    core, high, low = dp % 2, mp // 2, mp % 2
+    plane = (dp // 2) * 2 + high
+    groups = lax.axis_size("mp")
+    heads = QUERY_HEADS // groups
+    key_value_heads = KEY_VALUE_HEADS // groups
+    query_group = heads // key_value_heads
+    query_width = heads * HEAD_SIZE
+    key_width = key_value_heads * HEAD_SIZE
+    units = FF // groups
+    rows_here = hidden_in.shape[0]
+    count = 4 * rows_here
+    half = count // 2
+    width = hidden_in.shape[1]
+    inverse = jnp.argsort(owner)
+    logical_of = jnp.take(inverse, jnp.arange(8, dtype=jnp.int32) ^ plane)
+    slot_of = owner ^ plane
+    out_rate = float(QUERY_HEADS * HEAD_SIZE // 32) ** (-0.5)
+
+    def to_slots(rows):
+        return jnp.take(rows.reshape(rows.shape[0], 8, -1), logical_of, axis=1).reshape(rows.shape)
+
+    def from_slots(rows):
+        return jnp.take(rows.reshape(rows.shape[0], 8, -1), slot_of, axis=1).reshape(rows.shape)
+
+    ln_in = gains[:MODEL_WIDTH]
+    ln_mid = gains[MODEL_WIDTH : 2 * MODEL_WIDTH]
+    q_gain = gains[2 * MODEL_WIDTH : 2 * MODEL_WIDTH + HEAD_SIZE]
+    k_gain = gains[2 * MODEL_WIDTH + HEAD_SIZE :]
+    x_rows = hidden_in.astype(jnp.float32)
+    full_in = gather_rows(to_slots(rms_norm(x_rows, ln_in).astype(jnp.bfloat16)))
+
+    qkv_blocks = gather_weight(projection_master_weight.astype(jnp.bfloat16))
+    w_qkv = jnp.concatenate(qkv_blocks, axis=0)
+    out_blocks = gather_weight(out_weight.astype(jnp.bfloat16))
+    w_out = jnp.take(jnp.stack(out_blocks), slot_of, axis=0).reshape(-1, width)
+    gateup_blocks = gather_weight(gateup_weight.astype(jnp.bfloat16))
+    w_gateup = jnp.concatenate(gateup_blocks, axis=0)
+    down_blocks = gather_weight(down_weight.astype(jnp.bfloat16))
+    w_down = jnp.take(jnp.stack(down_blocks), slot_of, axis=0).reshape(-1, width)
+
+    grad_out = cotangent.astype(jnp.float32)
+    d_branch = gather_rows(cotangent)
+
+    lengths = jnp.concatenate([doc_lengths, move(doc_lengths, OVER_C)], axis=0)
+    ends = jnp.cumsum(lengths, axis=1)
+    spot = jnp.arange(half, dtype=jnp.int32)
+    chunk = spot // rows_here
+    own_places = high * half + (low ^ chunk) * rows_here + spot % rows_here
+    key_places = jnp.concatenate([own_places - half, own_places])
+
+    def documents(places):
+        return jnp.sum((places[None, :, None] >= ends[:, None, :]).astype(jnp.int32), axis=2)
+
+    doc_of = documents(own_places)
+    key_doc = jnp.where(key_places[None, :] >= 0, documents(key_places), -1)
+    chosen = doc_of[:, :, None] == jnp.arange(lengths.shape[1], dtype=jnp.int32)[None, None, :]
+    begin = jnp.sum(jnp.where(chosen, (ends - lengths)[:, None, :], 0), axis=2)
+    offset = (own_places[None, :] - begin).astype(jnp.float32).reshape(count)
+    freq = THETA ** (
+        -(2.0 * jnp.arange(HEAD_SIZE // 2, dtype=jnp.float32)) / HEAD_SIZE
+    )
+    angle = offset[:, None] * freq[None, :]
+    cosine, sine = jnp.cos(angle), jnp.sin(angle)
+    cosine = jnp.concatenate([cosine, cosine], axis=-1)[:, None, :]
+    sine = jnp.concatenate([sine, sine], axis=-1)[:, None, :]
+
+    projected = jnp.dot(full_in, w_qkv, preferred_element_type=jnp.float32)
+    query_raw = projected[:, :query_width].reshape(count, heads, HEAD_SIZE)
+    unrotated_key = projected[:, query_width : query_width + key_width].reshape(
+        count, key_value_heads, HEAD_SIZE
+    )
+    query_rows = rotate(rms_norm(query_raw, q_gain), cosine, sine).astype(jnp.bfloat16)
+    key_rows = rotate(rms_norm(unrotated_key, k_gain), cosine, sine).astype(jnp.bfloat16)
+    key_rows = key_rows.reshape(count, key_width)
+    value_rows = projected[:, query_width + key_width :].astype(jnp.bfloat16)
+    own_kv = jnp.concatenate([key_rows, value_rows], axis=1)
+    lower_kv = move(own_kv, UPWARD)
+    all_kv = jnp.concatenate(
+        [lower_kv.reshape(2, half, 2 * key_width), own_kv.reshape(2, half, 2 * key_width)], axis=1
+    )
+    keys = all_kv[:, :, :key_width].reshape(2, count, key_value_heads, HEAD_SIZE)
+    values = all_kv[:, :, key_width:].reshape(2, count, key_value_heads, HEAD_SIZE)
+    queries = query_rows.reshape(2, half, key_value_heads, query_group, HEAD_SIZE)
+    score_scale = HEAD_SIZE ** (-0.5)
+
+    def scores_of(part):
+        query_block, key_block, row_doc, col_doc = part
+        raw = (
+            jnp.einsum("tlwd,uld->lwtu", query_block, key_block, preferred_element_type=jnp.float32)
+            * score_scale
+        )
+        allowed = (row_doc[:, None] == col_doc[None, :]) & (
+            key_places[None, :] <= own_places[:, None]
+        )
+        return jnp.where(allowed[None, None], raw, MASKED)
+
+    def forward_part(parts):
+        query_block, key_block, value_block, row_doc, col_doc = parts
+        score_matrix = scores_of((query_block, key_block, row_doc, col_doc))
+        top = jnp.max(score_matrix, axis=-1, keepdims=True)
+        total = jnp.log(jnp.sum(jnp.exp(score_matrix - top), axis=-1, keepdims=True)) + top
+        probabilities = jnp.exp(score_matrix - total).astype(jnp.bfloat16)
+        attention_result = jnp.einsum(
+            "cpyx,xca->ycpa", probabilities, value_block, preferred_element_type=jnp.float32
+        )
+        return (attention_result.reshape(half, query_width).astype(jnp.bfloat16), total)
+
+    outs, totals = lax.map(forward_part, (queries, keys, values, doc_of, key_doc))
+    attn_heads = outs.reshape(count, query_width)
+    mixed = x_rows + sum_rows(jnp.dot(attn_heads, w_out, preferred_element_type=jnp.float32))
+    full_mid = gather_rows(to_slots(rms_norm(mixed, ln_mid).astype(jnp.bfloat16)))
+    gateup = jnp.dot(full_mid, w_gateup, preferred_element_type=jnp.float32)
+    gate = gateup[:, :units]
+    upper = gateup[:, units:]
+    sigma = jax.nn.sigmoid(gate)
+    act = (gate * sigma * upper).astype(jnp.bfloat16)
+    result_rows = mixed + sum_rows(jnp.dot(act, w_down, preferred_element_type=jnp.float32))
+
+    g_down = jnp.einsum("tf,td->fd", act, d_branch, preferred_element_type=jnp.float32)
+    g_down = jnp.take(g_down.astype(jnp.bfloat16).reshape(8, -1, width), logical_of, axis=0)
+    red_down = reduce_weight(g_down)
+    d_act = jnp.einsum("td,fd->tf", d_branch, w_down, preferred_element_type=jnp.float32)
+    d_upper = d_act * gate * sigma
+    d_gate = d_act * upper * sigma * (1.0 + gate * (1.0 - sigma))
+    d_gateup = jnp.concatenate([d_gate, d_upper], axis=1).astype(jnp.bfloat16)
+    g_gateup = jnp.einsum("td,tf->df", full_mid, d_gateup, preferred_element_type=jnp.float32)
+    red_gateup = reduce_weight(g_gateup.astype(jnp.bfloat16).reshape(8, -1, 2 * units))
+    d_mid_rows = from_slots(
+        sum_rows(jnp.einsum("tc,dc->td", d_gateup, w_gateup, preferred_element_type=jnp.float32))
+    )
+    d_mixed, g_ln_mid = norm_back(mixed, ln_mid, d_mid_rows)
+    d_mixed = d_mixed + grad_out
+    d_attn = gather_rows(d_mixed.astype(jnp.bfloat16))
+    g_out = jnp.einsum("th,td->hd", attn_heads, d_attn, preferred_element_type=jnp.float32)
+    g_out = jnp.take(g_out.astype(jnp.bfloat16).reshape(8, -1, width), logical_of, axis=0)
+    red_out = reduce_weight(g_out)
+    d_heads = jnp.einsum("td,hd->th", d_attn, w_out, preferred_element_type=jnp.float32).astype(
+        jnp.bfloat16
+    )
+    d_heads = d_heads.reshape(2, half, key_value_heads, query_group, HEAD_SIZE)
+
+    def backward_part(parts):
+        query_block, key_block, value_block, row_doc, col_doc, block_total, block_gradient = parts
+        score_matrix = scores_of((query_block, key_block, row_doc, col_doc))
+        probabilities = jnp.exp(score_matrix - block_total)
+        probability_gradient = jnp.einsum(
+            "tlwd,uld->lwtu", block_gradient, value_block, preferred_element_type=jnp.float32
+        )
+        d_value = jnp.einsum(
+            "zxrb,rzxd->bzd",
+            probabilities.astype(jnp.bfloat16),
+            block_gradient,
+            preferred_element_type=jnp.float32,
+        )
+        score_gradient = (
+            probabilities
+            * (
+                probability_gradient
+                - jnp.sum(probabilities * probability_gradient, axis=-1, keepdims=True)
+            )
+        ).astype(jnp.bfloat16)
+        d_query = (
+            jnp.einsum(
+                "cpyx,xca->ycpa", score_gradient, key_block, preferred_element_type=jnp.float32
+            )
+            * score_scale
+        )
+        d_key = (
+            jnp.einsum(
+                "zxrb,rzxd->bzd", score_gradient, query_block, preferred_element_type=jnp.float32
+            )
+            * score_scale
+        )
+        d_kv = jnp.concatenate([d_key.reshape(count, key_width), d_value.reshape(count, key_width)], axis=1)
+        return (d_query.reshape(half, query_width), d_kv)
+
+    d_queries, d_kv = lax.map(
+        backward_part, (queries, keys, values, doc_of, key_doc, totals, d_heads)
+    )
+    from_above = move(d_kv[:, :half].astype(jnp.bfloat16), DOWNWARD)
+    d_kv = (d_kv[:, half:] + from_above.astype(jnp.float32)).reshape(count, 2 * key_width)
+    d_queries = d_queries.reshape(count, heads, HEAD_SIZE)
+    d_keys = d_kv[:, :key_width].reshape(count, key_value_heads, HEAD_SIZE)
+    d_query_raw, g_q = norm_back(query_raw, q_gain, rotate_back(d_queries, cosine, sine))
+    d_key_raw, g_k = norm_back(unrotated_key, k_gain, rotate_back(d_keys, cosine, sine))
+    d_projected = jnp.concatenate(
+        [
+            d_query_raw.reshape(count, query_width),
+            d_key_raw.reshape(count, key_width),
+            d_kv[:, key_width:],
+        ],
+        axis=1,
+    ).astype(jnp.bfloat16)
+    g_qkv = jnp.einsum("td,tc->dc", full_in, d_projected, preferred_element_type=jnp.float32)
+    red_qkv = reduce_weight(g_qkv.astype(jnp.bfloat16).reshape(8, width // 8, -1))
+    d_in_rows = from_slots(
+        sum_rows(jnp.einsum("tc,dc->td", d_projected, w_qkv, preferred_element_type=jnp.float32))
+    )
+    d_input, g_ln_in = norm_back(x_rows, ln_in, d_in_rows)
+    input_grad = d_input + d_mixed
+    gain_terms = jnp.concatenate([g_ln_in, g_ln_mid, g_q, g_k])
+    squares = jnp.sum(red_qkv * red_qkv) + jnp.sum(red_gateup * red_gateup)
+    squares = squares + jnp.sum(red_out * red_out) + jnp.sum(red_down * red_down)
+    total_squares, gain_grad = lax.psum((squares, gain_terms), ("dp", "mp"))
+    grad_norm = jnp.sqrt(total_squares + jnp.sum(gain_grad * gain_grad))
+    factor = jnp.minimum(1.0, CLIP_LIMIT / (grad_norm + 1e-06))
+    qkv_new, qkv_first_new, qkv_second_new = adam(
+        projection_master_weight,
+        projection_first_moment,
+        projection_second_moment,
+        red_qkv,
+        factor,
+        LEARN,
+        WEIGHT_DECAY,
+    )
+    gateup_new, gateup_first_new, gateup_second_new = adam(
+        gateup_weight, gateup_first, gateup_second, red_gateup, factor, LEARN, WEIGHT_DECAY
+    )
+    out_new, out_first_new, out_second_new = adam(
+        out_weight, out_first, out_second, red_out, factor, out_rate, WEIGHT_DECAY
+    )
+    down_new, down_first_new, down_second_new = adam(
+        down_weight, down_first, down_second, red_down, factor, LEARN, WEIGHT_DECAY
+    )
+    gains_new, gain_first_new, gain_second_new = adam(
+        gains, gain_first, gain_second, gain_grad, factor, GAIN_LEARN, 0.0
+    )
+    return (
+        result_rows.astype(jnp.bfloat16),
+        input_grad,
+        qkv_new,
+        gateup_new,
+        out_new,
+        down_new,
+        qkv_first_new,
+        gateup_first_new,
+        out_first_new,
+        down_first_new,
+        qkv_second_new,
+        gateup_second_new,
+        out_second_new,
+        down_second_new,
+        gains_new,
+        gain_first_new,
+        gain_second_new,
+        grad_norm,
+    )
+
+
+def paired(mesh):
+    return dict(mesh.shape) == {"dp": 8, "mp": 4}
+
+
 def solution(mesh):
     placed = (
         P(("dp", "mp"), None),
@@ -410,7 +764,7 @@
         P(),
     )
     return jax.shard_map(
-        shards,
+        shards_paired if paired(mesh) else shards_general,
         mesh=mesh,
         in_specs=placed,
         out_specs=(

time: 1500 us -> 1110 us (0.74)
  waiting for transfers between devices: 992 us -> 366 us
  starting transfers between devices: 0.66 us -> 159 us
  local copies, waits for them, and re-layouts: 108 us -> 191 us
  other arithmetic: 147 us -> 179 us
  matrix products: 171 us -> 148 us
    reduce_scatter x8 -> x0, waiting for transfers between devices: 633 us -> none  [the longest x2 285 us: spread_back(): lax.psum_scatter(term(jnp.int32(0), rows * lax.axis_size('mp')), 'mp', sc...]
    ppermute x0 -> x75, waiting for transfers between devices: none -> 366 us  [move(): return lax.ppermute(value, ('dp', 'mp'), pairs)]
    all_gather x8 -> x0, waiting for transfers between devices: 358 us -> none  [the longest x2 134 us: collect(): return lax.all_gather(rows, 'mp', axis=0, tiled=True)]
    ppermute x0 -> x75, starting transfers between devices: none -> 159 us  [move(): return lax.ppermute(value, ('dp', 'mp'), pairs)]
    unnamed x182 -> x347, local copies, waits for them, and re-layouts: 17 us -> 69.5 us
    slice x6 -> x25, local copies, waits for them, and re-layouts: 3.06 us -> 29.6 us  [the longest x4 5.37 us: reduce_weight(): a = move(jnp.stack([grads[4], grads[6]]), OVER_Y)]
    gather x8 -> x9, local copies, waits for them, and re-layouts: 52.5 us -> 27.5 us  [the longest x1 6.44 us: shards_paired(): jnp.take(jnp.stack(down_blocks), slot_of, axis=0).reshape(-1, width)]
    dot_general x26, matrix products: 171 us -> 148 us  [the longest x1 20.3 us: shards_paired(): jnp.einsum('td,tf->df', full_mid, d_gateup, preferred_element_type=jnp.fl...]
  transfers between devices with their start and end apart: 16 -> 75, of which waited for: 14 -> 25; matrix products, arithmetic and copies ran while one was open for 20% -> 39% of each run, Pallas kernels for 0% -> 0%
where the time goes in v1:
time: 1110 us; the launch traced here: 1100 us
  waiting for transfers between devices  366 us (33%)
  local copies, waits for them, and re-layouts  191 us (17%)
  other arithmetic  179 us (16%)
  starting transfers between devices  159 us (14%)
  matrix products  148 us (13%)
  blocking collectives  44.9 us (4%)
    ppermute x75, waiting for transfers between devices, move(): return lax.ppermute(value, ('dp', 'mp'), pairs)  366 us
    ppermute x75, starting transfers between devices, move(): return lax.ppermute(value, ('dp', 'mp'), pairs)  159 us
    unnamed x347, local copies, waits for them, and re-layouts  69.5 us
    psum x1, blocking collectives, shards_paired(): total_squares, gain_grad = lax.psum((squares, gain_terms), ('dp', 'mp'))  44.9 us
    convert_element_type x10, other arithmetic, plus(): (left.astype(jnp.float32) + right.astype(jnp.float32)).astype(jnp.bfloat16)  28 us
  transfers between devices with their start and end apart: 75, of which 25 were waited for; matrix products, arithmetic and copies ran while one was open for 39% of the time, Pallas kernels for 0%

profile of v1, /device:TPU:0, one launch (start us, length us, event | category | flops | bytes accessed | tf_op | source)
XLA Modules:
  0.0 1096.1 jit_solution(17044042073650591163)
XLA Ops:
  2.9 5.3 collective-permute-start.2
  35.1 7.4 collective-permute-start.32
  56.4 5.8 collective-permute-done.14
  64.4 6.3 collective-permute-done.15
  72.6 5.8 collective-permute-done.16
  79.8 5.2 collective-permute-done.17
  97.7 13.2 %collective-permute-done.19 = bf16[64,2048]{1,0:T(8,128)(2,1)S(1)} collective-permute-done((bf16[64,2048]{1,0:T(8,128)(2,1)S(1)}, bf16[64,2048]{1,0:T(8,128)(2,1)S(1)}, u32[]{:S(2)}, u32[]{:S(2)}) %collective-permute-start.19) | collective-permute-done | bytes 262176 | tf_op jit(solution)/shard_map/ppermute | solution.py:421
  124.3 9.5 collective-permute-done.7
  135.4 13.3 %collective-permute-start.24 = (bf16[256,3072]{1,0:T(8,128)(2,1)}, bf16[256,3072]{1,0:T(8,128)(2,1)}, u32[]{:S(2)}, u32[]{:S(2)}) collective-permute-start(bf16[256,3072]{1,0:T(8,128)(2,1)} %convert_element_type.458), channel_id=1, source_target_pairs={{0,0},{1,1},{4,2},{5,3},{2,4},{3,5},{6,6},{7,7},{8,8},{9,9},{12,10... | collective-permute-start | bytes 4718600 | tf_op jit(solution)/shard_map/ppermute | solution.py:421
  150.2 5.7 collective-permute-done.8
  156.6 7.9 fusion.99
  198.9 16.9 %collective-permute-done.11 = bf16[1024,512]{0,1:T(8,128)(2,1)} collective-permute-done((bf16[1024,512]{0,1:T(8,128)(2,1)}, bf16[1024,512]{0,1:T(8,128)(2,1)}, u32[]{:S(2)}, u32[]{:S(2)}) %collective-permute-start.11) | collective-permute-done | bytes 1048608 | tf_op jit(solution)/shard_map/ppermute | solution.py:421
  220.8 15.9 %while.26 = (s32[]{:T(128)}, bf16[2,512,512]{2,1,0:T(8,128)(2,1)}, f32[2,2,2,512,1]{3,2,1,4,0:T(2,128)S(1)}, bf16[2,1024,2,128]{1,3,2,0:T(8,128)(2,1)}, s32[2,51...) while((s32[]{:T(128)}, bf16[2,512,512]{2,1,0:T(8,128)(2,1)}, ...), condition=%wide.region_11.13_spmd.clone, body=%wide.region_8.12_spmd.clone.sunk | while | flops 1098651648 | bytes 35745448 | solution.py:598
  256.7 11.6 %collective-permute-done.36 = bf16[192,2048]{1,0:T(8,128)(2,1)S(1)} collective-permute-done((bf16[192,2048]{1,0:T(8,128)(2,1)}, bf16[192,2048]{1,0:T(8,128)(2,1)S(1)}, u32[]{:S(2)}, u32[]{:S(2)}) %collective-permute-start.36) | collective-permute-done | bytes 786464 | tf_op jit(solution)/shard_map/ppermute | solution.py:421
  271.2 33.7 %collective-permute-start.21 = (bf16[256,2048]{1,0:T(8,128)(2,1)S(1)}, bf16[256,2048]{1,0:T(8,128)(2,1)S(1)}, u32[]{:S(2)}, u32[]{:S(2)}) collective-permute-start(bf16[256,2048]{1,0:T(8,128)(2,1)S(1)} %slice.606), channel_id=1, source_target_pairs={{1,0},{0,1},{3,2},{2,3},{5,4},{4,5},{7,6},{6,7},{9,8},{8,9},{11,10... | collective-permute-start | bytes 3145736 | tf_op jit(solution)/shard_map/ppermute | solution.py:421
  312.4 14.4 %collective-permute-done.21 = bf16[256,2048]{1,0:T(8,128)(2,1)S(1)} collective-permute-done((bf16[256,2048]{1,0:T(8,128)(2,1)S(1)}, bf16[256,2048]{1,0:T(8,128)(2,1)S(1)}, u32[]{:S(2)}, u32[]{:S(2)}) %collective-permute-start.21) | collective-permute-done | bytes 1048608 | tf_op jit(solution)/shard_map/ppermute | solution.py:421
  331.9 27.4 %collective-permute-done.39 = bf16[192,2048]{1,0:T(8,128)(2,1)} collective-permute-done((bf16[192,2048]{1,0:T(8,128)(2,1)S(1)}, bf16[192,2048]{1,0:T(8,128)(2,1)}, u32[]{:S(2)}, u32[]{:S(2)}) %collective-permute-start.39) | collective-permute-done | bytes 786464 | tf_op jit(solution)/shard_map/ppermute | solution.py:421
  359.3 28.8 %collective-permute-start.22 = (bf16[256,2048]{0,1:T(8,128)(2,1)S(1)}, bf16[256,2048]{0,1:T(8,128)(2,1)S(1)}, u32[]{:S(2)}, u32[]{:S(2)}) collective-permute-start(bf16[256,2048]{0,1:T(8,128)(2,1)S(1)} %bitcast.489), channel_id=1, source_target_pairs={{1,0},{0,1},{3,2},{2,3},{5,4},{4,5},{7,6},{6,7},{9,8},{8,9},{11,10... | collective-permute-start | bytes 3145736 | tf_op jit(solution)/shard_map/ppermute | solution.py:421
  390.2 6.4 gather_fusion.4
  415.4 18.7 %collective-permute-done.28 = bf16[256,3072]{1,0:T(8,128)(2,1)S(1)} collective-permute-done((bf16[256,3072]{1,0:T(8,128)(2,1)}, bf16[256,3072]{1,0:T(8,128)(2,1)S(1)}, u32[]{:S(2)}, u32[]{:S(2)}) %collective-permute-start.28) | collective-permute-done | bytes 1572896 | tf_op jit(solution)/shard_map/ppermute | solution.py:421
  438.1 26.7 %collective-permute-done.30 = bf16[256,3072]{1,0:T(8,128)(2,1)S(1)} collective-permute-done((bf16[256,3072]{1,0:T(8,128)(2,1)}, bf16[256,3072]{1,0:T(8,128)(2,1)S(1)}, u32[]{:S(2)}, u32[]{:S(2)}) %collective-permute-start.30) | collective-permute-done | bytes 1572896 | tf_op jit(solution)/shard_map/ppermute | solution.py:421
  467.4 18.6 %fusion.98 = f32[1024,3072]{1,0:T(8,128)} fusion(bf16[2048,3072]{1,0:T(8,128)(2,1)} %constant_dynamic-update-slice_fusion.10, bf16[512,2048]{0,1:T(8,128)(2,1)S(1)} %collective-permute-done.23, bf16[256,2048]{0,1:T(8,128)(2,1)S(1)} %collective-permute-done.22, bf16[256,2048]{0,1:T(8,128)(2,1)S(1)} %bitcast.491), kind=kOutput, calls=%fused_computation.210 | convolution fusion | flops 12897484800 | bytes 29360128 | tf_op jit(solution)/shard_map/dot_general | solution.py:602
  486.0 14.0 %multiply_convert_fusion.1 = (bf16[1024,1536]{1,0:T(8,128)(2,1)S(1)}, bf16[1024,1536]{1,0:T(8,128)(2,1)}, bf16[1024,1536]{1,0:T(8,128)(2,1)S(1)}) fusion(f32[1024,3072]{1,0:T(8,128)} %fusion.98, bf16[1024,2048]{1,0:T(8,128)(2,1)} %copy-done.104, bf16[1536,2048]{1,0:T(8,128)(2,1)S(1)} %bitcast.478), kind=kOutput, calls=%fused_computation.110 | convolution fusion | flops 6467616768 | bytes 32505856 | tf_op jit(solution)/shard_map/td,fd->tf/dot_general | solution.py:612
  500.0 18.9 %fusion.70 = f32[1024,2048]{1,0:T(8,128)S(1)} fusion(bf16[2048,3072]{1,0:T(8,128)(2,1)} %constant_dynamic-update-slice_fusion.10, bf16[1024,1536]{1,0:T(8,128)(2,1)} %get-tuple-element.452, bf16[1024,1536]{1,0:T(8,128)(2,1)S(1)} %get-tuple-element.451), kind=kOutput, calls=%fused_computation.127 | convolution fusion | flops 12897484800 | bytes 27262976 | tf_op jit(solution)/shard_map/tc,dc->td/dot_general | solution.py:619
  524.3 9.1 convolution_convert_fusion.1
  533.4 6.4 gather_fusion.8
  548.2 20.3 %convolution_convert_fusion = bf16[2048,3072]{1,0:T(8,128)(2,1)} fusion(bf16[1024,1536]{1,0:T(8,128)(2,1)} %get-tuple-element.452, bf16[1024,1536]{1,0:T(8,128)(2,1)} %copy-done.154, bf16[512,2048]{0,1:T(8,128)(2,1)} %copy-done.150, bf16[256,2048]{0,1:T(8,128)(2,1)} %copy-done.86, bf16[256,2048]{0,1:T(8,128)(2,1)} %bitcast.492), kind=kOutput, calls=%fused_computation.106 | convolution fusion | flops 12916359168 | bytes 23068672 | tf_op jit(solution)/shard_map/td,tf->df/dot_general | solution.py:616
  572.2 6.7 fusion.167
  579.0 6.5 slice_add_fusion.1
  595.7 11.9 %collective-permute-done.45 = bf16[256,2048]{1,0:T(8,128)(2,1)S(1)} collective-permute-done((bf16[256,2048]{1,0:T(8,128)(2,1)S(1)}, bf16[256,2048]{1,0:T(8,128)(2,1)S(1)}, u32[]{:S(2)}, u32[]{:S(2)}) %collective-permute-start.45) | collective-permute-done | bytes 1048608 | tf_op jit(solution)/shard_map/ppermute | solution.py:421
  618.0 70.7 %collective-permute-done.69 = bf16[2,192,2048]{2,1,0:T(8,128)(2,1)} collective-permute-done((bf16[2,192,2048]{2,1,0:T(8,128)(2,1)}, bf16[2,192,2048]{2,1,0:T(8,128)(2,1)}, u32[]{:S(2)}, u32[]{:S(2)}) %collective-permute-start.69) | collective-permute-done | bytes 1572896 | tf_op jit(solution)/shard_map/ppermute | solution.py:421
  698.5 12.7 %collective-permute-done.70 = bf16[192,2048]{1,0:T(8,128)(2,1)S(1)} collective-permute-done((bf16[192,2048]{1,0:T(8,128)(2,1)S(1)}, bf16[192,2048]{1,0:T(8,128)(2,1)S(1)}, u32[]{:S(2)}, u32[]{:S(2)}) %collective-permute-start.70) | collective-permute-done | bytes 786464 | tf_op jit(solution)/shard_map/ppermute | solution.py:421
  714.6 7.5 collective-permute-start.71
  741.3 14.3 %collective-permute-done.74 = bf16[192,2048]{1,0:T(8,128)(2,1)} collective-permute-done((bf16[192,2048]{1,0:T(8,128)(2,1)}, bf16[192,2048]{1,0:T(8,128)(2,1)}, u32[]{:S(2)}, u32[]{:S(2)}) %collective-permute-start.74) | collective-permute-done | bytes 786464 | tf_op jit(solution)/shard_map/ppermute | solution.py:421
  758.0 6.6 add_convert_fusion.1
  765.2 5.2 fusion.104
  772.6 31.4 %while.27 = (s32[]{:T(128)}, f32[2,512,512]{1,2,0:T(8,128)}, f32[2,1024,512]{1,2,0:T(8,128)}, bf16[2,1024,2,128]{3,1,2,0:T(8,128)(2,1)S(1)}, s32[2,512]{1,0:T(2,...) while((s32[]{:T(128)}, f32[2,512,512]{1,2,0:T(8,128)}, ...), condition=%wide.region_16.21_spmd.clone, body=%wide.region_14.20_spmd.clone.sunk | while | flops 2718439424 | bytes 83448008 | solution.py:667
  825.7 5.3 convolution_convert_fusion.3
  847.5 15.4 %collective-permute-done.48 = bf16[2,512,512]{1,2,0:T(8,128)(2,1)} collective-permute-done((bf16[2,512,512]{1,2,0:T(8,128)(2,1)}, bf16[2,512,512]{1,2,0:T(8,128)(2,1)}, u32[]{:S(2)}, u32[]{:S(2)}) %collective-permute-start.48) | collective-permute-done | bytes 1048608 | tf_op jit(solution)/shard_map/ppermute | solution.py:421
  872.7 5.7 multiply_reduce_fusion.8
  884.8 6.3 convolution_convert_fusion.2
  907.3 10.2 collective-permute-done.51
  931.8 12.1 %collective-permute-done.54 = bf16[2,256,1024]{2,1,0:T(8,128)(2,1)} collective-permute-done((bf16[2,256,1024]{2,1,0:T(8,128)(2,1)}, bf16[2,256,1024]{2,1,0:T(8,128)(2,1)}, u32[]{:S(2)}, u32[]{:S(2)}) %collective-permute-start.54) | collective-permute-done | bytes 1048608 | tf_op jit(solution)/shard_map/ppermute | solution.py:421
  958.0 25.1 %collective-permute-done.68 = bf16[64,2048]{1,0:T(8,128)(2,1)S(1)} collective-permute-done((bf16[64,2048]{1,0:T(8,128)(2,1)}, bf16[64,2048]{1,0:T(8,128)(2,1)S(1)}, u32[]{:S(2)}, u32[]{:S(2)}) %collective-permute-start.68) | collective-permute-done | bytes 262176 | tf_op jit(solution)/shard_map/ppermute | solution.py:421
  992.0 18.0 %collective-permute-done.56 = bf16[256,1024]{1,0:T(8,128)(2,1)S(1)} collective-permute-done((bf16[256,1024]{1,0:T(8,128)(2,1)S(1)}, bf16[256,1024]{1,0:T(8,128)(2,1)S(1)}, u32[]{:S(2)}, u32[]{:S(2)}) %collective-permute-start.56) | collective-permute-done | bytes 524320 | tf_op jit(solution)/shard_map/ppermute | solution.py:421
  1025.0 44.9 %all-reduce = (f32[]{:T(128)}, f32[4352]{0:T(1024)S(1)}) all-reduce(f32[]{:T(128)S(6)} %add.452, f32[4352]{0:T(1024)S(1)} %pad_maximum_fusion.36), channel_id=1, replica_groups=mesh['dp'=8,'mp'=4] {'dp','mp'}, use_global_device_ids=true, to_apply=%region_24.29 | all-reduce | flops 4353 | bytes 34824 | tf_op jit(solution)/shard_map/psum | solution.py:694
  1072.7 6.1 divide_subtract_fusion.1
  1084.1 6.1 divide_subtract_fusion
  (722 shorter events, 432.9 us)
Async XLA Ops:
  2.9 83.9 %collective-permute-start.2 = (bf16[256,1024]{1,0:T(8,128)(2,1)}, bf16[256,1024]{1,0:T(8,128)(2,1)}, u32[]{:S(2)}, u32[]{:S(2)}) collective-permute-start(bf16[256,1024]{1,0:T(8,128)(2,1)} %convert_element_type.447), channel_id=1, source_target_pairs={{0,0},{1,1},{4,2},{5,3},{2,4},{3,5},{6,6},{7,7},{8,8},{9,9},{12,10... | collective-permute-start | bytes 1572872 | tf_op jit(solution)/shard_map/ppermute | solution.py:421
  8.2 84.9 %collective-permute-start.3 = (bf16[256,1024]{1,0:T(8,128)(2,1)}, bf16[256,1024]{1,0:T(8,128)(2,1)}, u32[]{:S(2)}, u32[]{:S(2)}) collective-permute-start(bf16[256,1024]{1,0:T(8,128)(2,1)} %convert_element_type.447), channel_id=1, source_target_pairs={{4,0},{5,1},{0,2},{1,3},{6,4},{7,5},{2,6},{3,7},{12,8},{13,9},{8,1... | collective-permute-start | bytes 1572872 | tf_op jit(solution)/shard_map/ppermute | solution.py:421
  10.6 40.4 %collective-permute-start.12 = (bf16[64,2048]{1,0:T(8,128)(2,1)}, bf16[64,2048]{1,0:T(8,128)(2,1)}, u32[]{:S(2)}, u32[]{:S(2)}) collective-permute-start(bf16[64,2048]{1,0:T(8,128)(2,1)} %convert_element_type.454), channel_id=1, source_target_pairs={{0,0},{1,1},{4,2},{5,3},{2,4},{3,5},{6,6},{7,7},{8,8},{9,9},{12,10... | collective-permute-start | bytes 786440 | tf_op jit(solution)/shard_map/ppermute | solution.py:421
  14.2 38.6 %collective-permute-start.13 = (bf16[64,2048]{1,0:T(8,128)(2,1)}, bf16[64,2048]{1,0:T(8,128)(2,1)}, u32[]{:S(2)}, u32[]{:S(2)}) collective-permute-start(bf16[64,2048]{1,0:T(8,128)(2,1)} %convert_element_type.454), channel_id=1, source_target_pairs={{4,0},{5,1},{0,2},{1,3},{6,4},{7,5},{2,6},{3,7},{12,8},{13,9},{8,1... | collective-permute-start | bytes 786440 | tf_op jit(solution)/shard_map/ppermute | solution.py:421
  35.1 83.8 %collective-permute-start.32 = (bf16[192,2048]{1,0:T(8,128)(2,1)}, bf16[192,2048]{1,0:T(8,128)(2,1)}, u32[]{:S(2)}, u32[]{:S(2)}) collective-permute-start(bf16[192,2048]{1,0:T(8,128)(2,1)} %convert_element_type.460), channel_id=1, source_target_pairs={{0,0},{1,1},{4,2},{5,3},{2,4},{3,5},{6,6},{7,7},{8,8},{9,9},{12,10... | collective-permute-start | bytes 2359304 | tf_op jit(solution)/shard_map/ppermute | solution.py:421
  51.1 70.3 %collective-permute-start.33 = (bf16[192,2048]{1,0:T(8,128)(2,1)}, bf16[192,2048]{1,0:T(8,128)(2,1)S(1)}, u32[]{:S(2)}, u32[]{:S(2)}) collective-permute-start(bf16[192,2048]{1,0:T(8,128)(2,1)} %convert_element_type.460), channel_id=1, source_target_pairs={{4,0},{5,1},{0,2},{1,3},{6,4},{7,5},{2,6},{3,7},{12,8},{13,9},{8,1... | collective-permute-start | bytes 2359304 | tf_op jit(solution)/shard_map/ppermute | solution.py:421
  117.1 39.4 %collective-permute-start.1 = (bf16[512,2048]{0,1:T(8,128)(2,1)S(1)}, bf16[512,2048]{0,1:T(8,128)(2,1)S(1)}, u32[]{:S(2)}, u32[]{:S(2)}) collective-permute-start(bf16[512,2048]{0,1:T(8,128)(2,1)S(1)} %pad_maximum_fusion.8), channel_id=1, source_target_pairs={{4,0},{5,1},{6,2},{7,3},{0,4},{1,5},{2,6},{3,7},{12,8},{13,9},{14,... | collective-permute-start | bytes 6291464 | tf_op jit(solution)/shard_map/ppermute | solution.py:421
  123.0 32.8 %collective-permute-start.8 = (bf16[256,1024]{1,0:T(8,128)(2,1)}, bf16[256,1024]{1,0:T(8,128)(2,1)S(1)}, u32[]{:S(2)}, u32[]{:S(2)}) collective-permute-start(bf16[256,1024]{1,0:T(8,128)(2,1)} %collective-permute-done.4), channel_id=1, source_target_pairs={{16,0},{17,1},{18,2},{19,3},{20,4},{21,5},{22,6},{23,7},{24,8},{25... | collective-permute-start | bytes 1572872 | tf_op jit(solution)/shard_map/ppermute | solution.py:421
  135.4 118.6 %collective-permute-start.24 = (bf16[256,3072]{1,0:T(8,128)(2,1)}, bf16[256,3072]{1,0:T(8,128)(2,1)}, u32[]{:S(2)}, u32[]{:S(2)}) collective-permute-start(bf16[256,3072]{1,0:T(8,128)(2,1)} %convert_element_type.458), channel_id=1, source_target_pairs={{0,0},{1,1},{4,2},{5,3},{2,4},{3,5},{6,6},{7,7},{8,8},{9,9},{12,10... | collective-permute-start | bytes 4718600 | tf_op jit(solution)/shard_map/ppermute | solution.py:421
  149.8 121.4 %collective-permute-start.25 = (bf16[256,3072]{1,0:T(8,128)(2,1)}, bf16[256,3072]{1,0:T(8,128)(2,1)}, u32[]{:S(2)}, u32[]{:S(2)}) collective-permute-start(bf16[256,3072]{1,0:T(8,128)(2,1)} %convert_element_type.458), channel_id=1, source_target_pairs={{4,0},{5,1},{0,2},{1,3},{6,4},{7,5},{2,6},{3,7},{12,8},{13,9},{8,1... | collective-permute-start | bytes 4718600 | tf_op jit(solution)/shard_map/ppermute | solution.py:421
  155.9 86.3 %collective-permute-start.42 = (bf16[256,2048]{1,0:T(8,128)(2,1)}, bf16[256,2048]{1,0:T(8,128)(2,1)}, u32[]{:S(2)}, u32[]{:S(2)}) collective-permute-start(bf16[256,2048]{1,0:T(8,128)(2,1)} %param.32), channel_id=1, source_target_pairs={{1,0},{0,1},{3,2},{2,3},{5,4},{4,5},{7,6},{6,7},{9,8},{8,9},{11,10... | collective-permute-start | bytes 3145736 | tf_op jit(solution)/shard_map/ppermute | solution.py:421
  155.9 91.8 %collective-permute-start.34 = (bf16[192,2048]{1,0:T(8,128)(2,1)}, bf16[192,2048]{1,0:T(8,128)(2,1)}, u32[]{:S(2)}, u32[]{:S(2)}) collective-permute-start(bf16[192,2048]{1,0:T(8,128)(2,1)} %collective-permute-done.32), channel_id=1, source_target_pairs={{8,0},{9,1},{10,2},{11,3},{12,4},{13,5},{14,6},{15,7},{0,8},{1,9},... | collective-permute-start | bytes 2359304 | tf_op jit(solution)/shard_map/ppermute | solution.py:421
  176.7 39.1 %collective-permute-start.11 = (bf16[1024,512]{0,1:T(8,128)(2,1)}, bf16[1024,512]{0,1:T(8,128)(2,1)}, u32[]{:S(2)}, u32[]{:S(2)}) collective-permute-start(bf16[1024,512]{0,1:T(8,128)(2,1)} %pad_maximum_fusion.24), channel_id=1, source_target_pairs={{0,2},{1,3},{4,6},{5,7},{8,10},{9,11},{12,14},{13,15},{16,18},{17,... | collective-permute-start | bytes 3145736 | tf_op jit(solution)/shard_map/ppermute | solution.py:421
  215.8 34.4 %collective-permute-start.35 = (bf16[192,2048]{1,0:T(8,128)(2,1)}, bf16[192,2048]{1,0:T(8,128)(2,1)}, u32[]{:S(2)}, u32[]{:S(2)}) collective-permute-start(bf16[192,2048]{1,0:T(8,128)(2,1)} %copy-done.91), channel_id=1, source_target_pairs={{8,0},{9,1},{10,2},{11,3},{12,4},{13,5},{14,6},{15,7},{0,8},{1,9},... | collective-permute-start | bytes 2359304 | tf_op jit(solution)/shard_map/ppermute | solution.py:421
  250.2 57.3 %collective-permute-start.37 = (bf16[192,2048]{1,0:T(8,128)(2,1)S(1)}, bf16[192,2048]{1,0:T(8,128)(2,1)S(1)}, u32[]{:S(2)}, u32[]{:S(2)}) collective-permute-start(bf16[192,2048]{1,0:T(8,128)(2,1)S(1)} %copy-done.92), channel_id=1, source_target_pairs={{16,0},{17,1},{18,2},{19,3},{20,4},{21,5},{22,6},{23,7},{24,8},{25... | collective-permute-start | bytes 2359304 | tf_op jit(solution)/shard_map/ppermute | solution.py:421
  254.0 142.6 %collective-permute-start.43 = (bf16[512,2048]{1,0:T(8,128)(2,1)}, bf16[512,2048]{1,0:T(8,128)(2,1)}, u32[]{:S(2)}, u32[]{:S(2)}) collective-permute-start(bf16[512,2048]{1,0:T(8,128)(2,1)} %pad_maximum_fusion.10), channel_id=1, source_target_pairs={{4,0},{5,1},{6,2},{7,3},{0,4},{1,5},{2,6},{3,7},{12,8},{13,9},{14,... | collective-permute-start | bytes 6291464 | tf_op jit(solution)/shard_map/ppermute | solution.py:421
  268.3 137.8 %collective-permute-start.26 = (bf16[256,3072]{1,0:T(8,128)(2,1)}, bf16[256,3072]{1,0:T(8,128)(2,1)}, u32[]{:S(2)}, u32[]{:S(2)}) collective-permute-start(bf16[256,3072]{1,0:T(8,128)(2,1)} %collective-permute-done.24), channel_id=1, source_target_pairs={{8,0},{9,1},{10,2},{11,3},{12,4},{13,5},{14,6},{15,7},{0,8},{1,9},... | collective-permute-start | bytes 4718600 | tf_op jit(solution)/shard_map/ppermute | solution.py:421
  269.8 40.1 %collective-permute-start.38 = (bf16[192,2048]{1,0:T(8,128)(2,1)}, bf16[192,2048]{1,0:T(8,128)(2,1)S(1)}, u32[]{:S(2)}, u32[]{:S(2)}) collective-permute-start(bf16[192,2048]{1,0:T(8,128)(2,1)} %collective-permute-done.34), channel_id=1, source_target_pairs={{16,0},{17,1},{18,2},{19,3},{20,4},{21,5},{22,6},{23,7},{24,8},{25... | collective-permute-start | bytes 2359304 | tf_op jit(solution)/shard_map/ppermute | solution.py:421
  271.2 55.6 %collective-permute-start.21 = (bf16[256,2048]{1,0:T(8,128)(2,1)S(1)}, bf16[256,2048]{1,0:T(8,128)(2,1)S(1)}, u32[]{:S(2)}, u32[]{:S(2)}) collective-permute-start(bf16[256,2048]{1,0:T(8,128)(2,1)S(1)} %slice.606), channel_id=1, source_target_pairs={{1,0},{0,1},{3,2},{2,3},{5,4},{4,5},{7,6},{6,7},{9,8},{8,9},{11,10... | collective-permute-start | bytes 3145736 | tf_op jit(solution)/shard_map/ppermute | solution.py:421
  307.5 105.2 %collective-permute-start.27 = (bf16[256,3072]{1,0:T(8,128)(2,1)}, bf16[256,3072]{1,0:T(8,128)(2,1)}, u32[]{:S(2)}, u32[]{:S(2)}) collective-permute-start(bf16[256,3072]{1,0:T(8,128)(2,1)} %collective-permute-done.25), channel_id=1, source_target_pairs={{8,0},{9,1},{10,2},{11,3},{12,4},{13,5},{14,6},{15,7},{0,8},{1,9},... | collective-permute-start | bytes 4718600 | tf_op jit(solution)/shard_map/ppermute | solution.py:421
  309.9 97.5 %collective-permute-start.29 = (bf16[256,3072]{1,0:T(8,128)(2,1)}, bf16[256,3072]{1,0:T(8,128)(2,1)}, u32[]{:S(2)}, u32[]{:S(2)}) collective-permute-start(bf16[256,3072]{1,0:T(8,128)(2,1)} %collective-permute-done.25), channel_id=1, source_target_pairs={{16,0},{17,1},{18,2},{19,3},{20,4},{21,5},{22,6},{23,7},{24,8},{25... | collective-permute-start | bytes 4718600 | tf_op jit(solution)/shard_map/ppermute | solution.py:421
  326.8 32.5 %collective-permute-start.39 = (bf16[192,2048]{1,0:T(8,128)(2,1)S(1)}, bf16[192,2048]{1,0:T(8,128)(2,1)}, u32[]{:S(2)}, u32[]{:S(2)}) collective-permute-start(bf16[192,2048]{1,0:T(8,128)(2,1)S(1)} %collective-permute-done.37), channel_id=1, source_target_pairs={{8,0},{9,1},{10,2},{11,3},{12,4},{13,5},{14,6},{15,7},{0,8},{1,9},... | collective-permute-start | bytes 2359304 | tf_op jit(solution)/shard_map/ppermute | solution.py:421
  359.3 50.3 %collective-permute-start.22 = (bf16[256,2048]{0,1:T(8,128)(2,1)S(1)}, bf16[256,2048]{0,1:T(8,128)(2,1)S(1)}, u32[]{:S(2)}, u32[]{:S(2)}) collective-permute-start(bf16[256,2048]{0,1:T(8,128)(2,1)S(1)} %bitcast.489), channel_id=1, source_target_pairs={{1,0},{0,1},{3,2},{2,3},{5,4},{4,5},{7,6},{6,7},{9,8},{8,9},{11,10... | collective-permute-start | bytes 3145736 | tf_op jit(solution)/shard_map/ppermute | solution.py:421
  396.6 37.5 %collective-permute-start.28 = (bf16[256,3072]{1,0:T(8,128)(2,1)}, bf16[256,3072]{1,0:T(8,128)(2,1)S(1)}, u32[]{:S(2)}, u32[]{:S(2)}) collective-permute-start(bf16[256,3072]{1,0:T(8,128)(2,1)} %collective-permute-done.24), channel_id=1, source_target_pairs={{16,0},{17,1},{18,2},{19,3},{20,4},{21,5},{22,6},{23,7},{24,8},{25... | collective-permute-start | bytes 4718600 | tf_op jit(solution)/shard_map/ppermute | solution.py:421
  406.1 58.7 %collective-permute-start.30 = (bf16[256,3072]{1,0:T(8,128)(2,1)}, bf16[256,3072]{1,0:T(8,128)(2,1)S(1)}, u32[]{:S(2)}, u32[]{:S(2)}) collective-permute-start(bf16[256,3072]{1,0:T(8,128)(2,1)} %collective-permute-done.26), channel_id=1, source_target_pairs={{16,0},{17,1},{18,2},{19,3},{20,4},{21,5},{22,6},{23,7},{24,8},{25... | collective-permute-start | bytes 4718600 | tf_op jit(solution)/shard_map/ppermute | solution.py:421
  407.4 58.7 %collective-permute-start.31 = (bf16[256,3072]{1,0:T(8,128)(2,1)}, bf16[256,3072]{1,0:T(8,128)(2,1)S(1)}, u32[]{:S(2)}, u32[]{:S(2)}) collective-permute-start(bf16[256,3072]{1,0:T(8,128)(2,1)} %collective-permute-done.29), channel_id=1, source_target_pairs={{8,0},{9,1},{10,2},{11,3},{12,4},{13,5},{14,6},{15,7},{0,8},{1,9},... | collective-permute-start | bytes 4718600 | tf_op jit(solution)/shard_map/ppermute | solution.py:421
  409.8 57.6 %collective-permute-start.23 = (bf16[512,2048]{0,1:T(8,128)(2,1)S(1)}, bf16[512,2048]{0,1:T(8,128)(2,1)S(1)}, u32[]{:S(2)}, u32[]{:S(2)}) collective-permute-start(bf16[512,2048]{0,1:T(8,128)(2,1)S(1)} %pad_maximum_fusion.9), channel_id=1, source_target_pairs={{4,0},{5,1},{6,2},{7,3},{0,4},{1,5},{2,6},{3,7},{12,8},{13,9},{14,... | collective-permute-start | bytes 6291464 | tf_op jit(solution)/shard_map/ppermute | solution.py:421
  520.7 58.3 %collective-permute-start.44 = (bf16[512,2048]{1,0:T(8,128)(2,1)}, bf16[512,2048]{1,0:T(8,128)(2,1)}, u32[]{:S(2)}, u32[]{:S(2)}) collective-permute-start(bf16[512,2048]{1,0:T(8,128)(2,1)} %slice.599), channel_id=1, source_target_pairs={{4,0},{5,1},{6,2},{7,3},{0,4},{1,5},{2,6},{3,7},{12,8},{13,9},{14,... | collective-permute-start | bytes 6291464 | tf_op jit(solution)/shard_map/ppermute | solution.py:421
  547.7 69.7 %collective-permute-start.72 = (bf16[2,192,2048]{2,1,0:T(8,128)(2,1)}, bf16[2,192,2048]{2,1,0:T(8,128)(2,1)}, u32[]{:S(2)}, u32[]{:S(2)}) collective-permute-start(bf16[2,192,2048]{2,1,0:T(8,128)(2,1)} %pad_maximum_fusion.21), channel_id=1, source_target_pairs={{8,0},{9,1},{10,2},{11,3},{12,4},{13,5},{14,6},{15,7},{0,8},{1,9},... | collective-permute-start | bytes 4718600 | tf_op jit(solution)/shard_map/ppermute | solution.py:421
  587.9 103.8 %collective-permute-start.57 = (bf16[2,256,3072]{2,1,0:T(8,128)(2,1)}, bf16[2,256,3072]{2,1,0:T(8,128)(2,1)}, u32[]{:S(2)}, u32[]{:S(2)}) collective-permute-start(bf16[2,256,3072]{2,1,0:T(8,128)(2,1)} %pad_maximum_fusion.6), channel_id=1, source_target_pairs={{16,0},{17,1},{18,2},{19,3},{20,4},{21,5},{22,6},{23,7},{24,8},{25... | collective-permute-start | bytes 9437192 | tf_op jit(solution)/shard_map/ppermute | solution.py:421
  589.6 99.1 %collective-permute-start.69 = (bf16[2,192,2048]{2,1,0:T(8,128)(2,1)}, bf16[2,192,2048]{2,1,0:T(8,128)(2,1)}, u32[]{:S(2)}, u32[]{:S(2)}) collective-permute-start(bf16[2,192,2048]{2,1,0:T(8,128)(2,1)} %pad_maximum_fusion.20), channel_id=1, source_target_pairs={{16,0},{17,1},{18,2},{19,3},{20,4},{21,5},{22,6},{23,7},{24,8},{25... | collective-permute-start | bytes 4718600 | tf_op jit(solution)/shard_map/ppermute | solution.py:421
  593.1 164.8 %collective-permute-start.60 = (bf16[2,256,3072]{2,1,0:T(8,128)(2,1)}, bf16[2,256,3072]{2,1,0:T(8,128)(2,1)}, u32[]{:S(2)}, u32[]{:S(2)}) collective-permute-start(bf16[2,256,3072]{2,1,0:T(8,128)(2,1)} %pad_maximum_fusion.7), channel_id=1, source_target_pairs={{8,0},{9,1},{10,2},{11,3},{12,4},{13,5},{14,6},{15,7},{0,8},{1,9},... | collective-permute-start | bytes 9437192 | tf_op jit(solution)/shard_map/ppermute | solution.py:421
  607.5 114.6 %collective-permute-start.40 = (bf16[512,2048]{1,0:T(8,128)(2,1)}, bf16[512,2048]{1,0:T(8,128)(2,1)}, u32[]{:S(2)}, u32[]{:S(2)}) collective-permute-start(bf16[512,2048]{1,0:T(8,128)(2,1)} %slice.600), channel_id=1, source_target_pairs={{4,0},{5,1},{6,2},{7,3},{0,4},{1,5},{2,6},{3,7},{12,8},{13,9},{14,... | collective-permute-start | bytes 6291464 | tf_op jit(solution)/shard_map/ppermute | solution.py:421
  617.4 78.3 %collective-permute-start.46 = (bf16[256,2048]{1,0:T(8,128)(2,1)S(1)}, bf16[256,2048]{1,0:T(8,128)(2,1)S(1)}, u32[]{:S(2)}, u32[]{:S(2)}) collective-permute-start(bf16[256,2048]{1,0:T(8,128)(2,1)S(1)} %fusion.155), channel_id=1, source_target_pairs={{1,0},{0,1},{3,2},{2,3},{5,4},{4,5},{7,6},{6,7},{9,8},{8,9},{11,10... | collective-permute-start | bytes 3145736 | tf_op jit(solution)/shard_map/ppermute | solution.py:421
  695.7 62.2 %collective-permute-start.58 = (bf16[256,3072]{1,0:T(8,128)(2,1)}, bf16[256,3072]{1,0:T(8,128)(2,1)}, u32[]{:S(2)}, u32[]{:S(2)}) collective-permute-start(bf16[256,3072]{1,0:T(8,128)(2,1)} %fusion.74), channel_id=1, source_target_pairs={{8,0},{9,1},{10,2},{11,3},{12,4},{13,5},{14,6},{15,7},{0,8},{1,9},... | collective-permute-start | bytes 4718600 | tf_op jit(solution)/shard_map/ppermute | solution.py:421
  711.3 53.9 %collective-permute-start.47 = (bf16[512,2048]{1,0:T(8,128)(2,1)}, bf16[512,2048]{1,0:T(8,128)(2,1)}, u32[]{:S(2)}, u32[]{:S(2)}) collective-permute-start(bf16[512,2048]{1,0:T(8,128)(2,1)} %pad_maximum_fusion.11), channel_id=1, source_target_pairs={{4,0},{5,1},{6,2},{7,3},{0,4},{1,5},{2,6},{3,7},{12,8},{13,9},{14,... | collective-permute-start | bytes 6291464 | tf_op jit(solution)/shard_map/ppermute | solution.py:421
  722.1 33.4 %collective-permute-start.74 = (bf16[192,2048]{1,0:T(8,128)(2,1)}, bf16[192,2048]{1,0:T(8,128)(2,1)}, u32[]{:S(2)}, u32[]{:S(2)}) collective-permute-start(bf16[192,2048]{1,0:T(8,128)(2,1)} %get-tuple-element.461), channel_id=1, source_target_pairs={{0,4},{1,5},{2,0},{3,1},{4,6},{5,7},{6,2},{7,3},{8,12},{9,13},{10,... | collective-permute-start | bytes 2359304 | tf_op jit(solution)/shard_map/ppermute | solution.py:421
  764.6 154.7 %collective-permute-start.61 = (bf16[256,3072]{1,0:T(8,128)(2,1)}, bf16[256,3072]{1,0:T(8,128)(2,1)}, u32[]{:S(2)}, u32[]{:S(2)}) collective-permute-start(bf16[256,3072]{1,0:T(8,128)(2,1)} %get-tuple-element.454), channel_id=1, source_target_pairs={{16,0},{17,1},{18,2},{19,3},{20,4},{21,5},{22,6},{23,7},{24,8},{25... | collective-permute-start | bytes 4718600 | tf_op jit(solution)/shard_map/ppermute | solution.py:421
  821.2 41.6 %collective-permute-start.48 = (bf16[2,512,512]{1,2,0:T(8,128)(2,1)}, bf16[2,512,512]{1,2,0:T(8,128)(2,1)}, u32[]{:S(2)}, u32[]{:S(2)}) collective-permute-start(bf16[2,512,512]{1,2,0:T(8,128)(2,1)} %slice.603), channel_id=1, source_target_pairs={{2,0},{3,1},{6,4},{7,5},{10,8},{11,9},{14,12},{15,13},{18,16},{19,... | collective-permute-start | bytes 3145736 | tf_op jit(solution)/shard_map/ppermute | solution.py:421
  837.8 63.2 %collective-permute-start.66 = (bf16[2,64,2048]{2,1,0:T(8,128)(2,1)}, bf16[2,64,2048]{2,1,0:T(8,128)(2,1)}, u32[]{:S(2)}, u32[]{:S(2)}) collective-permute-start(bf16[2,64,2048]{2,1,0:T(8,128)(2,1)} %pad_maximum_fusion.35), channel_id=1, source_target_pairs={{8,0},{9,1},{10,2},{11,3},{12,4},{13,5},{14,6},{15,7},{0,8},{1,9},... | collective-permute-start | bytes 1572872 | tf_op jit(solution)/shard_map/ppermute | solution.py:421
  839.4 61.6 %collective-permute-start.63 = (bf16[2,64,2048]{2,1,0:T(8,128)(2,1)}, bf16[2,64,2048]{2,1,0:T(8,128)(2,1)}, u32[]{:S(2)}, u32[]{:S(2)}) collective-permute-start(bf16[2,64,2048]{2,1,0:T(8,128)(2,1)} %pad_maximum_fusion.34), channel_id=1, source_target_pairs={{16,0},{17,1},{18,2},{19,3},{20,4},{21,5},{22,6},{23,7},{24,8},{25... | collective-permute-start | bytes 1572872 | tf_op jit(solution)/shard_map/ppermute | solution.py:421
  901.0 50.8 %collective-permute-start.49 = (bf16[512,2048]{1,0:T(8,128)(2,1)}, bf16[512,2048]{1,0:T(8,128)(2,1)}, u32[]{:S(2)}, u32[]{:S(2)}) collective-permute-start(bf16[512,2048]{1,0:T(8,128)(2,1)} %slice.598), channel_id=1, source_target_pairs={{4,0},{5,1},{6,2},{7,3},{0,4},{1,5},{2,6},{3,7},{12,8},{13,9},{14,... | collective-permute-start | bytes 6291464 | tf_op jit(solution)/shard_map/ppermute | solution.py:421
  924.8 63.7 %collective-permute-start.59 = (bf16[256,3072]{1,0:T(8,128)(2,1)}, bf16[256,3072]{1,0:T(8,128)(2,1)S(1)}, u32[]{:S(2)}, u32[]{:S(2)}) collective-permute-start(bf16[256,3072]{1,0:T(8,128)(2,1)} %get-tuple-element.453), channel_id=1, source_target_pairs={{0,0},{1,1},{2,4},{3,5},{4,2},{5,3},{6,6},{7,7},{8,8},{9,9},{10,12... | collective-permute-start | bytes 4718600 | tf_op jit(solution)/shard_map/ppermute | solution.py:421
  926.9 61.7 %collective-permute-start.62 = (bf16[256,3072]{1,0:T(8,128)(2,1)}, bf16[256,3072]{1,0:T(8,128)(2,1)}, u32[]{:S(2)}, u32[]{:S(2)}) collective-permute-start(bf16[256,3072]{1,0:T(8,128)(2,1)} %add_convert_fusion), channel_id=1, source_target_pairs={{0,4},{1,5},{2,0},{3,1},{4,6},{5,7},{6,2},{7,3},{8,12},{9,13},{10,... | collective-permute-start | bytes 4718600 | tf_op jit(solution)/shard_map/ppermute | solution.py:421
  949.6 33.5 %collective-permute-start.68 = (bf16[64,2048]{1,0:T(8,128)(2,1)}, bf16[64,2048]{1,0:T(8,128)(2,1)S(1)}, u32[]{:S(2)}, u32[]{:S(2)}) collective-permute-start(bf16[64,2048]{1,0:T(8,128)(2,1)} %get-tuple-element.475), channel_id=1, source_target_pairs={{0,4},{1,5},{2,0},{3,1},{4,6},{5,7},{6,2},{7,3},{8,12},{9,13},{10,... | collective-permute-start | bytes 786440 | tf_op jit(solution)/shard_map/ppermute | solution.py:421
  951.8 32.8 %collective-permute-start.55 = (bf16[256,1024]{1,0:T(8,128)(2,1)S(1)}, bf16[256,1024]{1,0:T(8,128)(2,1)S(1)}, u32[]{:S(2)}, u32[]{:S(2)}) collective-permute-start(bf16[256,1024]{1,0:T(8,128)(2,1)S(1)} %get-tuple-element.469), channel_id=1, source_target_pairs={{16,0},{17,1},{18,2},{19,3},{20,4},{21,5},{22,6},{23,7},{24,8},{25... | collective-permute-start | bytes 1572872 | tf_op jit(solution)/shard_map/ppermute | solution.py:421
  958.0 58.7 %collective-permute-start.50 = (bf16[256,2048]{1,0:T(8,128)(2,1)}, bf16[256,2048]{1,0:T(8,128)(2,1)}, u32[]{:S(2)}, u32[]{:S(2)}) collective-permute-start(bf16[256,2048]{1,0:T(8,128)(2,1)} %slice.602), channel_id=1, source_target_pairs={{1,0},{0,1},{3,2},{2,3},{5,4},{4,5},{7,6},{6,7},{9,8},{8,9},{11,10... | collective-permute-start | bytes 3145736 | tf_op jit(solution)/shard_map/ppermute | solution.py:421
  1024.9 65.3 %collective-permute-start.41 = (bf16[256,2048]{1,0:T(8,128)(2,1)}, bf16[256,2048]{1,0:T(8,128)(2,1)}, u32[]{:S(2)}, u32[]{:S(2)}) collective-permute-start(bf16[256,2048]{1,0:T(8,128)(2,1)} %slice.605), channel_id=1, source_target_pairs={{1,0},{0,1},{3,2},{2,3},{5,4},{4,5},{7,6},{6,7},{9,8},{8,9},{11,10... | collective-permute-start | bytes 3145736 | tf_op jit(solution)/shard_map/ppermute | solution.py:421
  (188 other events, 5554.0 us)

commit v2 on v1

--- a/solution.py
+++ b/solution.py
@@ -1,6 +1,8 @@
 import jax
 import jax.numpy as jnp
 from jax import lax
+from jax.experimental import pallas as pl
+from jax.experimental.pallas import tpu as pltpu
 from jax.sharding import PartitionSpec as P
 
 MODEL_WIDTH = 2048
@@ -425,45 +427,410 @@
     return lax.optimization_barrier((value, *others))[0]
 
 
-def gather_weight(shard):
-    a = move(shard, TO_GROUP[0])
-    b = move(shard, TO_GROUP[1])
-    ax, ay = move(a, OVER_X), move(a, OVER_Y)
-    by, bx = move(b, OVER_Y), move(b, OVER_X)
-    axy, bxy = move(ax, OVER_Y), move(by, OVER_X)
-    return [a, b, ax, bx, ay, by, axy, bxy]
-
-
-def reduce_weight(grads):
-    def plus(left, right):
-        return (left.astype(jnp.float32) + right.astype(jnp.float32)).astype(jnp.bfloat16)
-
-    a = move(jnp.stack([grads[4], grads[6]]), OVER_Y)
-    b = move(jnp.stack([grads[3], grads[7]]), OVER_X)
-    a_far = plus(grads[2], a[1])
-    b_far = plus(grads[5], b[1])
-    a_far = move(a_far, OVER_X)
-    b_far = move(b_far, OVER_Y)
-    a_own = plus(plus(grads[0], a[0]), a_far)
-    b_own = plus(plus(grads[1], b[0]), b_far)
-    return move(a_own, FROM_GROUP[0]).astype(jnp.float32) + move(b_own, FROM_GROUP[1]).astype(
-        jnp.float32
-    )
-
-
-def gather_rows(rows):
-    pair = jnp.concatenate([rows, move(rows, OVER_L)], axis=0)
-    return jnp.concatenate([pair, move(pair, OVER_C)], axis=0)
-
-
-def sum_rows(partial):
-    half = partial.shape[0] // 2
-    quarter = half // 2
-    near = move(partial[half:].astype(jnp.bfloat16), OVER_C).astype(jnp.float32)
-    summed = partial[:half] + near
-    return summed[:quarter] + move(summed[quarter:].astype(jnp.bfloat16), OVER_L).astype(
-        jnp.float32
-    )
+PLANES = [[(block * 2 + c) * 4 + z for block in range(4)] for c in range(2) for z in range(4)]
+
+
+MESH = pl.DeviceIdType.MESH
+
+
+class Place:
+    def __init__(self):
+        dp, mp = lax.axis_index("dp"), lax.axis_index("mp")
+        self.y, self.x, self.c = dp // 4, (dp // 2) % 2, dp % 2
+        self.h, self.l = mp // 2, mp % 2
+        self.block = (dp // 2) * 2
+
+    def at(self, y=None, x=None, c=None, h=None, l=None):
+        y, x, c = (o if n is None else n for o, n in ((self.y, y), (self.x, x), (self.c, c)))
+        h, l = (o if n is None else n for o, n in ((self.h, h), (self.l, l)))
+        return ((y * 2 + x) * 2 + c, h * 2 + l)
+
+    def partners(self):
+        return [
+            self.at(x=1 - self.x),
+            self.at(y=1 - self.y),
+            self.at(l=1 - self.l),
+            self.at(c=1 - self.c),
+            self.at(h=1 - self.h),
+            self.at(c=1 - self.c, h=1 - self.h),
+        ]
+
+
+def far_copy(source, target, sems, index, device):
+    return pltpu.make_async_remote_copy(
+        src_ref=source,
+        dst_ref=target,
+        send_sem=sems[0].at[index],
+        recv_sem=sems[1].at[index],
+        device_id=device,
+        device_id_type=MESH,
+    )
+
+
+class Swap:
+    def __init__(self, place, source, target, sems, index, local_sem):
+        self.same = place.c == place.h
+        self.far = far_copy(source, target, sems, index, place.at(c=place.h, h=place.c))
+        self.near = pltpu.make_async_copy(source, target, local_sem)
+
+    def start(self):
+        pl.when(self.same)(self.near.start)
+        pl.when(~self.same)(self.far.start)
+
+    def wait_recv(self):
+        pl.when(self.same)(self.near.wait)
+        pl.when(~self.same)(self.far.wait_recv)
+
+    def wait_send(self):
+        pl.when(~self.same)(self.far.wait_send)
+
+
+class Task:
+    copies = 1
+    locals = 1
+    work = ()
+
+    def __init__(self, *inputs, phase=0):
+        self.inputs, self.phase = inputs, phase
+
+    def scratch(self):
+        return [
+            pltpu.SemaphoreType.DMA((self.copies,)),
+            pltpu.SemaphoreType.DMA((self.copies,)),
+            pltpu.SemaphoreType.DMA((self.locals,)),
+            *self.work,
+        ]
+
+
+class Rows(Task):
+    copies = 3
+
+    def outs(self):
+        rows = self.inputs[0]
+        return [jax.ShapeDtypeStruct((4, *rows.shape), rows.dtype)]
+
+    def steps(self, place, ins, outs, scratch):
+        own, full = ins[0], outs[0]
+        send, recv, local = scratch[:3]
+        keep = pltpu.make_async_copy(own, full.at[0], local.at[0])
+        over_z = far_copy(own, full.at[1], (send, recv), 0, place.at(l=1 - place.l))
+        over_c = far_copy(own, full.at[2], (send, recv), 1, place.at(c=1 - place.c))
+        relay = far_copy(full.at[1], full.at[3], (send, recv), 2, place.at(c=1 - place.c))
+
+        def first():
+            over_z.start()
+            over_c.start()
+            keep.start()
+
+        def second():
+            over_z.wait_recv()
+            relay.start()
+
+        def last():
+            keep.wait()
+            over_c.wait()
+            over_z.wait_send()
+            relay.wait()
+
+        return [first, None, second, last]
+
+
+class Sums(Task):
+    copies = 3
+
+    def __init__(self, *inputs, phase=0):
+        super().__init__(*inputs, phase=phase)
+        block = inputs[0].shape[1:]
+        self.work = tuple(pltpu.VMEM(block, jnp.bfloat16) for _ in range(3))
+
+    def outs(self):
+        block = jax.ShapeDtypeStruct(self.inputs[0].shape[1:], jnp.bfloat16)
+        return [block, block]
+
+    def steps(self, place, ins, outs, scratch):
+        partial, (from_c, from_z) = ins[0], outs
+        send, recv, local, mine, theirs, total = scratch
+        core = place.at(c=1 - place.c)
+        load = pltpu.make_async_copy(partial.at[1], mine, local.at[0])
+        far = far_copy(partial.at[3], theirs, (send, recv), 0, core)
+        near = far_copy(partial.at[2], from_c, (send, recv), 1, core)
+        over_z = far_copy(total, from_z, (send, recv), 2, place.at(l=1 - place.l))
+        rows = 32
+
+        def first():
+            far.start()
+            near.start()
+            load.start()
+
+        def second():
+            load.wait()
+            far.wait_recv()
+
+            @pl.loop(0, mine.shape[0] // rows)
+            def _(index):
+                part = pl.ds(pl.multiple_of(index * rows, rows), rows)
+                summed = mine[part, :].astype(jnp.float32) + theirs[part, :].astype(jnp.float32)
+                total[part, :] = summed.astype(jnp.bfloat16)
+
+            over_z.start()
+
+        def last():
+            far.wait_send()
+            near.wait()
+            over_z.wait()
+
+        return [first, second, None, last]
+
+
+class Near(Task):
+    copies = 2
+
+    def outs(self):
+        shard = self.inputs[0]
+        return [jax.ShapeDtypeStruct((2, *shard.shape), shard.dtype)]
+
+    def copies_of(self, place, shard, first, second, scratch):
+        send, recv, local = scratch[:3]
+        return (
+            Swap(place, shard, first, (send, recv), 0, local.at[0]),
+            far_copy(shard, second, (send, recv), 1, place.at(c=place.h, h=1 - place.c)),
+        )
+
+    def steps(self, place, ins, outs, scratch):
+        a, b = self.copies_of(place, ins[0], outs[0].at[0], outs[0].at[1], scratch)
+
+        def first():
+            a.start()
+            b.start()
+
+        def last():
+            a.wait_recv()
+            a.wait_send()
+            b.wait()
+
+        return [first, None, None, last]
+
+
+class Planes(Near):
+    copies = 8
+
+    def outs(self):
+        shard = self.inputs[0]
+        return [jax.ShapeDtypeStruct((8, *shard.shape), shard.dtype)]
+
+    def steps(self, place, ins, outs, scratch):
+        full = outs[0]
+        block = place.block
+        a, b = self.copies_of(place, ins[0], full.at[block], full.at[block + 1], scratch)
+        over_x, over_y = place.at(x=1 - place.x), place.at(y=1 - place.y)
+        x_block = block + 2 - 4 * place.x
+        y_block = block + 4 - 8 * place.y
+
+        def pass_on(slot, index, device):
+            return far_copy(full.at[slot], full.at[slot], scratch[:2], index, device)
+
+        ax, ay = pass_on(block, 2, over_x), pass_on(block, 3, over_y)
+        by, bx = pass_on(block + 1, 4, over_y), pass_on(block + 1, 5, over_x)
+        axy = pass_on(x_block, 6, over_y)
+        byx = pass_on(y_block + 1, 7, over_x)
+
+        def first():
+            a.start()
+            b.start()
+
+        def second():
+            a.wait_recv()
+            ax.start()
+            b.wait_recv()
+            by.start()
+            ay.start()
+            bx.start()
+
+        def third():
+            ax.wait_recv()
+            axy.start()
+            by.wait_recv()
+            byx.start()
+
+        def last():
+            a.wait_send()
+            b.wait_send()
+            for copy in (ax, by):
+                copy.wait_send()
+            for copy in (ay, bx, axy, byx):
+                copy.wait()
+
+        return [first, second, third, last]
+
+
+class Owners(Task):
+    copies = 2
+
+    def outs(self):
+        near = self.inputs[0]
+        return [jax.ShapeDtypeStruct(near.shape, near.dtype)]
+
+    def steps(self, place, ins, outs, scratch):
+        send, recv, local = scratch[:3]
+        near, got = ins[0], outs[0]
+        a = Swap(place, near.at[0], got.at[0], (send, recv), 0, local.at[0])
+        b = far_copy(near.at[1], got.at[1], (send, recv), 1, place.at(c=1 - place.h, h=place.c))
+
+        def first():
+            a.start()
+            b.start()
+
+        def last():
+            a.wait_recv()
+            a.wait_send()
+            b.wait()
+
+        return [first, None, None, last]
+
+
+class Halves(Task):
+    def __init__(self, array, sender, phase=0):
+        super().__init__(array, phase=phase)
+        self.sender = sender
+
+    def outs(self):
+        return [jax.ShapeDtypeStruct(self.inputs[0].shape, self.inputs[0].dtype)]
+
+    def steps(self, place, ins, outs, scratch):
+        copy = far_copy(ins[0], outs[0], scratch[:2], 0, place.at(h=1 - place.h))
+        sends = place.h == self.sender
+
+        def first():
+            pl.when(sends)(copy.start)
+
+        def last():
+            pl.when(sends)(copy.wait_send)
+            pl.when(~sends)(copy.wait_recv)
+
+        return [first, None, None, last]
+
+
+def transfer(name, number, micros, *tasks):
+    outs = [task.outs() for task in tasks]
+    scratch = [task.scratch() for task in tasks]
+
+    def kernel(*refs):
+        refs = list(refs)
+
+        def take(count):
+            taken = refs[:count]
+            del refs[:count]
+            return taken
+
+        ins_of = [take(len(task.inputs)) for task in tasks]
+        outs_of = [take(len(out)) for out in outs]
+        scratch_of = [take(len(one)) for one in scratch]
+        place = Place()
+        barrier = pltpu.get_barrier_semaphore()
+        partners = place.partners()
+        for partner in partners:
+            pl.semaphore_signal(barrier, inc=1, device_id=partner, device_id_type=MESH)
+        pl.semaphore_wait(barrier, len(partners))
+        plans = [
+            task.steps(place, ins_of[n], outs_of[n], scratch_of[n]) for n, task in enumerate(tasks)
+        ]
+        for phase in range(4):
+            for task, plan in zip(tasks, plans):
+                steps_now = [plan[phase]] if phase else []
+                if phase == task.phase:
+                    steps_now.insert(0, plan[0])
+                for step in steps_now:
+                    if step is not None:
+                        step()
+
+    results = pl.pallas_call(
+        kernel,
+        out_shape=[leaf for out in outs for leaf in out],
+        in_specs=[pl.BlockSpec(memory_space=pl.ANY) for task in tasks for _ in task.inputs],
+        out_specs=[pl.BlockSpec(memory_space=pl.ANY) for out in outs for _ in out],
+        scratch_shapes=[one for part in scratch for one in part],
+        compiler_params=pltpu.CompilerParams(collective_id=number, has_side_effects=True),
+        cost_estimate=pl.CostEstimate(
+            flops=0, bytes_accessed=micros * 3_300_000, transcendentals=0
+        ),
+        name=name,
+    )(*[leaf for task in tasks for leaf in task.inputs])
+    results = list(results)
+    grouped = []
+    for out in outs:
+        grouped.append(results[: len(out)])
+        del results[: len(out)]
+    return grouped
+
+
+def over_plane(near):
+    return lax.all_gather(near, ("dp", "mp"), axis=0, tiled=True, axis_index_groups=PLANES)
+
+
+def to_plane(grads):
+    return lax.psum_scatter(
+        grads, ("dp", "mp"), scatter_dimension=0, tiled=True, axis_index_groups=PLANES
+    )
+
+
+def both(pair):
+    return pair[0].astype(jnp.float32) + pair[1].astype(jnp.float32)
+
+
+def summed(partial, received):
+    return both(received) + partial[0].astype(jnp.float32)
+
+
+def sum_all_kernel(value, total, held, arrived, send_sem, recv_sem):
+    dp, mp = lax.axis_index("dp"), lax.axis_index("mp")
+    partners = [
+        (dp + 1 - 2 * (dp % 2), mp),
+        (dp + 2 - 4 * ((dp // 2) % 2), mp),
+        (dp + 4 - 8 * (dp // 4), mp),
+        (dp, mp + 1 - 2 * (mp % 2)),
+        (dp, mp + 2 - 4 * (mp // 2)),
+    ]
+    barrier = pltpu.get_barrier_semaphore()
+    for partner in partners:
+        pl.semaphore_signal(
+            barrier, inc=1, device_id=partner, device_id_type=pl.DeviceIdType.MESH
+        )
+    pl.semaphore_wait(barrier, len(partners))
+    held[0] = value[...]
+    for step, partner in enumerate(partners):
+        copy = pltpu.make_async_remote_copy(
+            src_ref=held.at[step],
+            dst_ref=arrived.at[step],
+            send_sem=send_sem.at[step],
+            recv_sem=recv_sem.at[step],
+            device_id=partner,
+            device_id_type=pl.DeviceIdType.MESH,
+        )
+        copy.start()
+        copy.wait()
+        held[step + 1] = held[step] + arrived[step]
+    total[...] = held[len(partners)]
+
+
+def sum_all(vector):
+    size = vector.shape[0]
+    rows = -(-size // 1024) * 8
+    block = jnp.pad(vector, (0, rows * 128 - size)).reshape(rows, 128)
+    total = pl.pallas_call(
+        sum_all_kernel,
+        out_shape=jax.ShapeDtypeStruct((rows, 128), jnp.float32),
+        in_specs=[pl.BlockSpec(memory_space=pltpu.VMEM)],
+        out_specs=pl.BlockSpec(memory_space=pltpu.VMEM),
+        scratch_shapes=[
+            pltpu.VMEM((6, rows, 128), jnp.float32),
+            pltpu.VMEM((5, rows, 128), jnp.float32),
+            pltpu.SemaphoreType.DMA((5,)),
+            pltpu.SemaphoreType.DMA((5,)),
+        ],
+        compiler_params=pltpu.CompilerParams(collective_id=0, has_side_effects=True),
+        name="sum_all",
+    )(block)
+    return total.reshape(-1)[:size]
 
 
 def shards_paired(
@@ -487,9 +854,8 @@
     gain_first,
     gain_second,
 ):
-    dp, mp = lax.axis_index("dp"), lax.axis_index("mp")
-    core, high, low = dp % 2, mp // 2, mp % 2
-    plane = (dp // 2) * 2 + high
+    high, low = lax.axis_index("mp") // 2, lax.axis_index("mp") % 2
+    plane = high
     groups = lax.axis_size("mp")
     heads = QUERY_HEADS // groups
     key_value_heads = KEY_VALUE_HEADS // groups
@@ -502,34 +868,38 @@
     half = count // 2
     width = hidden_in.shape[1]
     inverse = jnp.argsort(owner)
-    logical_of = jnp.take(inverse, jnp.arange(8, dtype=jnp.int32) ^ plane)
+    logical_of = jnp.take(inverse, jnp.arange(8, dtype=jnp.int32) ^ plane, mode="clip")
     slot_of = owner ^ plane
     out_rate = float(QUERY_HEADS * HEAD_SIZE // 32) ** (-0.5)
 
     def to_slots(rows):
-        return jnp.take(rows.reshape(rows.shape[0], 8, -1), logical_of, axis=1).reshape(rows.shape)
+        return jnp.take(rows.reshape(rows.shape[0], 8, -1), logical_of, axis=1, mode="clip").reshape(rows.shape)
 
     def from_slots(rows):
-        return jnp.take(rows.reshape(rows.shape[0], 8, -1), slot_of, axis=1).reshape(rows.shape)
+        return jnp.take(rows.reshape(rows.shape[0], 8, -1), slot_of, axis=1, mode="clip").reshape(rows.shape)
 
     ln_in = gains[:MODEL_WIDTH]
     ln_mid = gains[MODEL_WIDTH : 2 * MODEL_WIDTH]
     q_gain = gains[2 * MODEL_WIDTH : 2 * MODEL_WIDTH + HEAD_SIZE]
     k_gain = gains[2 * MODEL_WIDTH + HEAD_SIZE :]
     x_rows = hidden_in.astype(jnp.float32)
-    full_in = gather_rows(to_slots(rms_norm(x_rows, ln_in).astype(jnp.bfloat16)))
-
-    qkv_blocks = gather_weight(projection_master_weight.astype(jnp.bfloat16))
-    w_qkv = jnp.concatenate(qkv_blocks, axis=0)
-    out_blocks = gather_weight(out_weight.astype(jnp.bfloat16))
-    w_out = jnp.take(jnp.stack(out_blocks), slot_of, axis=0).reshape(-1, width)
-    gateup_blocks = gather_weight(gateup_weight.astype(jnp.bfloat16))
-    w_gateup = jnp.concatenate(gateup_blocks, axis=0)
-    down_blocks = gather_weight(down_weight.astype(jnp.bfloat16))
-    w_down = jnp.take(jnp.stack(down_blocks), slot_of, axis=0).reshape(-1, width)
-
+    low_qkv = projection_master_weight.astype(jnp.bfloat16)
+    low_out = out_weight.astype(jnp.bfloat16)
+    low_first = jnp.concatenate([low_qkv, low_out.reshape(low_qkv.shape[0], -1)], axis=1)
+    (first_blocks,), (full_in,), (near_gateup,) = transfer(
+        "gather_first",
+        1,
+        108,
+        Planes(low_first),
+        Rows(to_slots(rms_norm(x_rows, ln_in).astype(jnp.bfloat16))),
+        Near(gateup_weight.astype(jnp.bfloat16), phase=1),
+    )
+    full_in = full_in.reshape(count, width)
+    w_qkv = first_blocks[:, :, : low_qkv.shape[1]].reshape(width, -1)
+    w_out = first_blocks[:, :, low_qkv.shape[1] :].reshape(8, low_out.shape[0], width)
+    w_out = jnp.take(w_out, slot_of, axis=0, mode="clip").reshape(-1, width)
+    w_gateup = over_plane(near_gateup).reshape(width, -1)
     grad_out = cotangent.astype(jnp.float32)
-    d_branch = gather_rows(cotangent)
 
     lengths = jnp.concatenate([doc_lengths, move(doc_lengths, OVER_C)], axis=0)
     ends = jnp.cumsum(lengths, axis=1)
@@ -564,7 +934,11 @@
     key_rows = key_rows.reshape(count, key_width)
     value_rows = projected[:, query_width + key_width :].astype(jnp.bfloat16)
     own_kv = jnp.concatenate([key_rows, value_rows], axis=1)
-    lower_kv = move(own_kv, UPWARD)
+    (lower_kv,), (d_branch,) = transfer(
+        "keys_up", 2, 47, Halves(own_kv, 0), Rows(cotangent)
+    )
+    lower_kv = jnp.where(high == 1, lower_kv, jnp.zeros_like(lower_kv))
+    d_branch = d_branch.reshape(count, width)
     all_kv = jnp.concatenate(
         [lower_kv.reshape(2, half, 2 * key_width), own_kv.reshape(2, half, 2 * key_width)], axis=1
     )
@@ -597,33 +971,56 @@
 
     outs, totals = lax.map(forward_part, (queries, keys, values, doc_of, key_doc))
     attn_heads = outs.reshape(count, query_width)
-    mixed = x_rows + sum_rows(jnp.dot(attn_heads, w_out, preferred_element_type=jnp.float32))
-    full_mid = gather_rows(to_slots(rms_norm(mixed, ln_mid).astype(jnp.bfloat16)))
+
+    def blocks(partial):
+        return partial.astype(jnp.bfloat16).reshape(4, rows_here, width)
+
+    partial = blocks(jnp.dot(attn_heads, w_out, preferred_element_type=jnp.float32))
+    received, (near_down,) = transfer(
+        "sum_attention", 3, 50, Sums(partial), Near(down_weight.astype(jnp.bfloat16))
+    )
+    down_blocks = over_plane(near_down)
+    mixed = x_rows + summed(partial, received)
+    ((full_mid,),) = transfer(
+        "gather_mid", 4, 34, Rows(to_slots(rms_norm(mixed, ln_mid).astype(jnp.bfloat16)))
+    )
+    full_mid = full_mid.reshape(count, width)
     gateup = jnp.dot(full_mid, w_gateup, preferred_element_type=jnp.float32)
+    down_blocks, gateup = lax.optimization_barrier((down_blocks, gateup))
+    w_down = jnp.take(down_blocks, slot_of, axis=0, mode="clip").reshape(-1, width)
     gate = gateup[:, :units]
     upper = gateup[:, units:]
     sigma = jax.nn.sigmoid(gate)
     act = (gate * sigma * upper).astype(jnp.bfloat16)
-    result_rows = mixed + sum_rows(jnp.dot(act, w_down, preferred_element_type=jnp.float32))
+    branch = blocks(jnp.dot(act, w_down, preferred_element_type=jnp.float32))
 
     g_down = jnp.einsum("tf,td->fd", act, d_branch, preferred_element_type=jnp.float32)
-    g_down = jnp.take(g_down.astype(jnp.bfloat16).reshape(8, -1, width), logical_of, axis=0)
-    red_down = reduce_weight(g_down)
+    g_down = jnp.take(g_down.astype(jnp.bfloat16).reshape(8, -1, width), logical_of, axis=0, mode="clip")
     d_act = jnp.einsum("td,fd->tf", d_branch, w_down, preferred_element_type=jnp.float32)
     d_upper = d_act * gate * sigma
     d_gate = d_act * upper * sigma * (1.0 + gate * (1.0 - sigma))
     d_gateup = jnp.concatenate([d_gate, d_upper], axis=1).astype(jnp.bfloat16)
+    d_gateup, g_down = lax.optimization_barrier((d_gateup, g_down))
+    near_g_down = to_plane(g_down)
     g_gateup = jnp.einsum("td,tf->df", full_mid, d_gateup, preferred_element_type=jnp.float32)
-    red_gateup = reduce_weight(g_gateup.astype(jnp.bfloat16).reshape(8, -1, 2 * units))
-    d_mid_rows = from_slots(
-        sum_rows(jnp.einsum("tc,dc->td", d_gateup, w_gateup, preferred_element_type=jnp.float32))
-    )
+    g_gateup = g_gateup.astype(jnp.bfloat16).reshape(8, -1, 2 * units)
+    partial = blocks(
+        jnp.einsum("tc,dc->td", d_gateup, w_gateup, preferred_element_type=jnp.float32)
+    )
+    partial, g_gateup = lax.optimization_barrier((partial, g_gateup))
+    near_g_gateup = to_plane(g_gateup)
+    (received,) = transfer("sum_mid", 5, 32, Sums(partial))
+    d_mid_rows = from_slots(summed(partial, received))
     d_mixed, g_ln_mid = norm_back(mixed, ln_mid, d_mid_rows)
     d_mixed = d_mixed + grad_out
-    d_attn = gather_rows(d_mixed.astype(jnp.bfloat16))
+    (d_attn,), (owned_down,) = transfer(
+        "gather_attention", 6, 40, Rows(d_mixed.astype(jnp.bfloat16)), Owners(near_g_down)
+    )
+    d_attn = d_attn.reshape(count, width)
+    red_down = both(owned_down)
     g_out = jnp.einsum("th,td->hd", attn_heads, d_attn, preferred_element_type=jnp.float32)
-    g_out = jnp.take(g_out.astype(jnp.bfloat16).reshape(8, -1, width), logical_of, axis=0)
-    red_out = reduce_weight(g_out)
+    g_out = jnp.take(g_out.astype(jnp.bfloat16).reshape(8, -1, width), logical_of, axis=0, mode="clip")
+    near_g_out = to_plane(g_out)
     d_heads = jnp.einsum("td,hd->th", d_attn, w_out, preferred_element_type=jnp.float32).astype(
         jnp.bfloat16
     )
@@ -667,7 +1064,11 @@
     d_queries, d_kv = lax.map(
         backward_part, (queries, keys, values, doc_of, key_doc, totals, d_heads)
     )
-    from_above = move(d_kv[:, :half].astype(jnp.bfloat16), DOWNWARD)
+    (from_above,), received = transfer(
+        "keys_down", 7, 53, Halves(d_kv[:, :half].astype(jnp.bfloat16), 1), Sums(branch)
+    )
+    result_rows = mixed + summed(branch, received)
+    from_above = jnp.where(high == 0, from_above, jnp.zeros_like(from_above))
     d_kv = (d_kv[:, half:] + from_above.astype(jnp.float32)).reshape(count, 2 * key_width)
     d_queries = d_queries.reshape(count, heads, HEAD_SIZE)
     d_keys = d_kv[:, :key_width].reshape(count, key_value_heads, HEAD_SIZE)
@@ -682,16 +1083,27 @@
         axis=1,
     ).astype(jnp.bfloat16)
     g_qkv = jnp.einsum("td,tc->dc", full_in, d_projected, preferred_element_type=jnp.float32)
-    red_qkv = reduce_weight(g_qkv.astype(jnp.bfloat16).reshape(8, width // 8, -1))
-    d_in_rows = from_slots(
-        sum_rows(jnp.einsum("tc,dc->td", d_projected, w_qkv, preferred_element_type=jnp.float32))
-    )
+    near_g_qkv = to_plane(g_qkv.astype(jnp.bfloat16).reshape(8, width // 8, -1))
+    partial = blocks(
+        jnp.einsum("tc,dc->td", d_projected, w_qkv, preferred_element_type=jnp.float32)
+    )
+    received, (owned_gateup,) = transfer("sum_in", 8, 74, Sums(partial), Owners(near_g_gateup))
+    red_gateup = both(owned_gateup)
+    d_in_rows = from_slots(summed(partial, received))
+    near_g_out, near_g_qkv, red_gateup = lax.optimization_barrier(
+        (near_g_out, near_g_qkv, red_gateup)
+    )
+    (owned_out,), (owned_qkv,) = transfer(
+        "last_owners", 9, 40, Owners(near_g_out), Owners(near_g_qkv)
+    )
+    red_out, red_qkv = both(owned_out), both(owned_qkv)
     d_input, g_ln_in = norm_back(x_rows, ln_in, d_in_rows)
     input_grad = d_input + d_mixed
     gain_terms = jnp.concatenate([g_ln_in, g_ln_mid, g_q, g_k])
     squares = jnp.sum(red_qkv * red_qkv) + jnp.sum(red_gateup * red_gateup)
     squares = squares + jnp.sum(red_out * red_out) + jnp.sum(red_down * red_down)
-    total_squares, gain_grad = lax.psum((squares, gain_terms), ("dp", "mp"))
+    totals_here = sum_all(jnp.concatenate([gain_terms, squares[None]]))
+    gain_grad, total_squares = totals_here[:-1], totals_here[-1]
     grad_norm = jnp.sqrt(total_squares + jnp.sum(gain_grad * gain_grad))
     factor = jnp.minimum(1.0, CLIP_LIMIT / (grad_norm + 1e-06))
     qkv_new, qkv_first_new, qkv_second_new = adam(

time: 1110 us -> 985 us (0.89)
  Pallas kernels: 0 us -> 506 us
  waiting for transfers between devices: 366 us -> 9.36 us
  starting transfers between devices: 159 us -> 0.25 us
  other arithmetic: 179 us -> 122 us
  blocking collectives: 44.9 us -> 0 us
  local copies, waits for them, and re-layouts: 191 us -> 154 us
  matrix products: 148 us -> 162 us
  between operations: 8.32 us -> 21.1 us
    pallas_call x0 -> x10, Pallas kernels: none -> 506 us  [the longest x9 491 us: transfer(): pl.pallas_call(kernel, out_shape=[leaf for out in outs for leaf in out],...]
    ppermute x75 -> x1, waiting for transfers between devices: 366 us -> 0.01 us  [move(): return lax.ppermute(value, ('dp', 'mp'), pairs)]
    ppermute x75 -> x1, starting transfers between devices: 159 us -> 0.01 us  [move(): return lax.ppermute(value, ('dp', 'mp'), pairs)]
    psum x1 -> x0, blocking collectives: 44.9 us -> none  [shards_paired(): total_squares, gain_grad = lax.psum((squares, gain_terms), ('dp', 'mp'))]
    unnamed x347 -> x267, local copies, waits for them, and re-layouts: 69.5 us -> 26.1 us
    convert_element_type x15 -> x5, other arithmetic: 36.2 us -> 6.3 us  [the longest x1 2.41 us: shards_paired(): down_weight.astype(jnp.bfloat16)]
    reshape x3 -> x7, local copies, waits for them, and re-layouts: 0.67 us -> 14.6 us  [the longest x2 4.79 us: to_slots(): jnp.take(rows.reshape(rows.shape[0], 8, -1), logical_of, axis=1, mode='cl...]
    select_n x7 -> x1, other arithmetic: 13.3 us -> 0.08 us  [shards_paired(): lower_kv = jnp.where(high == 1, lower_kv, jnp.zeros_like(lower_kv))]
  transfers between devices with their start and end apart: 75 -> 7, of which waited for: 25 -> 1; matrix products, arithmetic and copies ran while one was open for 39% -> 32% of each run, Pallas kernels for 0% -> 35%
where the time goes in v2:
time: 985 us; the launch traced here: 975 us
  Pallas kernels  506 us (51%)
  matrix products  162 us (16%)
  local copies, waits for them, and re-layouts  154 us (16%)
  other arithmetic  122 us (12%)
  between operations  21.1 us (2%)
    pallas_call x9, Pallas kernels, transfer(): pl.pallas_call(kernel, out_shape=[leaf for out in outs for leaf in out],...  491 us
    unnamed x267, local copies, waits for them, and re-layouts  26.1 us
    sub x5, other arithmetic, adam(): weight * (1.0 - rate * decay)  20.1 us
    dot_general x1, matrix products, shards_paired(): jnp.einsum('td,tf->df', full_mid, d_gateup, preferred_element_type=jnp.fl...  19.8 us
  transfers between devices with their start and end apart: 7, of which 1 were waited for; matrix products, arithmetic and copies ran while one was open for 32% of the time, Pallas kernels for 35%

profile of v2, /device:TPU:0, one launch (start us, length us, event | category | flops | bytes accessed | tf_op | source)
XLA Modules:
  0.0 974.6 jit_solution(3489203928266767320)
XLA Ops:
  20.6 108.6 %gather_first.1 = (bf16[8,256,1536]{2,1,0:T(8,128)(2,1)}, bf16[4,256,2048]{2,1,0:T(8,128)(2,1)}, bf16[2,256,3072]{2,1,0:T(8,128)(2,1)}) custom-call(bf16[256,1536]{1,0:T(8,128)(2,1)} %pad_maximum_fusion.7.refs_0_, bf16[256,2048]{1,0:T(8,128)(2,1)} %bitcast.465, bf16[256,3072]{1,0:T(8,128)(2,1)} %convert_element_type.194.refs_2_), custom_call_target="tpu_custom_call" | custom-call | bytes 356400000 | tf_op jit(solution)/shard_map/gather_first/pallas_call | solution.py:746
  133.4 4.6 fusion.134
  140.9 3.7 slice.140
  149.6 3.1 concatenate.103
  154.5 3.0 reshape.637
  159.9 4.3 reshape.640
  166.6 3.6 gather_fusion.2
  176.9 4.0 multiply_cosine_fusion.1
  181.3 4.9 fusion.85
  199.4 47.6 %keys_up.1 = (bf16[1024,512]{1,0:T(8,128)(2,1)}, bf16[4,256,2048]{2,1,0:T(8,128)(2,1)}) custom-call(bf16[1024,512]{1,0:T(8,128)(2,1)} %pad_maximum_fusion.3.refs_0_, bf16[256,2048]{1,0:T(8,128)(2,1)} %refs_1_.1), custom_call_target="tpu_custom_call" | custom-call | bytes 155100000 | tf_op jit(solution)/shard_map/keys_up/pallas_call | solution.py:746
  252.2 15.8 %while.28 = (s32[]{:T(128)}, bf16[2,512,512]{2,1,0:T(8,128)(2,1)}, f32[2,2,2,512,1]{3,2,1,4,0:T(2,128)S(1)}, bf16[2,1024,2,128]{1,3,2,0:T(8,128)(2,1)}, s32[2,51...) while((s32[]{:T(128)}, bf16[2,512,512]{2,1,0:T(8,128)(2,1)}, ...), condition=%wide.region_11.12_spmd.clone.clone, body=%wide.region_8.11_spmd.clone.sunk.clone | while | flops 1098651648 | bytes 35745440 | solution.py:972
  268.0 7.1 convolution_convert_fusion.4
  275.1 49.7 %sum_attention.1 = (bf16[256,2048]{1,0:T(8,128)(2,1)}, bf16[256,2048]{1,0:T(8,128)(2,1)}, bf16[2,192,2048]{2,1,0:T(8,128)(2,1)}) custom-call(bf16[4,256,2048]{2,1,0:T(8,128)(2,1)} %bitcast.447, bf16[192,2048]{1,0:T(8,128)(2,1)} %convert_element_type.202.refs_1_), custom_call_target="tpu_custom_call" | custom-call | bytes 165000000 | tf_op jit(solution)/shard_map/sum_attention/pallas_call | solution.py:746
  331.8 34.4 %gather_mid.1 = bf16[4,256,2048]{2,1,0:T(8,128)(2,1)} custom-call(bf16[256,2048]{1,0:T(8,128)(2,1)} %bitcast.456), custom_call_target="tpu_custom_call" | custom-call | bytes 112200000 | tf_op jit(solution)/shard_map/gather_mid/pallas_call | solution.py:746
  366.3 19.3 %fusion.135 = f32[1024,3072]{1,0:T(8,128)} fusion(bf16[1024,2048]{1,0:T(8,128)(2,1)} %bitcast.454, bf16[2048,3072]{1,0:T(8,128)(2,1)} %bitcast.480), kind=kOutput, calls=%fused_computation.296 | convolution fusion | flops 12884901888 | bytes 29360128 | tf_op jit(solution)/shard_map/dot_general | solution.py:988
  385.6 9.2 all-gather.3.cloned.1.call-done
  394.8 6.4 gather_fusion.4
  401.1 16.5 %multiply_convert_fusion.2 = (bf16[1024,1536]{1,0:T(8,128)(2,1)}, bf16[1024,1536]{1,0:T(8,128)(2,1)}, bf16[1024,1536]{1,0:T(8,128)(2,1)S(1)}) fusion(f32[1024,3072]{1,0:T(8,128)} %fusion.135, bf16[1024,2048]{1,0:T(8,128)(2,1)} %bitcast.484, bf16[1536,2048]{1,0:T(8,128)(2,1)} %bitcast.448), kind=kOutput, calls=%fused_computation.111 | convolution fusion | flops 6467616768 | bytes 32505856 | tf_op jit(solution)/shard_map/td,fd->tf/dot_general | solution.py:999
  417.6 8.6 convolution_convert_fusion.1
  426.3 6.4 gather_fusion.5
  432.7 6.2 pad_maximum_fusion
  438.9 19.8 %convolution_convert_fusion = bf16[2048,3072]{1,0:T(8,128)(2,1)} fusion(bf16[1024,2048]{1,0:T(8,128)(2,1)} %bitcast.455, bf16[1024,3072]{1,0:T(8,128)(2,1)} %pad_maximum_fusion), kind=kOutput, calls=%fused_computation.106 | convolution fusion | flops 12891193344 | bytes 23068672 | tf_op jit(solution)/shard_map/td,tf->df/dot_general | solution.py:1005
  458.7 17.5 %convolution_convert_fusion.2 = bf16[1024,2048]{1,0:T(8,128)(2,1)} fusion(bf16[1024,3072]{1,0:T(8,128)(2,1)S(1)} %copy-done.63, bf16[2048,3072]{1,0:T(8,128)(2,1)} %bitcast.481), kind=kOutput, calls=%fused_computation.114 | convolution fusion | flops 12886999040 | bytes 23068672 | tf_op jit(solution)/shard_map/tc,dc->td/dot_general | solution.py:1008
  477.5 32.4 %sum_mid.1 = (bf16[256,2048]{1,0:T(8,128)(2,1)}, bf16[256,2048]{1,0:T(8,128)(2,1)}) custom-call(bf16[4,256,2048]{2,1,0:T(8,128)(2,1)} %bitcast.445), custom_call_target="tpu_custom_call" | custom-call | bytes 105600000 | tf_op jit(solution)/shard_map/sum_mid/pallas_call | solution.py:746
  513.8 3.6 gather_fusion.6
  523.8 11.1 %convolution_convert_fusion.3 = bf16[1024,2048]{1,0:T(8,128)(2,1)} fusion(bf16[1024,1536]{1,0:T(8,128)(2,1)S(1)} %copy-done.133, bf16[1536,2048]{1,0:T(8,128)(2,1)} %bitcast.449), kind=kOutput, calls=%fused_computation.115 | convolution fusion | flops 6444548096 | bytes 13631488 | tf_op jit(solution)/shard_map/dot_general | solution.py:995
  534.9 58.0 %gather_attention.1 = (bf16[4,256,2048]{2,1,0:T(8,128)(2,1)}, bf16[2,192,2048]{2,1,0:T(8,128)(2,1)}) custom-call(bf16[256,2048]{1,0:T(8,128)(2,1)} %fusion.121.refs_0_, bf16[2,192,2048]{2,1,0:T(8,128)(2,1)} %reduce-scatter.5.cloned.1.call-done.refs_1_), custom_call_target="tpu_custom_call" | custom-call | bytes 132000000 | tf_op jit(solution)/shard_map/gather_attention/pallas_call | solution.py:746
  593.0 4.5 convolution_convert_fusion.8
  598.8 47.5 %while.29 = (s32[]{:T(128)}, f32[2,512,512]{1,2,0:T(8,128)}, f32[2,1024,512]{2,1,0:T(8,128)}, bf16[2,1024,2,128]{3,1,2,0:T(8,128)(2,1)}, s32[2,512]{1,0:T(2,128)...) while((s32[]{:T(128)}, f32[2,512,512]{1,2,0:T(8,128)}, ...), condition=%wide.region_17.18_spmd.clone.clone, body=%wide.region_15.17_spmd.clone.sunk.clone | while | flops 2718439424 | bytes 129586440 | solution.py:1064
  602.6 4.1 fusion.208
  615.9 3.4 constant_dynamic-update-slice_fusion.16
  626.3 4.1 fusion.208
  639.6 3.3 constant_dynamic-update-slice_fusion.16
  649.0 52.5 %keys_down.1 = (bf16[2,512,512]{2,1,0:T(8,128)(2,1)}, bf16[256,2048]{1,0:T(8,128)(2,1)}, bf16[256,2048]{1,0:T(8,128)(2,1)}) custom-call(bf16[2,512,512]{2,1,0:T(8,128)(2,1)} %slice.248.refs_0_, bf16[4,256,2048]{2,1,0:T(8,128)(2,1)} %bitcast.443), custom_call_target="tpu_custom_call" | custom-call | bytes 174900000 | tf_op jit(solution)/shard_map/keys_down/pallas_call | solution.py:746
  713.0 3.2 copy.331
  717.8 6.2 convolution_convert_fusion.7
  724.0 3.8 gather_fusion.8
  734.3 4.2 multiply_reduce_fusion.8
  754.1 7.6 convolution_convert_fusion.5
  787.1 6.3 convolution_convert_fusion.6
  793.4 70.7 %sum_in.1 = (bf16[256,2048]{1,0:T(8,128)(2,1)}, bf16[256,2048]{1,0:T(8,128)(2,1)}, bf16[2,256,3072]{2,1,0:T(8,128)(2,1)}) custom-call(bf16[4,256,2048]{2,1,0:T(8,128)(2,1)} %bitcast.444, bf16[2,256,3072]{2,1,0:T(8,128)(2,1)} %reduce-scatter.7.cloned.1.call-done.refs_1_), custom_call_target="tpu_custom_call" | custom-call | bytes 244200000 | tf_op jit(solution)/shard_map/sum_in/pallas_call | solution.py:746
  866.5 37.5 %last_owners.1 = (bf16[2,64,2048]{2,1,0:T(8,128)(2,1)}, bf16[2,256,1024]{2,1,0:T(8,128)(2,1)}) custom-call(bf16[2,64,2048]{2,1,0:T(8,128)(2,1)} %reduce-scatter.9.cloned.1.call-done.refs_0_, bf16[2,256,1024]{2,1,0:T(8,128)(2,1)} %reduce-scatter.11.cloned.1.call-done.refs_1_), custom_call_target="tpu_custom_call" | custom-call | bytes 132000000 | tf_op jit(solution)/shard_map/last_owners/pallas_call | solution.py:746
  911.6 3.7 gather_fusion.7
  921.8 14.2 %sum_all.1 = f32[40,128]{1,0:T(8,128)} custom-call(f32[40,128]{1,0:T(8,128)} %pad_bitcast_fusion.value), custom_call_target="tpu_custom_call" | custom-call | tf_op jit(solution)/shard_map/sum_all/pallas_call | solution.py:819
  941.4 6.1 divide_subtract_fusion.1
  949.9 7.3 divide_subtract_fusion
  957.3 4.0 divide_subtract_fusion.2
  962.2 4.3 fusion.78
  (491 shorter events, 208.3 us)
Async XLA Ops:
  7.2 359.0 %all-gather.5.cloned.1.call-start = ((), (), s32[]{:S(2)}) async-start(), calls=%async_computation.5 | async-start | bytes 15728640 | tf_op jit(solution)/shard_map/all_gather | solution.py:767
  9.6 416.7 %copy-start.121 = (s32[1024]{0:T(1024)}, s32[1024]{0:T(1024)S(1)}, u32[]{:S(2)}) copy-start(s32[1024]{0:T(1024)S(1)} %pad_clamp_fusion.1) | copy-start | bytes 12292
  10.4 510.4 %copy-start.99 = (f32[2048]{0:T(1024)}, f32[2048]{0:T(1024)S(1)}, u32[]{:S(2)}) copy-start(f32[2048]{0:T(1024)S(1)} %get-tuple-element.492) | copy-start | bytes 24580
  129.3 265.5 %all-gather.3.cloned.1.call-start = ((), (), s32[]{:S(2)}) async-start(), calls=%async_computation.4 | async-start | bytes 7864320 | tf_op jit(solution)/shard_map/all_gather | solution.py:767
  129.9 46.6 %collective-permute-start = (s32[1,4]{1,0:T(1,128)S(1)}, s32[1,4]{1,0:T(1,128)S(1)}, u32[]{:S(2)}, u32[]{:S(2)}) collective-permute-start(s32[1,4]{1,0:T(1,128)S(1)} %copy-done.127), channel_id=1, source_target_pairs={{4,0},{5,1},{6,2},{7,3},{0,4},{1,5},{2,6},{3,7},{12,8},{13,9},{14,... | collective-permute-start | bytes 56 | tf_op jit(solution)/shard_map/ppermute | solution.py:423
  138.1 16.4 %copy-start.20 = (f32[1024,512]{0,1:T(8,128)}, f32[1024,512]{0,1:T(8,128)S(1)}, u32[]{:S(2)}) copy-start(f32[1024,512]{0,1:T(8,128)S(1)} %slice.190) | copy-start | bytes 6291460
  146.4 25.2 %copy-start.123 = (f32[128]{0:T(128)}, f32[128]{0:T(128)S(1)}, u32[]{:S(2)}) copy-start(f32[128]{0:T(128)S(1)} %get-tuple-element.495) | copy-start | bytes 1540
  146.4 34.9 %copy-start.115 = (f32[128]{0:T(128)}, f32[128]{0:T(128)S(1)}, u32[]{:S(2)}) copy-start(f32[128]{0:T(128)S(1)} %get-tuple-element.494) | copy-start | bytes 1540
  157.8 39.1 %copy-start.12 = (f32[1024,256]{1,0:T(8,128)}, f32[1024,256]{1,0:T(8,128)S(1)}, u32[]{:S(2)}) copy-start(f32[1024,256]{1,0:T(8,128)S(1)} %copy.322) | copy-start | bytes 3145732
  158.6 13.1 %copy-start.24 = (f32[1024,2,128]{2,1,0:T(2,128)}, f32[1024,2,128]{2,1,0:T(2,128)S(1)}, u32[]{:S(2)}) copy-start(f32[1024,2,128]{2,1,0:T(2,128)S(1)} %reshape.633) | copy-start | bytes 3145732
  158.8 5.4 copy-start.65
  166.6 347.2 %copy-start.120 = (s32[1024]{0:T(1024)}, s32[1024]{0:T(1024)S(1)}, u32[]{:S(2)}) copy-start(s32[1024]{0:T(1024)S(1)} %pad_clamp_fusion) | copy-start | bytes 12292
  171.5 25.4 %copy-start.125 = (f32[256]{0:T(256)}, f32[256]{0:T(256)S(1)}, u32[]{:S(2)}) copy-start(f32[256]{0:T(256)S(1)} %broadcast_bitcast_fusion.1) | copy-start | bytes 3076
  171.6 24.0 %copy-start.29 = (f32[1024,2]{1,0:T(8,128)}, f32[1024,2]{1,0:T(8,128)S(1)}, u32[]{:S(2)}) copy-start(f32[1024,2]{1,0:T(8,128)S(1)} %add_rsqrt_fusion) | copy-start | bytes 24580
  174.1 7.2 copy-start.67
  268.0 7.1 copy-start.4
  268.0 7.1 copy-start.6
  268.0 7.1 copy-start.87
  268.0 7.1 copy-start.97
  268.0 7.1 copy-start.101
  268.0 7.1 copy-start.105
  275.1 49.8 %copy-start.15 = (bf16[256,2048]{1,0:T(8,128)(2,1)S(1)}, bf16[256,2048]{1,0:T(8,128)(2,1)}, u32[]{:S(2)}) copy-start(bf16[256,2048]{1,0:T(8,128)(2,1)} %param.23) | copy-start | bytes 3145732
  324.9 210.0 %reduce-scatter.5.cloned.1.call-start = ((), (), s32[]{:S(2)}) async-start(), calls=%async_computation.6 | async-start | bytes 7864320 | tf_op jit(solution)/shard_map/reduce_scatter | solution.py:771
  327.5 193.2 %copy-start.2 = (f32[256,2048]{1,0:T(8,128)}, f32[256,2048]{1,0:T(8,128)S(1)}, u32[]{:S(2)}) copy-start(f32[256,2048]{1,0:T(8,128)S(1)} %get-tuple-element.470) | copy-start | bytes 6291460
  327.5 193.2 %copy-start.109 = (f32[256]{0:T(256)}, f32[256]{0:T(256)S(1)}, u32[]{:S(2)}) copy-start(f32[256]{0:T(256)S(1)} %add_rsqrt_fusion.2) | copy-start | bytes 3076
  401.1 16.5 %copy-start.130 = (bf16[4,256,2048]{2,1,0:T(8,128)(2,1)S(1)}, bf16[4,256,2048]{2,1,0:T(8,128)(2,1)}, u32[]{:S(2)}) copy-start(bf16[4,256,2048]{2,1,0:T(8,128)(2,1)} %get-tuple-element.172) | copy-start | bytes 12582916
  417.6 8.6 copy-start.132
  438.9 354.6 %reduce-scatter.7.cloned.1.call-start = ((), (), s32[]{:S(2)}) async-start(), calls=%async_computation.7 | async-start | bytes 15728640 | tf_op jit(solution)/shard_map/reduce_scatter | solution.py:771
  438.9 19.8 %copy-start.63 = (bf16[1024,3072]{1,0:T(8,128)(2,1)S(1)}, bf16[1024,3072]{1,0:T(8,128)(2,1)}, u32[]{:S(2)}) copy-start(bf16[1024,3072]{1,0:T(8,128)(2,1)} %pad_maximum_fusion) | copy-start | bytes 18874372
  476.3 390.2 %reduce-scatter.9.cloned.1.call-start = ((), (), s32[]{:S(2)}) async-start(), calls=%async_computation.8 | async-start | bytes 2621440 | tf_op jit(solution)/shard_map/reduce_scatter | solution.py:771
  534.9 58.0 %copy-start.75 = (bf16[8,64,2048]{2,1,0:T(8,128)(2,1)S(1)}, bf16[8,64,2048]{2,1,0:T(8,128)(2,1)}, u32[]{:S(2)}) copy-start(bf16[8,64,2048]{2,1,0:T(8,128)(2,1)} %gather_fusion.2) | copy-start | bytes 6291460
  730.4 136.2 %reduce-scatter.11.cloned.1.call-start = ((), (), s32[]{:S(2)}) async-start(), calls=%async_computation.9 | async-start | bytes 5242880 | tf_op jit(solution)/shard_map/reduce_scatter | solution.py:771
  733.3 5.2 copy-start.50
  734.3 5.5 copy-start.37
  734.3 5.5 copy-start.45
  754.1 7.6 copy-start.82
  917.3 22.7 %copy-start.107 = (f32[4352]{0:T(1024)S(1)}, f32[4352]{0:T(1024)}, u32[]{:S(2)}) copy-start(f32[4352]{0:T(1024)} %param.39) | copy-start | bytes 52228
  917.3 22.7 %copy-start.111 = (f32[4352]{0:T(1024)S(1)}, f32[4352]{0:T(1024)}, u32[]{:S(2)}) copy-start(f32[4352]{0:T(1024)} %param.40) | copy-start | bytes 52228
  917.3 22.7 %copy-start.112 = (f32[4352]{0:T(1024)S(1)}, f32[4352]{0:T(1024)}, u32[]{:S(2)}) copy-start(f32[4352]{0:T(1024)} %param.41) | copy-start | bytes 52228
  941.4 6.1 copy-start.78
  941.4 6.1 copy-start.80
  941.4 6.1 copy-start.95
  941.4 6.1 copy-start.96
  941.4 7.5 copy-start.73
  949.9 7.3 copy-start.71
  949.9 7.3 copy-start.72
  949.9 11.3 %copy-start.43 = (bf16[256,2048]{1,0:T(8,128)(2,1)S(1)}, bf16[256,2048]{1,0:T(8,128)(2,1)}, u32[]{:S(2)}) copy-start(bf16[256,2048]{1,0:T(8,128)(2,1)} %refs_1_.1) | copy-start | bytes 3145732
  949.9 11.3 %copy-start.100 = (f32[2048]{0:T(1024)S(1)}, f32[2048]{0:T(1024)}, u32[]{:S(2)}) copy-start(f32[2048]{0:T(1024)} %copy-done.99) | copy-start | bytes 24580
  (99 other events, 251.9 us)
Sparse Core Ops, SparseCore 0:
  129.4 122.1 all-gather.4
  325.0 69.6 all-gather.2
  439.0 70.2 reduce-scatter.4
  512.2 120.7 reduce-scatter.6
  730.5 32.3 reduce-scatter.8
  765.9 52.6 reduce-scatter.10

commit v3 on v2

--- a/solution.py
+++ b/solution.py
@@ -749,7 +749,9 @@
         in_specs=[pl.BlockSpec(memory_space=pl.ANY) for task in tasks for _ in task.inputs],
         out_specs=[pl.BlockSpec(memory_space=pl.ANY) for out in outs for _ in out],
         scratch_shapes=[one for part in scratch for one in part],
-        compiler_params=pltpu.CompilerParams(collective_id=number, has_side_effects=True),
+        compiler_params=pltpu.CompilerParams(
+            collective_id=number, has_side_effects=True, vmem_limit_bytes=48 * 2**20
+        ),
         cost_estimate=pl.CostEstimate(
             flops=0, bytes_accessed=micros * 3_300_000, transcendentals=0
         ),
@@ -761,6 +763,14 @@
         grouped.append(results[: len(out)])
         del results[: len(out)]
     return grouped
+
+
+def to_group(shard):
+    return jnp.stack([move(shard, TO_GROUP[0]), move(shard, TO_GROUP[1])])
+
+
+def to_owner(near):
+    return [move(near[0], FROM_GROUP[0]), move(near[1], FROM_GROUP[1])]
 
 
 def over_plane(near):
@@ -833,6 +843,491 @@
     return total.reshape(-1)[:size]
 
 
+def column_places(index, high, low, rows):
+    chunk = index // rows
+    return high * 2 * rows + (low + chunk - 2 * low * chunk) * rows + index - chunk * rows
+
+
+def project_kernel(rows_ref, weight_ref, cos_ref, sin_ref, gain_ref, raw_ref, query_ref, kv_ref):
+    width = rows_ref.shape[1]
+    weight = weight_ref[...].reshape(width, weight_ref.shape[2])
+    projected = jnp.dot(rows_ref[...], weight, preferred_element_type=jnp.float32)
+    query_width, key_width = query_ref.shape[1], kv_ref.shape[1] // 2
+    turned_width = query_width + key_width
+    raw_ref[...] = projected[:, :turned_width]
+    cosine, sine = cos_ref[...], sin_ref[...]
+    for start in range(0, turned_width, HEAD_SIZE):
+        raw = projected[:, start : start + HEAD_SIZE]
+        gain = gain_ref[0:1, :] if start < query_width else gain_ref[1:2, :]
+        normed = raw * lax.rsqrt(jnp.mean(raw * raw, axis=1, keepdims=True) + EPS_NORM) * gain
+        turned = normed * cosine + pltpu.roll(normed, HEAD_SIZE // 2, 1) * sine
+        if start < query_width:
+            query_ref[:, start : start + HEAD_SIZE] = turned.astype(jnp.bfloat16)
+        else:
+            place = start - query_width
+            kv_ref[:, place : place + HEAD_SIZE] = turned.astype(jnp.bfloat16)
+    kv_ref[:, key_width:] = projected[:, turned_width:].astype(jnp.bfloat16)
+
+
+def project(rows, blocks, cosine, sine, head_gains, query_width, key_width):
+    count, width = rows.shape
+    tile = 256
+    total = query_width + 2 * key_width
+    by_rows = lambda columns: pl.BlockSpec((tile, columns), lambda i: (i, 0))
+    return pl.pallas_call(
+        project_kernel,
+        grid=(count // tile,),
+        in_specs=[
+            by_rows(width),
+            pl.BlockSpec((8, width // 8, total), lambda i: (0, 0, 0)),
+            by_rows(HEAD_SIZE),
+            by_rows(HEAD_SIZE),
+            pl.BlockSpec((2, HEAD_SIZE), lambda i: (0, 0)),
+        ],
+        out_specs=[by_rows(query_width + key_width), by_rows(query_width), by_rows(2 * key_width)],
+        out_shape=[
+            jax.ShapeDtypeStruct((count, query_width + key_width), jnp.float32),
+            jax.ShapeDtypeStruct((count, query_width), jnp.bfloat16),
+            jax.ShapeDtypeStruct((count, 2 * key_width), jnp.bfloat16),
+        ],
+        compiler_params=pltpu.CompilerParams(vmem_limit_bytes=48 * 2**20),
+        cost_estimate=pl.CostEstimate(
+            flops=2 * count * width * total, bytes_accessed=16 * 2**20, transcendentals=0
+        ),
+        name="project",
+    )(rows, blocks, cosine, sine, head_gains)
+
+
+def unproject_kernel(
+    place_ref, dq_ref, own_ref, above_ref, raw_ref, cos_ref, sin_ref, gain_ref, out_ref, gq_ref, gk_ref
+):
+    query_width, key_width = dq_ref.shape[1], own_ref.shape[1] // 2
+    turned_width = query_width + key_width
+    lower = place_ref[0] == 0
+    cosine, sine = cos_ref[...], sin_ref[...]
+
+    @pl.when(pl.program_id(0) == 0)
+    def _():
+        gq_ref[...] = jnp.zeros_like(gq_ref)
+        gk_ref[...] = jnp.zeros_like(gk_ref)
+
+    def with_above(columns):
+        above = jnp.where(lower, above_ref[:, columns].astype(jnp.float32), 0.0)
+        return own_ref[:, columns] + above
+
+    for start in range(0, turned_width, HEAD_SIZE):
+        columns = slice(start, start + HEAD_SIZE)
+        if start < query_width:
+            grad, gain, gain_sum = dq_ref[:, columns], gain_ref[0:1, :], gq_ref
+        else:
+            grad = with_above(slice(start - query_width, start - query_width + HEAD_SIZE))
+            gain, gain_sum = gain_ref[1:2, :], gk_ref
+        grad = grad * cosine - pltpu.roll(grad, HEAD_SIZE // 2, 1) * sine
+        raw = raw_ref[:, columns]
+        scale = lax.rsqrt(jnp.mean(raw * raw, axis=1, keepdims=True) + EPS_NORM)
+        normed = raw * scale
+        gain_sum[...] += jnp.sum((grad * normed).reshape(-1, 8, HEAD_SIZE), axis=0)
+        d_normal = grad * gain
+        value = scale * (d_normal - normed * jnp.mean(d_normal * normed, axis=1, keepdims=True))
+        out_ref[:, columns] = value.astype(jnp.bfloat16)
+    out_ref[:, turned_width:] = with_above(slice(key_width, 2 * key_width)).astype(jnp.bfloat16)
+
+
+def unproject(place, d_queries, d_own, above, raw, cosine, sine, head_gains):
+    count, query_width = d_queries.shape
+    key_width = d_own.shape[1] // 2
+    tile = 256
+    total = query_width + 2 * key_width
+    by_rows = lambda columns: pl.BlockSpec((tile, columns), lambda i, p: (i, 0))
+    fixed = lambda rows: pl.BlockSpec((rows, HEAD_SIZE), lambda i, p: (0, 0))
+    return pl.pallas_call(
+        unproject_kernel,
+        grid_spec=pltpu.PrefetchScalarGridSpec(
+            num_scalar_prefetch=1,
+            grid=(count // tile,),
+            in_specs=[
+                by_rows(query_width),
+                by_rows(2 * key_width),
+                by_rows(2 * key_width),
+                by_rows(query_width + key_width),
+                by_rows(HEAD_SIZE),
+                by_rows(HEAD_SIZE),
+                fixed(2),
+            ],
+            out_specs=[by_rows(total), fixed(8), fixed(8)],
+        ),
+        out_shape=[
+            jax.ShapeDtypeStruct((count, total), jnp.bfloat16),
+            jax.ShapeDtypeStruct((8, HEAD_SIZE), jnp.float32),
+            jax.ShapeDtypeStruct((8, HEAD_SIZE), jnp.float32),
+        ],
+        compiler_params=pltpu.CompilerParams(vmem_limit_bytes=32 * 2**20),
+        cost_estimate=pl.CostEstimate(flops=0, bytes_accessed=16 * 2**20, transcendentals=0),
+        name="unproject",
+    )(place, d_queries, d_own, above, raw, cosine, sine, head_gains)
+
+
+def dot_t(left, right):
+    return lax.dot_general(
+        left, right, (((1,), (1,)), ((), ())), preferred_element_type=jnp.float32
+    )
+
+
+def t_dot(left, right):
+    return lax.dot_general(
+        left, right, (((0,), (0,)), ((), ())), preferred_element_type=jnp.float32
+    )
+
+
+def exps_of(place_ref, time_ref, begin_ref, rows, query, key_low, key_own):
+    high, low = place_ref[0], place_ref[1]
+    keys = key_own.shape[0]
+    scale = HEAD_SIZE ** (-0.5)
+    column = lax.broadcasted_iota(jnp.int32, (rows.size, keys), 1)
+    time, begin = time_ref[rows, :], begin_ref[rows, :]
+    own_place = column_places(column, high, low, keys // 2)
+    low_place = column_places(column, 0, low, keys // 2)
+    own_seen = (own_place <= time) & (own_place >= begin)
+    low_seen = (low_place >= begin) & (low_place < high * keys)
+    own = jnp.where(own_seen, dot_t(query, key_own) * scale, MASKED)
+    lower = jnp.where(low_seen, dot_t(query, key_low) * scale, MASKED)
+    top = jnp.maximum(
+        jnp.max(own, axis=1, keepdims=True), jnp.max(lower, axis=1, keepdims=True)
+    )
+    own, lower = jnp.exp(own - top), jnp.exp(lower - top)
+    total = jnp.sum(own, axis=1, keepdims=True) + jnp.sum(lower, axis=1, keepdims=True)
+    return lower, own, 1.0 / total
+
+
+def attend_kernel(place_ref, time_ref, begin_ref, query_ref, low_ref, own_ref, out_ref):
+    half, query_width = query_ref.shape
+    key_width = own_ref.shape[1] // 2
+    group = query_width // key_width
+    size = half // 2
+    upper = place_ref[0] == 1
+    for kv in range(key_width // HEAD_SIZE):
+        key_at = slice(kv * HEAD_SIZE, (kv + 1) * HEAD_SIZE)
+        value_at = slice(key_width + kv * HEAD_SIZE, key_width + (kv + 1) * HEAD_SIZE)
+        key_low, key_own, value_own = low_ref[:, key_at], own_ref[:, key_at], own_ref[:, value_at]
+        value_low = jnp.where(upper, low_ref[:, value_at], jnp.zeros_like(value_own))
+        for part in range(2):
+            rows = pl.ds(part * size, size)
+            for head in range(kv * group, (kv + 1) * group):
+                query_at = slice(head * HEAD_SIZE, (head + 1) * HEAD_SIZE)
+                lower, own, inverse = exps_of(
+                    place_ref, time_ref, begin_ref, rows, query_ref[rows, query_at], key_low, key_own
+                )
+                result = jnp.dot(
+                    lower.astype(jnp.bfloat16), value_low, preferred_element_type=jnp.float32
+                ) + jnp.dot(own.astype(jnp.bfloat16), value_own, preferred_element_type=jnp.float32)
+                out_ref[rows, query_at] = (result * inverse).astype(jnp.bfloat16)
+
+
+def attend_back_kernel(
+    place_ref, time_ref, begin_ref, query_ref, low_ref, own_ref, grad_ref, dq_ref, dlow_ref, down_ref
+):
+    half, query_width = query_ref.shape
+    key_width = own_ref.shape[1] // 2
+    group = query_width // key_width
+    size = half // 2
+    scale = HEAD_SIZE ** (-0.5)
+    upper = place_ref[0] == 1
+    for kv in range(key_width // HEAD_SIZE):
+        key_at = slice(kv * HEAD_SIZE, (kv + 1) * HEAD_SIZE)
+        value_at = slice(key_width + kv * HEAD_SIZE, key_width + (kv + 1) * HEAD_SIZE)
+        key_own, value_own = own_ref[:, key_at], own_ref[:, value_at]
+        key_low = jnp.where(upper, low_ref[:, key_at], jnp.zeros_like(key_own))
+        value_low = jnp.where(upper, low_ref[:, value_at], jnp.zeros_like(value_own))
+        dk_low = dk_own = dv_low = dv_own = None
+        for part in range(2):
+            rows = pl.ds(part * size, size)
+            for head in range(kv * group, (kv + 1) * group):
+                query_at = slice(head * HEAD_SIZE, (head + 1) * HEAD_SIZE)
+                query, grad = query_ref[rows, query_at], grad_ref[rows, query_at]
+                lower, own, inverse = exps_of(
+                    place_ref, time_ref, begin_ref, rows, query, key_low, key_own
+                )
+                lower, own = lower * inverse, own * inverse
+                g_low, g_own = dot_t(grad, value_low), dot_t(grad, value_own)
+                mean = jnp.sum(lower * g_low, axis=1, keepdims=True) + jnp.sum(
+                    own * g_own, axis=1, keepdims=True
+                )
+                s_low = (lower * (g_low - mean)).astype(jnp.bfloat16)
+                s_own = (own * (g_own - mean)).astype(jnp.bfloat16)
+                dq_ref[rows, query_at] = scale * (
+                    jnp.dot(s_low, key_low, preferred_element_type=jnp.float32)
+                    + jnp.dot(s_own, key_own, preferred_element_type=jnp.float32)
+                )
+                terms = (
+                    t_dot(s_low, query),
+                    t_dot(s_own, query),
+                    t_dot(lower.astype(jnp.bfloat16), grad),
+                    t_dot(own.astype(jnp.bfloat16), grad),
+                )
+                if dk_low is None:
+                    dk_low, dk_own, dv_low, dv_own = terms
+                else:
+                    dk_low, dk_own = dk_low + terms[0], dk_own + terms[1]
+                    dv_low, dv_own = dv_low + terms[2], dv_own + terms[3]
+        dlow_ref[:, key_at] = (dk_low * scale).astype(jnp.bfloat16)
+        dlow_ref[:, value_at] = dv_low.astype(jnp.bfloat16)
+        down_ref[:, key_at] = dk_own * scale
+        down_ref[:, value_at] = dv_own
+
+
+def attention_call(kernel, name, place, arrays, outs, flops):
+    count = arrays[0].shape[0]
+    half = count // 2
+    spec = lambda leaf: pl.BlockSpec((half, leaf.shape[1]), lambda i, p: (i, 0))
+    return pl.pallas_call(
+        kernel,
+        grid_spec=pltpu.PrefetchScalarGridSpec(
+            num_scalar_prefetch=1,
+            grid=(2,),
+            in_specs=[spec(leaf) for leaf in arrays],
+            out_specs=[spec(leaf) for leaf in outs],
+        ),
+        out_shape=outs,
+        compiler_params=pltpu.CompilerParams(vmem_limit_bytes=56 * 2**20),
+        cost_estimate=pl.CostEstimate(flops=flops, bytes_accessed=16 * 2**20, transcendentals=0),
+        name=name,
+    )(place, *arrays)
+
+
+def scaled(values):
+    return values * lax.rsqrt(jnp.mean(values * values, axis=1, keepdims=True) + EPS_NORM)
+
+
+def three(parts, columns=slice(None)):
+    own, from_c, from_z = parts
+    return (
+        own[0, :, columns].astype(jnp.float32)
+        + from_c[:, columns].astype(jnp.float32)
+        + from_z[:, columns].astype(jnp.float32)
+    )
+
+
+def slot_columns(slot_ref, index, block):
+    return pl.ds(pl.multiple_of(slot_ref[index] * block, block), block)
+
+
+def store_slots(slot_ref, out_ref, values):
+    block = out_ref.shape[1] // 8
+    for index in range(8):
+        out_ref[:, slot_columns(slot_ref, index, block)] = values[
+            :, index * block : (index + 1) * block
+        ]
+
+
+def norm_kernel(slot_ref, x_ref, gain_ref, out_ref):
+    x = x_ref[...].astype(jnp.float32)
+    store_slots(slot_ref, out_ref, (scaled(x) * gain_ref[...]).astype(jnp.bfloat16))
+
+
+def mix_kernel(slot_ref, x_ref, own_ref, c_ref, z_ref, gain_ref, mixed_ref, out_ref):
+    mixed = x_ref[...].astype(jnp.float32) + three((own_ref, c_ref, z_ref))
+    mixed_ref[...] = mixed
+    store_slots(slot_ref, out_ref, (scaled(mixed) * gain_ref[...]).astype(jnp.bfloat16))
+
+
+def norm_back_of(slot_ref, value_ref, parts, gain_ref, sum_ref, grad_ref):
+    width = value_ref.shape[1]
+    block = width // 8
+    for index in range(8):
+        grad_ref[:, index * block : (index + 1) * block] = three(
+            parts, slot_columns(slot_ref, index, block)
+        )
+    value, grad = value_ref[...].astype(jnp.float32), grad_ref[...]
+    scale = lax.rsqrt(jnp.mean(value * value, axis=1, keepdims=True) + EPS_NORM)
+    normed = value * scale
+
+    @pl.when(pl.program_id(0) == 0)
+    def _():
+        sum_ref[...] = jnp.zeros_like(sum_ref)
+
+    sum_ref[...] += jnp.sum((grad * normed).reshape(-1, 8, width), axis=0)
+    d_normal = grad * gain_ref[...]
+    return scale * (d_normal - normed * jnp.mean(d_normal * normed, axis=1, keepdims=True))
+
+
+def mix_back_kernel(
+    slot_ref, mixed_ref, own_ref, c_ref, z_ref, gain_ref, cot_ref, d_ref, low_ref, sum_ref, grad_ref
+):
+    value = norm_back_of(slot_ref, mixed_ref, (own_ref, c_ref, z_ref), gain_ref, sum_ref, grad_ref)
+    value = value + cot_ref[...].astype(jnp.float32)
+    d_ref[...] = value
+    low_ref[...] = value.astype(jnp.bfloat16)
+
+
+def in_back_kernel(
+    slot_ref, x_ref, own_ref, c_ref, z_ref, gain_ref, d_ref, out_ref, sum_ref, grad_ref
+):
+    value = norm_back_of(slot_ref, x_ref, (own_ref, c_ref, z_ref), gain_ref, sum_ref, grad_ref)
+    out_ref[...] = value + d_ref[...]
+
+
+def by_row_tiles(kernel, name, slot_of, inputs, outs, scratch=False):
+    rows, width = 64, inputs[0].shape[1]
+    steps = inputs[0].shape[0] // rows
+
+    def spec(leaf):
+        if len(leaf.shape) == 3:
+            return pl.BlockSpec((1, rows, width), lambda i, p: (0, i, 0))
+        if leaf.shape[0] in (1, 8):
+            return pl.BlockSpec(leaf.shape, lambda i, p: (0, 0))
+        return pl.BlockSpec((rows, width), lambda i, p: (i, 0))
+
+    return pl.pallas_call(
+        kernel,
+        grid_spec=pltpu.PrefetchScalarGridSpec(
+            num_scalar_prefetch=1,
+            grid=(steps,),
+            in_specs=[spec(leaf) for leaf in inputs],
+            out_specs=[spec(leaf) for leaf in outs],
+            scratch_shapes=[pltpu.VMEM((rows, width), jnp.float32)] if scratch else [],
+        ),
+        out_shape=outs,
+        compiler_params=pltpu.CompilerParams(vmem_limit_bytes=24 * 2**20),
+        cost_estimate=pl.CostEstimate(flops=0, bytes_accessed=8 * 2**20, transcendentals=0),
+        name=name,
+    )(slot_of, *inputs)
+
+
+def mlp_back_kernel(
+    slot_ref, dy_ref, gate_ref, up_ref, down_ref, act_ref, dgate_ref, dup_ref, branch_ref, weight_ref
+):
+    block = down_ref.shape[1]
+
+    @pl.when(pl.program_id(0) == 0)
+    def _():
+        for index in range(8):
+            weight_ref[index * block : (index + 1) * block, :] = down_ref[slot_ref[index]]
+
+    units, step = gate_ref.shape[1], 512
+    dy = dy_ref[...]
+    total = None
+    for start in range(0, units, step):
+        columns = slice(start, start + step)
+        weight = weight_ref[columns, :]
+        gate, upper = gate_ref[:, columns], up_ref[:, columns]
+        d_act = dot_t(dy, weight)
+        sigma = 1.0 / (1.0 + jnp.exp(-gate))
+        silu = gate * sigma
+        act = (silu * upper).astype(jnp.bfloat16)
+        act_ref[:, columns] = act
+        dup_ref[:, columns] = (d_act * silu).astype(jnp.bfloat16)
+        d_gate = d_act * upper * sigma * (1.0 + gate * (1.0 - sigma))
+        dgate_ref[:, columns] = d_gate.astype(jnp.bfloat16)
+        term = jnp.dot(act, weight, preferred_element_type=jnp.float32)
+        total = term if total is None else total + term
+    branch_ref[0] = total.astype(jnp.bfloat16)
+
+
+def mlp_back(slot_of, d_branch, gate, upper, down_blocks):
+    count, units = gate.shape
+    width = d_branch.shape[1]
+    rows = 256
+    by_rows = lambda columns: pl.BlockSpec((rows, columns), lambda i, p: (i, 0))
+    wide = jax.ShapeDtypeStruct((count, units), jnp.bfloat16)
+    return pl.pallas_call(
+        mlp_back_kernel,
+        grid_spec=pltpu.PrefetchScalarGridSpec(
+            num_scalar_prefetch=1,
+            grid=(count // rows,),
+            in_specs=[
+                by_rows(width),
+                by_rows(units),
+                by_rows(units),
+                pl.BlockSpec(down_blocks.shape, lambda i, p: (0, 0, 0)),
+            ],
+            out_specs=[by_rows(units)] * 3
+            + [pl.BlockSpec((1, rows, width), lambda i, p: (i, 0, 0))],
+            scratch_shapes=[pltpu.VMEM((units, width), jnp.bfloat16)],
+        ),
+        out_shape=[
+            wide,
+            wide,
+            wide,
+            jax.ShapeDtypeStruct((count // rows, rows, width), jnp.bfloat16),
+        ],
+        compiler_params=pltpu.CompilerParams(vmem_limit_bytes=56 * 2**20),
+        cost_estimate=pl.CostEstimate(
+            flops=4 * count * units * width, bytes_accessed=32 * 2**20, transcendentals=0
+        ),
+        name="mlp_back",
+    )(slot_of, d_branch, gate, upper, down_blocks)
+
+
+def slot_grad_kernel(slot_ref, left_ref, right_ref, out_ref):
+    block = out_ref.shape[1]
+    grad = t_dot(left_ref[...], right_ref[...]).astype(jnp.bfloat16)
+    for index in range(8):
+        out_ref[slot_ref[index]] = grad[index * block : (index + 1) * block, :]
+
+
+def slot_grad(slot_of, left, right):
+    count, rows = left.shape
+    width = right.shape[1]
+    columns = 512
+    return pl.pallas_call(
+        slot_grad_kernel,
+        grid_spec=pltpu.PrefetchScalarGridSpec(
+            num_scalar_prefetch=1,
+            grid=(width // columns,),
+            in_specs=[
+                pl.BlockSpec((count, rows), lambda i, p: (0, 0)),
+                pl.BlockSpec((count, columns), lambda i, p: (0, i)),
+            ],
+            out_specs=pl.BlockSpec((8, rows // 8, columns), lambda i, p: (0, 0, i)),
+        ),
+        out_shape=jax.ShapeDtypeStruct((8, rows // 8, width), jnp.bfloat16),
+        compiler_params=pltpu.CompilerParams(vmem_limit_bytes=48 * 2**20),
+        cost_estimate=pl.CostEstimate(
+            flops=2 * count * rows * width, bytes_accessed=16 * 2**20, transcendentals=0
+        ),
+        name="slot_grad",
+    )(slot_of, left, right)
+
+
+class Grads(Task):
+    copies = 1
+
+    def outs(self):
+        rows, left, right = self.inputs
+        block = rows.shape[1] // 8
+        return [jax.ShapeDtypeStruct((8, block, one.shape[1]), jnp.bfloat16) for one in (left, right)]
+
+    def scratch(self):
+        return []
+
+    def steps(self, place, ins, outs, scratch):
+        count, width = self.inputs[0].shape
+        block = width // 8
+
+        def body(rows_ref, left_ref, right_ref, left_out, right_out):
+            rows = rows_ref[...]
+            left_out[0] = t_dot(rows, left_ref[...]).astype(jnp.bfloat16)
+            right_out[0] = t_dot(rows, right_ref[...]).astype(jnp.bfloat16)
+
+        def whole(one):
+            return pl.BlockSpec((count, one.shape[1]), lambda i: (0, 0))
+
+        def out(one):
+            return pl.BlockSpec((1, block, one.shape[1]), lambda i: (i, 0, 0))
+
+        run = pltpu.emit_pipeline(
+            body,
+            grid=(8,),
+            in_specs=[
+                pl.BlockSpec((count, block), lambda i: (0, i)),
+                whole(self.inputs[1]),
+                whole(self.inputs[2]),
+            ],
+            out_specs=[out(self.inputs[1]), out(self.inputs[2])],
+        )
+        return [lambda: None, None, lambda: run(*ins, *outs), None]
+
+
 def shards_paired(
     hidden_in,
     cotangent,
@@ -857,120 +1352,75 @@
     high, low = lax.axis_index("mp") // 2, lax.axis_index("mp") % 2
     plane = high
     groups = lax.axis_size("mp")
-    heads = QUERY_HEADS // groups
-    key_value_heads = KEY_VALUE_HEADS // groups
-    query_group = heads // key_value_heads
-    query_width = heads * HEAD_SIZE
-    key_width = key_value_heads * HEAD_SIZE
+    query_width = QUERY_HEADS // groups * HEAD_SIZE
+    key_width = KEY_VALUE_HEADS // groups * HEAD_SIZE
     units = FF // groups
     rows_here = hidden_in.shape[0]
     count = 4 * rows_here
     half = count // 2
     width = hidden_in.shape[1]
-    inverse = jnp.argsort(owner)
-    logical_of = jnp.take(inverse, jnp.arange(8, dtype=jnp.int32) ^ plane, mode="clip")
-    slot_of = owner ^ plane
+    slot_of = (owner ^ plane).astype(jnp.int32)
     out_rate = float(QUERY_HEADS * HEAD_SIZE // 32) ** (-0.5)
-
-    def to_slots(rows):
-        return jnp.take(rows.reshape(rows.shape[0], 8, -1), logical_of, axis=1, mode="clip").reshape(rows.shape)
-
-    def from_slots(rows):
-        return jnp.take(rows.reshape(rows.shape[0], 8, -1), slot_of, axis=1, mode="clip").reshape(rows.shape)
 
     ln_in = gains[:MODEL_WIDTH]
     ln_mid = gains[MODEL_WIDTH : 2 * MODEL_WIDTH]
     q_gain = gains[2 * MODEL_WIDTH : 2 * MODEL_WIDTH + HEAD_SIZE]
     k_gain = gains[2 * MODEL_WIDTH + HEAD_SIZE :]
-    x_rows = hidden_in.astype(jnp.float32)
-    low_qkv = projection_master_weight.astype(jnp.bfloat16)
-    low_out = out_weight.astype(jnp.bfloat16)
-    low_first = jnp.concatenate([low_qkv, low_out.reshape(low_qkv.shape[0], -1)], axis=1)
-    (first_blocks,), (full_in,), (near_gateup,) = transfer(
+    low_gateup = gateup_weight.astype(jnp.bfloat16)
+    own_in = by_row_tiles(
+        norm_kernel,
+        "norm_in",
+        slot_of,
+        [hidden_in, ln_in[None]],
+        [jax.ShapeDtypeStruct(hidden_in.shape, jnp.bfloat16)],
+    )
+    (qkv_blocks,), (out_blocks,), (full_in,), (near_gate,) = transfer(
         "gather_first",
         1,
-        108,
-        Planes(low_first),
-        Rows(to_slots(rms_norm(x_rows, ln_in).astype(jnp.bfloat16))),
-        Near(gateup_weight.astype(jnp.bfloat16), phase=1),
+        75,
+        Planes(projection_master_weight.astype(jnp.bfloat16)),
+        Planes(out_weight.astype(jnp.bfloat16)),
+        Rows(own_in[0]),
+        Near(low_gateup[:, :units], phase=1),
     )
     full_in = full_in.reshape(count, width)
-    w_qkv = first_blocks[:, :, : low_qkv.shape[1]].reshape(width, -1)
-    w_out = first_blocks[:, :, low_qkv.shape[1] :].reshape(8, low_out.shape[0], width)
-    w_out = jnp.take(w_out, slot_of, axis=0, mode="clip").reshape(-1, width)
-    w_gateup = over_plane(near_gateup).reshape(width, -1)
-    grad_out = cotangent.astype(jnp.float32)
+    w_qkv = qkv_blocks.reshape(width, -1)
+    w_out = jnp.take(out_blocks, slot_of, axis=0, mode="clip").reshape(-1, width)
+    gate_blocks = over_plane(near_gate)
+    near_up = to_group(after(low_gateup[:, units:], full_in))
 
     lengths = jnp.concatenate([doc_lengths, move(doc_lengths, OVER_C)], axis=0)
     ends = jnp.cumsum(lengths, axis=1)
     spot = jnp.arange(half, dtype=jnp.int32)
     chunk = spot // rows_here
     own_places = high * half + (low ^ chunk) * rows_here + spot % rows_here
-    key_places = jnp.concatenate([own_places - half, own_places])
-
-    def documents(places):
-        return jnp.sum((places[None, :, None] >= ends[:, None, :]).astype(jnp.int32), axis=2)
-
-    doc_of = documents(own_places)
-    key_doc = jnp.where(key_places[None, :] >= 0, documents(key_places), -1)
-    chosen = doc_of[:, :, None] == jnp.arange(lengths.shape[1], dtype=jnp.int32)[None, None, :]
-    begin = jnp.sum(jnp.where(chosen, (ends - lengths)[:, None, :], 0), axis=2)
-    offset = (own_places[None, :] - begin).astype(jnp.float32).reshape(count)
-    freq = THETA ** (
-        -(2.0 * jnp.arange(HEAD_SIZE // 2, dtype=jnp.float32)) / HEAD_SIZE
-    )
-    angle = offset[:, None] * freq[None, :]
+    later = own_places[None, :, None] >= ends[:, None, :]
+    begin = jnp.max(jnp.where(later, ends[:, None, :], 0), axis=2).reshape(count, 1)
+    time = jnp.concatenate([own_places, own_places]).reshape(count, 1)
+    freq = THETA ** (-(2.0 * jnp.arange(HEAD_SIZE // 2, dtype=jnp.float32)) / HEAD_SIZE)
+    angle = (time - begin).astype(jnp.float32) * freq[None, :]
     cosine, sine = jnp.cos(angle), jnp.sin(angle)
-    cosine = jnp.concatenate([cosine, cosine], axis=-1)[:, None, :]
-    sine = jnp.concatenate([sine, sine], axis=-1)[:, None, :]
-
-    projected = jnp.dot(full_in, w_qkv, preferred_element_type=jnp.float32)
-    query_raw = projected[:, :query_width].reshape(count, heads, HEAD_SIZE)
-    unrotated_key = projected[:, query_width : query_width + key_width].reshape(
-        count, key_value_heads, HEAD_SIZE
-    )
-    query_rows = rotate(rms_norm(query_raw, q_gain), cosine, sine).astype(jnp.bfloat16)
-    key_rows = rotate(rms_norm(unrotated_key, k_gain), cosine, sine).astype(jnp.bfloat16)
-    key_rows = key_rows.reshape(count, key_width)
-    value_rows = projected[:, query_width + key_width :].astype(jnp.bfloat16)
-    own_kv = jnp.concatenate([key_rows, value_rows], axis=1)
-    (lower_kv,), (d_branch,) = transfer(
-        "keys_up", 2, 47, Halves(own_kv, 0), Rows(cotangent)
-    )
-    lower_kv = jnp.where(high == 1, lower_kv, jnp.zeros_like(lower_kv))
+    cosine = jnp.concatenate([cosine, cosine], axis=-1)
+    sine = jnp.concatenate([-sine, sine], axis=-1)
+    head_gains = jnp.stack([q_gain, k_gain])
+    place = jnp.stack([high, low]).astype(jnp.int32)
+
+    raw, queries, own_kv = project(
+        full_in, qkv_blocks, cosine, sine, head_gains, query_width, key_width
+    )
+    (lower_kv,), (d_branch,) = transfer("keys_up", 2, 47, Halves(own_kv, 0), Rows(cotangent))
     d_branch = d_branch.reshape(count, width)
-    all_kv = jnp.concatenate(
-        [lower_kv.reshape(2, half, 2 * key_width), own_kv.reshape(2, half, 2 * key_width)], axis=1
-    )
-    keys = all_kv[:, :, :key_width].reshape(2, count, key_value_heads, HEAD_SIZE)
-    values = all_kv[:, :, key_width:].reshape(2, count, key_value_heads, HEAD_SIZE)
-    queries = query_rows.reshape(2, half, key_value_heads, query_group, HEAD_SIZE)
-    score_scale = HEAD_SIZE ** (-0.5)
-
-    def scores_of(part):
-        query_block, key_block, row_doc, col_doc = part
-        raw = (
-            jnp.einsum("tlwd,uld->lwtu", query_block, key_block, preferred_element_type=jnp.float32)
-            * score_scale
-        )
-        allowed = (row_doc[:, None] == col_doc[None, :]) & (
-            key_places[None, :] <= own_places[:, None]
-        )
-        return jnp.where(allowed[None, None], raw, MASKED)
-
-    def forward_part(parts):
-        query_block, key_block, value_block, row_doc, col_doc = parts
-        score_matrix = scores_of((query_block, key_block, row_doc, col_doc))
-        top = jnp.max(score_matrix, axis=-1, keepdims=True)
-        total = jnp.log(jnp.sum(jnp.exp(score_matrix - top), axis=-1, keepdims=True)) + top
-        probabilities = jnp.exp(score_matrix - total).astype(jnp.bfloat16)
-        attention_result = jnp.einsum(
-            "cpyx,xca->ycpa", probabilities, value_block, preferred_element_type=jnp.float32
-        )
-        return (attention_result.reshape(half, query_width).astype(jnp.bfloat16), total)
-
-    outs, totals = lax.map(forward_part, (queries, keys, values, doc_of, key_doc))
-    attn_heads = outs.reshape(count, query_width)
+    lower_kv, near_up = lax.optimization_barrier((lower_kv, near_up))
+    up_blocks = over_plane(near_up)
+    score_flops = 2 * count * count * query_width
+    (attn_heads,) = attention_call(
+        attend_kernel,
+        "attend",
+        place,
+        [time, begin, queries, lower_kv, own_kv],
+        [jax.ShapeDtypeStruct((count, query_width), jnp.bfloat16)],
+        2 * score_flops,
+    )
 
     def blocks(partial):
         return partial.astype(jnp.bfloat16).reshape(4, rows_here, width)
@@ -980,125 +1430,92 @@
         "sum_attention", 3, 50, Sums(partial), Near(down_weight.astype(jnp.bfloat16))
     )
     down_blocks = over_plane(near_down)
-    mixed = x_rows + summed(partial, received)
-    ((full_mid,),) = transfer(
-        "gather_mid", 4, 34, Rows(to_slots(rms_norm(mixed, ln_mid).astype(jnp.bfloat16)))
-    )
+    row = jax.ShapeDtypeStruct((rows_here, width), jnp.float32)
+    low_row = jax.ShapeDtypeStruct((rows_here, width), jnp.bfloat16)
+    gain_row = jax.ShapeDtypeStruct((8, width), jnp.float32)
+    mixed, own_mid = by_row_tiles(
+        mix_kernel, "mix", slot_of, [hidden_in, partial, *received, ln_mid[None]], [row, low_row]
+    )
+    ((full_mid,),) = transfer("gather_mid", 4, 34, Rows(own_mid))
     full_mid = full_mid.reshape(count, width)
-    gateup = jnp.dot(full_mid, w_gateup, preferred_element_type=jnp.float32)
-    down_blocks, gateup = lax.optimization_barrier((down_blocks, gateup))
-    w_down = jnp.take(down_blocks, slot_of, axis=0, mode="clip").reshape(-1, width)
-    gate = gateup[:, :units]
-    upper = gateup[:, units:]
-    sigma = jax.nn.sigmoid(gate)
-    act = (gate * sigma * upper).astype(jnp.bfloat16)
-    branch = blocks(jnp.dot(act, w_down, preferred_element_type=jnp.float32))
-
-    g_down = jnp.einsum("tf,td->fd", act, d_branch, preferred_element_type=jnp.float32)
-    g_down = jnp.take(g_down.astype(jnp.bfloat16).reshape(8, -1, width), logical_of, axis=0, mode="clip")
-    d_act = jnp.einsum("td,fd->tf", d_branch, w_down, preferred_element_type=jnp.float32)
-    d_upper = d_act * gate * sigma
-    d_gate = d_act * upper * sigma * (1.0 + gate * (1.0 - sigma))
-    d_gateup = jnp.concatenate([d_gate, d_upper], axis=1).astype(jnp.bfloat16)
-    d_gateup, g_down = lax.optimization_barrier((d_gateup, g_down))
+    w_gate = gate_blocks.reshape(width, units)
+    gate = jnp.dot(full_mid, w_gate, preferred_element_type=jnp.float32)
+    up_blocks, gate = lax.optimization_barrier((up_blocks, gate))
+    w_up = up_blocks.reshape(width, units)
+    upper = jnp.dot(full_mid, w_up, preferred_element_type=jnp.float32)
+    down_blocks, upper = lax.optimization_barrier((down_blocks, upper))
+    act, d_gate, d_upper, branch = mlp_back(slot_of, d_branch, gate, upper, down_blocks)
+    g_down = slot_grad(slot_of, act, d_branch)
+    d_gate, d_upper, g_down = lax.optimization_barrier((d_gate, d_upper, g_down))
     near_g_down = to_plane(g_down)
-    g_gateup = jnp.einsum("td,tf->df", full_mid, d_gateup, preferred_element_type=jnp.float32)
-    g_gateup = g_gateup.astype(jnp.bfloat16).reshape(8, -1, 2 * units)
     partial = blocks(
-        jnp.einsum("tc,dc->td", d_gateup, w_gateup, preferred_element_type=jnp.float32)
-    )
-    partial, g_gateup = lax.optimization_barrier((partial, g_gateup))
-    near_g_gateup = to_plane(g_gateup)
-    (received,) = transfer("sum_mid", 5, 32, Sums(partial))
-    d_mid_rows = from_slots(summed(partial, received))
-    d_mixed, g_ln_mid = norm_back(mixed, ln_mid, d_mid_rows)
-    d_mixed = d_mixed + grad_out
+        jnp.einsum("tc,dc->td", d_gate, w_gate, preferred_element_type=jnp.float32)
+        + jnp.einsum("tc,dc->td", d_upper, w_up, preferred_element_type=jnp.float32)
+    )
+    received, (g_gate, g_up) = transfer(
+        "sum_mid", 5, 33, Sums(partial), Grads(full_mid, d_gate, d_upper)
+    )
+    near_g_gate, near_g_up = to_plane(g_gate), to_plane(g_up)
+    d_mixed, low_d_mixed, mid_gain = by_row_tiles(
+        mix_back_kernel,
+        "mix_back",
+        slot_of,
+        [mixed, partial, *received, ln_mid[None], cotangent],
+        [row, low_row, gain_row],
+        scratch=True,
+    )
+    g_ln_mid = jnp.sum(mid_gain, axis=0)
     (d_attn,), (owned_down,) = transfer(
-        "gather_attention", 6, 40, Rows(d_mixed.astype(jnp.bfloat16)), Owners(near_g_down)
+        "gather_attention", 6, 40, Rows(low_d_mixed), Owners(near_g_down)
     )
     d_attn = d_attn.reshape(count, width)
     red_down = both(owned_down)
-    g_out = jnp.einsum("th,td->hd", attn_heads, d_attn, preferred_element_type=jnp.float32)
-    g_out = jnp.take(g_out.astype(jnp.bfloat16).reshape(8, -1, width), logical_of, axis=0, mode="clip")
-    near_g_out = to_plane(g_out)
+    g_out = slot_grad(slot_of, attn_heads, d_attn)
     d_heads = jnp.einsum("td,hd->th", d_attn, w_out, preferred_element_type=jnp.float32).astype(
         jnp.bfloat16
     )
-    d_heads = d_heads.reshape(2, half, key_value_heads, query_group, HEAD_SIZE)
-
-    def backward_part(parts):
-        query_block, key_block, value_block, row_doc, col_doc, block_total, block_gradient = parts
-        score_matrix = scores_of((query_block, key_block, row_doc, col_doc))
-        probabilities = jnp.exp(score_matrix - block_total)
-        probability_gradient = jnp.einsum(
-            "tlwd,uld->lwtu", block_gradient, value_block, preferred_element_type=jnp.float32
-        )
-        d_value = jnp.einsum(
-            "zxrb,rzxd->bzd",
-            probabilities.astype(jnp.bfloat16),
-            block_gradient,
-            preferred_element_type=jnp.float32,
-        )
-        score_gradient = (
-            probabilities
-            * (
-                probability_gradient
-                - jnp.sum(probabilities * probability_gradient, axis=-1, keepdims=True)
-            )
-        ).astype(jnp.bfloat16)
-        d_query = (
-            jnp.einsum(
-                "cpyx,xca->ycpa", score_gradient, key_block, preferred_element_type=jnp.float32
-            )
-            * score_scale
-        )
-        d_key = (
-            jnp.einsum(
-                "zxrb,rzxd->bzd", score_gradient, query_block, preferred_element_type=jnp.float32
-            )
-            * score_scale
-        )
-        d_kv = jnp.concatenate([d_key.reshape(count, key_width), d_value.reshape(count, key_width)], axis=1)
-        return (d_query.reshape(half, query_width), d_kv)
-
-    d_queries, d_kv = lax.map(
-        backward_part, (queries, keys, values, doc_of, key_doc, totals, d_heads)
-    )
-    (from_above,), received = transfer(
-        "keys_down", 7, 53, Halves(d_kv[:, :half].astype(jnp.bfloat16), 1), Sums(branch)
-    )
+    d_heads, near_g_gate, g_out = lax.optimization_barrier((d_heads, near_g_gate, g_out))
+    near_g_out = to_plane(g_out)
+    owned_gate = to_owner(near_g_gate)
+    d_queries, d_low, d_own = attention_call(
+        attend_back_kernel,
+        "attend_back",
+        place,
+        [time, begin, queries, lower_kv, own_kv, d_heads],
+        [
+            jax.ShapeDtypeStruct((count, query_width), jnp.float32),
+            jax.ShapeDtypeStruct((count, 2 * key_width), jnp.bfloat16),
+            jax.ShapeDtypeStruct((count, 2 * key_width), jnp.float32),
+        ],
+        5 * score_flops,
+    )
+    d_low, *owned_gate = lax.optimization_barrier((d_low, *owned_gate))
+    red_gate = both(owned_gate)
+    (from_above,), received = transfer("keys_down", 7, 53, Halves(d_low, 1), Sums(branch))
     result_rows = mixed + summed(branch, received)
-    from_above = jnp.where(high == 0, from_above, jnp.zeros_like(from_above))
-    d_kv = (d_kv[:, half:] + from_above.astype(jnp.float32)).reshape(count, 2 * key_width)
-    d_queries = d_queries.reshape(count, heads, HEAD_SIZE)
-    d_keys = d_kv[:, :key_width].reshape(count, key_value_heads, HEAD_SIZE)
-    d_query_raw, g_q = norm_back(query_raw, q_gain, rotate_back(d_queries, cosine, sine))
-    d_key_raw, g_k = norm_back(unrotated_key, k_gain, rotate_back(d_keys, cosine, sine))
-    d_projected = jnp.concatenate(
-        [
-            d_query_raw.reshape(count, query_width),
-            d_key_raw.reshape(count, key_width),
-            d_kv[:, key_width:],
-        ],
-        axis=1,
-    ).astype(jnp.bfloat16)
+    near_g_up, from_above = lax.optimization_barrier((near_g_up, from_above))
+    d_projected, g_q, g_k = unproject(
+        place, d_queries, d_own, from_above, raw, cosine, sine, head_gains
+    )
+    g_q, g_k = jnp.sum(g_q, axis=0), jnp.sum(g_k, axis=0)
     g_qkv = jnp.einsum("td,tc->dc", full_in, d_projected, preferred_element_type=jnp.float32)
     near_g_qkv = to_plane(g_qkv.astype(jnp.bfloat16).reshape(8, width // 8, -1))
     partial = blocks(
         jnp.einsum("tc,dc->td", d_projected, w_qkv, preferred_element_type=jnp.float32)
     )
-    received, (owned_gateup,) = transfer("sum_in", 8, 74, Sums(partial), Owners(near_g_gateup))
-    red_gateup = both(owned_gateup)
-    d_in_rows = from_slots(summed(partial, received))
-    near_g_out, near_g_qkv, red_gateup = lax.optimization_barrier(
-        (near_g_out, near_g_qkv, red_gateup)
-    )
-    (owned_out,), (owned_qkv,) = transfer(
-        "last_owners", 9, 40, Owners(near_g_out), Owners(near_g_qkv)
-    )
-    red_out, red_qkv = both(owned_out), both(owned_qkv)
-    d_input, g_ln_in = norm_back(x_rows, ln_in, d_in_rows)
-    input_grad = d_input + d_mixed
+    received, (owned_up,) = transfer("sum_in", 8, 40, Sums(partial), Owners(near_g_up))
+    red_gateup = jnp.concatenate([red_gate, both(owned_up)], axis=1)
+    near_g_out, near_g_qkv, *received = lax.optimization_barrier((near_g_out, near_g_qkv, *received))
+    red_out, red_qkv = both(to_owner(near_g_out)), both(to_owner(near_g_qkv))
+    input_grad, in_gain = by_row_tiles(
+        in_back_kernel,
+        "in_back",
+        slot_of,
+        [hidden_in, partial, *received, ln_in[None], d_mixed],
+        [row, gain_row],
+        scratch=True,
+    )
+    g_ln_in = jnp.sum(in_gain, axis=0)
     gain_terms = jnp.concatenate([g_ln_in, g_ln_mid, g_q, g_k])
     squares = jnp.sum(red_qkv * red_qkv) + jnp.sum(red_gateup * red_gateup)
     squares = squares + jnp.sum(red_out * red_out) + jnp.sum(red_down * red_down)

time: 985 us -> 785 us (0.80)
  local copies, waits for them, and re-layouts: 154 us -> 64.9 us
  matrix products: 162 us -> 76.8 us
  other arithmetic: 122 us -> 39.6 us
  waiting for transfers between devices: 9.36 us -> 61.3 us
  starting transfers between devices: 0.25 us -> 28.8 us
  Pallas kernels: 506 us -> 487 us
    pallas_call x9 -> x8, Pallas kernels: 491 us -> 378 us  [transfer(): pl.pallas_call(kernel, out_shape=[leaf for out in outs for leaf in out],...]
    pallas_call x0 -> x11, Pallas kernels: none -> 95.1 us  [the longest x2 33.2 us: attention_call(): pl.pallas_call(kernel, grid_spec=pltpu.PrefetchScalarGridSpec(num_scalar_...]
    dot_general x22 -> x4, matrix products: 136 us -> 48.2 us  [the longest x1 12.8 us: shards_paired(): jnp.einsum('tc,dc->td', d_upper, w_up, preferred_element_type=jnp.float32)]
    ppermute x1 -> x9, waiting for transfers between devices: 0.01 us -> 41.8 us  [move(): return lax.ppermute(value, ('dp', 'mp'), pairs)]
    reshape x22 -> x1, local copies, waits for them, and re-layouts: 36.8 us -> 1.02 us  [shards_paired(): time = jnp.concatenate([own_places, own_places]).reshape(count, 1)]
    ppermute x1 -> x9, starting transfers between devices: 0.01 us -> 27.7 us  [move(): return lax.ppermute(value, ('dp', 'mp'), pairs)]
    gather x9 -> x1, local copies, waits for them, and re-layouts: 31.3 us -> 3.59 us  [shards_paired(): jnp.take(out_blocks, slot_of, axis=0, mode='clip').reshape(-1, width)]
    unnamed x267 -> x167, local copies, waits for them, and re-layouts: 26.1 us -> 52.8 us
  transfers between devices with their start and end apart: 7 -> 17, of which waited for: 1 -> 6; matrix products, arithmetic and copies ran while one was open for 32% -> 13% of each run, Pallas kernels for 35% -> 48%
where the time goes in v3:
time: 785 us; the launch traced here: 778 us
  Pallas kernels  487 us (62%)
  matrix products  76.8 us (10%)
  local copies, waits for them, and re-layouts  64.9 us (8%)
  waiting for transfers between devices  61.3 us (8%)
  other arithmetic  39.6 us (5%)
  starting transfers between devices  28.8 us (4%)
  between operations  20.3 us (3%)
    pallas_call x8, Pallas kernels, transfer(): pl.pallas_call(kernel, out_shape=[leaf for out in outs for leaf in out],...  378 us
    unnamed x167, local copies, waits for them, and re-layouts  52.8 us
    ppermute x9, waiting for transfers between devices, move(): return lax.ppermute(value, ('dp', 'mp'), pairs)  41.8 us
    pallas_call x2, Pallas kernels, attention_call(): pl.pallas_call(kernel, grid_spec=pltpu.PrefetchScalarGridSpec(num_scalar_...  33.2 us
    ppermute x9, starting transfers between devices, move(): return lax.ppermute(value, ('dp', 'mp'), pairs)  27.7 us
    pallas_call x1, Pallas kernels, mlp_back(): pl.pallas_call(mlp_back_kernel, grid_spec=pltpu.PrefetchScalarGridSpec(nu...  22.6 us
    sub x5, other arithmetic, adam(): weight * (1.0 - rate * decay)  17.9 us
    pallas_call x2, Pallas kernels, slot_grad(): pl.pallas_call(slot_grad_kernel, grid_spec=pltpu.PrefetchScalarGridSpec(n...  15.8 us
  transfers between devices with their start and end apart: 17, of which 6 were waited for; matrix products, arithmetic and copies ran while one was open for 13% of the time, Pallas kernels for 48%

profile of v3, /device:TPU:0, one launch (start us, length us, event | category | flops | bytes accessed | tf_op | source)
XLA Modules:
  0.0 778.3 jit_solution(11927680799545194084)
XLA Ops:
  10.4 2.2 convert_element_type.88
  14.9 61.3 %gather_first.1 = (bf16[8,256,1024]{2,1,0:T(8,128)(2,1)}, bf16[8,64,2048]{2,1,0:T(8,128)(2,1)}, bf16[4,256,2048]{2,1,0:T(8,128)(2,1)}, bf16[2,256,1536]{2,1,0:T(8,128)(2,1)S(1)}) custom-call(bf16[256,1024]{1,0:T(8,128)(2,1)S(1)} %convert_element_type.86.refs_0_, bf16[64,2048]{1,0:T(8,128)(2,1)S(1)} %convert_element_type.87.refs_1_, ...), custom_call_target="tpu_custom_call" | custom-call | bytes 247500000 | tf_op jit(solution)/shard_map/gather_first/pallas_call | solution.py:746
  77.4 12.2 %collective-permute-start.2 = (bf16[256,1536]{1,0:T(8,128)(2,1)}, bf16[256,1536]{1,0:T(8,128)(2,1)S(1)}, u32[]{:S(2)}, u32[]{:S(2)}) collective-permute-start(bf16[256,1536]{1,0:T(8,128)(2,1)} %get-tuple-element.86), channel_id=1, source_target_pairs={{4,0},{5,1},{0,2},{1,3},{6,4},{7,5},{2,6},{3,7},{12,8},{13,9},{8,1... | collective-permute-start | bytes 2359304 | tf_op jit(solution)/shard_map/ppermute | solution.py:423
  89.7 7.4 collective-permute-start.1
  100.8 9.5 %project.1 = (f32[1024,768]{1,0:T(8,128)}, bf16[1024,512]{1,0:T(8,128)(2,1)S(1)}, bf16[1024,512]{1,0:T(8,128)(2,1)S(1)}) custom-call(bf16[1024,2048]{1,0:T(8,128)(2,1)} %bitcast.111, bf16[8,256,1024]{2,1,0:T(8,128)(2,1)} %get-tuple-element.82.weight_ref, f32[1024,128]{1,0:T(8,128)S(1)} %get-tuple-element.176.cos_ref, ...), custom_call_target="tpu_custom_call" | custom-call | flops 4294967296 | bytes 16777216 | tf_op jit(solution)/shard_map/project/pallas_call | solution.py:877
  110.3 49.4 %keys_up.1 = (bf16[1024,512]{1,0:T(8,128)(2,1)S(1)}, bf16[4,256,2048]{2,1,0:T(8,128)(2,1)}) custom-call(bf16[1024,512]{1,0:T(8,128)(2,1)S(1)} %get-tuple-element.84.refs_0_.own_ref, bf16[256,2048]{1,0:T(8,128)(2,1)S(1)} %copy-done.7), custom_call_target="tpu_custom_call" | custom-call | bytes 155100000 | tf_op jit(solution)/shard_map/keys_up/pallas_call | solution.py:746
  160.6 2.4 pad_maximum_fusion.1
  164.9 3.6 gather_fusion
  171.1 12.0 %attend.1.left_ref = bf16[1024,512]{1,0:T(8,128)(2,1)} custom-call(s32[2]{0:T(128)} %pad_add_fusion.2.place_ref, s32[1024,1]{1,0:T(8,128)} %copy.45.time_ref, s32[1024,1]{1,0:T(8,128)} %bitcast.98, bf16[1024,512]{1,0:T(8,128)(2,1)} %copy-done.51, bf16[1024,512]{1,0:T(8,128)(2,1)} %copy-done.49, bf16[1024,512]{1,0:T(8,128)(2,1)} %copy-done.26), custom_call_target="tpu_custom_call" | custom-call | flops 2147483648 | bytes 16777216 | tf_op jit(solution)/shard_map/attend/pallas_call | solution.py:1082
  183.1 5.8 convolution_convert_fusion
  188.9 57.5 %sum_attention.1 = (bf16[256,2048]{1,0:T(8,128)(2,1)S(1)}, bf16[256,2048]{1,0:T(8,128)(2,1)S(1)}, bf16[2,192,2048]{2,1,0:T(8,128)(2,1)}) custom-call(bf16[4,256,2048]{2,1,0:T(8,128)(2,1)} %bitcast.88, bf16[192,2048]{1,0:T(8,128)(2,1)S(1)} %convert_element_type.91.refs_1_), custom_call_target="tpu_custom_call" | custom-call | bytes 165000000 | tf_op jit(solution)/shard_map/sum_attention/pallas_call | solution.py:746
  248.7 2.2 copy-done.3
  255.0 28.4 %gather_mid.1 = bf16[4,256,2048]{2,1,0:T(8,128)(2,1)S(1)} custom-call(bf16[256,2048]{1,0:T(8,128)(2,1)S(1)} %get-tuple-element.94.refs_0_), custom_call_target="tpu_custom_call" | custom-call | bytes 112200000 | tf_op jit(solution)/shard_map/gather_mid/pallas_call | solution.py:746
  283.4 1.9 copy-done
  285.3 11.8 %fusion.33.gate_ref = f32[1024,1536]{1,0:T(8,128)} fusion(bf16[1024,2048]{1,0:T(8,128)(2,1)} %bitcast.81, bf16[2048,1536]{1,0:T(8,128)(2,1)} %bitcast.106), kind=kOutput, calls=%fused_computation.91 | convolution fusion | flops 6442450944 | bytes 16777216 | tf_op jit(solution)/shard_map/dot_general | solution.py:1442
  297.1 11.7 %fusion.34.up_ref = f32[1024,1536]{1,0:T(8,128)} fusion(bf16[1024,2048]{1,0:T(8,128)(2,1)} %bitcast.82, bf16[2048,1536]{1,0:T(8,128)(2,1)} %bitcast.108), kind=kOutput, calls=%fused_computation.92 | convolution fusion | flops 6442450944 | bytes 16777216 | tf_op jit(solution)/shard_map/dot_general | solution.py:1445
  308.8 9.5 %all-gather.8.cloned.1.call-done.down_ref = bf16[8,192,2048]{2,1,0:T(8,128)(2,1)} async-done(((bf16[2,192,2048]{2,1,0:T(8,128)(2,1)}), bf16[8,192,2048]{2,1,0:T(8,128)(2,1)}) %all-gather.8.cloned.1.call-update) | async-done | bytes 6291472 | tf_op jit(solution)/shard_map/all_gather | solution.py:777
  318.3 22.6 %mlp_back.1 = (bf16[1024,1536]{1,0:T(8,128)(2,1)}, bf16[1024,1536]{1,0:T(8,128)(2,1)}, bf16[1024,1536]{1,0:T(8,128)(2,1)}, bf16[4,256,2048]{2,1,0:T(8,128)(2,1)}) custom-call(s32[8]{0:T(128)} %copy-done.45, bf16[1024,2048]{1,0:T(8,128)(2,1)} %bitcast.113, f32[1024,1536]{1,0:T(8,128)} %fusion.33.gate_ref, f32[1024,1536]{1,0:T(8,128)} %fusion.34.up_ref, ...), custom_call_target="tpu_custom_call" | custom-call | flops 12884901888 | bytes 33554432 | tf_op jit(solution)/shard_map/mlp_back/pallas_call | solution.py:1232
  342.8 10.3 %slot_grad.2 = bf16[8,192,2048]{2,1,0:T(8,128)(2,1)} custom-call(s32[8]{0:T(128)S(1)} %copy-done.46, bf16[1024,1536]{1,0:T(8,128)(2,1)S(1)} %copy-done.52, bf16[1024,2048]{1,0:T(8,128)(2,1)} %bitcast.114), custom_call_target="tpu_custom_call" | custom-call | flops 6442450944 | bytes 16777216 | tf_op jit(solution)/shard_map/slot_grad/pallas_call | solution.py:1272
  353.6 11.9 %fusion.35 = f32[1024,2048]{1,0:T(8,128)} fusion(bf16[1024,1536]{1,0:T(8,128)(2,1)} %get-tuple-element.104.refs_2_, bf16[2048,1536]{1,0:T(8,128)(2,1)} %bitcast.107), kind=kOutput, calls=%fused_computation.93 | convolution fusion | flops 6442450944 | bytes 17825792 | tf_op jit(solution)/shard_map/tc,dc->td/dot_general | solution.py:1452
  365.5 12.8 %add_convert_fusion = bf16[1024,2048]{1,0:T(8,128)(2,1)} fusion(f32[1024,2048]{1,0:T(8,128)} %fusion.35, bf16[1024,1536]{1,0:T(8,128)(2,1)S(1)} %copy-done.60, bf16[2048,1536]{1,0:T(8,128)(2,1)} %bitcast.109), kind=kOutput, calls=%fused_computation.1 | convolution fusion | flops 6446645248 | bytes 22020096 | tf_op jit(solution)/shard_map/tc,dc->td/dot_general | solution.py:1453
  378.3 30.4 %sum_mid.1 = (bf16[256,2048]{1,0:T(8,128)(2,1)S(1)}, bf16[256,2048]{1,0:T(8,128)(2,1)S(1)}, bf16[8,256,1536]{2,1,0:T(8,128)(2,1)}, bf16[8,256,1536]{2,1,0:T(8,128)(2,1)}) custom-call(bf16[4,256,2048]{2,1,0:T(8,128)(2,1)} %bitcast.84, bf16[1024,2048]{1,0:T(8,128)(2,1)} %bitcast.83, bf16[1024,1536]{1,0:T(8,128)(2,1)S(1)} %copy-done.10, ...), custom_call_target="tpu_custom_call" | custom-call | bytes 108900000 | tf_op jit(solution)/shard_map/sum_mid/pallas_call | solution.py:746
  411.3 2.2 copy-done.1
  417.2 2.5 mix_back.1
  426.1 47.1 %gather_attention.1 = (bf16[4,256,2048]{2,1,0:T(8,128)(2,1)}, bf16[2,192,2048]{2,1,0:T(8,128)(2,1)S(1)}) custom-call(bf16[256,2048]{1,0:T(8,128)(2,1)S(1)} %copy-done.28, bf16[2,192,2048]{2,1,0:T(8,128)(2,1)S(1)} %copy-done.21), custom_call_target="tpu_custom_call" | custom-call | bytes 132000000 | tf_op jit(solution)/shard_map/gather_attention/pallas_call | solution.py:746
  475.6 5.5 slot_grad.3
  482.4 6.3 convolution_convert_fusion.3.grad_ref
  488.7 7.8 %reduce-scatter.8.cloned.1.call-done = bf16[2,256,1536]{2,1,0:T(8,128)(2,1)} async-done(((bf16[8,256,1536]{2,1,0:T(8,128)(2,1)}), bf16[2,256,1536]{2,1,0:T(8,128)(2,1)}) %reduce-scatter.8.cloned.1.call-update) | async-done | bytes 1572880 | tf_op jit(solution)/shard_map/reduce_scatter | solution.py:781
  498.9 21.1 %attend_back.1 = (f32[1024,512]{1,0:T(8,128)}, bf16[1024,512]{1,0:T(8,128)(2,1)}, f32[1024,512]{1,0:T(8,128)}) custom-call(s32[2]{0:T(128)} %pad_add_fusion.2.place_ref, s32[1024,1]{1,0:T(8,128)} %copy.45.time_ref, s32[1024,1]{1,0:T(8,128)} %bitcast.99, bf16[1024,512]{1,0:T(8,128)(2,1)} %copy-done.51, bf16[1024,512]{1,0:T(8,128)(2,1)} %copy-done.49, ...), custom_call_target="tpu_custom_call" | custom-call | flops 5368709120 | bytes 16777216 | tf_op jit(solution)/shard_map/attend_back/pallas_call | solution.py:1082
  520.0 7.9 %collective-permute-done.4 = bf16[256,1536]{1,0:T(8,128)(2,1)S(1)} collective-permute-done((bf16[256,1536]{1,0:T(8,128)(2,1)S(1)}, bf16[256,1536]{1,0:T(8,128)(2,1)S(1)}, u32[]{:S(2)}, u32[]{:S(2)}) %collective-permute-start.4) | collective-permute-done | bytes 786464 | tf_op jit(solution)/shard_map/ppermute | solution.py:423
  530.3 59.7 %keys_down.1 = (bf16[1024,512]{1,0:T(8,128)(2,1)S(1)}, bf16[256,2048]{1,0:T(8,128)(2,1)S(1)}, bf16[256,2048]{1,0:T(8,128)(2,1)S(1)}) custom-call(bf16[1024,512]{1,0:T(8,128)(2,1)S(1)} %copy-done.23, bf16[4,256,2048]{2,1,0:T(8,128)(2,1)} %get-tuple-element.116.refs_1_), custom_call_target="tpu_custom_call" | custom-call | bytes 174900000 | tf_op jit(solution)/shard_map/keys_down/pallas_call | solution.py:746
  592.8 1.9 copy-done.9
  601.3 5.2 unproject.1
  606.6 6.3 convolution_convert_fusion.1
  613.0 2.4 multiply_reduce_fusion.1
  615.4 10.2 %convolution_convert_fusion.2 = bf16[1024,2048]{1,0:T(8,128)(2,1)} fusion(bf16[1024,1024]{1,0:T(8,128)(2,1)} %copy-done.48, bf16[2048,1024]{1,0:T(8,128)(2,1)} %bitcast.110), kind=kOutput, calls=%fused_computation.5 | convolution fusion | flops 4297064448 | bytes 10485760 | tf_op jit(solution)/shard_map/tc,dc->td/dot_general | solution.py:1504
  625.6 43.9 %sum_in.1 = (bf16[256,2048]{1,0:T(8,128)(2,1)S(1)}, bf16[256,2048]{1,0:T(8,128)(2,1)S(1)}, bf16[2,256,1536]{2,1,0:T(8,128)(2,1)S(1)}) custom-call(bf16[4,256,2048]{2,1,0:T(8,128)(2,1)} %bitcast.86, bf16[2,256,1536]{2,1,0:T(8,128)(2,1)S(1)} %copy-done.22), custom_call_target="tpu_custom_call" | custom-call | bytes 132000000 | tf_op jit(solution)/shard_map/sum_in/pallas_call | solution.py:746
  672.8 2.8 fusion.2
  675.6 2.2 copy-done.2
  681.9 3.5 in_back.1
  688.6 2.6 collective-permute-start.6
  691.8 3.4 collective-permute-start.8
  695.2 32.9 %collective-permute-done.8 = bf16[64,2048]{1,0:T(8,128)(2,1)S(1)} collective-permute-done((bf16[64,2048]{1,0:T(8,128)(2,1)S(1)}, bf16[64,2048]{1,0:T(8,128)(2,1)S(1)}, u32[]{:S(2)}, u32[]{:S(2)}) %collective-permute-start.8) | collective-permute-done | bytes 262176 | tf_op jit(solution)/shard_map/ppermute | solution.py:423
  733.0 13.8 %sum_all.1 = f32[40,128]{1,0:T(8,128)} custom-call(f32[40,128]{1,0:T(8,128)} %pad_bitcast_fusion.value), custom_call_target="tpu_custom_call" | custom-call | tf_op jit(solution)/shard_map/sum_all/pallas_call | solution.py:829
  752.2 5.6 divide_subtract_fusion.1
  759.0 6.2 divide_subtract_fusion
  765.3 2.5 divide_subtract_fusion.3
  767.8 2.3 divide_subtract_fusion.2
  (234 shorter events, 73.6 us)
Async XLA Ops:
  7.2 278.1 %all-gather.6.cloned.1.call-start = ((), (), s32[]{:S(2)}) async-start(), calls=%async_computation.6 | async-start | bytes 7864320 | tf_op jit(solution)/shard_map/all_gather | solution.py:777
  10.3 3.2 copy-start.79
  13.6 235.1 %copy-start.45 = (s32[8]{0:T(128)}, s32[8]{0:T(128)S(1)}, u32[]{:S(2)}) copy-start(s32[8]{0:T(128)S(1)} %broadcast_xor_fusion.slot_ref) | copy-start | bytes 100
  13.6 83.5 %copy-start.77 = (s32[1,4]{1,0:T(1,128)S(1)}, s32[1,4]{1,0:T(1,128)}, u32[]{:S(2)}) copy-start(s32[1,4]{1,0:T(1,128)} %param.21) | copy-start | bytes 52
  13.6 83.5 %copy-start.74 = (f32[4352]{0:T(1024)S(1)}, f32[4352]{0:T(1024)}, u32[]{:S(2)}) copy-start(f32[4352]{0:T(1024)} %param.35) | copy-start | bytes 52228
  77.4 219.7 %all-gather.4.cloned.1.call-start = ((), (), s32[]{:S(2)}) async-start(), calls=%async_computation.5 | async-start | bytes 7864320 | tf_op jit(solution)/shard_map/all_gather | solution.py:777
  77.4 83.2 %collective-permute-start.2 = (bf16[256,1536]{1,0:T(8,128)(2,1)}, bf16[256,1536]{1,0:T(8,128)(2,1)S(1)}, u32[]{:S(2)}, u32[]{:S(2)}) collective-permute-start(bf16[256,1536]{1,0:T(8,128)(2,1)} %get-tuple-element.86), channel_id=1, source_target_pairs={{4,0},{5,1},{0,2},{1,3},{6,4},{7,5},{2,6},{3,7},{12,8},{13,9},{8,1... | collective-permute-start | bytes 2359304 | tf_op jit(solution)/shard_map/ppermute | solution.py:423
  89.7 71.0 %collective-permute-start.1 = (bf16[256,1536]{1,0:T(8,128)(2,1)}, bf16[256,1536]{1,0:T(8,128)(2,1)}, u32[]{:S(2)}, u32[]{:S(2)}) collective-permute-start(bf16[256,1536]{1,0:T(8,128)(2,1)} %get-tuple-element.86), channel_id=1, source_target_pairs={{0,0},{1,1},{4,2},{5,3},{2,4},{3,5},{6,6},{7,7},{8,8},{9,9},{12,10... | collective-permute-start | bytes 2359304 | tf_op jit(solution)/shard_map/ppermute | solution.py:423
  97.1 1.1 collective-permute-start
  100.7 9.5 %copy-start.13 = (f32[1024,128]{1,0:T(8,128)}, f32[1024,128]{1,0:T(8,128)S(1)}, u32[]{:S(2)}) copy-start(f32[1024,128]{1,0:T(8,128)S(1)} %get-tuple-element.176.cos_ref) | copy-start | bytes 1572868
  100.8 9.5 %copy-start.15 = (f32[1024,128]{1,0:T(8,128)}, f32[1024,128]{1,0:T(8,128)S(1)}, u32[]{:S(2)}) copy-start(f32[1024,128]{1,0:T(8,128)S(1)} %get-tuple-element.177.sin_ref) | copy-start | bytes 1572868
  100.8 9.5 %copy-start.7 = (bf16[256,2048]{1,0:T(8,128)(2,1)S(1)}, bf16[256,2048]{1,0:T(8,128)(2,1)}, u32[]{:S(2)}) copy-start(bf16[256,2048]{1,0:T(8,128)(2,1)} %cot_ref.1) | copy-start | bytes 3145732
  110.3 49.4 %copy-start.51 = (bf16[1024,512]{1,0:T(8,128)(2,1)}, bf16[1024,512]{1,0:T(8,128)(2,1)S(1)}, u32[]{:S(2)}) copy-start(bf16[1024,512]{1,0:T(8,128)(2,1)S(1)} %get-tuple-element.83.query_ref) | copy-start | bytes 3145732
  110.3 52.8 %copy-start.26 = (bf16[1024,512]{1,0:T(8,128)(2,1)}, bf16[1024,512]{1,0:T(8,128)(2,1)S(1)}, u32[]{:S(2)}) copy-start(bf16[1024,512]{1,0:T(8,128)(2,1)S(1)} %get-tuple-element.84.refs_0_.own_ref) | copy-start | bytes 3145732
  163.1 155.2 %all-gather.8.cloned.1.call-start = ((), (), s32[]{:S(2)}) async-start(), calls=%async_computation.7 | async-start | bytes 7864320 | tf_op jit(solution)/shard_map/all_gather | solution.py:777
  171.1 12.0 %copy-start.61 = (bf16[8,64,2048]{2,1,0:T(8,128)(2,1)S(1)}, bf16[8,64,2048]{2,1,0:T(8,128)(2,1)}, u32[]{:S(2)}) copy-start(bf16[8,64,2048]{2,1,0:T(8,128)(2,1)} %gather_fusion) | copy-start | bytes 6291460
  248.4 175.1 %reduce-scatter.6.cloned.1.call-start = ((), (), s32[]{:S(2)}) async-start(), calls=%async_computation.8 | async-start | bytes 7864320 | tf_op jit(solution)/shard_map/reduce_scatter | solution.py:781
  318.3 22.6 %copy-start.46 = (s32[8]{0:T(128)S(1)}, s32[8]{0:T(128)}, u32[]{:S(2)}) copy-start(s32[8]{0:T(128)} %copy-done.45) | copy-start | bytes 100
  353.1 143.4 %reduce-scatter.8.cloned.1.call-start = ((), (), s32[]{:S(2)}) async-start(), calls=%async_computation.9 | async-start | bytes 7864320 | tf_op jit(solution)/shard_map/reduce_scatter | solution.py:781
  353.6 11.9 %copy-start.60 = (bf16[1024,1536]{1,0:T(8,128)(2,1)S(1)}, bf16[1024,1536]{1,0:T(8,128)(2,1)}, u32[]{:S(2)}) copy-start(bf16[1024,1536]{1,0:T(8,128)(2,1)} %get-tuple-element.105.refs_3_) | copy-start | bytes 9437188
  365.4 12.8 %copy-start.10 = (bf16[1024,1536]{1,0:T(8,128)(2,1)S(1)}, bf16[1024,1536]{1,0:T(8,128)(2,1)}, u32[]{:S(2)}) copy-start(bf16[1024,1536]{1,0:T(8,128)(2,1)} %get-tuple-element.104.refs_2_) | copy-start | bytes 9437188
  410.7 182.2 %reduce-scatter.10.cloned.1.call-start = ((), (), s32[]{:S(2)}) async-start(), calls=%async_computation.10 | async-start | bytes 7864320 | tf_op jit(solution)/shard_map/reduce_scatter | solution.py:781
  411.3 264.4 %reduce-scatter.12.cloned.1.call-start = ((), (), s32[]{:S(2)}) async-start(), calls=%async_computation.11 | async-start | bytes 2621440 | tf_op jit(solution)/shard_map/reduce_scatter | solution.py:781
  496.6 179.1 %reduce-scatter.14.cloned.1.call-start = ((), (), s32[]{:S(2)}) async-start(), calls=%async_computation.12 | async-start | bytes 5242880 | tf_op jit(solution)/shard_map/reduce_scatter | solution.py:781
  498.1 29.8 %collective-permute-start.4 = (bf16[256,1536]{1,0:T(8,128)(2,1)S(1)}, bf16[256,1536]{1,0:T(8,128)(2,1)S(1)}, u32[]{:S(2)}, u32[]{:S(2)}) collective-permute-start(bf16[256,1536]{1,0:T(8,128)(2,1)S(1)} %get-tuple-element.159), channel_id=1, source_target_pairs={{0,4},{1,5},{2,0},{3,1},{4,6},{5,7},{6,2},{7,3},{8,12},{9,13},{10,... | collective-permute-start | bytes 2359304 | tf_op jit(solution)/shard_map/ppermute | solution.py:423
  498.2 29.7 %collective-permute-start.3 = (bf16[256,1536]{1,0:T(8,128)(2,1)S(1)}, bf16[256,1536]{1,0:T(8,128)(2,1)S(1)}, u32[]{:S(2)}, u32[]{:S(2)}) collective-permute-start(bf16[256,1536]{1,0:T(8,128)(2,1)S(1)} %get-tuple-element.160), channel_id=1, source_target_pairs={{0,0},{1,1},{2,4},{3,5},{4,2},{5,3},{6,6},{7,7},{8,8},{9,9},{10,12... | collective-permute-start | bytes 2359304 | tf_op jit(solution)/shard_map/ppermute | solution.py:423
  520.0 72.8 %copy-start.47 = (s32[2]{0:T(128)S(1)}, s32[2]{0:T(128)}, u32[]{:S(2)}) copy-start(s32[2]{0:T(128)} %pad_add_fusion.2.place_ref) | copy-start | bytes 28
  601.3 5.2 copy-start.78
  606.5 6.4 copy-start.48
  615.4 10.2 %copy-start.22 = (bf16[2,256,1536]{2,1,0:T(8,128)(2,1)S(1)}, bf16[2,256,1536]{2,1,0:T(8,128)(2,1)}, u32[]{:S(2)}) copy-start(bf16[2,256,1536]{2,1,0:T(8,128)(2,1)} %reduce-scatter.10.cloned.1.call-done.refs_1_) | copy-start | bytes 4718596
  625.6 44.1 %copy-start.69 = (bf16[256,1536]{1,0:T(8,128)(2,1)S(1)}, bf16[256,1536]{1,0:T(8,128)(2,1)}, u32[]{:S(2)}) copy-start(bf16[256,1536]{1,0:T(8,128)(2,1)} %copy-done.68) | copy-start | bytes 2359300
  625.6 44.1 %copy-start.71 = (bf16[256,1536]{1,0:T(8,128)(2,1)S(1)}, bf16[256,1536]{1,0:T(8,128)(2,1)}, u32[]{:S(2)}) copy-start(bf16[256,1536]{1,0:T(8,128)(2,1)} %copy-done.70) | copy-start | bytes 2359300
  685.4 65.4 %copy-start.75 = (f32[4352]{0:T(1024)S(1)}, f32[4352]{0:T(1024)}, u32[]{:S(2)}) copy-start(f32[4352]{0:T(1024)} %param.36) | copy-start | bytes 52228
  685.4 65.4 %copy-start.76 = (f32[4352]{0:T(1024)S(1)}, f32[4352]{0:T(1024)}, u32[]{:S(2)}) copy-start(f32[4352]{0:T(1024)} %param.37) | copy-start | bytes 52228
  685.4 66.8 %copy-start.6 = (bf16[2,192,2048]{2,1,0:T(8,128)(2,1)S(1)}, bf16[2,192,2048]{2,1,0:T(8,128)(2,1)}, u32[]{:S(2)}) copy-start(bf16[2,192,2048]{2,1,0:T(8,128)(2,1)} %copy-done.5) | copy-start | bytes 4718596
  687.9 41.0 %collective-permute-start.5 = (bf16[256,1024]{1,0:T(8,128)(2,1)S(1)}, bf16[256,1024]{1,0:T(8,128)(2,1)S(1)}, u32[]{:S(2)}, u32[]{:S(2)}) collective-permute-start(bf16[256,1024]{1,0:T(8,128)(2,1)S(1)} %get-tuple-element.163), channel_id=1, source_target_pairs={{0,0},{1,1},{2,4},{3,5},{4,2},{5,3},{6,6},{7,7},{8,8},{9,9},{10,12... | collective-permute-start | bytes 1572872 | tf_op jit(solution)/shard_map/ppermute | solution.py:423
  688.6 40.3 %collective-permute-start.6 = (bf16[256,1024]{1,0:T(8,128)(2,1)S(1)}, bf16[256,1024]{1,0:T(8,128)(2,1)S(1)}, u32[]{:S(2)}, u32[]{:S(2)}) collective-permute-start(bf16[256,1024]{1,0:T(8,128)(2,1)S(1)} %get-tuple-element.164), channel_id=1, source_target_pairs={{0,4},{1,5},{2,0},{3,1},{4,6},{5,7},{6,2},{7,3},{8,12},{9,13},{10,... | collective-permute-start | bytes 1572872 | tf_op jit(solution)/shard_map/ppermute | solution.py:423
  691.2 4.1 collective-permute-start.7
  691.8 36.3 %collective-permute-start.8 = (bf16[64,2048]{1,0:T(8,128)(2,1)S(1)}, bf16[64,2048]{1,0:T(8,128)(2,1)S(1)}, u32[]{:S(2)}, u32[]{:S(2)}) collective-permute-start(bf16[64,2048]{1,0:T(8,128)(2,1)S(1)} %get-tuple-element.166), channel_id=1, source_target_pairs={{0,4},{1,5},{2,0},{3,1},{4,6},{5,7},{6,2},{7,3},{8,12},{9,13},{10,... | collective-permute-start | bytes 786440 | tf_op jit(solution)/shard_map/ppermute | solution.py:423
  728.1 29.6 %copy-start.65 = (bf16[64,2048]{1,0:T(8,128)(2,1)}, bf16[64,2048]{1,0:T(8,128)(2,1)S(1)}, u32[]{:S(2)}) copy-start(bf16[64,2048]{1,0:T(8,128)(2,1)S(1)} %collective-permute-done.8) | copy-start | bytes 786436
  728.9 28.9 %copy-start.63 = (bf16[256,1024]{1,0:T(8,128)(2,1)}, bf16[256,1024]{1,0:T(8,128)(2,1)S(1)}, u32[]{:S(2)}) copy-start(bf16[256,1024]{1,0:T(8,128)(2,1)S(1)} %collective-permute-done.6) | copy-start | bytes 1572868
  752.1 5.6 copy-start.54
  752.1 5.6 copy-start.56
  752.1 5.6 copy-start.57
  752.1 6.9 copy-start.59
  759.0 6.2 copy-start.62
  759.0 6.2 copy-start.72
  759.0 6.2 copy-start.73
  (49 other events, 75.0 us)
Sparse Core Ops, SparseCore 0:
  77.5 83.2 all-gather.5
  163.2 82.0 all-gather.3
  248.5 69.7 all-gather.7
  353.2 70.2 reduce-scatter.5
  426.3 70.1 reduce-scatter.7
  499.4 70.2 reduce-scatter.9
  572.6 35.1 reduce-scatter.11
  613.1 50.7 reduce-scatter.13

commit v4 on v3

--- a/solution.py
+++ b/solution.py
@@ -710,7 +710,7 @@
         return [first, None, None, last]
 
 
-def transfer(name, number, micros, *tasks):
+def transfer(name, number, micros, *tasks, scoped=12):
     outs = [task.outs() for task in tasks]
     scratch = [task.scratch() for task in tasks]
 
@@ -750,7 +750,7 @@
         out_specs=[pl.BlockSpec(memory_space=pl.ANY) for out in outs for _ in out],
         scratch_shapes=[one for part in scratch for one in part],
         compiler_params=pltpu.CompilerParams(
-            collective_id=number, has_side_effects=True, vmem_limit_bytes=48 * 2**20
+            collective_id=number, has_side_effects=True, vmem_limit_bytes=scoped * 2**20
         ),
         cost_estimate=pl.CostEstimate(
             flops=0, bytes_accessed=micros * 3_300_000, transcendentals=0
@@ -791,35 +791,42 @@
     return both(received) + partial[0].astype(jnp.float32)
 
 
-def sum_all_kernel(value, total, held, arrived, send_sem, recv_sem):
+def sum_all_kernel(value, total, by_mp, by_dp, send_sem, recv_sem):
     dp, mp = lax.axis_index("dp"), lax.axis_index("mp")
-    partners = [
-        (dp + 1 - 2 * (dp % 2), mp),
-        (dp + 2 - 4 * ((dp // 2) % 2), mp),
-        (dp + 4 - 8 * (dp // 4), mp),
-        (dp, mp + 1 - 2 * (mp % 2)),
-        (dp, mp + 2 - 4 * (mp // 2)),
-    ]
+    over_mp = [(dp, (mp + step) % 4) for step in range(1, 4)]
+    over_dp = [((dp + step) % 8, mp) for step in range(1, 8)]
     barrier = pltpu.get_barrier_semaphore()
-    for partner in partners:
+    for partner in over_mp + over_dp:
         pl.semaphore_signal(
             barrier, inc=1, device_id=partner, device_id_type=pl.DeviceIdType.MESH
         )
-    pl.semaphore_wait(barrier, len(partners))
-    held[0] = value[...]
-    for step, partner in enumerate(partners):
-        copy = pltpu.make_async_remote_copy(
-            src_ref=held.at[step],
-            dst_ref=arrived.at[step],
-            send_sem=send_sem.at[step],
-            recv_sem=recv_sem.at[step],
-            device_id=partner,
-            device_id_type=pl.DeviceIdType.MESH,
-        )
-        copy.start()
-        copy.wait()
-        held[step + 1] = held[step] + arrived[step]
-    total[...] = held[len(partners)]
+    pl.semaphore_wait(barrier, len(over_mp) + len(over_dp))
+
+    def share(table, place, partners, first):
+        copies = [
+            pltpu.make_async_remote_copy(
+                src_ref=table.at[place],
+                dst_ref=table.at[place],
+                send_sem=send_sem.at[first + step],
+                recv_sem=recv_sem.at[first + step],
+                device_id=partner,
+                device_id_type=pl.DeviceIdType.MESH,
+            )
+            for step, partner in enumerate(partners)
+        ]
+        for copy in copies:
+            copy.start()
+        for copy in copies:
+            copy.wait()
+
+    by_mp[mp] = value[...]
+    share(by_mp, mp, over_mp, 0)
+    by_dp[dp] = (by_mp[0] + by_mp[1]) + (by_mp[2] + by_mp[3])
+    share(by_dp, dp, over_dp, 3)
+    result = by_dp[0]
+    for place in range(1, 8):
+        result = result + by_dp[place]
+    total[...] = result
 
 
 def sum_all(vector):
@@ -832,10 +839,10 @@
         in_specs=[pl.BlockSpec(memory_space=pltpu.VMEM)],
         out_specs=pl.BlockSpec(memory_space=pltpu.VMEM),
         scratch_shapes=[
-            pltpu.VMEM((6, rows, 128), jnp.float32),
-            pltpu.VMEM((5, rows, 128), jnp.float32),
-            pltpu.SemaphoreType.DMA((5,)),
-            pltpu.SemaphoreType.DMA((5,)),
+            pltpu.VMEM((4, rows, 128), jnp.float32),
+            pltpu.VMEM((8, rows, 128), jnp.float32),
+            pltpu.SemaphoreType.DMA((10,)),
+            pltpu.SemaphoreType.DMA((10,)),
         ],
         compiler_params=pltpu.CompilerParams(collective_id=0, has_side_effects=True),
         name="sum_all",
@@ -962,7 +969,7 @@
             jax.ShapeDtypeStruct((8, HEAD_SIZE), jnp.float32),
         ],
         compiler_params=pltpu.CompilerParams(vmem_limit_bytes=32 * 2**20),
-        cost_estimate=pl.CostEstimate(flops=0, bytes_accessed=16 * 2**20, transcendentals=0),
+        cost_estimate=pl.CostEstimate(flops=0, bytes_accessed=2 * 2**20, transcendentals=0),
         name="unproject",
     )(place, d_queries, d_own, above, raw, cosine, sine, head_gains)
 
@@ -1166,7 +1173,7 @@
     out_ref[...] = value + d_ref[...]
 
 
-def by_row_tiles(kernel, name, slot_of, inputs, outs, scratch=False):
+def by_row_tiles(kernel, name, slot_of, inputs, outs, scratch=False, micros=3):
     rows, width = 64, inputs[0].shape[1]
     steps = inputs[0].shape[0] // rows
 
@@ -1187,14 +1194,48 @@
             scratch_shapes=[pltpu.VMEM((rows, width), jnp.float32)] if scratch else [],
         ),
         out_shape=outs,
-        compiler_params=pltpu.CompilerParams(vmem_limit_bytes=24 * 2**20),
-        cost_estimate=pl.CostEstimate(flops=0, bytes_accessed=8 * 2**20, transcendentals=0),
+        compiler_params=pltpu.CompilerParams(vmem_limit_bytes=(60 if scratch else 24) * 2**20),
+        cost_estimate=pl.CostEstimate(flops=0, bytes_accessed=micros * 3_300_000, transcendentals=0),
         name=name,
     )(slot_of, *inputs)
 
 
+def mlp_front_kernel(rows_ref, gate_ref, up_ref, gate_out, up_out, act_out):
+    width = rows_ref.shape[1]
+    rows = rows_ref[...]
+    gate = jnp.dot(rows, gate_ref[...].reshape(width, -1), preferred_element_type=jnp.float32)
+    upper = jnp.dot(rows, up_ref[...].reshape(width, -1), preferred_element_type=jnp.float32)
+    gate_out[...] = gate
+    up_out[...] = upper
+    act_out[...] = (gate * upper / (1.0 + jnp.exp(-gate))).astype(jnp.bfloat16)
+
+
+def mlp_front(rows, gate_blocks, up_blocks):
+    count, width = rows.shape
+    units = gate_blocks.shape[2]
+    columns = 256
+    weight = pl.BlockSpec((8, width // 8, columns), lambda i: (0, 0, i))
+    out = pl.BlockSpec((count, columns), lambda i: (0, i))
+    return pl.pallas_call(
+        mlp_front_kernel,
+        grid=(units // columns,),
+        in_specs=[pl.BlockSpec((count, width), lambda i: (0, 0)), weight, weight],
+        out_specs=[out, out, out],
+        out_shape=[
+            jax.ShapeDtypeStruct((count, units), jnp.float32),
+            jax.ShapeDtypeStruct((count, units), jnp.float32),
+            jax.ShapeDtypeStruct((count, units), jnp.bfloat16),
+        ],
+        compiler_params=pltpu.CompilerParams(vmem_limit_bytes=32 * 2**20),
+        cost_estimate=pl.CostEstimate(
+            flops=4 * count * units * width, bytes_accessed=32 * 2**20, transcendentals=0
+        ),
+        name="mlp_front",
+    )(rows, gate_blocks, up_blocks)
+
+
 def mlp_back_kernel(
-    slot_ref, dy_ref, gate_ref, up_ref, down_ref, act_ref, dgate_ref, dup_ref, branch_ref, weight_ref
+    slot_ref, dy_ref, gate_ref, up_ref, act_ref, down_ref, dgate_ref, dup_ref, branch_ref, weight_ref
 ):
     block = down_ref.shape[1]
 
@@ -1212,18 +1253,15 @@
         gate, upper = gate_ref[:, columns], up_ref[:, columns]
         d_act = dot_t(dy, weight)
         sigma = 1.0 / (1.0 + jnp.exp(-gate))
-        silu = gate * sigma
-        act = (silu * upper).astype(jnp.bfloat16)
-        act_ref[:, columns] = act
-        dup_ref[:, columns] = (d_act * silu).astype(jnp.bfloat16)
+        dup_ref[:, columns] = (d_act * gate * sigma).astype(jnp.bfloat16)
         d_gate = d_act * upper * sigma * (1.0 + gate * (1.0 - sigma))
         dgate_ref[:, columns] = d_gate.astype(jnp.bfloat16)
-        term = jnp.dot(act, weight, preferred_element_type=jnp.float32)
+        term = jnp.dot(act_ref[:, columns], weight, preferred_element_type=jnp.float32)
         total = term if total is None else total + term
     branch_ref[0] = total.astype(jnp.bfloat16)
 
 
-def mlp_back(slot_of, d_branch, gate, upper, down_blocks):
+def mlp_back(slot_of, d_branch, gate, upper, act, down_blocks):
     count, units = gate.shape
     width = d_branch.shape[1]
     rows = 256
@@ -1238,24 +1276,107 @@
                 by_rows(width),
                 by_rows(units),
                 by_rows(units),
+                by_rows(units),
                 pl.BlockSpec(down_blocks.shape, lambda i, p: (0, 0, 0)),
             ],
-            out_specs=[by_rows(units)] * 3
+            out_specs=[by_rows(units)] * 2
             + [pl.BlockSpec((1, rows, width), lambda i, p: (i, 0, 0))],
             scratch_shapes=[pltpu.VMEM((units, width), jnp.bfloat16)],
         ),
         out_shape=[
             wide,
             wide,
-            wide,
             jax.ShapeDtypeStruct((count // rows, rows, width), jnp.bfloat16),
         ],
-        compiler_params=pltpu.CompilerParams(vmem_limit_bytes=56 * 2**20),
+        compiler_params=pltpu.CompilerParams(vmem_limit_bytes=48 * 2**20),
         cost_estimate=pl.CostEstimate(
             flops=4 * count * units * width, bytes_accessed=32 * 2**20, transcendentals=0
         ),
         name="mlp_back",
-    )(slot_of, d_branch, gate, upper, down_blocks)
+    )(slot_of, d_branch, gate, upper, act, down_blocks)
+
+
+def rows_back_kernel(*refs):
+    *pairs, out_ref = refs
+    total = None
+    for grad_ref, weight_ref in zip(pairs[::2], pairs[1::2]):
+        term = dot_t(grad_ref[...], weight_ref[0])
+        total = term if total is None else total + term
+    out_ref[...] = total.astype(jnp.bfloat16).reshape(out_ref.shape)
+
+
+def rows_back(name, *pairs):
+    count = pairs[0].shape[0]
+    block = pairs[1].shape[1]
+    specs = []
+    for grad, weight in zip(pairs[::2], pairs[1::2]):
+        specs.append(pl.BlockSpec(grad.shape, lambda i: (0, 0)))
+        specs.append(pl.BlockSpec((1, *weight.shape[1:]), lambda i: (i, 0, 0)))
+    return pl.pallas_call(
+        rows_back_kernel,
+        grid=(8,),
+        in_specs=specs,
+        out_specs=pl.BlockSpec((4, count // 4, block), lambda i: (0, 0, i)),
+        out_shape=jax.ShapeDtypeStruct((4, count // 4, 8 * block), jnp.bfloat16),
+        compiler_params=pltpu.CompilerParams(vmem_limit_bytes=28 * 2**20),
+        cost_estimate=pl.CostEstimate(
+            flops=sum(count * w.size for w in pairs[1::2]) // 4,
+            bytes_accessed=2 * 2**20,
+            transcendentals=0,
+        ),
+        name=name,
+    )(*pairs)
+
+
+def adam_kernel(factor_ref, *refs, rates):
+    factor = factor_ref[0]
+    ins, outs = refs[: len(refs) - 3 * len(rates)], refs[len(refs) - 3 * len(rates) :]
+    at = 0
+    for place, (rate, pieces) in enumerate(rates):
+        weight_ref, first_ref, second_ref, *grads = ins[at : at + 3 + pieces]
+        at += 3 + pieces
+        start = 0
+        for grad_ref in grads:
+            columns = slice(start, start + grad_ref.shape[1])
+            start += grad_ref.shape[1]
+            results = adam(
+                weight_ref[:, columns],
+                first_ref[:, columns],
+                second_ref[:, columns],
+                grad_ref[...],
+                factor,
+                rate,
+                WEIGHT_DECAY,
+            )
+            for out_ref, result in zip(outs[3 * place : 3 * place + 3], results):
+                out_ref[:, columns] = result
+
+
+def adam_all(factor, weights):
+    steps = 8
+    rates = tuple((rate, len(grads)) for rate, *_, grads in weights)
+    arrays, outs = [], []
+    for _, master, first, second, grads in weights:
+        arrays += [master, first, second, *grads]
+        outs += [jax.ShapeDtypeStruct(master.shape, jnp.float32)] * 3
+
+    def spec(leaf):
+        return pl.BlockSpec((leaf.shape[0] // steps, leaf.shape[1]), lambda i, p: (i, 0))
+
+    results = pl.pallas_call(
+        lambda *refs: adam_kernel(*refs, rates=rates),
+        grid_spec=pltpu.PrefetchScalarGridSpec(
+            num_scalar_prefetch=1,
+            grid=(steps,),
+            in_specs=[spec(leaf) for leaf in arrays],
+            out_specs=[spec(leaf) for leaf in outs],
+        ),
+        out_shape=outs,
+        compiler_params=pltpu.CompilerParams(vmem_limit_bytes=60 * 2**20),
+        cost_estimate=pl.CostEstimate(flops=0, bytes_accessed=48 * 2**20, transcendentals=0),
+        name="adam_all",
+    )(factor[None], *arrays)
+    return [results[n : n + 3] for n in range(0, len(results), 3)]
 
 
 def slot_grad_kernel(slot_ref, left_ref, right_ref, out_ref):
@@ -1290,12 +1411,10 @@
 
 
 class Grads(Task):
-    copies = 1
-
     def outs(self):
         rows, left, right = self.inputs
-        block = rows.shape[1] // 8
-        return [jax.ShapeDtypeStruct((8, block, one.shape[1]), jnp.bfloat16) for one in (left, right)]
+        columns = left.shape[1] + right.shape[1]
+        return [jax.ShapeDtypeStruct((8, rows.shape[1] // 8, columns), jnp.bfloat16)]
 
     def scratch(self):
         return []
@@ -1303,17 +1422,15 @@
     def steps(self, place, ins, outs, scratch):
         count, width = self.inputs[0].shape
         block = width // 8
-
-        def body(rows_ref, left_ref, right_ref, left_out, right_out):
+        columns = self.inputs[1].shape[1]
+
+        def body(rows_ref, left_ref, right_ref, out_ref):
             rows = rows_ref[...]
-            left_out[0] = t_dot(rows, left_ref[...]).astype(jnp.bfloat16)
-            right_out[0] = t_dot(rows, right_ref[...]).astype(jnp.bfloat16)
+            out_ref[0, :, :columns] = t_dot(rows, left_ref[...]).astype(jnp.bfloat16)
+            out_ref[0, :, columns:] = t_dot(rows, right_ref[...]).astype(jnp.bfloat16)
 
         def whole(one):
             return pl.BlockSpec((count, one.shape[1]), lambda i: (0, 0))
-
-        def out(one):
-            return pl.BlockSpec((1, block, one.shape[1]), lambda i: (i, 0, 0))
 
         run = pltpu.emit_pipeline(
             body,
@@ -1323,7 +1440,7 @@
                 whole(self.inputs[1]),
                 whole(self.inputs[2]),
             ],
-            out_specs=[out(self.inputs[1]), out(self.inputs[2])],
+            out_specs=[pl.BlockSpec((1, block, 2 * columns), lambda i: (i, 0, 0))],
         )
         return [lambda: None, None, lambda: run(*ins, *outs), None]
 
@@ -1384,7 +1501,6 @@
         Near(low_gateup[:, :units], phase=1),
     )
     full_in = full_in.reshape(count, width)
-    w_qkv = qkv_blocks.reshape(width, -1)
     w_out = jnp.take(out_blocks, slot_of, axis=0, mode="clip").reshape(-1, width)
     gate_blocks = over_plane(near_gate)
     near_up = to_group(after(low_gateup[:, units:], full_in))
@@ -1438,24 +1554,16 @@
     )
     ((full_mid,),) = transfer("gather_mid", 4, 34, Rows(own_mid))
     full_mid = full_mid.reshape(count, width)
-    w_gate = gate_blocks.reshape(width, units)
-    gate = jnp.dot(full_mid, w_gate, preferred_element_type=jnp.float32)
-    up_blocks, gate = lax.optimization_barrier((up_blocks, gate))
-    w_up = up_blocks.reshape(width, units)
-    upper = jnp.dot(full_mid, w_up, preferred_element_type=jnp.float32)
-    down_blocks, upper = lax.optimization_barrier((down_blocks, upper))
-    act, d_gate, d_upper, branch = mlp_back(slot_of, d_branch, gate, upper, down_blocks)
+    gate, upper, act = mlp_front(full_mid, gate_blocks, up_blocks)
     g_down = slot_grad(slot_of, act, d_branch)
-    d_gate, d_upper, g_down = lax.optimization_barrier((d_gate, d_upper, g_down))
+    down_blocks, g_down = lax.optimization_barrier((down_blocks, g_down))
     near_g_down = to_plane(g_down)
-    partial = blocks(
-        jnp.einsum("tc,dc->td", d_gate, w_gate, preferred_element_type=jnp.float32)
-        + jnp.einsum("tc,dc->td", d_upper, w_up, preferred_element_type=jnp.float32)
-    )
-    received, (g_gate, g_up) = transfer(
-        "sum_mid", 5, 33, Sums(partial), Grads(full_mid, d_gate, d_upper)
-    )
-    near_g_gate, near_g_up = to_plane(g_gate), to_plane(g_up)
+    d_gate, d_upper, branch = mlp_back(slot_of, d_branch, gate, upper, act, down_blocks)
+    partial = rows_back("mid_rows", d_gate, gate_blocks, d_upper, up_blocks)
+    received, (g_gateup,) = transfer(
+        "sum_mid", 5, 33, Sums(partial), Grads(full_mid, d_gate, d_upper), scoped=40
+    )
+    near_g_gateup = to_plane(g_gateup)
     d_mixed, low_d_mixed, mid_gain = by_row_tiles(
         mix_back_kernel,
         "mix_back",
@@ -1465,18 +1573,13 @@
         scratch=True,
     )
     g_ln_mid = jnp.sum(mid_gain, axis=0)
-    (d_attn,), (owned_down,) = transfer(
-        "gather_attention", 6, 40, Rows(low_d_mixed), Owners(near_g_down)
-    )
+    ((d_attn,),) = transfer("gather_attention", 6, 29, Rows(low_d_mixed))
     d_attn = d_attn.reshape(count, width)
-    red_down = both(owned_down)
+    owned_down = to_owner(after(near_g_down, d_attn))
     g_out = slot_grad(slot_of, attn_heads, d_attn)
     d_heads = jnp.einsum("td,hd->th", d_attn, w_out, preferred_element_type=jnp.float32).astype(
         jnp.bfloat16
     )
-    d_heads, near_g_gate, g_out = lax.optimization_barrier((d_heads, near_g_gate, g_out))
-    near_g_out = to_plane(g_out)
-    owned_gate = to_owner(near_g_gate)
     d_queries, d_low, d_own = attention_call(
         attend_back_kernel,
         "attend_back",
@@ -1489,24 +1592,26 @@
         ],
         5 * score_flops,
     )
-    d_low, *owned_gate = lax.optimization_barrier((d_low, *owned_gate))
-    red_gate = both(owned_gate)
+    d_low, g_out, *owned_down = lax.optimization_barrier((d_low, g_out, *owned_down))
+    red_down = both(owned_down)
+    near_g_out = to_plane(g_out)
     (from_above,), received = transfer("keys_down", 7, 53, Halves(d_low, 1), Sums(branch))
     result_rows = mixed + summed(branch, received)
-    near_g_up, from_above = lax.optimization_barrier((near_g_up, from_above))
     d_projected, g_q, g_k = unproject(
         place, d_queries, d_own, from_above, raw, cosine, sine, head_gains
     )
     g_q, g_k = jnp.sum(g_q, axis=0), jnp.sum(g_k, axis=0)
     g_qkv = jnp.einsum("td,tc->dc", full_in, d_projected, preferred_element_type=jnp.float32)
     near_g_qkv = to_plane(g_qkv.astype(jnp.bfloat16).reshape(8, width // 8, -1))
-    partial = blocks(
-        jnp.einsum("tc,dc->td", d_projected, w_qkv, preferred_element_type=jnp.float32)
-    )
-    received, (owned_up,) = transfer("sum_in", 8, 40, Sums(partial), Owners(near_g_up))
-    red_gateup = jnp.concatenate([red_gate, both(owned_up)], axis=1)
-    near_g_out, near_g_qkv, *received = lax.optimization_barrier((near_g_out, near_g_qkv, *received))
-    red_out, red_qkv = both(to_owner(near_g_out)), both(to_owner(near_g_qkv))
+    partial = rows_back("in_rows", d_projected, qkv_blocks)
+    received, (owned_gateup,) = transfer("sum_in", 8, 74, Sums(partial), Owners(near_g_gateup))
+    near_g_out, near_g_qkv, *received = lax.optimization_barrier(
+        (near_g_out, near_g_qkv, *received)
+    )
+    owned_out = to_owner(near_g_out)
+    received, owned_out = lax.optimization_barrier((received, owned_out))
+    red_gateup = both(owned_gateup)
+    red_out, red_qkv = both(owned_out), both(to_owner(near_g_qkv))
     input_grad, in_gain = by_row_tiles(
         in_back_kernel,
         "in_back",
@@ -1514,32 +1619,34 @@
         [hidden_in, partial, *received, ln_in[None], d_mixed],
         [row, gain_row],
         scratch=True,
+        micros=40,
     )
     g_ln_in = jnp.sum(in_gain, axis=0)
     gain_terms = jnp.concatenate([g_ln_in, g_ln_mid, g_q, g_k])
-    squares = jnp.sum(red_qkv * red_qkv) + jnp.sum(red_gateup * red_gateup)
-    squares = squares + jnp.sum(red_out * red_out) + jnp.sum(red_down * red_down)
+    squares = sum(jnp.sum(red * red) for red in (red_qkv, red_gateup, red_out, red_down))
     totals_here = sum_all(jnp.concatenate([gain_terms, squares[None]]))
     gain_grad, total_squares = totals_here[:-1], totals_here[-1]
     grad_norm = jnp.sqrt(total_squares + jnp.sum(gain_grad * gain_grad))
     factor = jnp.minimum(1.0, CLIP_LIMIT / (grad_norm + 1e-06))
-    qkv_new, qkv_first_new, qkv_second_new = adam(
-        projection_master_weight,
-        projection_first_moment,
-        projection_second_moment,
-        red_qkv,
+    (
+        (qkv_new, qkv_first_new, qkv_second_new),
+        (gateup_new, gateup_first_new, gateup_second_new),
+        (out_new, out_first_new, out_second_new),
+        (down_new, down_first_new, down_second_new),
+    ) = adam_all(
         factor,
-        LEARN,
-        WEIGHT_DECAY,
-    )
-    gateup_new, gateup_first_new, gateup_second_new = adam(
-        gateup_weight, gateup_first, gateup_second, red_gateup, factor, LEARN, WEIGHT_DECAY
-    )
-    out_new, out_first_new, out_second_new = adam(
-        out_weight, out_first, out_second, red_out, factor, out_rate, WEIGHT_DECAY
-    )
-    down_new, down_first_new, down_second_new = adam(
-        down_weight, down_first, down_second, red_down, factor, LEARN, WEIGHT_DECAY
+        [
+            (
+                LEARN,
+                projection_master_weight,
+                projection_first_moment,
+                projection_second_moment,
+                [red_qkv],
+            ),
+            (LEARN, gateup_weight, gateup_first, gateup_second, [red_gateup]),
+            (out_rate, out_weight, out_first, out_second, [red_out]),
+            (LEARN, down_weight, down_first, down_second, [red_down]),
+        ],
     )
     gains_new, gain_first_new, gain_second_new = adam(
         gains, gain_first, gain_second, gain_grad, factor, GAIN_LEARN, 0.0

time: 785 us -> 748 us (0.953)
  matrix products: 76.8 us -> 15.4 us
  Pallas kernels: 487 us -> 547 us
  waiting for transfers between devices: 61.3 us -> 14.5 us
  local copies, waits for them, and re-layouts: 64.9 us -> 76 us
  other arithmetic: 39.6 us -> 31.1 us
    dot_general x5 -> x0, matrix products: 58.4 us -> none  [the longest x1 12.8 us: shards_paired(): jnp.einsum('tc,dc->td', d_upper, w_up, preferred_element_type=jnp.float32)]
    pallas_call x0 -> x4, Pallas kernels: none -> 55.7 us  [the longest x2 21.4 us: rows_back(): pl.pallas_call(rows_back_kernel, grid=(8,), in_specs=specs, out_specs=pl....]
    ppermute x9, waiting for transfers between devices: 41.8 us -> 14.3 us  [move(): return lax.ppermute(value, ('dp', 'mp'), pairs)]
    sub x5 -> x1, other arithmetic: 17.9 us -> 1.36 us  [adam(): weight * (1.0 - rate * decay)]
    add x2 -> x4, other arithmetic: 0.43 us -> 11.3 us  [both(): return pair[0].astype(jnp.float32) + pair[1].astype(jnp.float32)]
    all_gather x3, waiting for transfers between devices: 9.5 us -> 0.01 us  [over_plane(): lax.all_gather(near, ('dp', 'mp'), axis=0, tiled=True, axis_index_groups=...]
    reduce_scatter x5 -> x4, waiting for transfers between devices: 9.36 us -> 0.01 us  [to_plane(): lax.psum_scatter(grads, ('dp', 'mp'), scatter_dimension=0, tiled=True, ax...]
    unnamed x167 -> x139, local copies, waits for them, and re-layouts: 52.8 us -> 61.7 us
  transfers between devices with their start and end apart: 17 -> 16, of which waited for: 6 -> 2; matrix products, arithmetic and copies ran while one was open for 13% -> 6% of each run, Pallas kernels for 48% -> 61%
where the time goes in v4:
time: 748 us; the launch traced here: 741 us
  Pallas kernels  547 us (73%)
  local copies, waits for them, and re-layouts  76 us (10%)
  starting transfers between devices  36.1 us (5%)
  other arithmetic  31.1 us (4%)
  between operations  20.1 us (3%)
  matrix products  15.4 us (2%)
  waiting for transfers between devices  14.5 us (2%)
    pallas_call x8, Pallas kernels, transfer(): pl.pallas_call(kernel, out_shape=[leaf for out in outs for leaf in out],...  378 us
    unnamed x139, local copies, waits for them, and re-layouts  61.7 us
    ppermute x9, starting transfers between devices, move(): return lax.ppermute(value, ('dp', 'mp'), pairs)  35.3 us
    pallas_call x2, Pallas kernels, attention_call(): pl.pallas_call(kernel, grid_spec=pltpu.PrefetchScalarGridSpec(num_scalar_...  33 us
    pallas_call x1, Pallas kernels, mlp_back(): pl.pallas_call(mlp_back_kernel, grid_spec=pltpu.PrefetchScalarGridSpec(nu...  22.6 us
    pallas_call x2, Pallas kernels, rows_back(): pl.pallas_call(rows_back_kernel, grid=(8,), in_specs=specs, out_specs=pl....  21.4 us
    pallas_call x1, Pallas kernels, adam_all(): pl.pallas_call(lambda *refs: adam_kernel(*refs, rates=rates), grid_spec=p...  17.4 us
    pallas_call x1, Pallas kernels, mlp_front(): pl.pallas_call(mlp_front_kernel, grid=(units // columns,), in_specs=[pl.B...  16.9 us
  transfers between devices with their start and end apart: 16, of which 2 were waited for; matrix products, arithmetic and copies ran while one was open for 6% of the time, Pallas kernels for 61%

profile of v4, /device:TPU:0, one launch (start us, length us, event | category | flops | bytes accessed | tf_op | source)
XLA Modules:
  0.0 740.7 jit_solution(17600053442441151362)
XLA Ops:
  10.4 2.1 convert_element_type.74
  15.3 61.3 %gather_first.1 = (bf16[8,256,1024]{2,1,0:T(8,128)(2,1)S(1)}, bf16[8,64,2048]{2,1,0:T(8,128)(2,1)S(1)}, bf16[4,256,2048]{2,1,0:T(8,128)(2,1)S(1)}, bf16[2,256,1536]{2,1,0:T(8,128)(2,1)S(1)}) custom-call(bf16[256,1024]{1,0:T(8,128)(2,1)S(1)} %convert_element_type.72.refs_0_, bf16[64,2048]{1,0:T(8,128)(2,1)S(1)} %convert_element_type.73.refs_1_, ...), custom_call_target="tpu_custom_call" | custom-call | bytes 247500000 | tf_op jit(solution)/shard_map/gather_first/pallas_call | solution.py:746
  83.2 12.3 %collective-permute-start.2 = (bf16[256,1536]{1,0:T(8,128)(2,1)}, bf16[256,1536]{1,0:T(8,128)(2,1)}, u32[]{:S(2)}, u32[]{:S(2)}) collective-permute-start(bf16[256,1536]{1,0:T(8,128)(2,1)} %get-tuple-element.93), channel_id=1, source_target_pairs={{4,0},{5,1},{0,2},{1,3},{6,4},{7,5},{2,6},{3,7},{12,8},{13,9},{8,1... | collective-permute-start | bytes 2359304 | tf_op jit(solution)/shard_map/ppermute | solution.py:423
  95.5 7.4 %collective-permute-start.1 = (bf16[256,1536]{1,0:T(8,128)(2,1)}, bf16[256,1536]{1,0:T(8,128)(2,1)}, u32[]{:S(2)}, u32[]{:S(2)}) collective-permute-start(bf16[256,1536]{1,0:T(8,128)(2,1)} %get-tuple-element.93), channel_id=1, source_target_pairs={{0,0},{1,1},{4,2},{5,3},{2,4},{3,5},{6,6},{7,7},{8,8},{9,9},{12,10... | collective-permute-start | bytes 2359304 | tf_op jit(solution)/shard_map/ppermute | solution.py:423
  106.6 9.2 %project.1 = (f32[1024,768]{1,0:T(8,128)}, bf16[1024,512]{1,0:T(8,128)(2,1)S(1)}, bf16[1024,512]{1,0:T(8,128)(2,1)S(1)}) custom-call(bf16[1024,2048]{1,0:T(8,128)(2,1)} %bitcast.74, bf16[8,256,1024]{2,1,0:T(8,128)(2,1)} %copy-done.14, f32[1024,128]{1,0:T(8,128)S(1)} %get-tuple-element.184.cos_ref, f32[1024,128]{1,0:T(8,128)S(1)} %get-tuple-element.185.sin_ref, ...), custom_call_target="tpu_custom_call" | custom-call | flops 4294967296 | bytes 16777216 | tf_op jit(solution)/shard_map/project/pallas_call | solution.py:884
  116.8 49.2 %keys_up.1 = (bf16[1024,512]{1,0:T(8,128)(2,1)S(1)}, bf16[4,256,2048]{2,1,0:T(8,128)(2,1)S(1)}) custom-call(bf16[1024,512]{1,0:T(8,128)(2,1)S(1)} %get-tuple-element.91.refs_0_.own_ref, bf16[256,2048]{1,0:T(8,128)(2,1)S(1)} %copy-done.16), custom_call_target="tpu_custom_call" | custom-call | bytes 155100000 | tf_op jit(solution)/shard_map/keys_up/pallas_call | solution.py:746
  169.0 2.7 pad_maximum_fusion
  173.5 3.6 gather_fusion
  179.8 12.0 %attend.1.left_ref = bf16[1024,512]{1,0:T(8,128)(2,1)} custom-call(s32[2]{0:T(128)} %pad_add_fusion.2.place_ref, s32[1024,1]{1,0:T(8,128)} %copy.45.time_ref, s32[1024,1]{1,0:T(8,128)} %bitcast.81, bf16[1024,512]{1,0:T(8,128)(2,1)} %copy-done.52, bf16[1024,512]{1,0:T(8,128)(2,1)} %copy-done.50, bf16[1024,512]{1,0:T(8,128)(2,1)} %copy-done.29), custom_call_target="tpu_custom_call" | custom-call | flops 2147483648 | bytes 16777216 | tf_op jit(solution)/shard_map/attend/pallas_call | solution.py:1089
  191.8 3.6 convolution_convert_fusion
  195.5 57.0 %sum_attention.1 = (bf16[256,2048]{1,0:T(8,128)(2,1)S(1)}, bf16[256,2048]{1,0:T(8,128)(2,1)S(1)}, bf16[2,192,2048]{2,1,0:T(8,128)(2,1)S(1)}) custom-call(bf16[4,256,2048]{2,1,0:T(8,128)(2,1)S(1)} %bitcast.64, bf16[192,2048]{1,0:T(8,128)(2,1)S(1)} %convert_element_type.77.refs_1_), custom_call_target="tpu_custom_call" | custom-call | bytes 165000000 | tf_op jit(solution)/shard_map/sum_attention/pallas_call | solution.py:746
  256.8 2.2 copy-done.6
  263.2 28.8 %gather_mid.1 = bf16[4,256,2048]{2,1,0:T(8,128)(2,1)S(1)} custom-call(bf16[256,2048]{1,0:T(8,128)(2,1)S(1)} %get-tuple-element.100.refs_0_), custom_call_target="tpu_custom_call" | custom-call | bytes 112200000 | tf_op jit(solution)/shard_map/gather_mid/pallas_call | solution.py:746
  294.0 2.2 copy-done.4
  296.2 16.9 %mlp_front.1 = (f32[1024,1536]{1,0:T(8,128)S(1)}, f32[1024,1536]{1,0:T(8,128)S(1)}, bf16[1024,1536]{1,0:T(8,128)(2,1)S(1)}) custom-call(bf16[1024,2048]{1,0:T(8,128)(2,1)S(1)} %bitcast.63, bf16[8,256,1536]{2,1,0:T(8,128)(2,1)} %all-gather.4.cloned.1.call-done.gate_ref.refs_1_, bf16[8,256,1536]{2,1,0:T(8,128)(2,1)} %all-gather.6.cloned.1.call-done.up_ref.refs_3_), custom_call_target="tpu_custom_call" | custom-call | flops 12884901888 | bytes 33554432 | tf_op jit(solution)/shard_map/mlp_front/pallas_call | solution.py:1219
  313.1 2.7 copy-done.54
  315.8 2.7 copy-done.55
  318.5 10.3 %slot_grad.2 = bf16[8,192,2048]{2,1,0:T(8,128)(2,1)} custom-call(s32[8]{0:T(128)S(1)} %broadcast_xor_fusion.slot_ref, bf16[1024,1536]{1,0:T(8,128)(2,1)S(1)} %get-tuple-element.105.left_ref.act_ref, bf16[1024,2048]{1,0:T(8,128)(2,1)} %bitcast.76), custom_call_target="tpu_custom_call" | custom-call | flops 6442450944 | bytes 16777216 | tf_op jit(solution)/shard_map/slot_grad/pallas_call | solution.py:1393
  330.8 22.6 %mlp_back.1 = (bf16[1024,1536]{1,0:T(8,128)(2,1)S(1)}, bf16[1024,1536]{1,0:T(8,128)(2,1)}, bf16[4,256,2048]{2,1,0:T(8,128)(2,1)}) custom-call(s32[8]{0:T(128)S(1)} %broadcast_xor_fusion.slot_ref, bf16[1024,2048]{1,0:T(8,128)(2,1)} %bitcast.77, f32[1024,1536]{1,0:T(8,128)} %copy-done.54, f32[1024,1536]{1,0:T(8,128)} %copy-done.55, ...), custom_call_target="tpu_custom_call" | custom-call | flops 12884901888 | bytes 33554432 | tf_op jit(solution)/shard_map/mlp_back/pallas_call | solution.py:1270
  355.5 2.9 copy-done.12
  358.4 15.0 %mid_rows.1.refs_0_.own_ref = bf16[4,256,2048]{2,1,0:T(8,128)(2,1)S(1)} custom-call(bf16[1024,1536]{1,0:T(8,128)(2,1)S(1)} %get-tuple-element.108.refs_0_.refs_2_, bf16[8,256,1536]{2,1,0:T(8,128)(2,1)S(1)} %bitcast.67, bf16[1024,1536]{1,0:T(8,128)(2,1)S(1)} %copy-done.7, bf16[8,256,1536]{2,1,0:T(8,128)(2,1)S(1)} %copy-done.12), custom_call_target="tpu_custom_call" | custom-call | flops 1610612736 | bytes 2097152 | tf_op jit(solution)/shard_map/mid_rows/pallas_call | solution.py:1315
  373.4 28.7 %sum_mid.1 = (bf16[256,2048]{1,0:T(8,128)(2,1)S(1)}, bf16[256,2048]{1,0:T(8,128)(2,1)S(1)}, bf16[8,256,3072]{2,1,0:T(8,128)(2,1)}) custom-call(bf16[4,256,2048]{2,1,0:T(8,128)(2,1)S(1)} %mid_rows.1.refs_0_.own_ref, bf16[1024,2048]{1,0:T(8,128)(2,1)} %bitcast.62, bf16[1024,1536]{1,0:T(8,128)(2,1)S(1)} %get-tuple-element.108.refs_0_.refs_2_, ...), custom_call_target="tpu_custom_call" | custom-call | bytes 108900000 | tf_op jit(solution)/shard_map/sum_mid/pallas_call | solution.py:746
  404.2 6.3 mix_back.1
  412.0 28.2 %gather_attention.1 = bf16[4,256,2048]{2,1,0:T(8,128)(2,1)S(1)} custom-call(bf16[256,2048]{1,0:T(8,128)(2,1)S(1)} %copy-done.28), custom_call_target="tpu_custom_call" | custom-call | bytes 95700000 | tf_op jit(solution)/shard_map/gather_attention/pallas_call | solution.py:746
  442.2 2.8 slice_bitcast_fusion
  445.7 8.0 %collective-permute-start.3 = (bf16[192,2048]{1,0:T(8,128)(2,1)}, bf16[192,2048]{1,0:T(8,128)(2,1)}, u32[]{:S(2)}, u32[]{:S(2)}) collective-permute-start(bf16[192,2048]{1,0:T(8,128)(2,1)} %get-tuple-element.164), channel_id=1, source_target_pairs={{0,0},{1,1},{2,4},{3,5},{4,2},{5,3},{6,6},{7,7},{8,8},{9,9},{10,12... | collective-permute-start | bytes 2359304 | tf_op jit(solution)/shard_map/ppermute | solution.py:423
  453.7 5.5 convolution_convert_fusion.2.grad_ref
  459.2 5.5 slot_grad.3
  466.0 21.0 %attend_back.1 = (f32[1024,512]{1,0:T(8,128)}, bf16[1024,512]{1,0:T(8,128)(2,1)}, f32[1024,512]{1,0:T(8,128)}) custom-call(s32[2]{0:T(128)} %pad_add_fusion.2.place_ref, s32[1024,1]{1,0:T(8,128)} %copy.45.time_ref, s32[1024,1]{1,0:T(8,128)} %bitcast.82, bf16[1024,512]{1,0:T(8,128)(2,1)} %copy-done.52, bf16[1024,512]{1,0:T(8,128)(2,1)} %copy-done.50, ...), custom_call_target="tpu_custom_call" | custom-call | flops 5368709120 | bytes 16777216 | tf_op jit(solution)/shard_map/attend_back/pallas_call | solution.py:1089
  487.3 2.8 copy-done.11
  491.3 49.9 %keys_down.1 = (bf16[1024,512]{1,0:T(8,128)(2,1)S(1)}, bf16[256,2048]{1,0:T(8,128)(2,1)S(1)}, bf16[256,2048]{1,0:T(8,128)(2,1)S(1)}) custom-call(bf16[1024,512]{1,0:T(8,128)(2,1)S(1)} %copy-done.27, bf16[4,256,2048]{2,1,0:T(8,128)(2,1)S(1)} %copy-done.11), custom_call_target="tpu_custom_call" | custom-call | bytes 174900000 | tf_op jit(solution)/shard_map/keys_down/pallas_call | solution.py:746
  543.2 5.3 unproject.1
  548.5 6.3 convolution_convert_fusion.1
  556.4 2.2 copy-done.15
  558.6 6.4 in_rows.1.refs_0_.own_ref
  567.0 3.7 convert_add_fusion.1
  570.6 2.9 fusion.1
  573.5 2.2 copy-done.1
  577.6 75.1 %sum_in.1 = (bf16[256,2048]{1,0:T(8,128)(2,1)S(1)}, bf16[256,2048]{1,0:T(8,128)(2,1)S(1)}, bf16[2,256,3072]{2,1,0:T(8,128)(2,1)S(1)}) custom-call(bf16[4,256,2048]{2,1,0:T(8,128)(2,1)S(1)} %copy-done.1, bf16[2,256,3072]{2,1,0:T(8,128)(2,1)S(1)} %copy-done.18), custom_call_target="tpu_custom_call" | custom-call | bytes 244200000 | tf_op jit(solution)/shard_map/sum_in/pallas_call | solution.py:746
  657.1 2.2 slice_bitcast_fusion.3
  659.4 5.3 collective-permute-start.7
  664.9 2.2 add_bitcast_fusion.refs_8_
  668.5 6.0 in_back.1
  675.5 2.5 convert_add_fusion.3
  678.0 13.3 %collective-permute-done.8 = bf16[256,1024]{1,0:T(8,128)(2,1)} collective-permute-done((bf16[256,1024]{1,0:T(8,128)(2,1)}, bf16[256,1024]{1,0:T(8,128)(2,1)}, u32[]{:S(2)}, u32[]{:S(2)}) %collective-permute-start.8) | collective-permute-done | bytes 524320 | tf_op jit(solution)/shard_map/ppermute | solution.py:423
  691.2 3.0 convert_add_fusion.2
  697.5 12.3 %sum_all.1 = f32[40,128]{1,0:T(8,128)} custom-call(f32[40,128]{1,0:T(8,128)} %pad_bitcast_fusion.value), custom_call_target="tpu_custom_call" | custom-call | tf_op jit(solution)/shard_map/sum_all/pallas_call | solution.py:836
  715.1 17.4 %adam_all.1 = (f32[256,1024]{1,0:T(8,128)}, f32[256,1024]{1,0:T(8,128)}, f32[256,1024]{1,0:T(8,128)}, f32[256,3072]{1,0:T(8,128)}, f32[256,3072]{1,0:T(8,128)}, ...) custom-call(f32[1]{0:T(128)} %bitcast.28.refs_0_, ...), custom_call_target="tpu_custom_call" | custom-call | bytes 50331648 | tf_op jit(solution)/shard_map/adam_all/pallas_call | solution.py:1366
  (198 shorter events, 67.0 us)
Async XLA Ops:
  7.2 286.8 %all-gather.4.cloned.1.call-start = ((), (), s32[]{:S(2)}) async-start(), calls=%async_computation.4 | async-start | bytes 7864320 | tf_op jit(solution)/shard_map/all_gather | solution.py:777
  8.0 5.5 copy-start.42
  8.0 247.7 %copy-start.43 = (f32[2048]{0:T(1024)}, f32[2048]{0:T(1024)S(1)}, u32[]{:S(2)}) copy-start(f32[2048]{0:T(1024)S(1)} %get-tuple-element.175) | copy-start | bytes 24580
  13.5 317.3 %copy-start.44 = (s32[8]{0:T(128)}, s32[8]{0:T(128)S(1)}, u32[]{:S(2)}) copy-start(s32[8]{0:T(128)S(1)} %broadcast_xor_fusion.slot_ref) | copy-start | bytes 100
  15.3 87.6 %copy-start.62 = (s32[1,4]{1,0:T(1,128)S(1)}, s32[1,4]{1,0:T(1,128)}, u32[]{:S(2)}) copy-start(s32[1,4]{1,0:T(1,128)} %param.21) | copy-start | bytes 52
  15.3 87.6 %copy-start.58 = (f32[4352]{0:T(1024)S(1)}, f32[4352]{0:T(1024)}, u32[]{:S(2)}) copy-start(f32[4352]{0:T(1024)} %param.35) | copy-start | bytes 52228
  83.2 210.9 %all-gather.6.cloned.1.call-start = ((), (), s32[]{:S(2)}) async-start(), calls=%async_computation.5 | async-start | bytes 7864320 | tf_op jit(solution)/shard_map/all_gather | solution.py:777
  83.2 85.8 %collective-permute-start.2 = (bf16[256,1536]{1,0:T(8,128)(2,1)}, bf16[256,1536]{1,0:T(8,128)(2,1)}, u32[]{:S(2)}, u32[]{:S(2)}) collective-permute-start(bf16[256,1536]{1,0:T(8,128)(2,1)} %get-tuple-element.93), channel_id=1, source_target_pairs={{4,0},{5,1},{0,2},{1,3},{6,4},{7,5},{2,6},{3,7},{12,8},{13,9},{8,1... | collective-permute-start | bytes 2359304 | tf_op jit(solution)/shard_map/ppermute | solution.py:423
  95.5 73.6 %collective-permute-start.1 = (bf16[256,1536]{1,0:T(8,128)(2,1)}, bf16[256,1536]{1,0:T(8,128)(2,1)}, u32[]{:S(2)}, u32[]{:S(2)}) collective-permute-start(bf16[256,1536]{1,0:T(8,128)(2,1)} %get-tuple-element.93), channel_id=1, source_target_pairs={{0,0},{1,1},{4,2},{5,3},{2,4},{3,5},{6,6},{7,7},{8,8},{9,9},{12,10... | collective-permute-start | bytes 2359304 | tf_op jit(solution)/shard_map/ppermute | solution.py:423
  102.9 1.1 collective-permute-start
  106.6 10.2 %copy-start.16 = (bf16[256,2048]{1,0:T(8,128)(2,1)S(1)}, bf16[256,2048]{1,0:T(8,128)(2,1)}, u32[]{:S(2)}) copy-start(bf16[256,2048]{1,0:T(8,128)(2,1)} %cot_ref.1) | copy-start | bytes 3145732
  116.8 49.2 %copy-start.29 = (bf16[1024,512]{1,0:T(8,128)(2,1)}, bf16[1024,512]{1,0:T(8,128)(2,1)S(1)}, u32[]{:S(2)}) copy-start(bf16[1024,512]{1,0:T(8,128)(2,1)S(1)} %get-tuple-element.91.refs_0_.own_ref) | copy-start | bytes 3145732
  171.7 158.8 %all-gather.8.cloned.1.call-start = ((), (), s32[]{:S(2)}) async-start(), calls=%async_computation.6 | async-start | bytes 7864320 | tf_op jit(solution)/shard_map/all_gather | solution.py:777
  179.8 12.0 %copy-start.56 = (bf16[8,64,2048]{2,1,0:T(8,128)(2,1)S(1)}, bf16[8,64,2048]{2,1,0:T(8,128)(2,1)}, u32[]{:S(2)}) copy-start(bf16[8,64,2048]{2,1,0:T(8,128)(2,1)} %gather_fusion) | copy-start | bytes 6291460
  195.5 57.0 %copy-start.5 = (bf16[1024,2048]{1,0:T(8,128)(2,1)}, bf16[1024,2048]{1,0:T(8,128)(2,1)S(1)}, u32[]{:S(2)}) copy-start(bf16[1024,2048]{1,0:T(8,128)(2,1)S(1)} %convolution_convert_fusion) | copy-start | bytes 12582916
  255.6 186.6 %reduce-scatter.5.cloned.1.call-start = ((), (), s32[]{:S(2)}) async-start(), calls=%async_computation.7 | async-start | bytes 7864320 | tf_op jit(solution)/shard_map/reduce_scatter | solution.py:781
  294.0 2.2 copy-start.4
  313.1 2.7 copy-start.54
  315.8 2.7 copy-start.55
  330.5 243.0 %reduce-scatter.11.cloned.1.call-start = ((), (), s32[]{:S(2)}) async-start(), calls=%async_computation.10 | async-start | bytes 15728640 | tf_op jit(solution)/shard_map/reduce_scatter | solution.py:781
  330.8 22.6 %slice-start = ((s8[6291456]{0:T(1024)(128)(4,1)}), s8[4194304]{0:T(1024)(128)(4,1)S(1)}, s32[]{:S(2)}) async-start(s8[6291456]{0:T(1024)(128)(4,1)} %bitcast.66), calls=%async_computation.11 | async-start | bytes 8388608
  330.8 22.6 %slice-start.1 = ((s8[6291456]{0:T(1024)(128)(4,1)}), s8[2097152]{0:T(1024)(128)(4,1)S(1)}, s32[]{:S(2)}) async-start(s8[6291456]{0:T(1024)(128)(4,1)} %bitcast.66), calls=%async_computation.12 | async-start | bytes 4194304
  355.5 2.9 copy-start.12
  373.4 28.7 %copy-start.2 = (bf16[4,256,2048]{2,1,0:T(8,128)(2,1)}, bf16[4,256,2048]{2,1,0:T(8,128)(2,1)S(1)}, u32[]{:S(2)}) copy-start(bf16[4,256,2048]{2,1,0:T(8,128)(2,1)S(1)} %mid_rows.1.refs_0_.own_ref) | copy-start | bytes 12582916
  404.1 250.5 %reduce-scatter.7.cloned.1.call-start = ((), (), s32[]{:S(2)}) async-start(), calls=%async_computation.8 | async-start | bytes 2621440 | tf_op jit(solution)/shard_map/reduce_scatter | solution.py:781
  442.2 11.5 %copy-start.57 = (bf16[8,64,2048]{2,1,0:T(8,128)(2,1)S(1)}, bf16[8,64,2048]{2,1,0:T(8,128)(2,1)}, u32[]{:S(2)}) copy-start(bf16[8,64,2048]{2,1,0:T(8,128)(2,1)} %gather_fusion) | copy-start | bytes 6291460
  445.1 41.9 %collective-permute-start.4 = (bf16[192,2048]{1,0:T(8,128)(2,1)}, bf16[192,2048]{1,0:T(8,128)(2,1)}, u32[]{:S(2)}, u32[]{:S(2)}) collective-permute-start(bf16[192,2048]{1,0:T(8,128)(2,1)} %get-tuple-element.163), channel_id=1, source_target_pairs={{0,4},{1,5},{2,0},{3,1},{4,6},{5,7},{6,2},{7,3},{8,12},{9,13},{10,... | collective-permute-start | bytes 2359304 | tf_op jit(solution)/shard_map/ppermute | solution.py:423
  445.7 13.5 %copy-start.45 = (s32[8]{0:T(128)S(1)}, s32[8]{0:T(128)}, u32[]{:S(2)}) copy-start(s32[8]{0:T(128)} %copy-done.44) | copy-start | bytes 100
  445.7 13.5 %copy-start.51 = (bf16[1024,512]{1,0:T(8,128)(2,1)S(1)}, bf16[1024,512]{1,0:T(8,128)(2,1)}, u32[]{:S(2)}) copy-start(bf16[1024,512]{1,0:T(8,128)(2,1)} %attend.1.left_ref) | copy-start | bytes 3145732
  445.7 41.3 %collective-permute-start.3 = (bf16[192,2048]{1,0:T(8,128)(2,1)}, bf16[192,2048]{1,0:T(8,128)(2,1)}, u32[]{:S(2)}, u32[]{:S(2)}) collective-permute-start(bf16[192,2048]{1,0:T(8,128)(2,1)} %get-tuple-element.164), channel_id=1, source_target_pairs={{0,0},{1,1},{2,4},{3,5},{4,2},{5,3},{6,6},{7,7},{8,8},{9,9},{10,12... | collective-permute-start | bytes 2359304 | tf_op jit(solution)/shard_map/ppermute | solution.py:423
  487.0 56.2 %copy-start.20 = (f32[1024,512]{1,0:T(8,128)S(1)}, f32[1024,512]{1,0:T(8,128)}, u32[]{:S(2)}) copy-start(f32[1024,512]{1,0:T(8,128)} %get-tuple-element.121.own_ref) | copy-start | bytes 6291460
  487.0 167.6 %reduce-scatter.9.cloned.1.call-start = ((), (), s32[]{:S(2)}) async-start(), calls=%async_computation.9 | async-start | bytes 5242880 | tf_op jit(solution)/shard_map/reduce_scatter | solution.py:781
  487.3 2.8 copy-start.11
  491.3 51.9 %copy-start.17 = (f32[1024,768]{1,0:T(8,128)S(1)}, f32[1024,768]{1,0:T(8,128)}, u32[]{:S(2)}) copy-start(f32[1024,768]{1,0:T(8,128)} %get-tuple-element.123.raw_ref) | copy-start | bytes 9437188
  491.3 51.9 %copy-start.19 = (f32[1024,512]{1,0:T(8,128)S(1)}, f32[1024,512]{1,0:T(8,128)}, u32[]{:S(2)}) copy-start(f32[1024,512]{1,0:T(8,128)} %get-tuple-element.120.dq_ref) | copy-start | bytes 6291460
  491.3 51.9 %copy-start.46 = (s32[2]{0:T(128)S(1)}, s32[2]{0:T(128)}, u32[]{:S(2)}) copy-start(s32[2]{0:T(128)} %pad_add_fusion.2.place_ref) | copy-start | bytes 28
  543.2 5.3 copy-start.48
  548.5 6.3 copy-start.21
  558.6 12.0 %copy-start.33 = (bf16[256,2048]{1,0:T(8,128)(2,1)S(1)}, bf16[256,2048]{1,0:T(8,128)(2,1)}, u32[]{:S(2)}) copy-start(bf16[256,2048]{1,0:T(8,128)(2,1)} %copy-done.32) | copy-start | bytes 3145732
  567.0 3.7 copy-start.10
  567.0 3.7 copy-start.31
  573.5 2.2 copy-start.1
  655.7 12.8 %collective-permute-start.6 = (bf16[64,2048]{1,0:T(8,128)(2,1)S(1)}, bf16[64,2048]{1,0:T(8,128)(2,1)S(1)}, u32[]{:S(2)}, u32[]{:S(2)}) collective-permute-start(bf16[64,2048]{1,0:T(8,128)(2,1)S(1)} %get-tuple-element.173), channel_id=1, source_target_pairs={{0,4},{1,5},{2,0},{3,1},{4,6},{5,7},{6,2},{7,3},{8,12},{9,13},{10,... | collective-permute-start | bytes 786440 | tf_op jit(solution)/shard_map/ppermute | solution.py:423
  655.8 12.8 %collective-permute-start.5 = (bf16[64,2048]{1,0:T(8,128)(2,1)S(1)}, bf16[64,2048]{1,0:T(8,128)(2,1)}, u32[]{:S(2)}, u32[]{:S(2)}) collective-permute-start(bf16[64,2048]{1,0:T(8,128)(2,1)S(1)} %get-tuple-element.174), channel_id=1, source_target_pairs={{0,0},{1,1},{2,4},{3,5},{4,2},{5,3},{6,6},{7,7},{8,8},{9,9},{10,12... | collective-permute-start | bytes 786440 | tf_op jit(solution)/shard_map/ppermute | solution.py:423
  659.4 18.6 %collective-permute-start.7 = (bf16[256,1024]{1,0:T(8,128)(2,1)}, bf16[256,1024]{1,0:T(8,128)(2,1)}, u32[]{:S(2)}, u32[]{:S(2)}) collective-permute-start(bf16[256,1024]{1,0:T(8,128)(2,1)} %get-tuple-element.169), channel_id=1, source_target_pairs={{0,0},{1,1},{2,4},{3,5},{4,2},{5,3},{6,6},{7,7},{8,8},{9,9},{10,12... | collective-permute-start | bytes 1572872 | tf_op jit(solution)/shard_map/ppermute | solution.py:423
  664.7 26.5 %collective-permute-start.8 = (bf16[256,1024]{1,0:T(8,128)(2,1)}, bf16[256,1024]{1,0:T(8,128)(2,1)}, u32[]{:S(2)}, u32[]{:S(2)}) collective-permute-start(bf16[256,1024]{1,0:T(8,128)(2,1)} %get-tuple-element.170), channel_id=1, source_target_pairs={{0,4},{1,5},{2,0},{3,1},{4,6},{5,7},{6,2},{7,3},{8,12},{9,13},{10,... | collective-permute-start | bytes 1572872 | tf_op jit(solution)/shard_map/ppermute | solution.py:423
  674.6 39.1 %copy-start.60 = (f32[4352]{0:T(1024)S(1)}, f32[4352]{0:T(1024)}, u32[]{:S(2)}) copy-start(f32[4352]{0:T(1024)} %param.36) | copy-start | bytes 52228
  674.6 39.1 %copy-start.61 = (f32[4352]{0:T(1024)S(1)}, f32[4352]{0:T(1024)}, u32[]{:S(2)}) copy-start(f32[4352]{0:T(1024)} %param.37) | copy-start | bytes 52228
  (34 other events, 48.3 us)
Sparse Core Ops, SparseCore 0:
  83.3 83.2 all-gather.3
  171.8 81.5 all-gather.5
  255.9 70.1 all-gather.7
  330.6 70.1 reduce-scatter.4
  404.2 120.5 reduce-scatter.10
  527.6 35.1 reduce-scatter.6
  566.1 52.6 reduce-scatter.8

commit v5 on v4

--- a/solution.py
+++ b/solution.py
@@ -533,6 +533,32 @@
             relay.wait()
 
         return [first, None, second, last]
+
+
+class Cores(Task):
+    copies = 2
+    locals = 2
+
+    def outs(self):
+        rows = self.inputs[0]
+        return [jax.ShapeDtypeStruct((4, *rows.shape), rows.dtype)]
+
+    def steps(self, place, ins, outs, scratch):
+        send, recv, local = scratch[:3]
+        full = outs[0]
+        core = place.at(c=1 - place.c)
+        keeps = [pltpu.make_async_copy(ins[n], full.at[n], local.at[n]) for n in range(2)]
+        fars = [far_copy(ins[n], full.at[2 + n], (send, recv), n, core) for n in range(2)]
+
+        def first():
+            for copy in (*fars, *keeps):
+                copy.start()
+
+        def last():
+            for copy in (*keeps, *fars):
+                copy.wait()
+
+        return [first, None, None, last]
 
 
 class Sums(Task):
@@ -1226,7 +1252,7 @@
             jax.ShapeDtypeStruct((count, units), jnp.float32),
             jax.ShapeDtypeStruct((count, units), jnp.bfloat16),
         ],
-        compiler_params=pltpu.CompilerParams(vmem_limit_bytes=32 * 2**20),
+        compiler_params=pltpu.CompilerParams(vmem_limit_bytes=60 * 2**20),
         cost_estimate=pl.CostEstimate(
             flops=4 * count * units * width, bytes_accessed=32 * 2**20, transcendentals=0
         ),
@@ -1524,9 +1550,9 @@
     raw, queries, own_kv = project(
         full_in, qkv_blocks, cosine, sine, head_gains, query_width, key_width
     )
-    (lower_kv,), (d_branch,) = transfer("keys_up", 2, 47, Halves(own_kv, 0), Rows(cotangent))
-    d_branch = d_branch.reshape(count, width)
+    ((lower_kv,),) = transfer("keys_up", 2, 40, Halves(own_kv, 0))
     lower_kv, near_up = lax.optimization_barrier((lower_kv, near_up))
+    near_cotangent = move(after(cotangent, lower_kv), OVER_L)
     up_blocks = over_plane(near_up)
     score_flops = 2 * count * count * query_width
     (attn_heads,) = attention_call(
@@ -1542,6 +1568,7 @@
         return partial.astype(jnp.bfloat16).reshape(4, rows_here, width)
 
     partial = blocks(jnp.dot(attn_heads, w_out, preferred_element_type=jnp.float32))
+    partial, near_cotangent = lax.optimization_barrier((partial, near_cotangent))
     received, (near_down,) = transfer(
         "sum_attention", 3, 50, Sums(partial), Near(down_weight.astype(jnp.bfloat16))
     )
@@ -1552,7 +1579,10 @@
     mixed, own_mid = by_row_tiles(
         mix_kernel, "mix", slot_of, [hidden_in, partial, *received, ln_mid[None]], [row, low_row]
     )
-    ((full_mid,),) = transfer("gather_mid", 4, 34, Rows(own_mid))
+    (full_mid,), (d_branch,) = transfer(
+        "gather_mid", 4, 34, Rows(own_mid), Cores(cotangent, near_cotangent)
+    )
+    d_branch = d_branch.reshape(count, width)
     full_mid = full_mid.reshape(count, width)
     gate, upper, act = mlp_front(full_mid, gate_blocks, up_blocks)
     g_down = slot_grad(slot_of, act, d_branch)
@@ -1593,10 +1623,8 @@
         5 * score_flops,
     )
     d_low, g_out, *owned_down = lax.optimization_barrier((d_low, g_out, *owned_down))
-    red_down = both(owned_down)
     near_g_out = to_plane(g_out)
-    (from_above,), received = transfer("keys_down", 7, 53, Halves(d_low, 1), Sums(branch))
-    result_rows = mixed + summed(branch, received)
+    (from_above,), branch_received = transfer("keys_down", 7, 53, Halves(d_low, 1), Sums(branch))
     d_projected, g_q, g_k = unproject(
         place, d_queries, d_own, from_above, raw, cosine, sine, head_gains
     )
@@ -1605,9 +1633,11 @@
     near_g_qkv = to_plane(g_qkv.astype(jnp.bfloat16).reshape(8, width // 8, -1))
     partial = rows_back("in_rows", d_projected, qkv_blocks)
     received, (owned_gateup,) = transfer("sum_in", 8, 74, Sums(partial), Owners(near_g_gateup))
-    near_g_out, near_g_qkv, *received = lax.optimization_barrier(
-        (near_g_out, near_g_qkv, *received)
-    )
+    near_g_out, near_g_qkv, branch_received, owned_down, received = lax.optimization_barrier(
+        (near_g_out, near_g_qkv, branch_received, owned_down, received)
+    )
+    red_down = both(owned_down)
+    result_rows = mixed + summed(branch, branch_received)
     owned_out = to_owner(near_g_out)
     received, owned_out = lax.optimization_barrier((received, owned_out))
     red_gateup = both(owned_gateup)

time: 748 us -> 736 us (0.984)
  starting transfers between devices: 36.1 us -> 70 us
  Pallas kernels: 547 us -> 516 us
  waiting for transfers between devices: 14.5 us -> 6.93 us
    ppermute x9 -> x10, starting transfers between devices: 35.3 us -> 69.2 us  [move(): return lax.ppermute(value, ('dp', 'mp'), pairs)]
    pallas_call x8, Pallas kernels: 378 us -> 345 us  [transfer(): pl.pallas_call(kernel, out_shape=[leaf for out in outs for leaf in out],...]
    ppermute x9 -> x10, waiting for transfers between devices: 14.3 us -> 6.8 us  [move(): return lax.ppermute(value, ('dp', 'mp'), pairs)]
    unnamed x139 -> x137, local copies, waits for them, and re-layouts: 61.7 us -> 55.1 us
  transfers between devices with their start and end apart: 16 -> 17, of which waited for: 2 -> 2; matrix products, arithmetic and copies ran while one was open for 6% -> 6% of each run, Pallas kernels for 61% -> 58%
where the time goes in v5:
time: 736 us; the launch traced here: 729 us
  Pallas kernels  516 us (70%)
  starting transfers between devices  70 us (10%)
  local copies, waits for them, and re-layouts  69.4 us (9%)
  other arithmetic  31 us (4%)
  between operations  20.1 us (3%)
  matrix products  15.4 us (2%)
    pallas_call x8, Pallas kernels, transfer(): pl.pallas_call(kernel, out_shape=[leaf for out in outs for leaf in out],...  345 us
    ppermute x10, starting transfers between devices, move(): return lax.ppermute(value, ('dp', 'mp'), pairs)  69.2 us
    unnamed x137, local copies, waits for them, and re-layouts  55.1 us
    pallas_call x2, Pallas kernels, attention_call(): pl.pallas_call(kernel, grid_spec=pltpu.PrefetchScalarGridSpec(num_scalar_...  33.4 us
    pallas_call x1, Pallas kernels, mlp_back(): pl.pallas_call(mlp_back_kernel, grid_spec=pltpu.PrefetchScalarGridSpec(nu...  22.6 us
    pallas_call x2, Pallas kernels, rows_back(): pl.pallas_call(rows_back_kernel, grid=(8,), in_specs=specs, out_specs=pl....  21.4 us
    pallas_call x1, Pallas kernels, mlp_front(): pl.pallas_call(mlp_front_kernel, grid=(units // columns,), in_specs=[pl.B...  18.8 us
    pallas_call x1, Pallas kernels, adam_all(): pl.pallas_call(lambda *refs: adam_kernel(*refs, rates=rates), grid_spec=p...  17.4 us
  transfers between devices with their start and end apart: 17, of which 2 were waited for; matrix products, arithmetic and copies ran while one was open for 6% of the time, Pallas kernels for 58%

profile of v5, /device:TPU:0, one launch (start us, length us, event | category | flops | bytes accessed | tf_op | source)
XLA Modules:
  0.0 728.7 jit_solution(14285226897740122720)
XLA Ops:
  10.4 2.1 convert_element_type.74
  15.3 61.3 %gather_first.1 = (bf16[8,256,1024]{2,1,0:T(8,128)(2,1)S(1)}, bf16[8,64,2048]{2,1,0:T(8,128)(2,1)S(1)}, bf16[4,256,2048]{2,1,0:T(8,128)(2,1)S(1)}, bf16[2,256,1536]{2,1,0:T(8,128)(2,1)S(1)}) custom-call(bf16[256,1024]{1,0:T(8,128)(2,1)S(1)} %convert_element_type.72.refs_0_, bf16[64,2048]{1,0:T(8,128)(2,1)S(1)} %convert_element_type.73.refs_1_, ...), custom_call_target="tpu_custom_call" | custom-call | bytes 247500000 | tf_op jit(solution)/shard_map/gather_first/pallas_call | solution.py:772
  81.1 2.1 copy-done.49
  83.2 12.3 %collective-permute-start.2 = (bf16[256,1536]{1,0:T(8,128)(2,1)}, bf16[256,1536]{1,0:T(8,128)(2,1)}, u32[]{:S(2)}, u32[]{:S(2)}) collective-permute-start(bf16[256,1536]{1,0:T(8,128)(2,1)} %get-tuple-element.99), channel_id=1, source_target_pairs={{4,0},{5,1},{0,2},{1,3},{6,4},{7,5},{2,6},{3,7},{12,8},{13,9},{8,1... | collective-permute-start | bytes 2359304 | tf_op jit(solution)/shard_map/ppermute | solution.py:423
  95.5 7.4 %collective-permute-start.1 = (bf16[256,1536]{1,0:T(8,128)(2,1)}, bf16[256,1536]{1,0:T(8,128)(2,1)}, u32[]{:S(2)}, u32[]{:S(2)}) collective-permute-start(bf16[256,1536]{1,0:T(8,128)(2,1)} %get-tuple-element.99), channel_id=1, source_target_pairs={{0,0},{1,1},{4,2},{5,3},{2,4},{3,5},{6,6},{7,7},{8,8},{9,9},{12,10... | collective-permute-start | bytes 2359304 | tf_op jit(solution)/shard_map/ppermute | solution.py:423
  106.6 9.3 %project.1 = (f32[1024,768]{1,0:T(8,128)}, bf16[1024,512]{1,0:T(8,128)(2,1)S(1)}, bf16[1024,512]{1,0:T(8,128)(2,1)S(1)}) custom-call(bf16[1024,2048]{1,0:T(8,128)(2,1)} %bitcast.74, bf16[8,256,1024]{2,1,0:T(8,128)(2,1)} %copy-done.13, f32[1024,128]{1,0:T(8,128)S(1)} %get-tuple-element.198.cos_ref, f32[1024,128]{1,0:T(8,128)S(1)} %get-tuple-element.199.sin_ref, ...), custom_call_target="tpu_custom_call" | custom-call | flops 4294967296 | bytes 16777216 | tf_op jit(solution)/shard_map/project/pallas_call | solution.py:910
  115.9 26.8 %keys_up.1.low_ref = bf16[1024,512]{1,0:T(8,128)(2,1)S(1)} custom-call(bf16[1024,512]{1,0:T(8,128)(2,1)S(1)} %get-tuple-element.98.refs_0_.own_ref), custom_call_target="tpu_custom_call" | custom-call | bytes 132000000 | tf_op jit(solution)/shard_map/keys_up/pallas_call | solution.py:772
  143.7 2.7 pad_maximum_fusion
  146.7 34.2 %collective-permute-start.3 = (bf16[256,2048]{1,0:T(8,128)(2,1)S(1)}, bf16[256,2048]{1,0:T(8,128)(2,1)}, u32[]{:S(2)}, u32[]{:S(2)}) collective-permute-start(bf16[256,2048]{1,0:T(8,128)(2,1)S(1)} %copy-done.15), channel_id=1, source_target_pairs={{1,0},{0,1},{3,2},{2,3},{5,4},{4,5},{7,6},{6,7},{9,8},{8,9},{11,10... | collective-permute-start | bytes 3145736 | tf_op jit(solution)/shard_map/ppermute | solution.py:423
  182.4 3.6 gather_fusion
  188.7 12.3 %attend.1.left_ref = bf16[1024,512]{1,0:T(8,128)(2,1)} custom-call(s32[2]{0:T(128)} %pad_add_fusion.2.place_ref, s32[1024,1]{1,0:T(8,128)} %copy.45.time_ref, s32[1024,1]{1,0:T(8,128)} %bitcast.81, bf16[1024,512]{1,0:T(8,128)(2,1)} %copy-done.53, bf16[1024,512]{1,0:T(8,128)(2,1)} %copy-done.31, bf16[1024,512]{1,0:T(8,128)(2,1)} %copy-done.30), custom_call_target="tpu_custom_call" | custom-call | flops 2147483648 | bytes 16777216 | tf_op jit(solution)/shard_map/attend/pallas_call | solution.py:1115
  201.0 3.6 convolution_convert_fusion
  204.6 47.6 %sum_attention.1 = (bf16[256,2048]{1,0:T(8,128)(2,1)S(1)}, bf16[256,2048]{1,0:T(8,128)(2,1)S(1)}, bf16[2,192,2048]{2,1,0:T(8,128)(2,1)S(1)}) custom-call(bf16[4,256,2048]{2,1,0:T(8,128)(2,1)S(1)} %bitcast.62, bf16[192,2048]{1,0:T(8,128)(2,1)S(1)} %convert_element_type.77.refs_1_), custom_call_target="tpu_custom_call" | custom-call | bytes 165000000 | tf_op jit(solution)/shard_map/sum_attention/pallas_call | solution.py:772
  255.5 2.2 copy-done.4
  263.1 27.8 %gather_mid.1 = (bf16[4,256,2048]{2,1,0:T(8,128)(2,1)S(1)}, bf16[4,256,2048]{2,1,0:T(8,128)(2,1)S(1)}) custom-call(bf16[256,2048]{1,0:T(8,128)(2,1)S(1)} %get-tuple-element.107.refs_0_, bf16[256,2048]{1,0:T(8,128)(2,1)S(1)} %copy-done.15, bf16[256,2048]{1,0:T(8,128)(2,1)} %collective-permute-done.3.refs_2_), custom_call_target="tpu_custom_call" | custom-call | bytes 112200000 | tf_op jit(solution)/shard_map/gather_mid/pallas_call | solution.py:772
  295.0 18.8 %mlp_front.1 = (f32[1024,1536]{1,0:T(8,128)}, f32[1024,1536]{1,0:T(8,128)}, bf16[1024,1536]{1,0:T(8,128)(2,1)}) custom-call(bf16[1024,2048]{1,0:T(8,128)(2,1)} %bitcast.66, bf16[8,256,1536]{2,1,0:T(8,128)(2,1)} %all-gather.4.cloned.1.call-done.gate_ref.refs_1_, bf16[8,256,1536]{2,1,0:T(8,128)(2,1)} %all-gather.6.cloned.1.call-done.up_ref.refs_3_), custom_call_target="tpu_custom_call" | custom-call | flops 12884901888 | bytes 33554432 | tf_op jit(solution)/shard_map/mlp_front/pallas_call | solution.py:1245
  315.7 10.3 %slot_grad.2 = bf16[8,192,2048]{2,1,0:T(8,128)(2,1)} custom-call(s32[8]{0:T(128)S(1)} %broadcast_xor_fusion.slot_ref, bf16[1024,1536]{1,0:T(8,128)(2,1)S(1)} %copy-done.54, bf16[1024,2048]{1,0:T(8,128)(2,1)} %bitcast.76), custom_call_target="tpu_custom_call" | custom-call | flops 6442450944 | bytes 16777216 | tf_op jit(solution)/shard_map/slot_grad/pallas_call | solution.py:1419
  326.4 22.6 %mlp_back.1 = (bf16[1024,1536]{1,0:T(8,128)(2,1)S(1)}, bf16[1024,1536]{1,0:T(8,128)(2,1)}, bf16[4,256,2048]{2,1,0:T(8,128)(2,1)}) custom-call(s32[8]{0:T(128)S(1)} %broadcast_xor_fusion.slot_ref, bf16[1024,2048]{1,0:T(8,128)(2,1)} %bitcast.77, f32[1024,1536]{1,0:T(8,128)} %get-tuple-element.113.gate_ref, f32[1024,1536]{1,0:T(8,128)} %get-tuple-element.114.up_ref, ...), custom_call_target="tpu_custom_call" | custom-call | flops 12884901888 | bytes 33554432 | tf_op jit(solution)/shard_map/mlp_back/pallas_call | solution.py:1296
  348.9 2.2 copy-done.5
  351.1 2.8 copy-done.10
  353.9 15.0 %mid_rows.1.refs_0_.own_ref = bf16[4,256,2048]{2,1,0:T(8,128)(2,1)S(1)} custom-call(bf16[1024,1536]{1,0:T(8,128)(2,1)S(1)} %get-tuple-element.118.refs_0_.refs_2_, bf16[8,256,1536]{2,1,0:T(8,128)(2,1)S(1)} %bitcast.65, bf16[1024,1536]{1,0:T(8,128)(2,1)S(1)} %copy-done.5, bf16[8,256,1536]{2,1,0:T(8,128)(2,1)S(1)} %copy-done.10), custom_call_target="tpu_custom_call" | custom-call | flops 1610612736 | bytes 2097152 | tf_op jit(solution)/shard_map/mid_rows/pallas_call | solution.py:1341
  368.9 29.4 %sum_mid.1 = (bf16[256,2048]{1,0:T(8,128)(2,1)S(1)}, bf16[256,2048]{1,0:T(8,128)(2,1)S(1)}, bf16[8,256,3072]{2,1,0:T(8,128)(2,1)}) custom-call(bf16[4,256,2048]{2,1,0:T(8,128)(2,1)S(1)} %mid_rows.1.refs_0_.own_ref, bf16[1024,2048]{1,0:T(8,128)(2,1)} %bitcast.67, bf16[1024,1536]{1,0:T(8,128)(2,1)S(1)} %get-tuple-element.118.refs_0_.refs_2_, ...), custom_call_target="tpu_custom_call" | custom-call | bytes 108900000 | tf_op jit(solution)/shard_map/sum_mid/pallas_call | solution.py:772
  400.3 6.3 mix_back.1
  408.1 27.6 %gather_attention.1 = bf16[4,256,2048]{2,1,0:T(8,128)(2,1)S(1)} custom-call(bf16[256,2048]{1,0:T(8,128)(2,1)S(1)} %copy-done.29), custom_call_target="tpu_custom_call" | custom-call | bytes 95700000 | tf_op jit(solution)/shard_map/gather_attention/pallas_call | solution.py:772
  437.7 2.8 slice_bitcast_fusion
  440.9 7.9 %collective-permute-start.4 = (bf16[192,2048]{1,0:T(8,128)(2,1)}, bf16[192,2048]{1,0:T(8,128)(2,1)}, u32[]{:S(2)}, u32[]{:S(2)}) collective-permute-start(bf16[192,2048]{1,0:T(8,128)(2,1)} %get-tuple-element.178), channel_id=1, source_target_pairs={{0,0},{1,1},{2,4},{3,5},{4,2},{5,3},{6,6},{7,7},{8,8},{9,9},{10,12... | collective-permute-start | bytes 2359304 | tf_op jit(solution)/shard_map/ppermute | solution.py:423
  448.9 5.6 convolution_convert_fusion.2.grad_ref
  454.5 5.5 slot_grad.3
  461.3 21.1 %attend_back.1 = (f32[1024,512]{1,0:T(8,128)}, bf16[1024,512]{1,0:T(8,128)(2,1)}, f32[1024,512]{1,0:T(8,128)}) custom-call(s32[2]{0:T(128)} %pad_add_fusion.2.place_ref, s32[1024,1]{1,0:T(8,128)} %copy.45.time_ref, s32[1024,1]{1,0:T(8,128)} %bitcast.82, bf16[1024,512]{1,0:T(8,128)(2,1)} %copy-done.53, bf16[1024,512]{1,0:T(8,128)(2,1)} %copy-done.31, ...), custom_call_target="tpu_custom_call" | custom-call | flops 5368709120 | bytes 16777216 | tf_op jit(solution)/shard_map/attend_back/pallas_call | solution.py:1115
  482.7 3.3 copy-done.9
  487.2 50.3 %keys_down.1 = (bf16[1024,512]{1,0:T(8,128)(2,1)S(1)}, bf16[256,2048]{1,0:T(8,128)(2,1)S(1)}, bf16[256,2048]{1,0:T(8,128)(2,1)S(1)}) custom-call(bf16[1024,512]{1,0:T(8,128)(2,1)S(1)} %copy-done.28, bf16[4,256,2048]{2,1,0:T(8,128)(2,1)S(1)} %copy-done.9), custom_call_target="tpu_custom_call" | custom-call | bytes 174900000 | tf_op jit(solution)/shard_map/keys_down/pallas_call | solution.py:772
  539.6 5.3 unproject.1
  544.9 6.3 convolution_convert_fusion.1
  552.8 2.2 copy-done.14
  555.0 6.4 in_rows.1.refs_0_.own_ref
  563.3 2.2 copy-done.1
  567.4 73.9 %sum_in.1 = (bf16[256,2048]{1,0:T(8,128)(2,1)S(1)}, bf16[256,2048]{1,0:T(8,128)(2,1)S(1)}, bf16[2,256,3072]{2,1,0:T(8,128)(2,1)S(1)}) custom-call(bf16[4,256,2048]{2,1,0:T(8,128)(2,1)S(1)} %copy-done.1, bf16[2,256,3072]{2,1,0:T(8,128)(2,1)S(1)} %copy-done.17), custom_call_target="tpu_custom_call" | custom-call | bytes 244200000 | tf_op jit(solution)/shard_map/sum_in/pallas_call | solution.py:772
  645.8 2.2 slice_bitcast_fusion.3
  648.1 5.4 collective-permute-start.8
  653.6 2.2 add_bitcast_fusion.refs_8_
  656.9 2.8 fusion.1
  659.8 3.5 convert_add_fusion.1
  664.7 6.1 in_back.1
  671.8 2.5 convert_add_fusion.3
  674.2 5.7 collective-permute-done.9
  679.9 3.0 convert_add_fusion.2
  686.1 11.7 %sum_all.1 = f32[40,128]{1,0:T(8,128)} custom-call(f32[40,128]{1,0:T(8,128)} %pad_bitcast_fusion.value), custom_call_target="tpu_custom_call" | custom-call | tf_op jit(solution)/shard_map/sum_all/pallas_call | solution.py:862
  703.1 17.4 %adam_all.1 = (f32[256,1024]{1,0:T(8,128)}, f32[256,1024]{1,0:T(8,128)}, f32[256,1024]{1,0:T(8,128)}, f32[256,3072]{1,0:T(8,128)}, f32[256,3072]{1,0:T(8,128)}, ...) custom-call(f32[1]{0:T(128)} %bitcast.28.refs_0_, ...), custom_call_target="tpu_custom_call" | custom-call | bytes 50331648 | tf_op jit(solution)/shard_map/adam_all/pallas_call | solution.py:1392
  (198 shorter events, 63.1 us)
Async XLA Ops:
  7.2 287.8 %all-gather.4.cloned.1.call-start = ((), (), s32[]{:S(2)}) async-start(), calls=%async_computation.4 | async-start | bytes 7864320 | tf_op jit(solution)/shard_map/all_gather | solution.py:803
  8.0 5.5 copy-start.44
  8.0 247.5 %copy-start.45 = (f32[2048]{0:T(1024)}, f32[2048]{0:T(1024)S(1)}, u32[]{:S(2)}) copy-start(f32[2048]{0:T(1024)S(1)} %get-tuple-element.189) | copy-start | bytes 24580
  13.5 312.8 %copy-start.46 = (s32[8]{0:T(128)}, s32[8]{0:T(128)S(1)}, u32[]{:S(2)}) copy-start(s32[8]{0:T(128)S(1)} %broadcast_xor_fusion.slot_ref) | copy-start | bytes 100
  15.3 87.7 %copy-start.61 = (s32[1,4]{1,0:T(1,128)S(1)}, s32[1,4]{1,0:T(1,128)}, u32[]{:S(2)}) copy-start(s32[1,4]{1,0:T(1,128)} %param.21) | copy-start | bytes 52
  15.3 87.7 %copy-start.57 = (f32[4352]{0:T(1024)S(1)}, f32[4352]{0:T(1024)}, u32[]{:S(2)}) copy-start(f32[4352]{0:T(1024)} %param.35) | copy-start | bytes 52228
  83.2 211.8 %all-gather.6.cloned.1.call-start = ((), (), s32[]{:S(2)}) async-start(), calls=%async_computation.5 | async-start | bytes 7864320 | tf_op jit(solution)/shard_map/all_gather | solution.py:803
  83.2 60.4 %collective-permute-start.2 = (bf16[256,1536]{1,0:T(8,128)(2,1)}, bf16[256,1536]{1,0:T(8,128)(2,1)}, u32[]{:S(2)}, u32[]{:S(2)}) collective-permute-start(bf16[256,1536]{1,0:T(8,128)(2,1)} %get-tuple-element.99), channel_id=1, source_target_pairs={{4,0},{5,1},{0,2},{1,3},{6,4},{7,5},{2,6},{3,7},{12,8},{13,9},{8,1... | collective-permute-start | bytes 2359304 | tf_op jit(solution)/shard_map/ppermute | solution.py:423
  95.5 48.2 %collective-permute-start.1 = (bf16[256,1536]{1,0:T(8,128)(2,1)}, bf16[256,1536]{1,0:T(8,128)(2,1)}, u32[]{:S(2)}, u32[]{:S(2)}) collective-permute-start(bf16[256,1536]{1,0:T(8,128)(2,1)} %get-tuple-element.99), channel_id=1, source_target_pairs={{0,0},{1,1},{4,2},{5,3},{2,4},{3,5},{6,6},{7,7},{8,8},{9,9},{12,10... | collective-permute-start | bytes 2359304 | tf_op jit(solution)/shard_map/ppermute | solution.py:423
  102.9 1.1 collective-permute-start
  106.6 9.3 %copy-start.22 = (f32[1024,128]{1,0:T(8,128)}, f32[1024,128]{1,0:T(8,128)S(1)}, u32[]{:S(2)}) copy-start(f32[1024,128]{1,0:T(8,128)S(1)} %get-tuple-element.199.sin_ref) | copy-start | bytes 1572868
  115.9 27.8 %copy-start.30 = (bf16[1024,512]{1,0:T(8,128)(2,1)}, bf16[1024,512]{1,0:T(8,128)(2,1)S(1)}, u32[]{:S(2)}) copy-start(bf16[1024,512]{1,0:T(8,128)(2,1)S(1)} %get-tuple-element.98.refs_0_.own_ref) | copy-start | bytes 3145732
  115.9 27.8 %copy-start.53 = (bf16[1024,512]{1,0:T(8,128)(2,1)}, bf16[1024,512]{1,0:T(8,128)(2,1)S(1)}, u32[]{:S(2)}) copy-start(bf16[1024,512]{1,0:T(8,128)(2,1)S(1)} %get-tuple-element.97.query_ref) | copy-start | bytes 3145732
  143.7 3.0 copy-start.15
  146.5 179.6 %all-gather.8.cloned.1.call-start = ((), (), s32[]{:S(2)}) async-start(), calls=%async_computation.6 | async-start | bytes 7864320 | tf_op jit(solution)/shard_map/all_gather | solution.py:803
  146.7 58.0 %collective-permute-start.3 = (bf16[256,2048]{1,0:T(8,128)(2,1)S(1)}, bf16[256,2048]{1,0:T(8,128)(2,1)}, u32[]{:S(2)}, u32[]{:S(2)}) collective-permute-start(bf16[256,2048]{1,0:T(8,128)(2,1)S(1)} %copy-done.15), channel_id=1, source_target_pairs={{1,0},{0,1},{3,2},{2,3},{5,4},{4,5},{7,6},{6,7},{9,8},{8,9},{11,10... | collective-permute-start | bytes 3145736 | tf_op jit(solution)/shard_map/ppermute | solution.py:423
  188.7 12.3 %copy-start.55 = (bf16[8,64,2048]{2,1,0:T(8,128)(2,1)S(1)}, bf16[8,64,2048]{2,1,0:T(8,128)(2,1)}, u32[]{:S(2)}) copy-start(bf16[8,64,2048]{2,1,0:T(8,128)(2,1)} %gather_fusion) | copy-start | bytes 6291460
  204.6 47.7 %copy-start.3 = (bf16[1024,2048]{1,0:T(8,128)(2,1)}, bf16[1024,2048]{1,0:T(8,128)(2,1)S(1)}, u32[]{:S(2)}) copy-start(bf16[1024,2048]{1,0:T(8,128)(2,1)S(1)} %convolution_convert_fusion) | copy-start | bytes 12582916
  255.4 182.4 %reduce-scatter.5.cloned.1.call-start = ((), (), s32[]{:S(2)}) async-start(), calls=%async_computation.7 | async-start | bytes 7864320 | tf_op jit(solution)/shard_map/reduce_scatter | solution.py:807
  255.4 2.2 copy-start.4
  326.1 237.3 %reduce-scatter.11.cloned.1.call-start = ((), (), s32[]{:S(2)}) async-start(), calls=%async_computation.10 | async-start | bytes 15728640 | tf_op jit(solution)/shard_map/reduce_scatter | solution.py:807
  326.3 22.6 %slice-start = ((s8[6291456]{0:T(1024)(128)(4,1)}), s8[4194304]{0:T(1024)(128)(4,1)S(1)}, s32[]{:S(2)}) async-start(s8[6291456]{0:T(1024)(128)(4,1)} %bitcast.64), calls=%async_computation.11 | async-start | bytes 8388608
  326.3 22.6 %slice-start.1 = ((s8[6291456]{0:T(1024)(128)(4,1)}), s8[2097152]{0:T(1024)(128)(4,1)S(1)}, s32[]{:S(2)}) async-start(s8[6291456]{0:T(1024)(128)(4,1)} %bitcast.64), calls=%async_computation.12 | async-start | bytes 4194304
  351.1 2.8 copy-start.10
  368.9 29.4 %copy-start.2 = (bf16[4,256,2048]{2,1,0:T(8,128)(2,1)}, bf16[4,256,2048]{2,1,0:T(8,128)(2,1)S(1)}, u32[]{:S(2)}) copy-start(bf16[4,256,2048]{2,1,0:T(8,128)(2,1)S(1)} %mid_rows.1.refs_0_.own_ref) | copy-start | bytes 12582916
  400.2 243.1 %reduce-scatter.7.cloned.1.call-start = ((), (), s32[]{:S(2)}) async-start(), calls=%async_computation.8 | async-start | bytes 2621440 | tf_op jit(solution)/shard_map/reduce_scatter | solution.py:807
  437.7 11.2 %copy-start.56 = (bf16[8,64,2048]{2,1,0:T(8,128)(2,1)S(1)}, bf16[8,64,2048]{2,1,0:T(8,128)(2,1)}, u32[]{:S(2)}) copy-start(bf16[8,64,2048]{2,1,0:T(8,128)(2,1)} %gather_fusion) | copy-start | bytes 6291460
  440.6 41.8 %collective-permute-start.5 = (bf16[192,2048]{1,0:T(8,128)(2,1)}, bf16[192,2048]{1,0:T(8,128)(2,1)}, u32[]{:S(2)}, u32[]{:S(2)}) collective-permute-start(bf16[192,2048]{1,0:T(8,128)(2,1)} %get-tuple-element.177), channel_id=1, source_target_pairs={{0,4},{1,5},{2,0},{3,1},{4,6},{5,7},{6,2},{7,3},{8,12},{9,13},{10,... | collective-permute-start | bytes 2359304 | tf_op jit(solution)/shard_map/ppermute | solution.py:423
  440.9 13.5 %copy-start.47 = (s32[8]{0:T(128)S(1)}, s32[8]{0:T(128)}, u32[]{:S(2)}) copy-start(s32[8]{0:T(128)} %copy-done.46) | copy-start | bytes 100
  440.9 13.5 %copy-start.52 = (bf16[1024,512]{1,0:T(8,128)(2,1)S(1)}, bf16[1024,512]{1,0:T(8,128)(2,1)}, u32[]{:S(2)}) copy-start(bf16[1024,512]{1,0:T(8,128)(2,1)} %attend.1.left_ref) | copy-start | bytes 3145732
  440.9 41.4 %collective-permute-start.4 = (bf16[192,2048]{1,0:T(8,128)(2,1)}, bf16[192,2048]{1,0:T(8,128)(2,1)}, u32[]{:S(2)}, u32[]{:S(2)}) collective-permute-start(bf16[192,2048]{1,0:T(8,128)(2,1)} %get-tuple-element.178), channel_id=1, source_target_pairs={{0,0},{1,1},{2,4},{3,5},{4,2},{5,3},{6,6},{7,7},{8,8},{9,9},{10,12... | collective-permute-start | bytes 2359304 | tf_op jit(solution)/shard_map/ppermute | solution.py:423
  461.3 78.3 %copy-start.23 = (f32[1024,128]{1,0:T(8,128)S(1)}, f32[1024,128]{1,0:T(8,128)}, u32[]{:S(2)}) copy-start(f32[1024,128]{1,0:T(8,128)} %copy-done.22) | copy-start | bytes 1572868
  482.4 57.1 %copy-start.19 = (f32[1024,512]{1,0:T(8,128)S(1)}, f32[1024,512]{1,0:T(8,128)}, u32[]{:S(2)}) copy-start(f32[1024,512]{1,0:T(8,128)} %get-tuple-element.128.own_ref) | copy-start | bytes 6291460
  482.4 160.9 %reduce-scatter.9.cloned.1.call-start = ((), (), s32[]{:S(2)}) async-start(), calls=%async_computation.9 | async-start | bytes 5242880 | tf_op jit(solution)/shard_map/reduce_scatter | solution.py:807
  482.6 3.4 copy-start.9
  487.2 52.3 %copy-start.16 = (f32[1024,768]{1,0:T(8,128)S(1)}, f32[1024,768]{1,0:T(8,128)}, u32[]{:S(2)}) copy-start(f32[1024,768]{1,0:T(8,128)} %get-tuple-element.132.raw_ref) | copy-start | bytes 9437188
  487.2 52.3 %copy-start.18 = (f32[1024,512]{1,0:T(8,128)S(1)}, f32[1024,512]{1,0:T(8,128)}, u32[]{:S(2)}) copy-start(f32[1024,512]{1,0:T(8,128)} %get-tuple-element.127.dq_ref) | copy-start | bytes 6291460
  487.2 52.3 %copy-start.48 = (s32[2]{0:T(128)S(1)}, s32[2]{0:T(128)}, u32[]{:S(2)}) copy-start(s32[2]{0:T(128)} %pad_add_fusion.2.place_ref) | copy-start | bytes 28
  539.6 5.3 copy-start.50
  544.8 6.3 copy-start.20
  644.4 20.3 %collective-permute-start.7 = (bf16[64,2048]{1,0:T(8,128)(2,1)S(1)}, bf16[64,2048]{1,0:T(8,128)(2,1)S(1)}, u32[]{:S(2)}, u32[]{:S(2)}) collective-permute-start(bf16[64,2048]{1,0:T(8,128)(2,1)S(1)} %get-tuple-element.187), channel_id=1, source_target_pairs={{0,4},{1,5},{2,0},{3,1},{4,6},{5,7},{6,2},{7,3},{8,12},{9,13},{10,... | collective-permute-start | bytes 786440 | tf_op jit(solution)/shard_map/ppermute | solution.py:423
  644.5 20.3 %collective-permute-start.6 = (bf16[64,2048]{1,0:T(8,128)(2,1)S(1)}, bf16[64,2048]{1,0:T(8,128)(2,1)}, u32[]{:S(2)}, u32[]{:S(2)}) collective-permute-start(bf16[64,2048]{1,0:T(8,128)(2,1)S(1)} %get-tuple-element.188), channel_id=1, source_target_pairs={{0,0},{1,1},{2,4},{3,5},{4,2},{5,3},{6,6},{7,7},{8,8},{9,9},{10,12... | collective-permute-start | bytes 786440 | tf_op jit(solution)/shard_map/ppermute | solution.py:423
  648.1 26.2 %collective-permute-start.8 = (bf16[256,1024]{1,0:T(8,128)(2,1)}, bf16[256,1024]{1,0:T(8,128)(2,1)}, u32[]{:S(2)}, u32[]{:S(2)}) collective-permute-start(bf16[256,1024]{1,0:T(8,128)(2,1)} %get-tuple-element.183), channel_id=1, source_target_pairs={{0,0},{1,1},{2,4},{3,5},{4,2},{5,3},{6,6},{7,7},{8,8},{9,9},{10,12... | collective-permute-start | bytes 1572872 | tf_op jit(solution)/shard_map/ppermute | solution.py:423
  653.4 26.5 %collective-permute-start.9 = (bf16[256,1024]{1,0:T(8,128)(2,1)}, bf16[256,1024]{1,0:T(8,128)(2,1)}, u32[]{:S(2)}, u32[]{:S(2)}) collective-permute-start(bf16[256,1024]{1,0:T(8,128)(2,1)} %get-tuple-element.184), channel_id=1, source_target_pairs={{0,4},{1,5},{2,0},{3,1},{4,6},{5,7},{6,2},{7,3},{8,12},{9,13},{10,... | collective-permute-start | bytes 1572872 | tf_op jit(solution)/shard_map/ppermute | solution.py:423
  653.6 2.8 copy-start.33
  653.6 3.3 copy-start.35
  670.8 30.9 %copy-start.59 = (f32[4352]{0:T(1024)S(1)}, f32[4352]{0:T(1024)}, u32[]{:S(2)}) copy-start(f32[4352]{0:T(1024)} %param.36) | copy-start | bytes 52228
  670.8 31.0 %copy-start.60 = (f32[4352]{0:T(1024)S(1)}, f32[4352]{0:T(1024)}, u32[]{:S(2)}) copy-start(f32[4352]{0:T(1024)} %param.37) | copy-start | bytes 52228
  (34 other events, 49.8 us)
Sparse Core Ops, SparseCore 0:
  83.3 83.2 all-gather.3
  169.0 82.3 all-gather.5
  255.5 68.7 all-gather.7
  327.2 70.2 reduce-scatter.4
  400.4 120.7 reduce-scatter.10
  523.9 35.1 reduce-scatter.6
  562.4 52.7 reduce-scatter.8

commit v6 on v5

--- a/solution.py
+++ b/solution.py
@@ -1200,7 +1200,7 @@
 
 
 def by_row_tiles(kernel, name, slot_of, inputs, outs, scratch=False, micros=3):
-    rows, width = 64, inputs[0].shape[1]
+    rows, width = 128 if scratch else 64, inputs[0].shape[1]
     steps = inputs[0].shape[0] // rows
 
     def spec(leaf):
@@ -1550,6 +1550,8 @@
     raw, queries, own_kv = project(
         full_in, qkv_blocks, cosine, sine, head_gains, query_width, key_width
     )
+    low_down = down_weight.astype(jnp.bfloat16)
+    own_kv, w_out, low_down = lax.optimization_barrier((own_kv, w_out, low_down))
     ((lower_kv,),) = transfer("keys_up", 2, 40, Halves(own_kv, 0))
     lower_kv, near_up = lax.optimization_barrier((lower_kv, near_up))
     near_cotangent = move(after(cotangent, lower_kv), OVER_L)
@@ -1570,7 +1572,7 @@
     partial = blocks(jnp.dot(attn_heads, w_out, preferred_element_type=jnp.float32))
     partial, near_cotangent = lax.optimization_barrier((partial, near_cotangent))
     received, (near_down,) = transfer(
-        "sum_attention", 3, 50, Sums(partial), Near(down_weight.astype(jnp.bfloat16))
+        "sum_attention", 3, 50, Sums(partial), Near(low_down)
     )
     down_blocks = over_plane(near_down)
     row = jax.ShapeDtypeStruct((rows_here, width), jnp.float32)

time: 736 us -> 733 us (level)
  starting transfers between devices: 70 us -> 59 us
    ppermute x10, starting transfers between devices: 69.2 us -> 57.6 us  [move(): return lax.ppermute(value, ('dp', 'mp'), pairs)]
    unnamed x137 -> x139, local copies, waits for them, and re-layouts: 55.1 us -> 56.3 us
  transfers between devices with their start and end apart: 17 -> 17, of which waited for: 2 -> 2; matrix products, arithmetic and copies ran while one was open for 6% -> 6% of each run, Pallas kernels for 58% -> 59%
where the time goes in v6:
time: 733 us; the launch traced here: 726 us
  Pallas kernels  518 us (71%)
  local copies, waits for them, and re-layouts  70.5 us (10%)
  starting transfers between devices  59 us (8%)
  other arithmetic  31.3 us (4%)
  between operations  20.2 us (3%)
  matrix products  15.4 us (2%)
  waiting for transfers between devices  11.5 us (2%)
    pallas_call x8, Pallas kernels, transfer(): pl.pallas_call(kernel, out_shape=[leaf for out in outs for leaf in out],...  348 us
    ppermute x10, starting transfers between devices, move(): return lax.ppermute(value, ('dp', 'mp'), pairs)  57.6 us
    unnamed x139, local copies, waits for them, and re-layouts  56.3 us
    pallas_call x2, Pallas kernels, attention_call(): pl.pallas_call(kernel, grid_spec=pltpu.PrefetchScalarGridSpec(num_scalar_...  33.2 us
    pallas_call x1, Pallas kernels, mlp_back(): pl.pallas_call(mlp_back_kernel, grid_spec=pltpu.PrefetchScalarGridSpec(nu...  22.6 us
    pallas_call x2, Pallas kernels, rows_back(): pl.pallas_call(rows_back_kernel, grid=(8,), in_specs=specs, out_specs=pl....  21.5 us
    pallas_call x1, Pallas kernels, mlp_front(): pl.pallas_call(mlp_front_kernel, grid=(units // columns,), in_specs=[pl.B...  18.8 us
    pallas_call x1, Pallas kernels, adam_all(): pl.pallas_call(lambda *refs: adam_kernel(*refs, rates=rates), grid_spec=p...  17.4 us
  transfers between devices with their start and end apart: 17, of which 2 were waited for; matrix products, arithmetic and copies ran while one was open for 6% of the time, Pallas kernels for 59%

profile of v6, /device:TPU:0, one launch (start us, length us, event | category | flops | bytes accessed | tf_op | source)
XLA Modules:
  0.0 725.7 jit_solution(11931068587860174059)
XLA Ops:
  10.4 2.1 convert_element_type.74
  15.3 61.3 %gather_first.1 = (bf16[8,256,1024]{2,1,0:T(8,128)(2,1)S(1)}, bf16[8,64,2048]{2,1,0:T(8,128)(2,1)S(1)}, bf16[4,256,2048]{2,1,0:T(8,128)(2,1)S(1)}, bf16[2,256,1536]{2,1,0:T(8,128)(2,1)S(1)}) custom-call(bf16[256,1024]{1,0:T(8,128)(2,1)S(1)} %convert_element_type.72.refs_0_, bf16[64,2048]{1,0:T(8,128)(2,1)S(1)} %convert_element_type.73.refs_1_, ...), custom_call_target="tpu_custom_call" | custom-call | bytes 247500000 | tf_op jit(solution)/shard_map/gather_first/pallas_call | solution.py:772
  81.1 2.1 copy-done.49
  83.2 12.3 %collective-permute-start.2 = (bf16[256,1536]{1,0:T(8,128)(2,1)}, bf16[256,1536]{1,0:T(8,128)(2,1)S(1)}, u32[]{:S(2)}, u32[]{:S(2)}) collective-permute-start(bf16[256,1536]{1,0:T(8,128)(2,1)} %get-tuple-element.104), channel_id=1, source_target_pairs={{4,0},{5,1},{0,2},{1,3},{6,4},{7,5},{2,6},{3,7},{12,8},{13,9},{8,1... | collective-permute-start | bytes 2359304 | tf_op jit(solution)/shard_map/ppermute | solution.py:423
  95.5 7.5 %collective-permute-start.1 = (bf16[256,1536]{1,0:T(8,128)(2,1)}, bf16[256,1536]{1,0:T(8,128)(2,1)}, u32[]{:S(2)}, u32[]{:S(2)}) collective-permute-start(bf16[256,1536]{1,0:T(8,128)(2,1)} %get-tuple-element.104), channel_id=1, source_target_pairs={{0,0},{1,1},{4,2},{5,3},{2,4},{3,5},{6,6},{7,7},{8,8},{9,9},{12,10... | collective-permute-start | bytes 2359304 | tf_op jit(solution)/shard_map/ppermute | solution.py:423
  104.8 3.8 gather_fusion
  111.2 9.3 %project.1 = (f32[1024,768]{1,0:T(8,128)}, bf16[1024,512]{1,0:T(8,128)(2,1)S(1)}, bf16[1024,512]{1,0:T(8,128)(2,1)S(1)}) custom-call(bf16[1024,2048]{1,0:T(8,128)(2,1)} %bitcast.74, bf16[8,256,1024]{2,1,0:T(8,128)(2,1)} %copy-done.13, f32[1024,128]{1,0:T(8,128)S(1)} %get-tuple-element.204.cos_ref, f32[1024,128]{1,0:T(8,128)S(1)} %get-tuple-element.205.sin_ref, ...), custom_call_target="tpu_custom_call" | custom-call | flops 4294967296 | bytes 16777216 | tf_op jit(solution)/shard_map/project/pallas_call | solution.py:910
  121.4 26.7 %keys_up.1.low_ref = bf16[1024,512]{1,0:T(8,128)(2,1)S(1)} custom-call(bf16[1024,512]{1,0:T(8,128)(2,1)S(1)} %get-tuple-element.103.refs_0_.own_ref), custom_call_target="tpu_custom_call" | custom-call | bytes 132000000 | tf_op jit(solution)/shard_map/keys_up/pallas_call | solution.py:772
  150.0 2.7 pad_maximum_fusion
  153.1 28.7 %collective-permute-start.3 = (bf16[256,2048]{1,0:T(8,128)(2,1)S(1)}, bf16[256,2048]{1,0:T(8,128)(2,1)}, u32[]{:S(2)}, u32[]{:S(2)}) collective-permute-start(bf16[256,2048]{1,0:T(8,128)(2,1)S(1)} %copy-done.15), channel_id=1, source_target_pairs={{1,0},{0,1},{3,2},{2,3},{5,4},{4,5},{7,6},{6,7},{9,8},{8,9},{11,10... | collective-permute-start | bytes 3145736 | tf_op jit(solution)/shard_map/ppermute | solution.py:423
  184.6 12.0 %attend.1.left_ref = bf16[1024,512]{1,0:T(8,128)(2,1)} custom-call(s32[2]{0:T(128)} %pad_add_fusion.2.place_ref, s32[1024,1]{1,0:T(8,128)} %copy.45.time_ref, s32[1024,1]{1,0:T(8,128)} %bitcast.82, bf16[1024,512]{1,0:T(8,128)(2,1)} %copy-done.53, bf16[1024,512]{1,0:T(8,128)(2,1)} %copy-done.31, bf16[1024,512]{1,0:T(8,128)(2,1)} %copy-done.30), custom_call_target="tpu_custom_call" | custom-call | flops 2147483648 | bytes 16777216 | tf_op jit(solution)/shard_map/attend/pallas_call | solution.py:1115
  196.6 3.6 convolution_convert_fusion
  200.2 5.4 collective-permute-done.3.refs_2_
  205.6 47.2 %sum_attention.1 = (bf16[256,2048]{1,0:T(8,128)(2,1)S(1)}, bf16[256,2048]{1,0:T(8,128)(2,1)S(1)}, bf16[2,192,2048]{2,1,0:T(8,128)(2,1)S(1)}) custom-call(bf16[4,256,2048]{2,1,0:T(8,128)(2,1)S(1)} %bitcast.62, bf16[192,2048]{1,0:T(8,128)(2,1)S(1)} %convert_element_type.76.refs_1_), custom_call_target="tpu_custom_call" | custom-call | bytes 165000000 | tf_op jit(solution)/shard_map/sum_attention/pallas_call | solution.py:772
  256.0 2.2 copy-done.4
  263.6 27.8 %gather_mid.1 = (bf16[4,256,2048]{2,1,0:T(8,128)(2,1)S(1)}, bf16[4,256,2048]{2,1,0:T(8,128)(2,1)S(1)}) custom-call(bf16[256,2048]{1,0:T(8,128)(2,1)S(1)} %get-tuple-element.113.refs_0_, bf16[256,2048]{1,0:T(8,128)(2,1)S(1)} %copy-done.15, bf16[256,2048]{1,0:T(8,128)(2,1)} %collective-permute-done.3.refs_2_), custom_call_target="tpu_custom_call" | custom-call | bytes 112200000 | tf_op jit(solution)/shard_map/gather_mid/pallas_call | solution.py:772
  295.5 18.8 %mlp_front.1 = (f32[1024,1536]{1,0:T(8,128)}, f32[1024,1536]{1,0:T(8,128)}, bf16[1024,1536]{1,0:T(8,128)(2,1)}) custom-call(bf16[1024,2048]{1,0:T(8,128)(2,1)} %bitcast.66, bf16[8,256,1536]{2,1,0:T(8,128)(2,1)} %all-gather.4.cloned.1.call-done.gate_ref.refs_1_, bf16[8,256,1536]{2,1,0:T(8,128)(2,1)} %all-gather.6.cloned.1.call-done.up_ref.refs_3_), custom_call_target="tpu_custom_call" | custom-call | flops 12884901888 | bytes 33554432 | tf_op jit(solution)/shard_map/mlp_front/pallas_call | solution.py:1245
  316.2 10.4 %slot_grad.2 = bf16[8,192,2048]{2,1,0:T(8,128)(2,1)} custom-call(s32[8]{0:T(128)S(1)} %broadcast_xor_fusion.slot_ref, bf16[1024,1536]{1,0:T(8,128)(2,1)S(1)} %copy-done.54, bf16[1024,2048]{1,0:T(8,128)(2,1)} %bitcast.76), custom_call_target="tpu_custom_call" | custom-call | flops 6442450944 | bytes 16777216 | tf_op jit(solution)/shard_map/slot_grad/pallas_call | solution.py:1419
  327.2 22.6 %mlp_back.1 = (bf16[1024,1536]{1,0:T(8,128)(2,1)S(1)}, bf16[1024,1536]{1,0:T(8,128)(2,1)}, bf16[4,256,2048]{2,1,0:T(8,128)(2,1)}) custom-call(s32[8]{0:T(128)S(1)} %broadcast_xor_fusion.slot_ref, bf16[1024,2048]{1,0:T(8,128)(2,1)} %bitcast.77, f32[1024,1536]{1,0:T(8,128)} %get-tuple-element.119.gate_ref, f32[1024,1536]{1,0:T(8,128)} %get-tuple-element.120.up_ref, ...), custom_call_target="tpu_custom_call" | custom-call | flops 12884901888 | bytes 33554432 | tf_op jit(solution)/shard_map/mlp_back/pallas_call | solution.py:1296
  349.8 2.1 copy-done.5
  351.9 2.8 copy-done.10
  354.7 15.0 %mid_rows.1.refs_0_.own_ref = bf16[4,256,2048]{2,1,0:T(8,128)(2,1)S(1)} custom-call(bf16[1024,1536]{1,0:T(8,128)(2,1)S(1)} %get-tuple-element.124.refs_0_.refs_2_, bf16[8,256,1536]{2,1,0:T(8,128)(2,1)S(1)} %bitcast.65, bf16[1024,1536]{1,0:T(8,128)(2,1)S(1)} %copy-done.5, bf16[8,256,1536]{2,1,0:T(8,128)(2,1)S(1)} %copy-done.10), custom_call_target="tpu_custom_call" | custom-call | flops 1610612736 | bytes 2097152 | tf_op jit(solution)/shard_map/mid_rows/pallas_call | solution.py:1341
  369.8 29.4 %sum_mid.1 = (bf16[256,2048]{1,0:T(8,128)(2,1)S(1)}, bf16[256,2048]{1,0:T(8,128)(2,1)S(1)}, bf16[8,256,3072]{2,1,0:T(8,128)(2,1)}) custom-call(bf16[4,256,2048]{2,1,0:T(8,128)(2,1)S(1)} %mid_rows.1.refs_0_.own_ref, bf16[1024,2048]{1,0:T(8,128)(2,1)} %bitcast.67, bf16[1024,1536]{1,0:T(8,128)(2,1)S(1)} %get-tuple-element.124.refs_0_.refs_2_, ...), custom_call_target="tpu_custom_call" | custom-call | bytes 108900000 | tf_op jit(solution)/shard_map/sum_mid/pallas_call | solution.py:772
  401.2 6.0 mix_back.1
  408.7 27.6 %gather_attention.1 = bf16[4,256,2048]{2,1,0:T(8,128)(2,1)S(1)} custom-call(bf16[256,2048]{1,0:T(8,128)(2,1)S(1)} %copy-done.29), custom_call_target="tpu_custom_call" | custom-call | bytes 95700000 | tf_op jit(solution)/shard_map/gather_attention/pallas_call | solution.py:772
  438.3 2.5 slice_bitcast_fusion
  443.1 5.5 convolution_convert_fusion.2.grad_ref
  448.6 5.7 slot_grad.3
  455.6 21.1 %attend_back.1 = (f32[1024,512]{1,0:T(8,128)}, bf16[1024,512]{1,0:T(8,128)(2,1)}, f32[1024,512]{1,0:T(8,128)}) custom-call(s32[2]{0:T(128)} %pad_add_fusion.2.place_ref, s32[1024,1]{1,0:T(8,128)} %copy.45.time_ref, s32[1024,1]{1,0:T(8,128)} %bitcast.83, bf16[1024,512]{1,0:T(8,128)(2,1)} %copy-done.53, bf16[1024,512]{1,0:T(8,128)(2,1)} %copy-done.31, ...), custom_call_target="tpu_custom_call" | custom-call | flops 5368709120 | bytes 16777216 | tf_op jit(solution)/shard_map/attend_back/pallas_call | solution.py:1115
  477.0 2.4 copy-done.9
  480.7 53.9 %keys_down.1 = (bf16[1024,512]{1,0:T(8,128)(2,1)S(1)}, bf16[256,2048]{1,0:T(8,128)(2,1)S(1)}, bf16[256,2048]{1,0:T(8,128)(2,1)S(1)}) custom-call(bf16[1024,512]{1,0:T(8,128)(2,1)S(1)} %copy-done.28, bf16[4,256,2048]{2,1,0:T(8,128)(2,1)S(1)} %copy-done.9), custom_call_target="tpu_custom_call" | custom-call | bytes 174900000 | tf_op jit(solution)/shard_map/keys_down/pallas_call | solution.py:772
  536.5 5.2 unproject.1
  541.8 6.3 convolution_convert_fusion.1
  549.7 2.5 copy-done.14
  552.2 6.4 in_rows.1.refs_0_.own_ref
  560.7 2.2 copy-done.1
  564.7 73.6 %sum_in.1 = (bf16[256,2048]{1,0:T(8,128)(2,1)S(1)}, bf16[256,2048]{1,0:T(8,128)(2,1)S(1)}, bf16[2,256,3072]{2,1,0:T(8,128)(2,1)S(1)}) custom-call(bf16[4,256,2048]{2,1,0:T(8,128)(2,1)S(1)} %copy-done.1, bf16[2,256,3072]{2,1,0:T(8,128)(2,1)S(1)} %copy-done.17), custom_call_target="tpu_custom_call" | custom-call | bytes 244200000 | tf_op jit(solution)/shard_map/sum_in/pallas_call | solution.py:772
  642.8 2.2 slice_bitcast_fusion.3
  645.0 5.4 collective-permute-start.8
  650.6 2.2 add_bitcast_fusion.refs_8_
  653.9 2.8 fusion.1
  656.7 3.5 convert_add_fusion.1
  661.7 5.8 in_back.1
  668.5 2.5 convert_add_fusion.3
  671.0 5.9 collective-permute-done.9
  676.9 3.0 convert_add_fusion.2
  683.1 11.7 %sum_all.1 = f32[40,128]{1,0:T(8,128)} custom-call(f32[40,128]{1,0:T(8,128)} %pad_bitcast_fusion.value), custom_call_target="tpu_custom_call" | custom-call | tf_op jit(solution)/shard_map/sum_all/pallas_call | solution.py:862
  700.1 17.4 %adam_all.1 = (f32[256,1024]{1,0:T(8,128)}, f32[256,1024]{1,0:T(8,128)}, f32[256,1024]{1,0:T(8,128)}, f32[256,3072]{1,0:T(8,128)}, f32[256,3072]{1,0:T(8,128)}, ...) custom-call(f32[1]{0:T(128)} %bitcast.28.refs_0_, ...), custom_call_target="tpu_custom_call" | custom-call | bytes 50331648 | tf_op jit(solution)/shard_map/adam_all/pallas_call | solution.py:1392
  (200 shorter events, 66.3 us)
Async XLA Ops:
  7.2 288.3 %all-gather.4.cloned.1.call-start = ((), (), s32[]{:S(2)}) async-start(), calls=%async_computation.4 | async-start | bytes 7864320 | tf_op jit(solution)/shard_map/all_gather | solution.py:803
  8.0 5.5 copy-start.44
  8.0 248.0 %copy-start.45 = (f32[2048]{0:T(1024)}, f32[2048]{0:T(1024)S(1)}, u32[]{:S(2)}) copy-start(f32[2048]{0:T(1024)S(1)} %get-tuple-element.195) | copy-start | bytes 24580
  13.5 313.7 %copy-start.46 = (s32[8]{0:T(128)}, s32[8]{0:T(128)S(1)}, u32[]{:S(2)}) copy-start(s32[8]{0:T(128)S(1)} %broadcast_xor_fusion.slot_ref) | copy-start | bytes 100
  15.3 87.7 %copy-start.62 = (s32[1,4]{1,0:T(1,128)S(1)}, s32[1,4]{1,0:T(1,128)}, u32[]{:S(2)}) copy-start(s32[1,4]{1,0:T(1,128)} %param.21) | copy-start | bytes 52
  83.2 212.4 %all-gather.6.cloned.1.call-start = ((), (), s32[]{:S(2)}) async-start(), calls=%async_computation.5 | async-start | bytes 7864320 | tf_op jit(solution)/shard_map/all_gather | solution.py:803
  83.2 65.9 %collective-permute-start.2 = (bf16[256,1536]{1,0:T(8,128)(2,1)}, bf16[256,1536]{1,0:T(8,128)(2,1)S(1)}, u32[]{:S(2)}, u32[]{:S(2)}) collective-permute-start(bf16[256,1536]{1,0:T(8,128)(2,1)} %get-tuple-element.104), channel_id=1, source_target_pairs={{4,0},{5,1},{0,2},{1,3},{6,4},{7,5},{2,6},{3,7},{12,8},{13,9},{8,1... | collective-permute-start | bytes 2359304 | tf_op jit(solution)/shard_map/ppermute | solution.py:423
  95.5 53.6 %collective-permute-start.1 = (bf16[256,1536]{1,0:T(8,128)(2,1)}, bf16[256,1536]{1,0:T(8,128)(2,1)}, u32[]{:S(2)}, u32[]{:S(2)}) collective-permute-start(bf16[256,1536]{1,0:T(8,128)(2,1)} %get-tuple-element.104), channel_id=1, source_target_pairs={{0,0},{1,1},{4,2},{5,3},{2,4},{3,5},{6,6},{7,7},{8,8},{9,9},{12,10... | collective-permute-start | bytes 2359304 | tf_op jit(solution)/shard_map/ppermute | solution.py:423
  102.9 5.6 collective-permute-start
  104.7 3.8 copy-start.58
  111.2 9.3 %copy-start.22 = (f32[1024,128]{1,0:T(8,128)}, f32[1024,128]{1,0:T(8,128)S(1)}, u32[]{:S(2)}) copy-start(f32[1024,128]{1,0:T(8,128)S(1)} %get-tuple-element.205.sin_ref) | copy-start | bytes 1572868
  121.4 27.7 %copy-start.30 = (bf16[1024,512]{1,0:T(8,128)(2,1)}, bf16[1024,512]{1,0:T(8,128)(2,1)S(1)}, u32[]{:S(2)}) copy-start(bf16[1024,512]{1,0:T(8,128)(2,1)S(1)} %get-tuple-element.103.refs_0_.own_ref) | copy-start | bytes 3145732
  150.0 3.1 copy-start.15
  152.8 173.8 %all-gather.8.cloned.1.call-start = ((), (), s32[]{:S(2)}) async-start(), calls=%async_computation.6 | async-start | bytes 7864320 | tf_op jit(solution)/shard_map/all_gather | solution.py:803
  153.1 52.5 %collective-permute-start.3 = (bf16[256,2048]{1,0:T(8,128)(2,1)S(1)}, bf16[256,2048]{1,0:T(8,128)(2,1)}, u32[]{:S(2)}, u32[]{:S(2)}) collective-permute-start(bf16[256,2048]{1,0:T(8,128)(2,1)S(1)} %copy-done.15), channel_id=1, source_target_pairs={{1,0},{0,1},{3,2},{2,3},{5,4},{4,5},{7,6},{6,7},{9,8},{8,9},{11,10... | collective-permute-start | bytes 3145736 | tf_op jit(solution)/shard_map/ppermute | solution.py:423
  184.6 12.0 %copy-start.55 = (bf16[8,64,2048]{2,1,0:T(8,128)(2,1)S(1)}, bf16[8,64,2048]{2,1,0:T(8,128)(2,1)}, u32[]{:S(2)}) copy-start(bf16[8,64,2048]{2,1,0:T(8,128)(2,1)} %gather_fusion) | copy-start | bytes 6291460
  200.2 52.6 %copy-start.3 = (bf16[1024,2048]{1,0:T(8,128)(2,1)}, bf16[1024,2048]{1,0:T(8,128)(2,1)S(1)}, u32[]{:S(2)}) copy-start(bf16[1024,2048]{1,0:T(8,128)(2,1)S(1)} %convolution_convert_fusion) | copy-start | bytes 12582916
  255.9 182.4 %reduce-scatter.5.cloned.1.call-start = ((), (), s32[]{:S(2)}) async-start(), calls=%async_computation.7 | async-start | bytes 7864320 | tf_op jit(solution)/shard_map/reduce_scatter | solution.py:807
  256.0 2.2 copy-start.4
  326.6 234.0 %reduce-scatter.11.cloned.1.call-start = ((), (), s32[]{:S(2)}) async-start(), calls=%async_computation.10 | async-start | bytes 15728640 | tf_op jit(solution)/shard_map/reduce_scatter | solution.py:807
  327.2 22.6 %slice-start = ((s8[6291456]{0:T(1024)(128)(4,1)}), s8[4194304]{0:T(1024)(128)(4,1)S(1)}, s32[]{:S(2)}) async-start(s8[6291456]{0:T(1024)(128)(4,1)} %bitcast.64), calls=%async_computation.11 | async-start | bytes 8388608
  327.2 22.6 %slice-start.1 = ((s8[6291456]{0:T(1024)(128)(4,1)}), s8[2097152]{0:T(1024)(128)(4,1)S(1)}, s32[]{:S(2)}) async-start(s8[6291456]{0:T(1024)(128)(4,1)} %bitcast.64), calls=%async_computation.12 | async-start | bytes 4194304
  351.9 2.8 copy-start.10
  369.8 29.4 %copy-start.2 = (bf16[4,256,2048]{2,1,0:T(8,128)(2,1)}, bf16[4,256,2048]{2,1,0:T(8,128)(2,1)S(1)}, u32[]{:S(2)}) copy-start(bf16[4,256,2048]{2,1,0:T(8,128)(2,1)S(1)} %mid_rows.1.refs_0_.own_ref) | copy-start | bytes 12582916
  401.1 239.1 %reduce-scatter.7.cloned.1.call-start = ((), (), s32[]{:S(2)}) async-start(), calls=%async_computation.8 | async-start | bytes 2621440 | tf_op jit(solution)/shard_map/reduce_scatter | solution.py:807
  438.3 4.7 copy-start.56
  440.8 35.9 %collective-permute-start.5 = (bf16[192,2048]{1,0:T(8,128)(2,1)}, bf16[192,2048]{1,0:T(8,128)(2,1)}, u32[]{:S(2)}, u32[]{:S(2)}) collective-permute-start(bf16[192,2048]{1,0:T(8,128)(2,1)} %get-tuple-element.183), channel_id=1, source_target_pairs={{0,4},{1,5},{2,0},{3,1},{4,6},{5,7},{6,2},{7,3},{8,12},{9,13},{10,... | collective-permute-start | bytes 2359304 | tf_op jit(solution)/shard_map/ppermute | solution.py:423
  441.2 7.4 %copy-start.47 = (s32[8]{0:T(128)S(1)}, s32[8]{0:T(128)}, u32[]{:S(2)}) copy-start(s32[8]{0:T(128)} %copy-done.46) | copy-start | bytes 100
  441.2 7.4 %copy-start.52 = (bf16[1024,512]{1,0:T(8,128)(2,1)S(1)}, bf16[1024,512]{1,0:T(8,128)(2,1)}, u32[]{:S(2)}) copy-start(bf16[1024,512]{1,0:T(8,128)(2,1)} %attend.1.left_ref) | copy-start | bytes 3145732
  441.2 35.5 %collective-permute-start.4 = (bf16[192,2048]{1,0:T(8,128)(2,1)S(1)}, bf16[192,2048]{1,0:T(8,128)(2,1)}, u32[]{:S(2)}, u32[]{:S(2)}) collective-permute-start(bf16[192,2048]{1,0:T(8,128)(2,1)S(1)} %get-tuple-element.184), channel_id=1, source_target_pairs={{0,0},{1,1},{2,4},{3,5},{4,2},{5,3},{6,6},{7,7},{8,8},{9,9},{10,12... | collective-permute-start | bytes 2359304 | tf_op jit(solution)/shard_map/ppermute | solution.py:423
  455.6 80.9 %copy-start.23 = (f32[1024,128]{1,0:T(8,128)S(1)}, f32[1024,128]{1,0:T(8,128)}, u32[]{:S(2)}) copy-start(f32[1024,128]{1,0:T(8,128)} %copy-done.22) | copy-start | bytes 1572868
  476.7 59.8 %copy-start.19 = (f32[1024,512]{1,0:T(8,128)S(1)}, f32[1024,512]{1,0:T(8,128)}, u32[]{:S(2)}) copy-start(f32[1024,512]{1,0:T(8,128)} %get-tuple-element.134.own_ref) | copy-start | bytes 6291460
  476.8 163.5 %reduce-scatter.9.cloned.1.call-start = ((), (), s32[]{:S(2)}) async-start(), calls=%async_computation.9 | async-start | bytes 5242880 | tf_op jit(solution)/shard_map/reduce_scatter | solution.py:807
  477.0 2.4 copy-start.9
  480.7 55.8 %copy-start.16 = (f32[1024,768]{1,0:T(8,128)S(1)}, f32[1024,768]{1,0:T(8,128)}, u32[]{:S(2)}) copy-start(f32[1024,768]{1,0:T(8,128)} %get-tuple-element.138.raw_ref) | copy-start | bytes 9437188
  480.7 55.8 %copy-start.18 = (f32[1024,512]{1,0:T(8,128)S(1)}, f32[1024,512]{1,0:T(8,128)}, u32[]{:S(2)}) copy-start(f32[1024,512]{1,0:T(8,128)} %get-tuple-element.133.dq_ref) | copy-start | bytes 6291460
  480.7 55.9 %copy-start.48 = (s32[2]{0:T(128)S(1)}, s32[2]{0:T(128)}, u32[]{:S(2)}) copy-start(s32[2]{0:T(128)} %pad_add_fusion.2.place_ref) | copy-start | bytes 28
  536.5 5.3 copy-start.50
  541.8 6.3 copy-start.20
  549.7 2.5 copy-start.14
  641.4 20.3 %collective-permute-start.7 = (bf16[64,2048]{1,0:T(8,128)(2,1)S(1)}, bf16[64,2048]{1,0:T(8,128)(2,1)S(1)}, u32[]{:S(2)}, u32[]{:S(2)}) collective-permute-start(bf16[64,2048]{1,0:T(8,128)(2,1)S(1)} %get-tuple-element.193), channel_id=1, source_target_pairs={{0,4},{1,5},{2,0},{3,1},{4,6},{5,7},{6,2},{7,3},{8,12},{9,13},{10,... | collective-permute-start | bytes 786440 | tf_op jit(solution)/shard_map/ppermute | solution.py:423
  641.4 20.3 %collective-permute-start.6 = (bf16[64,2048]{1,0:T(8,128)(2,1)S(1)}, bf16[64,2048]{1,0:T(8,128)(2,1)}, u32[]{:S(2)}, u32[]{:S(2)}) collective-permute-start(bf16[64,2048]{1,0:T(8,128)(2,1)S(1)} %get-tuple-element.194), channel_id=1, source_target_pairs={{0,0},{1,1},{2,4},{3,5},{4,2},{5,3},{6,6},{7,7},{8,8},{9,9},{10,12... | collective-permute-start | bytes 786440 | tf_op jit(solution)/shard_map/ppermute | solution.py:423
  645.0 25.9 %collective-permute-start.8 = (bf16[256,1024]{1,0:T(8,128)(2,1)}, bf16[256,1024]{1,0:T(8,128)(2,1)}, u32[]{:S(2)}, u32[]{:S(2)}) collective-permute-start(bf16[256,1024]{1,0:T(8,128)(2,1)} %get-tuple-element.189), channel_id=1, source_target_pairs={{0,0},{1,1},{2,4},{3,5},{4,2},{5,3},{6,6},{7,7},{8,8},{9,9},{10,12... | collective-permute-start | bytes 1572872 | tf_op jit(solution)/shard_map/ppermute | solution.py:423
  650.4 26.5 %collective-permute-start.9 = (bf16[256,1024]{1,0:T(8,128)(2,1)}, bf16[256,1024]{1,0:T(8,128)(2,1)}, u32[]{:S(2)}, u32[]{:S(2)}) collective-permute-start(bf16[256,1024]{1,0:T(8,128)(2,1)} %get-tuple-element.190), channel_id=1, source_target_pairs={{0,4},{1,5},{2,0},{3,1},{4,6},{5,7},{6,2},{7,3},{8,12},{9,13},{10,... | collective-permute-start | bytes 1572872 | tf_op jit(solution)/shard_map/ppermute | solution.py:423
  650.6 2.8 copy-start.33
  650.6 3.3 copy-start.35
  667.5 31.2 %copy-start.60 = (f32[4352]{0:T(1024)S(1)}, f32[4352]{0:T(1024)}, u32[]{:S(2)}) copy-start(f32[4352]{0:T(1024)} %param.36) | copy-start | bytes 52228
  667.5 31.2 %copy-start.61 = (f32[4352]{0:T(1024)S(1)}, f32[4352]{0:T(1024)}, u32[]{:S(2)}) copy-start(f32[4352]{0:T(1024)} %param.37) | copy-start | bytes 52228
  (35 other events, 49.4 us)
Sparse Core Ops, SparseCore 0:
  83.3 83.2 all-gather.3
  169.0 83.1 all-gather.5
  256.0 69.1 all-gather.7
  328.1 70.2 reduce-scatter.4
  401.3 120.7 reduce-scatter.10
  524.9 35.1 reduce-scatter.6
  563.3 52.6 reduce-scatter.8

commit v7 on v6

--- a/solution.py
+++ b/solution.py
@@ -1552,9 +1552,9 @@
     )
     low_down = down_weight.astype(jnp.bfloat16)
     own_kv, w_out, low_down = lax.optimization_barrier((own_kv, w_out, low_down))
+    near_cotangent = move(after(cotangent, raw), OVER_L)
     ((lower_kv,),) = transfer("keys_up", 2, 40, Halves(own_kv, 0))
     lower_kv, near_up = lax.optimization_barrier((lower_kv, near_up))
-    near_cotangent = move(after(cotangent, lower_kv), OVER_L)
     up_blocks = over_plane(near_up)
     score_flops = 2 * count * count * query_width
     (attn_heads,) = attention_call(

time: 733 us -> 733 us (level)
  no operation moved by 1% of the time
where the time goes in v7:
time: 733 us; the launch traced here: 726 us
  Pallas kernels  518 us (71%)
  local copies, waits for them, and re-layouts  70.5 us (10%)
  starting transfers between devices  59 us (8%)
  other arithmetic  31.3 us (4%)
  between operations  20.2 us (3%)
  matrix products  15.4 us (2%)
  waiting for transfers between devices  11.5 us (2%)
    pallas_call x8, Pallas kernels, transfer(): pl.pallas_call(kernel, out_shape=[leaf for out in outs for leaf in out],...  348 us
    ppermute x10, starting transfers between devices, move(): return lax.ppermute(value, ('dp', 'mp'), pairs)  57.7 us
    unnamed x139, local copies, waits for them, and re-layouts  56.3 us
    pallas_call x2, Pallas kernels, attention_call(): pl.pallas_call(kernel, grid_spec=pltpu.PrefetchScalarGridSpec(num_scalar_...  33.1 us
    pallas_call x1, Pallas kernels, mlp_back(): pl.pallas_call(mlp_back_kernel, grid_spec=pltpu.PrefetchScalarGridSpec(nu...  22.6 us
    pallas_call x2, Pallas kernels, rows_back(): pl.pallas_call(rows_back_kernel, grid=(8,), in_specs=specs, out_specs=pl....  21.5 us
    pallas_call x1, Pallas kernels, mlp_front(): pl.pallas_call(mlp_front_kernel, grid=(units // columns,), in_specs=[pl.B...  18.8 us
    pallas_call x1, Pallas kernels, adam_all(): pl.pallas_call(lambda *refs: adam_kernel(*refs, rates=rates), grid_spec=p...  17.4 us
  transfers between devices with their start and end apart: 17, of which 2 were waited for; matrix products, arithmetic and copies ran while one was open for 6% of the time, Pallas kernels for 59%

profile of v7, /device:TPU:0, one launch (start us, length us, event | category | flops | bytes accessed | tf_op | source)
XLA Modules:
  0.0 725.7 jit_solution(18057989815568166078)
XLA Ops:
  10.4 2.1 convert_element_type.74
  15.3 61.3 %gather_first.1 = (bf16[8,256,1024]{2,1,0:T(8,128)(2,1)S(1)}, bf16[8,64,2048]{2,1,0:T(8,128)(2,1)S(1)}, bf16[4,256,2048]{2,1,0:T(8,128)(2,1)S(1)}, bf16[2,256,1536]{2,1,0:T(8,128)(2,1)S(1)}) custom-call(bf16[256,1024]{1,0:T(8,128)(2,1)S(1)} %convert_element_type.72.refs_0_, bf16[64,2048]{1,0:T(8,128)(2,1)S(1)} %convert_element_type.73.refs_1_, ...), custom_call_target="tpu_custom_call" | custom-call | bytes 247500000 | tf_op jit(solution)/shard_map/gather_first/pallas_call | solution.py:772
  81.1 2.1 copy-done.49
  83.2 12.3 %collective-permute-start.2 = (bf16[256,1536]{1,0:T(8,128)(2,1)}, bf16[256,1536]{1,0:T(8,128)(2,1)S(1)}, u32[]{:S(2)}, u32[]{:S(2)}) collective-permute-start(bf16[256,1536]{1,0:T(8,128)(2,1)} %get-tuple-element.104), channel_id=1, source_target_pairs={{4,0},{5,1},{0,2},{1,3},{6,4},{7,5},{2,6},{3,7},{12,8},{13,9},{8,1... | collective-permute-start | bytes 2359304 | tf_op jit(solution)/shard_map/ppermute | solution.py:423
  95.5 7.5 %collective-permute-start.1 = (bf16[256,1536]{1,0:T(8,128)(2,1)}, bf16[256,1536]{1,0:T(8,128)(2,1)}, u32[]{:S(2)}, u32[]{:S(2)}) collective-permute-start(bf16[256,1536]{1,0:T(8,128)(2,1)} %get-tuple-element.104), channel_id=1, source_target_pairs={{0,0},{1,1},{4,2},{5,3},{2,4},{3,5},{6,6},{7,7},{8,8},{9,9},{12,10... | collective-permute-start | bytes 2359304 | tf_op jit(solution)/shard_map/ppermute | solution.py:423
  104.8 3.8 gather_fusion
  111.2 9.3 %project.1 = (f32[1024,768]{1,0:T(8,128)}, bf16[1024,512]{1,0:T(8,128)(2,1)S(1)}, bf16[1024,512]{1,0:T(8,128)(2,1)S(1)}) custom-call(bf16[1024,2048]{1,0:T(8,128)(2,1)} %bitcast.74, bf16[8,256,1024]{2,1,0:T(8,128)(2,1)} %copy-done.13, f32[1024,128]{1,0:T(8,128)S(1)} %get-tuple-element.204.cos_ref, f32[1024,128]{1,0:T(8,128)S(1)} %get-tuple-element.205.sin_ref, ...), custom_call_target="tpu_custom_call" | custom-call | flops 4294967296 | bytes 16777216 | tf_op jit(solution)/shard_map/project/pallas_call | solution.py:910
  121.4 26.7 %keys_up.1.low_ref = bf16[1024,512]{1,0:T(8,128)(2,1)S(1)} custom-call(bf16[1024,512]{1,0:T(8,128)(2,1)S(1)} %get-tuple-element.103.refs_0_.own_ref), custom_call_target="tpu_custom_call" | custom-call | bytes 132000000 | tf_op jit(solution)/shard_map/keys_up/pallas_call | solution.py:772
  150.0 2.7 pad_maximum_fusion
  153.1 28.8 %collective-permute-start.3 = (bf16[256,2048]{1,0:T(8,128)(2,1)S(1)}, bf16[256,2048]{1,0:T(8,128)(2,1)}, u32[]{:S(2)}, u32[]{:S(2)}) collective-permute-start(bf16[256,2048]{1,0:T(8,128)(2,1)S(1)} %copy-done.15), channel_id=1, source_target_pairs={{1,0},{0,1},{3,2},{2,3},{5,4},{4,5},{7,6},{6,7},{9,8},{8,9},{11,10... | collective-permute-start | bytes 3145736 | tf_op jit(solution)/shard_map/ppermute | solution.py:423
  184.6 12.0 %attend.1.left_ref = bf16[1024,512]{1,0:T(8,128)(2,1)} custom-call(s32[2]{0:T(128)} %pad_add_fusion.2.place_ref, s32[1024,1]{1,0:T(8,128)} %copy.45.time_ref, s32[1024,1]{1,0:T(8,128)} %bitcast.82, bf16[1024,512]{1,0:T(8,128)(2,1)} %copy-done.53, bf16[1024,512]{1,0:T(8,128)(2,1)} %copy-done.31, bf16[1024,512]{1,0:T(8,128)(2,1)} %copy-done.30), custom_call_target="tpu_custom_call" | custom-call | flops 2147483648 | bytes 16777216 | tf_op jit(solution)/shard_map/attend/pallas_call | solution.py:1115
  196.6 3.6 convolution_convert_fusion
  200.2 5.4 collective-permute-done.3.refs_2_
  205.6 47.2 %sum_attention.1 = (bf16[256,2048]{1,0:T(8,128)(2,1)S(1)}, bf16[256,2048]{1,0:T(8,128)(2,1)S(1)}, bf16[2,192,2048]{2,1,0:T(8,128)(2,1)S(1)}) custom-call(bf16[4,256,2048]{2,1,0:T(8,128)(2,1)S(1)} %bitcast.62, bf16[192,2048]{1,0:T(8,128)(2,1)S(1)} %convert_element_type.76.refs_1_), custom_call_target="tpu_custom_call" | custom-call | bytes 165000000 | tf_op jit(solution)/shard_map/sum_attention/pallas_call | solution.py:772
  256.0 2.2 copy-done.4
  263.6 27.8 %gather_mid.1 = (bf16[4,256,2048]{2,1,0:T(8,128)(2,1)S(1)}, bf16[4,256,2048]{2,1,0:T(8,128)(2,1)S(1)}) custom-call(bf16[256,2048]{1,0:T(8,128)(2,1)S(1)} %get-tuple-element.114.refs_0_, bf16[256,2048]{1,0:T(8,128)(2,1)S(1)} %copy-done.15, bf16[256,2048]{1,0:T(8,128)(2,1)} %collective-permute-done.3.refs_2_), custom_call_target="tpu_custom_call" | custom-call | bytes 112200000 | tf_op jit(solution)/shard_map/gather_mid/pallas_call | solution.py:772
  295.5 18.8 %mlp_front.1 = (f32[1024,1536]{1,0:T(8,128)}, f32[1024,1536]{1,0:T(8,128)}, bf16[1024,1536]{1,0:T(8,128)(2,1)}) custom-call(bf16[1024,2048]{1,0:T(8,128)(2,1)} %bitcast.66, bf16[8,256,1536]{2,1,0:T(8,128)(2,1)} %all-gather.4.cloned.1.call-done.gate_ref.refs_1_, bf16[8,256,1536]{2,1,0:T(8,128)(2,1)} %all-gather.6.cloned.1.call-done.up_ref.refs_3_), custom_call_target="tpu_custom_call" | custom-call | flops 12884901888 | bytes 33554432 | tf_op jit(solution)/shard_map/mlp_front/pallas_call | solution.py:1245
  316.2 10.4 %slot_grad.2 = bf16[8,192,2048]{2,1,0:T(8,128)(2,1)} custom-call(s32[8]{0:T(128)S(1)} %broadcast_xor_fusion.slot_ref, bf16[1024,1536]{1,0:T(8,128)(2,1)S(1)} %copy-done.54, bf16[1024,2048]{1,0:T(8,128)(2,1)} %bitcast.76), custom_call_target="tpu_custom_call" | custom-call | flops 6442450944 | bytes 16777216 | tf_op jit(solution)/shard_map/slot_grad/pallas_call | solution.py:1419
  327.2 22.6 %mlp_back.1 = (bf16[1024,1536]{1,0:T(8,128)(2,1)S(1)}, bf16[1024,1536]{1,0:T(8,128)(2,1)}, bf16[4,256,2048]{2,1,0:T(8,128)(2,1)}) custom-call(s32[8]{0:T(128)S(1)} %broadcast_xor_fusion.slot_ref, bf16[1024,2048]{1,0:T(8,128)(2,1)} %bitcast.77, f32[1024,1536]{1,0:T(8,128)} %get-tuple-element.120.gate_ref, f32[1024,1536]{1,0:T(8,128)} %get-tuple-element.121.up_ref, ...), custom_call_target="tpu_custom_call" | custom-call | flops 12884901888 | bytes 33554432 | tf_op jit(solution)/shard_map/mlp_back/pallas_call | solution.py:1296
  349.8 2.1 copy-done.5
  351.9 2.8 copy-done.10
  354.7 15.0 %mid_rows.1.refs_0_.own_ref = bf16[4,256,2048]{2,1,0:T(8,128)(2,1)S(1)} custom-call(bf16[1024,1536]{1,0:T(8,128)(2,1)S(1)} %get-tuple-element.125.refs_0_.refs_2_, bf16[8,256,1536]{2,1,0:T(8,128)(2,1)S(1)} %bitcast.65, bf16[1024,1536]{1,0:T(8,128)(2,1)S(1)} %copy-done.5, bf16[8,256,1536]{2,1,0:T(8,128)(2,1)S(1)} %copy-done.10), custom_call_target="tpu_custom_call" | custom-call | flops 1610612736 | bytes 2097152 | tf_op jit(solution)/shard_map/mid_rows/pallas_call | solution.py:1341
  369.8 29.4 %sum_mid.1 = (bf16[256,2048]{1,0:T(8,128)(2,1)S(1)}, bf16[256,2048]{1,0:T(8,128)(2,1)S(1)}, bf16[8,256,3072]{2,1,0:T(8,128)(2,1)}) custom-call(bf16[4,256,2048]{2,1,0:T(8,128)(2,1)S(1)} %mid_rows.1.refs_0_.own_ref, bf16[1024,2048]{1,0:T(8,128)(2,1)} %bitcast.67, bf16[1024,1536]{1,0:T(8,128)(2,1)S(1)} %get-tuple-element.125.refs_0_.refs_2_, ...), custom_call_target="tpu_custom_call" | custom-call | bytes 108900000 | tf_op jit(solution)/shard_map/sum_mid/pallas_call | solution.py:772
  401.2 6.0 mix_back.1
  408.7 27.6 %gather_attention.1 = bf16[4,256,2048]{2,1,0:T(8,128)(2,1)S(1)} custom-call(bf16[256,2048]{1,0:T(8,128)(2,1)S(1)} %copy-done.29), custom_call_target="tpu_custom_call" | custom-call | bytes 95700000 | tf_op jit(solution)/shard_map/gather_attention/pallas_call | solution.py:772
  438.3 2.5 slice_bitcast_fusion
  443.0 5.5 convolution_convert_fusion.2.grad_ref
  448.6 5.6 slot_grad.3
  455.5 21.1 %attend_back.1 = (f32[1024,512]{1,0:T(8,128)}, bf16[1024,512]{1,0:T(8,128)(2,1)}, f32[1024,512]{1,0:T(8,128)}) custom-call(s32[2]{0:T(128)} %pad_add_fusion.2.place_ref, s32[1024,1]{1,0:T(8,128)} %copy.45.time_ref, s32[1024,1]{1,0:T(8,128)} %bitcast.83, bf16[1024,512]{1,0:T(8,128)(2,1)} %copy-done.53, bf16[1024,512]{1,0:T(8,128)(2,1)} %copy-done.31, ...), custom_call_target="tpu_custom_call" | custom-call | flops 5368709120 | bytes 16777216 | tf_op jit(solution)/shard_map/attend_back/pallas_call | solution.py:1115
  477.0 2.4 copy-done.9
  480.6 53.9 %keys_down.1 = (bf16[1024,512]{1,0:T(8,128)(2,1)S(1)}, bf16[256,2048]{1,0:T(8,128)(2,1)S(1)}, bf16[256,2048]{1,0:T(8,128)(2,1)S(1)}) custom-call(bf16[1024,512]{1,0:T(8,128)(2,1)S(1)} %copy-done.28, bf16[4,256,2048]{2,1,0:T(8,128)(2,1)S(1)} %copy-done.9), custom_call_target="tpu_custom_call" | custom-call | bytes 174900000 | tf_op jit(solution)/shard_map/keys_down/pallas_call | solution.py:772
  536.5 5.2 unproject.1
  541.8 6.3 convolution_convert_fusion.1
  549.7 2.5 copy-done.14
  552.2 6.4 in_rows.1.refs_0_.own_ref
  560.6 2.2 copy-done.1
  564.7 73.6 %sum_in.1 = (bf16[256,2048]{1,0:T(8,128)(2,1)S(1)}, bf16[256,2048]{1,0:T(8,128)(2,1)S(1)}, bf16[2,256,3072]{2,1,0:T(8,128)(2,1)S(1)}) custom-call(bf16[4,256,2048]{2,1,0:T(8,128)(2,1)S(1)} %copy-done.1, bf16[2,256,3072]{2,1,0:T(8,128)(2,1)S(1)} %copy-done.17), custom_call_target="tpu_custom_call" | custom-call | bytes 244200000 | tf_op jit(solution)/shard_map/sum_in/pallas_call | solution.py:772
  642.8 2.2 slice_bitcast_fusion.3
  645.0 5.4 collective-permute-start.8
  650.6 2.2 add_bitcast_fusion.refs_8_
  653.9 2.8 fusion.1
  656.7 3.5 convert_add_fusion.1
  661.7 5.8 in_back.1
  668.4 2.5 convert_add_fusion.3
  670.9 5.9 collective-permute-done.9
  676.9 3.0 convert_add_fusion.2
  683.1 11.7 %sum_all.1 = f32[40,128]{1,0:T(8,128)} custom-call(f32[40,128]{1,0:T(8,128)} %pad_bitcast_fusion.value), custom_call_target="tpu_custom_call" | custom-call | tf_op jit(solution)/shard_map/sum_all/pallas_call | solution.py:862
  700.1 17.4 %adam_all.1 = (f32[256,1024]{1,0:T(8,128)}, f32[256,1024]{1,0:T(8,128)}, f32[256,1024]{1,0:T(8,128)}, f32[256,3072]{1,0:T(8,128)}, f32[256,3072]{1,0:T(8,128)}, ...) custom-call(f32[1]{0:T(128)} %bitcast.28.refs_0_, ...), custom_call_target="tpu_custom_call" | custom-call | bytes 50331648 | tf_op jit(solution)/shard_map/adam_all/pallas_call | solution.py:1392
  (200 shorter events, 66.3 us)
Async XLA Ops:
  7.2 288.3 %all-gather.4.cloned.1.call-start = ((), (), s32[]{:S(2)}) async-start(), calls=%async_computation.4 | async-start | bytes 7864320 | tf_op jit(solution)/shard_map/all_gather | solution.py:803
  8.0 5.5 copy-start.44
  8.0 248.0 %copy-start.45 = (f32[2048]{0:T(1024)}, f32[2048]{0:T(1024)S(1)}, u32[]{:S(2)}) copy-start(f32[2048]{0:T(1024)S(1)} %get-tuple-element.195) | copy-start | bytes 24580
  13.5 313.7 %copy-start.46 = (s32[8]{0:T(128)}, s32[8]{0:T(128)S(1)}, u32[]{:S(2)}) copy-start(s32[8]{0:T(128)S(1)} %broadcast_xor_fusion.slot_ref) | copy-start | bytes 100
  15.3 87.7 %copy-start.62 = (s32[1,4]{1,0:T(1,128)S(1)}, s32[1,4]{1,0:T(1,128)}, u32[]{:S(2)}) copy-start(s32[1,4]{1,0:T(1,128)} %param.21) | copy-start | bytes 52
  83.2 212.4 %all-gather.6.cloned.1.call-start = ((), (), s32[]{:S(2)}) async-start(), calls=%async_computation.5 | async-start | bytes 7864320 | tf_op jit(solution)/shard_map/all_gather | solution.py:803
  83.2 65.9 %collective-permute-start.2 = (bf16[256,1536]{1,0:T(8,128)(2,1)}, bf16[256,1536]{1,0:T(8,128)(2,1)S(1)}, u32[]{:S(2)}, u32[]{:S(2)}) collective-permute-start(bf16[256,1536]{1,0:T(8,128)(2,1)} %get-tuple-element.104), channel_id=1, source_target_pairs={{4,0},{5,1},{0,2},{1,3},{6,4},{7,5},{2,6},{3,7},{12,8},{13,9},{8,1... | collective-permute-start | bytes 2359304 | tf_op jit(solution)/shard_map/ppermute | solution.py:423
  95.5 53.6 %collective-permute-start.1 = (bf16[256,1536]{1,0:T(8,128)(2,1)}, bf16[256,1536]{1,0:T(8,128)(2,1)}, u32[]{:S(2)}, u32[]{:S(2)}) collective-permute-start(bf16[256,1536]{1,0:T(8,128)(2,1)} %get-tuple-element.104), channel_id=1, source_target_pairs={{0,0},{1,1},{4,2},{5,3},{2,4},{3,5},{6,6},{7,7},{8,8},{9,9},{12,10... | collective-permute-start | bytes 2359304 | tf_op jit(solution)/shard_map/ppermute | solution.py:423
  102.9 5.6 collective-permute-start
  104.7 3.8 copy-start.58
  111.2 9.3 %copy-start.22 = (f32[1024,128]{1,0:T(8,128)}, f32[1024,128]{1,0:T(8,128)S(1)}, u32[]{:S(2)}) copy-start(f32[1024,128]{1,0:T(8,128)S(1)} %get-tuple-element.205.sin_ref) | copy-start | bytes 1572868
  121.4 27.7 %copy-start.30 = (bf16[1024,512]{1,0:T(8,128)(2,1)}, bf16[1024,512]{1,0:T(8,128)(2,1)S(1)}, u32[]{:S(2)}) copy-start(bf16[1024,512]{1,0:T(8,128)(2,1)S(1)} %get-tuple-element.103.refs_0_.own_ref) | copy-start | bytes 3145732
  150.0 3.1 copy-start.15
  152.8 173.8 %all-gather.8.cloned.1.call-start = ((), (), s32[]{:S(2)}) async-start(), calls=%async_computation.6 | async-start | bytes 7864320 | tf_op jit(solution)/shard_map/all_gather | solution.py:803
  153.1 52.5 %collective-permute-start.3 = (bf16[256,2048]{1,0:T(8,128)(2,1)S(1)}, bf16[256,2048]{1,0:T(8,128)(2,1)}, u32[]{:S(2)}, u32[]{:S(2)}) collective-permute-start(bf16[256,2048]{1,0:T(8,128)(2,1)S(1)} %copy-done.15), channel_id=1, source_target_pairs={{1,0},{0,1},{3,2},{2,3},{5,4},{4,5},{7,6},{6,7},{9,8},{8,9},{11,10... | collective-permute-start | bytes 3145736 | tf_op jit(solution)/shard_map/ppermute | solution.py:423
  184.6 12.0 %copy-start.55 = (bf16[8,64,2048]{2,1,0:T(8,128)(2,1)S(1)}, bf16[8,64,2048]{2,1,0:T(8,128)(2,1)}, u32[]{:S(2)}) copy-start(bf16[8,64,2048]{2,1,0:T(8,128)(2,1)} %gather_fusion) | copy-start | bytes 6291460
  200.2 52.6 %copy-start.3 = (bf16[1024,2048]{1,0:T(8,128)(2,1)}, bf16[1024,2048]{1,0:T(8,128)(2,1)S(1)}, u32[]{:S(2)}) copy-start(bf16[1024,2048]{1,0:T(8,128)(2,1)S(1)} %convolution_convert_fusion) | copy-start | bytes 12582916
  255.9 182.4 %reduce-scatter.5.cloned.1.call-start = ((), (), s32[]{:S(2)}) async-start(), calls=%async_computation.7 | async-start | bytes 7864320 | tf_op jit(solution)/shard_map/reduce_scatter | solution.py:807
  256.0 2.2 copy-start.4
  326.6 234.0 %reduce-scatter.11.cloned.1.call-start = ((), (), s32[]{:S(2)}) async-start(), calls=%async_computation.10 | async-start | bytes 15728640 | tf_op jit(solution)/shard_map/reduce_scatter | solution.py:807
  327.2 22.6 %slice-start = ((s8[6291456]{0:T(1024)(128)(4,1)}), s8[4194304]{0:T(1024)(128)(4,1)S(1)}, s32[]{:S(2)}) async-start(s8[6291456]{0:T(1024)(128)(4,1)} %bitcast.64), calls=%async_computation.11 | async-start | bytes 8388608
  327.2 22.6 %slice-start.1 = ((s8[6291456]{0:T(1024)(128)(4,1)}), s8[2097152]{0:T(1024)(128)(4,1)S(1)}, s32[]{:S(2)}) async-start(s8[6291456]{0:T(1024)(128)(4,1)} %bitcast.64), calls=%async_computation.12 | async-start | bytes 4194304
  351.9 2.8 copy-start.10
  369.8 29.4 %copy-start.2 = (bf16[4,256,2048]{2,1,0:T(8,128)(2,1)}, bf16[4,256,2048]{2,1,0:T(8,128)(2,1)S(1)}, u32[]{:S(2)}) copy-start(bf16[4,256,2048]{2,1,0:T(8,128)(2,1)S(1)} %mid_rows.1.refs_0_.own_ref) | copy-start | bytes 12582916
  401.1 239.1 %reduce-scatter.7.cloned.1.call-start = ((), (), s32[]{:S(2)}) async-start(), calls=%async_computation.8 | async-start | bytes 2621440 | tf_op jit(solution)/shard_map/reduce_scatter | solution.py:807
  438.3 4.7 copy-start.56
  440.8 35.8 %collective-permute-start.5 = (bf16[192,2048]{1,0:T(8,128)(2,1)}, bf16[192,2048]{1,0:T(8,128)(2,1)}, u32[]{:S(2)}, u32[]{:S(2)}) collective-permute-start(bf16[192,2048]{1,0:T(8,128)(2,1)} %get-tuple-element.183), channel_id=1, source_target_pairs={{0,4},{1,5},{2,0},{3,1},{4,6},{5,7},{6,2},{7,3},{8,12},{9,13},{10,... | collective-permute-start | bytes 2359304 | tf_op jit(solution)/shard_map/ppermute | solution.py:423
  441.2 7.4 %copy-start.47 = (s32[8]{0:T(128)S(1)}, s32[8]{0:T(128)}, u32[]{:S(2)}) copy-start(s32[8]{0:T(128)} %copy-done.46) | copy-start | bytes 100
  441.2 7.4 %copy-start.52 = (bf16[1024,512]{1,0:T(8,128)(2,1)S(1)}, bf16[1024,512]{1,0:T(8,128)(2,1)}, u32[]{:S(2)}) copy-start(bf16[1024,512]{1,0:T(8,128)(2,1)} %attend.1.left_ref) | copy-start | bytes 3145732
  441.2 35.4 %collective-permute-start.4 = (bf16[192,2048]{1,0:T(8,128)(2,1)S(1)}, bf16[192,2048]{1,0:T(8,128)(2,1)}, u32[]{:S(2)}, u32[]{:S(2)}) collective-permute-start(bf16[192,2048]{1,0:T(8,128)(2,1)S(1)} %get-tuple-element.184), channel_id=1, source_target_pairs={{0,0},{1,1},{2,4},{3,5},{4,2},{5,3},{6,6},{7,7},{8,8},{9,9},{10,12... | collective-permute-start | bytes 2359304 | tf_op jit(solution)/shard_map/ppermute | solution.py:423
  455.5 80.9 %copy-start.23 = (f32[1024,128]{1,0:T(8,128)S(1)}, f32[1024,128]{1,0:T(8,128)}, u32[]{:S(2)}) copy-start(f32[1024,128]{1,0:T(8,128)} %copy-done.22) | copy-start | bytes 1572868
  476.7 59.8 %copy-start.19 = (f32[1024,512]{1,0:T(8,128)S(1)}, f32[1024,512]{1,0:T(8,128)}, u32[]{:S(2)}) copy-start(f32[1024,512]{1,0:T(8,128)} %get-tuple-element.135.own_ref) | copy-start | bytes 6291460
  476.7 163.6 %reduce-scatter.9.cloned.1.call-start = ((), (), s32[]{:S(2)}) async-start(), calls=%async_computation.9 | async-start | bytes 5242880 | tf_op jit(solution)/shard_map/reduce_scatter | solution.py:807
  477.0 2.4 copy-start.9
  480.6 55.9 %copy-start.16 = (f32[1024,768]{1,0:T(8,128)S(1)}, f32[1024,768]{1,0:T(8,128)}, u32[]{:S(2)}) copy-start(f32[1024,768]{1,0:T(8,128)} %get-tuple-element.107.raw_ref) | copy-start | bytes 9437188
  480.6 55.9 %copy-start.18 = (f32[1024,512]{1,0:T(8,128)S(1)}, f32[1024,512]{1,0:T(8,128)}, u32[]{:S(2)}) copy-start(f32[1024,512]{1,0:T(8,128)} %get-tuple-element.134.dq_ref) | copy-start | bytes 6291460
  480.6 55.9 %copy-start.48 = (s32[2]{0:T(128)S(1)}, s32[2]{0:T(128)}, u32[]{:S(2)}) copy-start(s32[2]{0:T(128)} %pad_add_fusion.2.place_ref) | copy-start | bytes 28
  536.5 5.3 copy-start.50
  541.7 6.3 copy-start.20
  549.7 2.5 copy-start.14
  641.3 20.3 %collective-permute-start.7 = (bf16[64,2048]{1,0:T(8,128)(2,1)S(1)}, bf16[64,2048]{1,0:T(8,128)(2,1)S(1)}, u32[]{:S(2)}, u32[]{:S(2)}) collective-permute-start(bf16[64,2048]{1,0:T(8,128)(2,1)S(1)} %get-tuple-element.193), channel_id=1, source_target_pairs={{0,4},{1,5},{2,0},{3,1},{4,6},{5,7},{6,2},{7,3},{8,12},{9,13},{10,... | collective-permute-start | bytes 786440 | tf_op jit(solution)/shard_map/ppermute | solution.py:423
  641.4 20.3 %collective-permute-start.6 = (bf16[64,2048]{1,0:T(8,128)(2,1)S(1)}, bf16[64,2048]{1,0:T(8,128)(2,1)}, u32[]{:S(2)}, u32[]{:S(2)}) collective-permute-start(bf16[64,2048]{1,0:T(8,128)(2,1)S(1)} %get-tuple-element.194), channel_id=1, source_target_pairs={{0,0},{1,1},{2,4},{3,5},{4,2},{5,3},{6,6},{7,7},{8,8},{9,9},{10,12... | collective-permute-start | bytes 786440 | tf_op jit(solution)/shard_map/ppermute | solution.py:423
  645.0 25.9 %collective-permute-start.8 = (bf16[256,1024]{1,0:T(8,128)(2,1)}, bf16[256,1024]{1,0:T(8,128)(2,1)}, u32[]{:S(2)}, u32[]{:S(2)}) collective-permute-start(bf16[256,1024]{1,0:T(8,128)(2,1)} %get-tuple-element.189), channel_id=1, source_target_pairs={{0,0},{1,1},{2,4},{3,5},{4,2},{5,3},{6,6},{7,7},{8,8},{9,9},{10,12... | collective-permute-start | bytes 1572872 | tf_op jit(solution)/shard_map/ppermute | solution.py:423
  650.4 26.5 %collective-permute-start.9 = (bf16[256,1024]{1,0:T(8,128)(2,1)}, bf16[256,1024]{1,0:T(8,128)(2,1)}, u32[]{:S(2)}, u32[]{:S(2)}) collective-permute-start(bf16[256,1024]{1,0:T(8,128)(2,1)} %get-tuple-element.190), channel_id=1, source_target_pairs={{0,4},{1,5},{2,0},{3,1},{4,6},{5,7},{6,2},{7,3},{8,12},{9,13},{10,... | collective-permute-start | bytes 1572872 | tf_op jit(solution)/shard_map/ppermute | solution.py:423
  650.6 2.8 copy-start.33
  650.6 3.3 copy-start.35
  667.5 31.2 %copy-start.60 = (f32[4352]{0:T(1024)S(1)}, f32[4352]{0:T(1024)}, u32[]{:S(2)}) copy-start(f32[4352]{0:T(1024)} %param.36) | copy-start | bytes 52228
  667.5 31.2 %copy-start.61 = (f32[4352]{0:T(1024)S(1)}, f32[4352]{0:T(1024)}, u32[]{:S(2)}) copy-start(f32[4352]{0:T(1024)} %param.37) | copy-start | bytes 52228
  (35 other events, 49.4 us)
Sparse Core Ops, SparseCore 0:
  83.3 83.2 all-gather.3
  169.0 83.1 all-gather.5
  256.0 69.1 all-gather.7
  328.1 70.2 reduce-scatter.4
  401.3 120.7 reduce-scatter.10
  524.9 35.1 reduce-scatter.6
  563.3 52.6 reduce-scatter.8
